TPU v7x, 32 devices: a whole 2x2x4 slice. The times are simulated.
32 devices in a mesh: rep: 4 (over y, x), wide: 8 (over z, core).
Axes of the slice: x: 2, y: 2, z: 4, core: 2. Of those that a mesh axis runs over, the one named last changes fastest.
Arguments:
- tokens: bfloat16 [64, 576, 768], P(('rep', 'wide')), may hold values from -6 to 6
- live_count: int32 [32], P(('rep', 'wide')), may hold values from 1 to 2, as said below
- dataset_id: int32 [64], P(('rep', 'wide')), may hold values from 0 to 9
- shift_flag: int32 [64], P(('rep', 'wide')), may hold values 0 or 1
- norm_gains: bfloat16 [2, 768], P(None, 'wide'), may hold values from 0.099609375 to 1.8984375
- w_qkv: bfloat16 [768, 2304], P('wide'), may hold values from -0.21875 to 0.21875
- w_attn_out: bfloat16 [768, 768], P('wide'), may hold values from -0.625 to 0.625
- w_fc1: bfloat16 [768, 3072], P('wide'), may hold values from -0.21875 to 0.21875
- w_fc2: bfloat16 [3072, 768], P('wide'), may hold values from -0.109375 to 0.109375
- w_reassemble: bfloat16 [768, 256], P('wide'), may hold values from -0.21875 to 0.21875
- conv_kernels: bfloat16 [4, 2304, 256], P(None, 'wide'), may hold values from -0.125 to 0.125
- w_head: bfloat16 [256, 256], P('wide'), may hold values from -0.375 to 0.375
- scale_table: bfloat16 [10, 256], P(None, 'wide'), may hold values from 0.5 to 2
- shift_table: bfloat16 [10, 256], P(None, 'wide'), may hold values from -3 to 3
- d_tokens_out: bfloat16 [64, 576, 768], P(('rep', 'wide')), may hold values from -6 to 6
- d_joined: bfloat16 [64, 2304, 256], P(('rep', 'wide')), may hold values from -6 to 6
Outputs:
- tokens_out: bfloat16 [64, 576, 768], P(('rep', 'wide'))
- joined: bfloat16 [64, 2304, 256], P(('rep', 'wide'))
- d_tokens: bfloat16 [64, 576, 768], P(('rep', 'wide'))
- g_norm_gains: float32 [2, 768], P(None, 'wide')
- g_w_qkv: float32 [768, 2304], P('wide')
- g_w_attn_out: float32 [768, 768], P('wide')
- g_w_fc1: float32 [768, 3072], P('wide')
- g_w_fc2: float32 [3072, 768], P('wide')
- g_w_reassemble: float32 [768, 256], P('wide')
- g_conv_kernels: float32 [4, 2304, 256], P(None, 'wide')
- g_w_head: float32 [256, 256], P('wide')
- g_scale_table: float32 [10, 256], P(None, 'wide')
- g_shift_table: float32 [10, 256], P(None, 'wide')
Inputs may be any that keep to these rules, and one draw needn't show every extreme that they name: `live_count`: each device's count of live slots; slots at or past it are left out of every output and sum; the first device holds 2, the last one 1.
All inputs are finite; a program needn't handle non-finite values. No bound on the sum of `shift_flag` on one device may be relied on, other than what follows from the above.
Results may differ from a plain program's by a relative error of at most 0.024.
Values may be sent and summed in bfloat16 or wider, within the bound.
No kernel may reach another device: no remote copies, remote signals or barrier semaphores. Data moves between devices by JAX's collectives and lax.ppermute only.
A program may use at most 320 MiB of HBM per device.

v0:
```python
import jax
import jax.numpy as jnp
from jax import lax
from jax.sharding import PartitionSpec as P

D = 768
HEADS = 12
HD = 64
GRID = 24
DATASETS = 10


HIGH = lax.Precision.HIGHEST


def product(left, right):
    return jnp.dot(left, right, preferred_element_type=jnp.float32)


def product_tn(left, right):
    return lax.dot_general(
        left, right, (((0,), (0,)), ((), ())), preferred_element_type=jnp.float32
    )


def product_nt(left, right):
    return lax.dot_general(
        left, right, (((1,), (1,)), ((), ())), preferred_element_type=jnp.float32
    )


def tuple_adder(running_total, summand_terms):
    return tuple(
        (
            summed_result + summand_term
            for summed_result, summand_term in zip(running_total, summand_terms)
        )
    )


def smooth_act(values):
    return jax.nn.gelu(values, approximate=False)


def gelu_back(pre_values, grad_values):
    return jax.vjp(smooth_act, pre_values)[1](grad_values)[0]


def normalize(values):
    centred = values - jnp.mean(values, -1, keepdims=True)
    recip = lax.rsqrt(jnp.mean(centred * centred, -1, keepdims=True) + 1e-06)
    return (centred * recip, recip)


def norm_transpose(grad_normed, normed, recip):
    return recip * (
        grad_normed
        - jnp.mean(grad_normed, -1, keepdims=True)
        - normed * jnp.mean(grad_normed * normed, -1, keepdims=True)
    )


def upsample_table():
    target = jnp.arange(2 * GRID, dtype=jnp.int32)
    numer = target * (GRID - 1)
    lower = numer // (2 * GRID - 1)
    frac_part = (numer - lower * (2 * GRID - 1)).astype(jnp.float32) / (2 * GRID - 1)
    source = jnp.arange(GRID, dtype=jnp.int32)
    below = (source[None, :] == lower[:, None]).astype(jnp.float32) * (1.0 - frac_part[:, None])
    above = (source[None, :] == lower[:, None] + 1).astype(jnp.float32) * frac_part[:, None]
    return below + above


def upsample(field):
    grid_map = field.reshape(GRID, GRID, field.shape[-1])
    table = upsample_table()
    half_way = jnp.einsum("ay,yxc->axc", table, grid_map, precision=HIGH)
    return jnp.einsum("bx,axc->abc", table, half_way, precision=HIGH).reshape(
        4 * GRID * GRID, field.shape[-1]
    )


def upsample_adjoint(grad_map):
    grid_map = grad_map.reshape(2 * GRID, 2 * GRID, grad_map.shape[-1])
    table = upsample_table()
    half_way = jnp.einsum("ay,abc->ybc", table, grid_map, precision=HIGH)
    return jnp.einsum("bx,ybc->yxc", table, half_way, precision=HIGH).reshape(
        GRID * GRID, grad_map.shape[-1]
    )


def columns(field):
    grid_map = field.reshape(GRID, GRID, field.shape[-1])
    padded = jnp.pad(grid_map, ((1, 1), (1, 1), (0, 0)))
    parts = [
        padded[row_off : row_off + GRID, col_off : col_off + GRID, :]
        for row_off in range(3)
        for col_off in range(3)
    ]
    return jnp.concatenate(parts, axis=-1).reshape(GRID * GRID, 9 * field.shape[-1])


def columns_adjoint(grad_cols):
    channels = grad_cols.shape[1] // 9
    blocks = grad_cols.reshape(GRID, GRID, 9, channels)
    padded = jnp.zeros((GRID + 2, GRID + 2, channels), jnp.float32)
    for row_off in range(3):
        for col_off in range(3):
            padded = padded.at[row_off : row_off + GRID, col_off : col_off + GRID, :].add(
                blocks[:, :, 3 * row_off + col_off, :]
            )
    return padded[1:-1, 1:-1, :].reshape(GRID * GRID, channels)


def attention_weights(queries, key_rows, lse_kept):
    scores = (
        jnp.einsum("phd,qhd->hpq", queries, key_rows, preferred_element_type=jnp.float32) * 0.125
    )
    if lse_kept is None:
        top_score = jnp.max(scores, -1, keepdims=True)
        lse_rows = top_score[..., 0] + jnp.log(jnp.sum(jnp.exp(scores - top_score), -1))
    else:
        lse_rows = lse_kept
    attn_prob = jnp.exp(scores - lse_rows[..., None])
    return (attn_prob, attn_prob.astype(jnp.bfloat16), lse_rows)


def run_forward(weights, image_rows, hot_row, flag_value, lse_kept):
    (
        norm_gain,
        w_qkv,
        w_attn_out,
        w_fc1,
        w_fc2,
        w_reassemble,
        conv_kernels,
        w_head,
        scale_table,
        shift_table,
    ) = weights
    row_count = image_rows.shape[0]
    stored = {}
    x_input = image_rows.astype(jnp.float32)
    normed_one, recip_one = normalize(x_input)
    first_in = (normed_one * norm_gain[0].astype(jnp.float32)).astype(jnp.bfloat16)
    qkv_rows = product(first_in, w_qkv).astype(jnp.bfloat16)
    queries = qkv_rows[:, :D].reshape(row_count, HEADS, HD)
    key_rows = qkv_rows[:, D : 2 * D].reshape(row_count, HEADS, HD)
    value_rows = qkv_rows[:, 2 * D :].reshape(row_count, HEADS, HD)
    attn_prob, prob_low, lse_rows = attention_weights(queries, key_rows, lse_kept)
    mixed = (
        jnp.einsum("hpq,qhd->phd", prob_low, value_rows, preferred_element_type=jnp.float32)
        .reshape(row_count, D)
        .astype(jnp.bfloat16)
    )
    middle = x_input + product(mixed, w_attn_out)
    normed_two, recip_two = normalize(middle)
    second_in = (normed_two * norm_gain[1].astype(jnp.float32)).astype(jnp.bfloat16)
    hidden = product(second_in, w_fc1)
    gelu_out = smooth_act(hidden).astype(jnp.bfloat16)
    block_out = middle + product(gelu_out, w_fc2)
    block_low = block_out.astype(jnp.bfloat16)
    feature = product(block_low, w_reassemble)
    unit_inputs = []
    first_acts = []
    inner_maps = []
    second_acts = []
    for unit in range(2):
        unit_inputs.append(feature)
        first_act = smooth_act(feature).astype(jnp.bfloat16)
        inner = product(columns(first_act), conv_kernels[2 * unit])
        second_act = smooth_act(inner).astype(jnp.bfloat16)
        feature = feature + product(columns(second_act), conv_kernels[2 * unit + 1])
        first_acts.append(first_act)
        inner_maps.append(inner)
        second_acts.append(second_act)
    head_in = upsample(feature).astype(jnp.bfloat16)
    head_out = product(head_in, w_head)
    scale_row = jnp.sum(hot_row[:, None] * scale_table.astype(jnp.float32), 0)
    shift_row = flag_value * jnp.sum(hot_row[:, None] * shift_table.astype(jnp.float32), 0)
    stored["normed_one"] = normed_one
    stored["recip_one"] = recip_one
    stored["first_in"] = first_in
    stored["queries"] = queries
    stored["key_rows"] = key_rows
    stored["value_rows"] = value_rows
    stored["lse_rows"] = lse_rows
    stored["attn_prob"] = attn_prob
    stored["prob_low"] = prob_low
    stored["mixed"] = mixed
    stored["normed_two"] = normed_two
    stored["recip_two"] = recip_two
    stored["second_in"] = second_in
    stored["hidden"] = hidden
    stored["gelu_out"] = gelu_out
    stored["block_out"] = block_out
    stored["block_low"] = block_low
    stored["unit_inputs"] = unit_inputs
    stored["first_acts"] = first_acts
    stored["inner_maps"] = inner_maps
    stored["second_acts"] = second_acts
    stored["head_in"] = head_in
    stored["head_out"] = head_out
    stored["scale_row"] = scale_row
    stored["joined"] = head_out * scale_row[None, :] + shift_row[None, :]
    return stored


def unit_backward(unit_input, first_act, inner, second_act, kernel_one, kernel_two, grad_out):
    grad_second = grad_out.astype(jnp.bfloat16)
    grad_kernel_two = product_tn(columns(second_act), grad_second)
    grad_inner = gelu_back(inner, columns_adjoint(product_nt(grad_second, kernel_two))).astype(
        jnp.bfloat16
    )
    grad_kernel_one = product_tn(columns(first_act), grad_inner)
    grad_input = grad_out + gelu_back(
        unit_input, columns_adjoint(product_nt(grad_inner, kernel_one))
    )
    return (grad_input, grad_kernel_one, grad_kernel_two)


def backward_joining(weights, stored, hot_row, flag_value, grad_out, grad_map):
    (
        norm_gain,
        w_qkv,
        w_attn_out,
        w_fc1,
        w_fc2,
        w_reassemble,
        conv_kernels,
        w_head,
        scale_table,
        shift_table,
    ) = weights
    grad_scale = hot_row[:, None] * jnp.sum(grad_map * stored["head_out"], 0)[None, :]
    grad_shift = hot_row[:, None] * (flag_value * jnp.sum(grad_map, 0))[None, :]
    grad_head = (grad_map * stored["scale_row"][None, :]).astype(jnp.bfloat16)
    grad_w_head = product_tn(stored["head_in"], grad_head)
    grad_feature = upsample_adjoint(product_nt(grad_head, w_head))
    kernel_grads = [None, None, None, None]
    for unit in (1, 0):
        grad_feature, kernel_grads[2 * unit], kernel_grads[2 * unit + 1] = unit_backward(
            stored["unit_inputs"][unit],
            stored["first_acts"][unit],
            stored["inner_maps"][unit],
            stored["second_acts"][unit],
            conv_kernels[2 * unit],
            conv_kernels[2 * unit + 1],
            grad_feature,
        )
    grad_reassembled = grad_feature.astype(jnp.bfloat16)
    reassemble_weight_grad = product_tn(stored["block_low"], grad_reassembled)
    grad_block = grad_out + product_nt(grad_reassembled, w_reassemble)
    return (
        grad_block,
        (reassemble_weight_grad, jnp.stack(kernel_grads), grad_w_head, grad_scale, grad_shift),
    )


def backward_mlp(weights, stored, grad_block):
    (
        norm_gain,
        w_qkv,
        w_attn_out,
        w_fc1,
        w_fc2,
        w_reassemble,
        conv_kernels,
        w_head,
        scale_table,
        shift_table,
    ) = weights
    grad_mlp = grad_block.astype(jnp.bfloat16)
    grad_w_fc2 = product_tn(stored["gelu_out"], grad_mlp)
    grad_gelu = product_nt(grad_mlp, w_fc2)
    grad_hidden = gelu_back(stored["hidden"], grad_gelu).astype(jnp.bfloat16)
    grad_w_fc1 = product_tn(stored["second_in"], grad_hidden)
    grad_second_in = product_nt(grad_hidden, w_fc1)
    grad_gain_two = jnp.sum(grad_second_in * stored["normed_two"], 0)
    grad_middle = grad_block + norm_transpose(
        grad_second_in * norm_gain[1].astype(jnp.float32), stored["normed_two"], stored["recip_two"]
    )
    return (grad_middle, (grad_gain_two, grad_w_fc1, grad_w_fc2))


def backward_attention(weights, stored, attn_prob, prob_low, grad_middle):
    (
        norm_gain,
        w_qkv,
        w_attn_out,
        w_fc1,
        w_fc2,
        w_reassemble,
        conv_kernels,
        w_head,
        scale_table,
        shift_table,
    ) = weights
    row_count = grad_middle.shape[0]
    grad_attn = grad_middle.astype(jnp.bfloat16)
    grad_w_attn_out = product_tn(stored["mixed"], grad_attn)
    grad_mixed = (
        product_nt(grad_attn, w_attn_out).astype(jnp.bfloat16).reshape(row_count, HEADS, HD)
    )
    value_grad = jnp.einsum(
        "hpq,phd->qhd", prob_low, grad_mixed, preferred_element_type=jnp.float32
    )
    prob_grad = jnp.einsum(
        "phd,qhd->hpq", grad_mixed, stored["value_rows"], preferred_element_type=jnp.float32
    )
    score_grad = (
        attn_prob * (prob_grad - jnp.sum(attn_prob * prob_grad, -1, keepdims=True))
    ).astype(jnp.bfloat16)
    query_grad = (
        jnp.einsum(
            "hpq,qhd->phd", score_grad, stored["key_rows"], preferred_element_type=jnp.float32
        )
        * 0.125
    )
    key_grad = (
        jnp.einsum(
            "hpq,phd->qhd", score_grad, stored["queries"], preferred_element_type=jnp.float32
        )
        * 0.125
    )
    qkv_grad = jnp.concatenate(
        [
            query_grad.reshape(row_count, D),
            key_grad.reshape(row_count, D),
            value_grad.reshape(row_count, D),
        ],
        axis=1,
    ).astype(jnp.bfloat16)
    grad_w_qkv = product_tn(stored["first_in"], qkv_grad)
    grad_first_in = product_nt(qkv_grad, w_qkv)
    grad_gain_one = jnp.sum(grad_first_in * stored["normed_one"], 0)
    grad_input = grad_middle + norm_transpose(
        grad_first_in * norm_gain[0].astype(jnp.float32), stored["normed_one"], stored["recip_one"]
    )
    return (grad_input, (grad_gain_one, grad_w_qkv, grad_w_attn_out))


def run_backward(weights, stored, hot_row, flag_value, grad_out, grad_map):
    grad_block, joining_grads = backward_joining(
        weights, stored, hot_row, flag_value, grad_out, grad_map
    )
    grad_middle, mlp_grads = backward_mlp(weights, stored, grad_block)
    grad_input, attn_grads = backward_attention(
        weights, stored, stored["attn_prob"], stored["prob_low"], grad_middle
    )
    grad_terms = (
        jnp.stack([attn_grads[0], mlp_grads[0]]),
        attn_grads[1],
        attn_grads[2],
        mlp_grads[1],
        mlp_grads[2],
        joining_grads[0],
        joining_grads[1],
        joining_grads[2],
        joining_grads[3],
        joining_grads[4],
    )
    return (grad_input.astype(jnp.bfloat16), grad_terms)


def shards(
    tokens,
    live_count,
    dataset_id,
    shift_flag,
    norm_gains,
    w_qkv,
    w_attn_out,
    w_fc1,
    w_fc2,
    w_reassemble,
    conv_kernels,
    w_head,
    scale_table,
    shift_table,
    d_tokens_out,
    d_joined,
):
    gathered = (
        lax.all_gather(norm_gains, "wide", axis=1, tiled=True),
        lax.all_gather(w_qkv, "wide", axis=0, tiled=True),
        lax.all_gather(w_attn_out, "wide", axis=0, tiled=True),
        lax.all_gather(w_fc1, "wide", axis=0, tiled=True),
        lax.all_gather(w_fc2, "wide", axis=0, tiled=True),
        lax.all_gather(w_reassemble, "wide", axis=0, tiled=True),
        lax.all_gather(conv_kernels, "wide", axis=1, tiled=True),
        lax.all_gather(w_head, "wide", axis=0, tiled=True),
        lax.all_gather(scale_table, "wide", axis=1, tiled=True),
        lax.all_gather(shift_table, "wide", axis=1, tiled=True),
    )
    slot_count = tokens.shape[0]
    live_mask = (jnp.arange(slot_count, dtype=jnp.int32) < live_count[0]).astype(jnp.float32)
    onehot = (dataset_id[:, None] == jnp.arange(DATASETS, dtype=jnp.int32)[None, :]).astype(
        jnp.float32
    )
    flag_values = shift_flag.astype(jnp.float32)

    def forward_image(packed):
        image_rows, hot_row, flag_value, live_value = packed
        stored = run_forward(gathered, image_rows, hot_row, flag_value, None)
        return (
            (stored["block_out"] * live_value).astype(jnp.bfloat16),
            (stored["joined"] * live_value).astype(jnp.bfloat16),
            stored["lse_rows"],
        )

    tokens_out, joined, lse_all = lax.map(forward_image, (tokens, onehot, flag_values, live_mask))
    weights_back = (
        lax.all_gather(norm_gains, "wide", axis=1, tiled=True),
        lax.all_gather(w_qkv, "wide", axis=0, tiled=True),
        lax.all_gather(w_attn_out, "wide", axis=0, tiled=True),
        lax.all_gather(w_fc1, "wide", axis=0, tiled=True),
        lax.all_gather(w_fc2, "wide", axis=0, tiled=True),
        lax.all_gather(w_reassemble, "wide", axis=0, tiled=True),
        lax.all_gather(conv_kernels, "wide", axis=1, tiled=True),
        lax.all_gather(w_head, "wide", axis=0, tiled=True),
        lax.all_gather(scale_table, "wide", axis=1, tiled=True),
        lax.all_gather(shift_table, "wide", axis=1, tiled=True),
    )
    start_sums = tuple((jnp.zeros(weight.shape, jnp.float32) for weight in weights_back))

    def backward_image(running_total, packed):
        image_rows, hot_row, flag_value, live_value, lse_kept, grad_rows, grad_field = packed
        stored = run_forward(weights_back, image_rows, hot_row, flag_value, lse_kept)
        grad_input, grad_terms = run_backward(
            weights_back,
            stored,
            hot_row,
            flag_value,
            grad_rows.astype(jnp.float32) * live_value,
            grad_field.astype(jnp.float32) * live_value,
        )
        return (tuple_adder(running_total, grad_terms), grad_input)

    grad_sums, d_tokens = lax.scan(
        backward_image,
        start_sums,
        (tokens, onehot, flag_values, live_mask, lse_all, d_tokens_out, d_joined),
    )
    shares = (
        lax.psum_scatter(
            grad_sums[0].astype(jnp.bfloat16), "wide", scatter_dimension=1, tiled=True
        ).astype(jnp.float32),
        lax.psum_scatter(
            grad_sums[1].astype(jnp.bfloat16), "wide", scatter_dimension=0, tiled=True
        ).astype(jnp.float32),
        lax.psum_scatter(
            grad_sums[2].astype(jnp.bfloat16), "wide", scatter_dimension=0, tiled=True
        ).astype(jnp.float32),
        lax.psum_scatter(
            grad_sums[3].astype(jnp.bfloat16), "wide", scatter_dimension=0, tiled=True
        ).astype(jnp.float32),
        lax.psum_scatter(
            grad_sums[4].astype(jnp.bfloat16), "wide", scatter_dimension=0, tiled=True
        ).astype(jnp.float32),
        lax.psum_scatter(
            grad_sums[5].astype(jnp.bfloat16), "wide", scatter_dimension=0, tiled=True
        ).astype(jnp.float32),
        lax.psum_scatter(
            grad_sums[6].astype(jnp.bfloat16), "wide", scatter_dimension=1, tiled=True
        ).astype(jnp.float32),
        lax.psum_scatter(
            grad_sums[7].astype(jnp.bfloat16), "wide", scatter_dimension=0, tiled=True
        ).astype(jnp.float32),
        lax.psum_scatter(
            grad_sums[8].astype(jnp.bfloat16), "wide", scatter_dimension=1, tiled=True
        ).astype(jnp.float32),
        lax.psum_scatter(
            grad_sums[9].astype(jnp.bfloat16), "wide", scatter_dimension=1, tiled=True
        ).astype(jnp.float32),
    )
    totals = (
        lax.psum(shares[0].astype(jnp.bfloat16), "rep").astype(jnp.float32),
        lax.psum(shares[1].astype(jnp.bfloat16), "rep").astype(jnp.float32),
        lax.psum(shares[2].astype(jnp.bfloat16), "rep").astype(jnp.float32),
        lax.psum(shares[3].astype(jnp.bfloat16), "rep").astype(jnp.float32),
        lax.psum(shares[4].astype(jnp.bfloat16), "rep").astype(jnp.float32),
        lax.psum(shares[5].astype(jnp.bfloat16), "rep").astype(jnp.float32),
        lax.psum(shares[6].astype(jnp.bfloat16), "rep").astype(jnp.float32),
        lax.psum(shares[7].astype(jnp.bfloat16), "rep").astype(jnp.float32),
        lax.psum(shares[8].astype(jnp.bfloat16), "rep").astype(jnp.float32),
        lax.psum(shares[9].astype(jnp.bfloat16), "rep").astype(jnp.float32),
    )
    return (
        tokens_out,
        joined,
        d_tokens,
        totals[0],
        totals[1],
        totals[2],
        totals[3],
        totals[4],
        totals[5],
        totals[6],
        totals[7],
        totals[8],
        totals[9],
    )


def solution(mesh):
    placed = (
        P(("rep", "wide"), None, None),
        P(("rep", "wide")),
        P(("rep", "wide")),
        P(("rep", "wide")),
        P(None, "wide"),
        P("wide", None),
        P("wide", None),
        P("wide", None),
        P("wide", None),
        P("wide", None),
        P(None, "wide", None),
        P("wide", None),
        P(None, "wide"),
        P(None, "wide"),
        P(("rep", "wide"), None, None),
        P(("rep", "wide"), None, None),
    )
    return jax.shard_map(
        shards,
        mesh=mesh,
        in_specs=placed,
        out_specs=(
            P(("rep", "wide"), None, None),
            P(("rep", "wide"), None, None),
            P(("rep", "wide"), None, None),
            P(None, "wide"),
            P("wide", None),
            P("wide", None),
            P("wide", None),
            P("wide", None),
            P("wide", None),
            P(None, "wide", None),
            P("wide", None),
            P(None, "wide"),
            P(None, "wide"),
        ),
        check_vma=False,
    )
```

profile of v0, /device:TPU:0, one launch (start us, length us, event | category | flops | bytes accessed | tf_op | source)
XLA Modules:
  0.0 1819.1 jit_solution(18035901510217829841)
XLA Ops:
  12.5 13.5 all-gather
  26.2 14.1 all-gather.1
  40.4 14.2 all-gather.2
  54.8 15.4 all_gather.46
  70.7 16.8 all_gather.44
  88.2 44.9 %all-gather.13.cloned.1.call-done = bf16[768,3072]{1,0:T(8,128)(2,1)} async-done(((bf16[96,3072]{1,0:T(8,128)(2,1)}), bf16[768,3072]{1,0:T(8,128)(2,1)}) %all-gather.13.cloned.1.call-update) | async-done | bytes 4718608 | tf_op jit(solution)/shard_map/all_gather | solution.py:388
  133.0 52.0 %all-gather.15.cloned.1.call-done = bf16[3072,768]{1,0:T(8,128)(2,1)} async-done(((bf16[384,768]{1,0:T(8,128)(2,1)}), bf16[3072,768]{1,0:T(8,128)(2,1)}) %all-gather.15.cloned.1.call-update) | async-done | bytes 4718608 | tf_op jit(solution)/shard_map/all_gather | solution.py:389
  185.1 52.0 %all-gather.17.cloned.1.call-done = bf16[4,2304,256]{2,1,0:T(8,128)(2,1)} async-done(((bf16[4,288,256]{2,1,0:T(8,128)(2,1)}), bf16[4,2304,256]{2,1,0:T(8,128)(2,1)}) %all-gather.17.cloned.1.call-update) | async-done | bytes 4718608 | tf_op jit(solution)/shard_map/all_gather | solution.py:391
  238.3 193.5 %while.86 = (s32[]{:T(128)}, bf16[2,576,768]{2,1,0:T(8,128)(2,1)}, bf16[2,2304,256]{2,1,0:T(8,128)(2,1)}, f32[2,12,576]{2,1,0:T(8,128)}, bf16[2,576,768]{2,1,0:T...) while((s32[]{:T(128)}, bf16[2,576,768]{2,1,0:T(8,128)(2,1)}, ...), condition=%wide.region_9.10_spmd, body=%wide.region_0.9_spmd.sunk | while | flops 12875440128 | bytes 189870096 | solution.py:412
  257.9 10.1 multiply_reduce_fusion.17
  268.0 9.0 exponential_reduce_fusion.2
  277.7 9.4 fusion.618
  289.1 25.1 %fusion.620 = (bf16[2,576,768]{2,1,0:T(8,128)(2,1)}, bf16[576,768]{1,0:T(8,128)(2,1)}) fusion(bf16[2,576,768]{2,1,0:T(8,128)(2,1)} %get-tuple-element.2035, s32[]{:T(128)S(6)} %copy.412, f32[]{:T(128)} %bitcast.922, f32[576,768]{1,0:T(8,128)S(1)} %get-tuple-element.1856, bf16[3072,768]{1,0:T(8,128)(2,1)} %get-tuple-element.2062, ...), kind=kOutput, calls=%fused_computation.63.clone.1 | convolution fusion | flops 5554372608 | bytes 14758404 | tf_op jit(solution)/shard_map/while/body/eval_jaxpr/dot_general | solution.py:17
  354.2 10.1 multiply_reduce_fusion.17
  364.3 9.0 exponential_reduce_fusion.2
  374.0 9.4 fusion.618
  385.4 24.9 %fusion.620 = (bf16[2,576,768]{2,1,0:T(8,128)(2,1)}, bf16[576,768]{1,0:T(8,128)(2,1)}) fusion(bf16[2,576,768]{2,1,0:T(8,128)(2,1)} %get-tuple-element.2035, s32[]{:T(128)S(6)} %copy.412, f32[]{:T(128)} %bitcast.922, f32[576,768]{1,0:T(8,128)S(1)} %get-tuple-element.1856, bf16[3072,768]{1,0:T(8,128)(2,1)} %get-tuple-element.2062, ...), kind=kOutput, calls=%fused_computation.63.clone.1 | convolution fusion | flops 5554372608 | bytes 14758404 | tf_op jit(solution)/shard_map/while/body/eval_jaxpr/dot_general | solution.py:17
  433.2 846.1 %while.87 = (s32[]{:T(128)}, f32[2,768]{1,0:T(2,128)}, f32[768,2304]{1,0:T(8,128)}, f32[768,768]{1,0:T(8,128)}, f32[768,3072]{1,0:T(8,128)}, /*index=5*/f32[3072...) while((s32[]{:T(128)}, f32[2,768]{1,0:T(2,128)}, ...), condition=%wide.region_26.27_spmd.clone, body=%wide.region_10.26_spmd.clone.sunk | while | flops 38107766784 | bytes 1198951808 | solution.py:440
  472.6 21.8 %multiply_convert_fusion.35 = (bf16[576,3072]{1,0:T(8,128)(2,1)S(1)}, f32[576,3072]{1,0:T(8,128)}, f32[576,3072]{1,0:T(8,128)}) fusion(bf16[768,3072]{1,0:T(8,128)(2,1)} %get-tuple-element.2163, f32[576,768]{1,0:T(8,128)S(1)} %get-tuple-element.1936, f32[768]{0:T(1024)S(1)} %get-tuple-element.1937, f32[576]{0:T(1024)S(1)} %add_rsqrt_fusion.11, ...), kind=kOutput, calls=%fused_computation.297.clone.1 | convolution fusion | flops 2834694144 | bytes 24190464 | tf_op jit(solution)/shard_map/while/body/eval_jaxpr/dot_general | solution.py:17
  528.5 7.4 scatter-add.281
  539.9 7.4 scatter-add.282
  589.5 7.4 scatter-add.288
  601.0 7.4 scatter-add.289
  650.8 7.4 scatter-add.295
  661.4 6.3 scatter-add.296
  707.4 7.4 scatter-add.302
  718.0 6.3 scatter-add.303
  755.5 9.5 add_convert_fusion.5
  773.9 10.4 convolution_convert_fusion.20
  786.9 8.6 select_add_fusion.22
  795.6 6.2 select_add_fusion.23
  801.9 15.2 multiply_reduce_fusion.22
  817.1 12.4 multiply_convert_fusion.41
  840.4 10.1 select_add_fusion.20
  888.7 21.5 %multiply_convert_fusion.35 = (bf16[576,3072]{1,0:T(8,128)(2,1)S(1)}, f32[576,3072]{1,0:T(8,128)}, f32[576,3072]{1,0:T(8,128)}) fusion(bf16[768,3072]{1,0:T(8,128)(2,1)} %get-tuple-element.2163, f32[576,768]{1,0:T(8,128)S(1)} %get-tuple-element.1936, f32[768]{0:T(1024)S(1)} %get-tuple-element.1937, f32[576]{0:T(1024)S(1)} %add_rsqrt_fusion.11, ...), kind=kOutput, calls=%fused_computation.297.clone.1 | convolution fusion | flops 2834694144 | bytes 24190464 | tf_op jit(solution)/shard_map/while/body/eval_jaxpr/dot_general | solution.py:17
  944.6 7.4 scatter-add.281
  956.0 7.4 scatter-add.282
  1005.6 7.4 scatter-add.288
  1017.0 7.4 scatter-add.289
  1066.9 7.4 scatter-add.295
  1077.5 6.3 scatter-add.296
  1115.4 9.0 maximum_add_fusion.5
  1127.9 7.4 scatter-add.302
  1138.5 6.3 scatter-add.303
  1176.0 9.5 add_convert_fusion.5
  1194.6 10.4 convolution_convert_fusion.20
  1209.4 10.2 select_add_fusion.22
  1226.2 15.2 multiply_reduce_fusion.22
  1241.4 12.4 multiply_convert_fusion.41
  1264.8 11.1 select_add_fusion.20
  1295.8 6.6 convert_element_type.556
  1302.5 6.4 convert_element_type.558
  1309.0 6.4 convert_element_type.562
  1316.8 23.9 %reduce-scatter.35.cloned.1.call-done = bf16[32,10]{1,0:T(8,128)(2,1)} async-done(((bf16[256,10]{1,0:T(8,128)(2,1)}), bf16[32,10]{1,0:T(8,128)(2,1)}) %reduce-scatter.35.cloned.1.call-update) | async-done | bytes 656
  1342.1 29.6 %reduce-scatter.33.cloned.1.call-done = bf16[32,10]{1,0:T(8,128)(2,1)} async-done(((bf16[256,10]{1,0:T(8,128)(2,1)}), bf16[32,10]{1,0:T(8,128)(2,1)}) %reduce-scatter.33.cloned.1.call-update) | async-done | bytes 656
  1373.1 29.8 %reduce-scatter.29.cloned.1.call-done = bf16[32,256]{1,0:T(8,128)(2,1)} async-done(((bf16[256,256]{1,0:T(8,128)(2,1)}), bf16[32,256]{1,0:T(8,128)(2,1)}) %reduce-scatter.29.cloned.1.call-update) | async-done | bytes 16400 | tf_op jit(solution)/shard_map/reduce_scatter | solution.py:467
  1402.9 31.5 %reduce-scatter.25.cloned.1.call-done = bf16[96,256]{1,0:T(8,128)(2,1)} async-done(((bf16[768,256]{1,0:T(8,128)(2,1)}), bf16[96,256]{1,0:T(8,128)(2,1)}) %reduce-scatter.25.cloned.1.call-update) | async-done | bytes 49168 | tf_op jit(solution)/shard_map/reduce_scatter | solution.py:461
  1434.4 33.9 %reduce-scatter.19.cloned.1.call-done = bf16[96,768]{1,0:T(8,128)(2,1)} async-done(((bf16[768,768]{1,0:T(8,128)(2,1)}), bf16[96,768]{1,0:T(8,128)(2,1)}) %reduce-scatter.19.cloned.1.call-update) | async-done | bytes 147472 | tf_op jit(solution)/shard_map/reduce_scatter | solution.py:452
  1468.3 44.3 %reduce-scatter.17.cloned.1.call-done = bf16[96,2304]{1,0:T(8,128)(2,1)} async-done(((bf16[768,2304]{1,0:T(8,128)(2,1)}), bf16[96,2304]{1,0:T(8,128)(2,1)}) %reduce-scatter.17.cloned.1.call-update) | async-done | bytes 442384 | tf_op jit(solution)/shard_map/reduce_scatter | solution.py:449
  1512.6 55.8 %reduce-scatter.21.cloned.1.call-done = bf16[96,3072]{1,0:T(8,128)(2,1)} async-done(((bf16[768,3072]{1,0:T(8,128)(2,1)}), bf16[96,3072]{1,0:T(8,128)(2,1)}) %reduce-scatter.21.cloned.1.call-update) | async-done | bytes 589840 | tf_op jit(solution)/shard_map/reduce_scatter | solution.py:455
  1568.4 55.5 %reduce-scatter.23.cloned.1.call-done = bf16[384,768]{1,0:T(8,128)(2,1)} async-done(((bf16[3072,768]{1,0:T(8,128)(2,1)}), bf16[384,768]{1,0:T(8,128)(2,1)}) %reduce-scatter.23.cloned.1.call-update) | async-done | bytes 589840 | tf_op jit(solution)/shard_map/reduce_scatter | solution.py:458
  1623.9 55.5 %reduce-scatter.27.cloned.1.call-done = bf16[4,288,256]{2,1,0:T(8,128)(2,1)} async-done(((bf16[4,2304,256]{2,1,0:T(8,128)(2,1)}), bf16[4,288,256]{2,1,0:T(8,128)(2,1)}) %reduce-scatter.27.cloned.1.call-update) | async-done | bytes 589840 | tf_op jit(solution)/shard_map/reduce_scatter | solution.py:464
  1679.5 44.9 %all-reduce.17.cloned.1.call-done = (bf16[2,96]{1,0:T(2,128)(2,1)}, bf16[96,256]{1,0:T(8,128)(2,1)}, bf16[32,256]{1,0:T(8,128)(2,1)}, bf16[10,32]{1,0:T(8,128)(2,1)}, bf16[10,32]{1,0:T(8,128)(2,1)}) async-done(((bf16[2,96]{1,0:T(2,128)(2,1)}, bf16[96,256]{1,0:T(8,128)(2,1)}, bf16[32,256]{1,0:T(8,128)(2,1)}, bf16[10,32]{1,0:T(8,128)(2,1)}, bf16[10,32]{1,0:T(8,128)(2,1)}), (bf16[2,96]{1,0:T(2,128)(2,1)}, ...) | async-done | bytes 67216 | tf_op jit(solution)/shard_map/psum | solution.py:478
  1730.9 73.2 %all-reduce.19.cloned.1.call-done = (bf16[96,2304]{1,0:T(8,128)(2,1)}, bf16[96,768]{1,0:T(8,128)(2,1)}, bf16[96,3072]{1,0:T(8,128)(2,1)}, bf16[384,768]{1,0:T(8,128)(2,1)}, bf16[4,288,256]{2,1,0:T(8,128)(2,1)}) async-done(((bf16[96,2304]{1,0:T(8,128)(2,1)}, bf16[96,768]{1,0:T(8,128)(2,1)}, bf16[96,3072]{1,0:T(8,128)(2,1)}, bf16[384,768]{1,0:T(8,128)(2,1)}, bf16[4,288,256]{2,1,0:T(8,128)(2,1)}), ...) | async-done | bytes 2359312 | tf_op jit(solution)/shard_map/psum | solution.py:479
  (999 shorter events, 656.1 us)
Async XLA Ops:
  7.2 47.6 %copy-start.86 = (bf16[32,256]{1,0:T(8,128)(2,1)S(1)}, bf16[32,256]{1,0:T(8,128)(2,1)}, u32[]{:S(2)}) copy-start(bf16[32,256]{1,0:T(8,128)(2,1)} %param.103) | copy-start | bytes 49156
  7.2 63.5 %copy-start.83 = (bf16[96,256]{1,0:T(8,128)(2,1)S(1)}, bf16[96,256]{1,0:T(8,128)(2,1)}, u32[]{:S(2)}) copy-start(bf16[96,256]{1,0:T(8,128)(2,1)} %param.101) | copy-start | bytes 147460
  7.2 80.3 %copy-start.92 = (s32[2]{0:T(128)S(1)}, s32[2]{0:T(128)}, u32[]{:S(2)}) copy-start(s32[2]{0:T(128)} %param.94) | copy-start | bytes 28
  7.2 231.1 %copy-start.10 = (bf16[2,576,768]{2,1,0:T(8,128)(2,1)S(1)}, bf16[2,576,768]{2,1,0:T(8,128)(2,1)}, u32[]{:S(2)}) copy-start(bf16[2,576,768]{2,1,0:T(8,128)(2,1)} %param.92) | copy-start | bytes 5308420
  7.2 80.9 %all-gather.11.cloned.1.call-start = ((), (), s32[]{:S(2)}) async-start(), calls=%async_computation.11 | async-start | bytes 1327104 | tf_op jit(solution)/shard_map/all_gather | solution.py:387
  8.0 80.2 %all-gather.9.cloned.1.call-start = ((), (), s32[]{:S(2)}) async-start(), calls=%async_computation.10 | async-start | bytes 3981312 | tf_op jit(solution)/shard_map/all_gather | solution.py:386
  8.7 124.3 %all-gather.13.cloned.1.call-start = ((), (), s32[]{:S(2)}) async-start(), calls=%async_computation.12 | async-start | bytes 5308416 | tf_op jit(solution)/shard_map/all_gather | solution.py:388
  9.4 175.6 %all-gather.15.cloned.1.call-start = ((), (), s32[]{:S(2)}) async-start(), calls=%async_computation.13 | async-start | bytes 5308416 | tf_op jit(solution)/shard_map/all_gather | solution.py:389
  10.0 227.0 %all-gather.17.cloned.1.call-start = ((), (), s32[]{:S(2)}) async-start(), calls=%async_computation.14 | async-start | bytes 5308416 | tf_op jit(solution)/shard_map/all_gather | solution.py:391
  10.6 1304.8 %reduce-scatter.31.cloned.1.call-start = ((), (), s32[]{:S(2)}) async-start(), calls=%async_computation.22 | async-start | bytes 221184
  434.9 13.0 copy-start.47
  434.9 13.0 copy-start.49
  435.0 13.7 copy-start.11
  444.4 18.6 %copy-start.32 = (f32[12,576]{1,0:T(8,128)}, f32[12,576]{1,0:T(8,128)S(1)}, u32[]{:S(2)}) copy-start(f32[12,576]{1,0:T(8,128)S(1)} %dynamic-slice_bitcast_fusion.2) | copy-start | bytes 82948 | tf_op jit(solution)/shard_map/while
  453.0 10.0 copy-start.15
  469.5 24.8 %slice-start.9 = ((s8[4718592]{0:T(1024)(128)(4,1)}), s8[4194304]{0:T(1024)(128)(4,1)S(1)}, s32[]{:S(2)}) async-start(s8[4718592]{0:T(1024)(128)(4,1)} %bitcast.1271), calls=%async_computation.36 | async-start | bytes 8388608 | tf_op jit(solution)/shard_map/while
  469.5 30.7 %slice-start.5 = ((s8[4718592]{0:T(1024)(128)(4,1)}), s8[4194304]{0:T(1024)(128)(4,1)S(1)}, s32[]{:S(2)}) async-start(s8[4718592]{0:T(1024)(128)(4,1)} %bitcast.1163), calls=%async_computation.32 | async-start | bytes 8388608 | tf_op jit(solution)/shard_map/while
  472.5 21.8 %slice-start.10 = ((s8[4718592]{0:T(1024)(128)(4,1)}), s8[524288]{0:T(1024)(128)(4,1)S(1)}, s32[]{:S(2)}) async-start(s8[4718592]{0:T(1024)(128)(4,1)} %bitcast.1271), calls=%async_computation.37 | async-start | bytes 1048576 | tf_op jit(solution)/shard_map/while
  472.5 27.6 %slice-start.6 = ((s8[4718592]{0:T(1024)(128)(4,1)}), s8[524288]{0:T(1024)(128)(4,1)S(1)}, s32[]{:S(2)}) async-start(s8[4718592]{0:T(1024)(128)(4,1)} %bitcast.1163), calls=%async_computation.33 | async-start | bytes 1048576 | tf_op jit(solution)/shard_map/while
  752.8 12.2 slice-start.7
  755.5 12.9 copy-start.6
  773.9 10.4 copy-start.25
  784.3 11.2 slice-start
  801.8 15.2 copy-start.1
  817.1 12.5 copy-start.9
  840.4 10.2 copy-start.46
  840.4 10.2 copy-start.13
  840.4 10.2 copy-start.48
  840.4 10.2 copy-start.50
  851.1 13.0 copy-start.47
  851.1 13.0 copy-start.49
  851.1 13.7 copy-start.11
  860.5 18.5 %copy-start.32 = (f32[12,576]{1,0:T(8,128)}, f32[12,576]{1,0:T(8,128)S(1)}, u32[]{:S(2)}) copy-start(f32[12,576]{1,0:T(8,128)S(1)} %dynamic-slice_bitcast_fusion.2) | copy-start | bytes 82948 | tf_op jit(solution)/shard_map/while
  869.1 10.0 copy-start.15
  885.6 24.6 %slice-start.9 = ((s8[4718592]{0:T(1024)(128)(4,1)}), s8[4194304]{0:T(1024)(128)(4,1)S(1)}, s32[]{:S(2)}) async-start(s8[4718592]{0:T(1024)(128)(4,1)} %bitcast.1271), calls=%async_computation.36 | async-start | bytes 8388608 | tf_op jit(solution)/shard_map/while
  885.6 30.5 %slice-start.5 = ((s8[4718592]{0:T(1024)(128)(4,1)}), s8[4194304]{0:T(1024)(128)(4,1)S(1)}, s32[]{:S(2)}) async-start(s8[4718592]{0:T(1024)(128)(4,1)} %bitcast.1163), calls=%async_computation.32 | async-start | bytes 8388608 | tf_op jit(solution)/shard_map/while
  888.6 21.6 %slice-start.10 = ((s8[4718592]{0:T(1024)(128)(4,1)}), s8[524288]{0:T(1024)(128)(4,1)S(1)}, s32[]{:S(2)}) async-start(s8[4718592]{0:T(1024)(128)(4,1)} %bitcast.1271), calls=%async_computation.37 | async-start | bytes 1048576 | tf_op jit(solution)/shard_map/while
  888.6 27.4 %slice-start.6 = ((s8[4718592]{0:T(1024)(128)(4,1)}), s8[524288]{0:T(1024)(128)(4,1)S(1)}, s32[]{:S(2)}) async-start(s8[4718592]{0:T(1024)(128)(4,1)} %bitcast.1163), calls=%async_computation.33 | async-start | bytes 1048576 | tf_op jit(solution)/shard_map/while
  1173.3 12.2 slice-start.7
  1176.0 12.9 copy-start.6
  1176.0 9.5 slice-start.8
  1194.6 10.4 copy-start.25
  1205.1 14.5 slice-start
  1209.4 10.2 slice-start.1
  1209.4 10.2 slice-start.2
  1209.4 10.2 copy-start.7
  1209.4 10.5 copy-start.20
  1226.2 15.3 copy-start.1
  1241.4 12.5 copy-start.9
  1264.8 11.2 copy-start.46
  1264.8 11.1 copy-start.13
  1264.8 11.1 copy-start.48
  1264.8 11.1 copy-start.50
  1280.9 59.8 %reduce-scatter.35.cloned.1.call-start = ((), (), s32[]{:S(2)}) async-start(), calls=%async_computation.24 | async-start | bytes 73728
  1282.4 89.3 %reduce-scatter.33.cloned.1.call-start = ((), (), s32[]{:S(2)}) async-start(), calls=%async_computation.23 | async-start | bytes 73728
  1284.0 118.9 %reduce-scatter.29.cloned.1.call-start = ((), (), s32[]{:S(2)}) async-start(), calls=%async_computation.21 | async-start | bytes 147456 | tf_op jit(solution)/shard_map/reduce_scatter | solution.py:467
  1285.7 148.7 %reduce-scatter.25.cloned.1.call-start = ((), (), s32[]{:S(2)}) async-start(), calls=%async_computation.19 | async-start | bytes 442368 | tf_op jit(solution)/shard_map/reduce_scatter | solution.py:461
  1287.7 180.7 %reduce-scatter.19.cloned.1.call-start = ((), (), s32[]{:S(2)}) async-start(), calls=%async_computation.16 | async-start | bytes 1327104 | tf_op jit(solution)/shard_map/reduce_scatter | solution.py:452
  1290.5 222.1 %reduce-scatter.17.cloned.1.call-start = ((), (), s32[]{:S(2)}) async-start(), calls=%async_computation.15 | async-start | bytes 3981312 | tf_op jit(solution)/shard_map/reduce_scatter | solution.py:449
  1295.8 272.7 %reduce-scatter.21.cloned.1.call-start = ((), (), s32[]{:S(2)}) async-start(), calls=%async_computation.17 | async-start | bytes 5308416 | tf_op jit(solution)/shard_map/reduce_scatter | solution.py:455
  1302.5 321.4 %reduce-scatter.23.cloned.1.call-start = ((), (), s32[]{:S(2)}) async-start(), calls=%async_computation.18 | async-start | bytes 5308416 | tf_op jit(solution)/shard_map/reduce_scatter | solution.py:458
  1308.9 370.5 %reduce-scatter.27.cloned.1.call-start = ((), (), s32[]{:S(2)}) async-start(), calls=%async_computation.20 | async-start | bytes 5308416 | tf_op jit(solution)/shard_map/reduce_scatter | solution.py:464
  1315.4 409.0 %all-reduce.17.cloned.1.call-start = ((), (), s32[]{:S(2)}) async-start(), calls=%async_computation.25 | async-start | bytes 148480 | tf_op jit(solution)/shard_map/psum | solution.py:478
  1434.4 369.7 %all-reduce.19.cloned.1.call-start = ((), (), s32[]{:S(2)}) async-start(), calls=%async_computation.26 | async-start | bytes 4718592 | tf_op jit(solution)/shard_map/psum | solution.py:479
  (159 other events, 570.8 us)
Sparse Core Ops, SparseCore 0:
  9.7 25.4 all-gather.10
  36.8 43.6 all-gather.8
  82.1 50.8 all-gather.12
  134.5 50.5 all-gather.14
  186.5 50.4 all-gather.16
  1281.0 29.1 reduce-scatter.30
  1312.5 28.1 reduce-scatter.34
  1343.5 28.1 reduce-scatter.32
  1374.6 28.2 reduce-scatter.28
  1405.6 28.7 reduce-scatter.24
  1437.3 30.9 reduce-scatter.18
  1470.6 41.9 reduce-scatter.16
  1514.9 53.4 reduce-scatter.20
  1570.6 53.2 reduce-scatter.22
  1626.0 53.3 reduce-scatter.26
  1683.8 40.5 all-reduce.16
  1728.2 75.8 all-reduce.18
where the time goes:
time: 1830 us; the launch traced here: 1820 us
  waiting for transfers between devices  630 us (34%)
  matrix products  432 us (24%)
  local copies, waits for them, and re-layouts  380 us (21%)
  other arithmetic  274 us (15%)
  blocking collectives  74.1 us (4%)
    scatter-add x56, local copies, waits for them, and re-layouts, columns_adjoint(): padded.at[row_off:row_off + GRID, col_off:col_off + GRID, :]  286 us
    dot_general x38, matrix products, product(): return jnp.dot(left, right, preferred_element_type=jnp.float32)  172 us
    dot_general x20, matrix products, product_tn(): lax.dot_general(left, right, (((0,), (0,)), ((), ())), preferred_element_...  80.8 us
    psum x1, waiting for transfers between devices, shards(): lax.psum(shares[1].astype(jnp.bfloat16), 'rep').astype(jnp.float32)  73.2 us
    add x40, other arithmetic, columns_adjoint(): padded.at[row_off:row_off + GRID, col_off:col_off + GRID, :]  70.1 us
    unnamed x20, waiting for transfers between devices  56.9 us
    reduce_scatter x1, waiting for transfers between devices, shards(): lax.psum_scatter(grad_sums[3].astype(jnp.bfloat16), 'wide', scatter_dimen...  55.8 us
    reduce_scatter x1, waiting for transfers between devices, shards(): lax.psum_scatter(grad_sums[6].astype(jnp.bfloat16), 'wide', scatter_dimen...  55.5 us
  transfers between devices with their start and end apart: 17, of which 14 were waited for; matrix products, arithmetic and copies ran while one was open for 3% of the time, Pallas kernels for 0%

commit v1 on v0

v1 whole, which is shorter than its diff:
```python
import jax
import jax.numpy as jnp
from jax import lax
from jax.sharding import PartitionSpec as P

D = 768
HEADS = 12
HD = 64
GRID = 24
DATASETS = 10
F32 = jnp.float32
BF16 = jnp.bfloat16
BOTH = ("rep", "wide")


def mm(left, right):
    return jnp.dot(left, right, preferred_element_type=F32)


def mm_tn(left, right):
    return lax.dot_general(left, right, (((0,), (0,)), ((), ())), preferred_element_type=F32)


def mm_nt(left, right):
    return lax.dot_general(left, right, (((1,), (1,)), ((), ())), preferred_element_type=F32)


class Links:
    def __init__(self):
        rep = lax.axis_index("rep")
        wide = lax.axis_index("wide")
        self.bit = {
            "y": rep // 2,
            "x": rep % 2,
            "z1": wide // 4,
            "z0": (wide // 2) % 2,
            "c": wide % 2,
        }
        self.flip = {"y": 16, "x": 8, "z1": 4, "z0": 2, "c": 1}

    def swap(self, value, name):
        pairs = [(i, i ^ self.flip[name]) for i in range(32)]
        return lax.ppermute(value, BOTH, pairs)

    def both(self, value, name, axis):
        other = self.swap(value, name)
        first = self.bit[name] == 0
        return jnp.stack([jnp.where(first, value, other), jnp.where(first, other, value)], axis)

    def halve(self, value, name, axis):
        mine = lax.dynamic_index_in_dim(value, self.bit[name], axis, keepdims=False)
        theirs = lax.dynamic_index_in_dim(value, 1 - self.bit[name], axis, keepdims=False)
        got = self.swap(theirs, name)
        return (mine.astype(F32) + got.astype(F32)).astype(value.dtype)

    def gather_small(self, value):
        value = self.both(value, "z0", 0)
        value = self.both(value, "z1", 0)
        value = self.both(value, "c", 2)
        return value.reshape((8,) + value.shape[3:])

    def plane_gather(self, first, second):
        first = self.both(self.both(first, "x", 0), "y", 0)
        second = self.both(self.both(second, "y", 0), "x", 1)
        return first, second

    def gather(self, piece):
        piece = self.both(piece, "z0", 0)
        piece = self.both(piece, "z1", 0)
        first, second = self.plane_gather(piece[:, :, 0], piece[:, :, 1])
        value = jnp.stack([first, second], 4)
        value = self.both(value, "c", 4)
        return value

    def scatter(self, value):
        value = self.halve(value, "c", 0)
        first, second = value[:, :, :, 0], value[:, :, :, 1]
        first = self.halve(self.halve(first, "x", 2), "y", 1)
        second = self.halve(self.halve(second, "y", 1), "x", 1)
        value = jnp.stack([first, second], 1)
        value = value.reshape((2, 2) + value.shape[1:])
        value = self.halve(value, "z1", 0)
        value = self.halve(value, "z0", 0)
        first, second = self.plane_gather(value[0], value[1])
        return jnp.stack([first, second], 2)

    def quarter(self, shard):
        rows, cols = shard.shape[-2] // 2, shard.shape[-1] // 2
        shard = lax.dynamic_slice_in_dim(shard, self.bit["y"] * rows, rows, shard.ndim - 2)
        return lax.dynamic_slice_in_dim(shard, self.bit["x"] * cols, cols, shard.ndim - 1)


def gather_weight(links, shard):
    rows, cols = shard.shape
    piece = links.quarter(shard).reshape(2, rows // 4, cols // 2)
    value = links.gather(piece)
    return value.transpose(2, 3, 4, 0, 5, 6, 1, 7).reshape(8 * rows, cols)


def scatter_grad(links, grad):
    rows, cols = grad.shape[0] // 8, grad.shape[1]
    value = grad.astype(BF16).reshape(4, 2, 2, 2, rows // 4, 2, cols // 2)
    value = value.transpose(1, 0, 2, 5, 3, 4, 6)
    value = links.scatter(value)
    return value.transpose(0, 2, 3, 1, 4).reshape(rows, cols).astype(F32)


def sum_small(links, value):
    value = value.reshape((4, 2) + value.shape[1:])
    value = links.halve(value, "c", 1)
    value = value.reshape((2, 2) + value.shape[1:])
    value = links.halve(value, "z1", 0)
    value = links.halve(value, "z0", 0)
    value = value + links.swap(value, "x")
    return value + links.swap(value, "y")


def normalize(values):
    centred = values - jnp.mean(values, -1, keepdims=True)
    recip = lax.rsqrt(jnp.mean(centred * centred, -1, keepdims=True) + 1e-06)
    return centred * recip, recip


def norm_transpose(grad_normed, normed, recip):
    return recip * (
        grad_normed
        - jnp.mean(grad_normed, -1, keepdims=True)
        - normed * jnp.mean(grad_normed * normed, -1, keepdims=True)
    )


def gelu_pair(values):
    cdf = 0.5 * (1.0 + lax.erf(values * 0.7071067811865476))
    pdf = 0.3989422804014327 * jnp.exp(-0.5 * values * values)
    return values * cdf, cdf + values * pdf


def upsample_pair():
    target = jnp.arange(2 * GRID, dtype=jnp.int32)
    numer = target * (GRID - 1)
    lower = numer // (2 * GRID - 1)
    frac_part = (numer - lower * (2 * GRID - 1)).astype(F32) / (2 * GRID - 1)
    source = jnp.arange(GRID, dtype=jnp.int32)
    below = (source[None, :] == lower[:, None]).astype(F32) * (1.0 - frac_part[:, None])
    above = (source[None, :] == lower[:, None] + 1).astype(F32) * frac_part[:, None]
    table = below + above
    pair = table[:, None, :, None] * table[None, :, None, :]
    return pair.reshape(4 * GRID * GRID, GRID * GRID).astype(BF16)


def conv(maps, kernel):
    field = maps.reshape(-1, GRID, GRID, maps.shape[-1])
    out = lax.conv_general_dilated(
        field, kernel.reshape(3, 3, maps.shape[-1], -1), (1, 1), "SAME",
        dimension_numbers=("NHWC", "HWIO", "NHWC"), preferred_element_type=F32)
    return out.reshape(maps.shape[0], GRID * GRID, -1)


def conv_back(grads, kernel):
    flipped = kernel.reshape(3, 3, -1, kernel.shape[-1])[::-1, ::-1]
    field = grads.reshape(-1, GRID, GRID, grads.shape[-1])
    out = lax.conv_general_dilated(
        field, flipped, (1, 1), "SAME",
        dimension_numbers=("NHWC", "HWOI", "NHWC"), preferred_element_type=F32)
    return out.reshape(grads.shape[0], GRID * GRID, -1)


def columns(maps):
    field = maps.reshape(-1, GRID, GRID, maps.shape[-1])
    padded = jnp.pad(field, ((0, 0), (1, 1), (1, 1), (0, 0)))
    parts = [padded[:, r:r + GRID, c:c + GRID, :] for r in range(3) for c in range(3)]
    return jnp.concatenate(parts, -1).reshape(-1, 9 * maps.shape[-1])


def conv_weight_grad(maps, grads):
    return mm_tn(columns(maps), grads.reshape(-1, grads.shape[-1]))


def layer(weights, tokens, live, onehot, flags, d_tokens_out, d_joined):
    gains, w_qkv, w_out, w_fc1, w_fc2, w_re, w_conv, w_head, scale_table, shift_table = weights
    images, count = tokens.shape[0], tokens.shape[1]
    rows = images * count
    live_rows = jnp.repeat(live, count)[:, None]
    gains = gains.astype(F32)
    scale = jnp.sum(onehot[:, :, None] * scale_table.astype(F32)[None], 1)
    shift = flags[:, None] * jnp.sum(onehot[:, :, None] * shift_table.astype(F32)[None], 1)
    pair = upsample_pair()
    down = jnp.einsum("ts,itc->isc", pair, d_joined, preferred_element_type=F32) * live[:, None, None]
    g_shift_rows = flags[:, None] * jnp.sum(d_joined.astype(F32), 1) * live[:, None]

    x = tokens.reshape(rows, D).astype(F32)
    n1, rs1 = normalize(x)
    a1 = (n1 * gains[0]).astype(BF16)
    qkv = mm(a1, w_qkv).astype(BF16)
    heads = qkv.reshape(images, count, 3, HEADS, HD)
    query, key, value = heads[:, :, 0], heads[:, :, 1], heads[:, :, 2]
    scores = jnp.einsum("iphd,iqhd->ihpq", query, key, preferred_element_type=F32) * 0.125
    top = jnp.max(scores, -1, keepdims=True)
    powers = jnp.exp(scores - top)
    prob = (powers / jnp.sum(powers, -1, keepdims=True)).astype(BF16)
    mixed = jnp.einsum("ihpq,iqhd->iphd", prob, value, preferred_element_type=F32).astype(BF16)
    o = mixed.reshape(rows, D)
    x2 = x + mm(o, w_out)
    n2, rs2 = normalize(x2)
    a2 = (n2 * gains[1]).astype(BF16)
    gg, slope = gelu_pair(mm(a2, w_fc1))
    gg, slope = gg.astype(BF16), slope.astype(BF16)
    x3 = x2 + mm(gg, w_fc2)
    tokens_out = (x3 * live_rows).astype(BF16).reshape(tokens.shape)
    x3b = x3.astype(BF16)
    z = mm(x3b, w_re).reshape(images, count, -1)
    kept = []
    for unit in range(2):
        t1, s1 = gelu_pair(z)
        t1 = t1.astype(BF16)
        t2, s2 = gelu_pair(conv(t1, w_conv[2 * unit]))
        t2 = t2.astype(BF16)
        z = z + conv(t2, w_conv[2 * unit + 1])
        kept.append((t1, s1.astype(BF16), t2, s2.astype(BF16)))
    zb = z.astype(BF16).reshape(rows, -1)
    head = mm(zb, w_head).reshape(images, count, -1)
    hd = jnp.einsum("ts,isc->itc", pair, head.astype(BF16), preferred_element_type=F32)
    joined = ((hd * scale[:, None] + shift[:, None]) * live[:, None, None]).astype(BF16)

    g_scale_rows = jnp.sum(head * down, 1)
    g_scale = jnp.einsum("ik,ic->kc", onehot, g_scale_rows, precision=lax.Precision.HIGHEST)
    g_shift = jnp.einsum("ik,ic->kc", onehot, g_shift_rows, precision=lax.Precision.HIGHEST)
    dq_map = (down * scale[:, None]).astype(BF16).reshape(rows, -1)
    g_head = mm_tn(zb, dq_map)
    dz = mm_nt(dq_map, w_head).reshape(images, count, -1)
    g_conv = [None] * 4
    for unit in (1, 0):
        t1, s1, t2, s2 = kept[unit]
        dc2 = dz.astype(BF16)
        g_conv[2 * unit + 1] = conv_weight_grad(t2, dc2)
        dc1 = (conv_back(dc2, w_conv[2 * unit + 1]) * s2).astype(BF16)
        g_conv[2 * unit] = conv_weight_grad(t1, dc1)
        dz = dz + s1 * conv_back(dc1, w_conv[2 * unit])
    dr = dz.astype(BF16).reshape(rows, -1)
    g_re = mm_tn(x3b, dr)
    dx3 = d_tokens_out.reshape(rows, D).astype(F32) * live_rows + mm_nt(dr, w_re)
    dm = dx3.astype(BF16)
    g_fc2 = mm_tn(gg, dm)
    du = (mm_nt(dm, w_fc2) * slope).astype(BF16)
    g_fc1 = mm_tn(a2, du)
    da2 = mm_nt(du, w_fc1)
    g_gain2 = jnp.sum(da2 * n2, 0)
    dx2 = dx3 + norm_transpose(da2 * gains[1], n2, rs2)
    da = dx2.astype(BF16)
    g_out = mm_tn(o, da)
    do = mm_nt(da, w_out).astype(BF16).reshape(images, count, HEADS, HD)
    dv = jnp.einsum("ihpq,iphd->iqhd", prob, do, preferred_element_type=F32)
    dp = jnp.einsum("iphd,iqhd->ihpq", do, value, preferred_element_type=F32)
    probf = prob.astype(F32)
    ds = (probf * (dp - jnp.sum(probf * dp, -1, keepdims=True))).astype(BF16)
    dq = jnp.einsum("ihpq,iqhd->iphd", ds, key, preferred_element_type=F32) * 0.125
    dk = jnp.einsum("ihpq,iphd->iqhd", ds, query, preferred_element_type=F32) * 0.125
    dqkv = jnp.stack([dq, dk, dv], 2).astype(BF16).reshape(rows, 3 * D)
    g_qkv = mm_tn(a1, dqkv)
    da1 = mm_nt(dqkv, w_qkv)
    g_gain1 = jnp.sum(da1 * n1, 0)
    d_tokens = (dx2 + norm_transpose(da1 * gains[0], n1, rs1)).astype(BF16).reshape(tokens.shape)
    grads = (jnp.stack([g_gain1, g_gain2]), g_qkv, g_out, g_fc1, g_fc2, g_re, g_conv, g_head, g_scale, g_shift)
    return tokens_out, joined, d_tokens, grads


def shards(tokens, live_count, dataset_id, shift_flag, norm_gains, w_qkv, w_attn_out, w_fc1, w_fc2, w_reassemble,
           conv_kernels, w_head, scale_table, shift_table, d_tokens_out, d_joined):
    slots = tokens.shape[0]
    live = (jnp.arange(slots, dtype=jnp.int32) < live_count[0]).astype(F32)
    onehot = (dataset_id[:, None] == jnp.arange(DATASETS, dtype=jnp.int32)[None, :]).astype(F32)
    flags = shift_flag.astype(F32)
    neighbours = (lax.axis_size("rep"), lax.axis_size("wide")) == (4, 8)
    if neighbours:
        links = Links()
        small = jnp.concatenate([norm_gains.reshape(-1), scale_table.reshape(-1), shift_table.reshape(-1)])
        small = links.gather_small(small)
        g, t = norm_gains.shape[1], scale_table.shape[1]
        def wide_cols(part, lead):
            return part.reshape(8, lead, -1).transpose(1, 0, 2).reshape(lead, -1)
        gains = wide_cols(small[:, :2 * g], 2)
        scales = wide_cols(small[:, 2 * g:2 * g + DATASETS * t], DATASETS)
        shifts = wide_cols(small[:, 2 * g + DATASETS * t:], DATASETS)
        weights = (gains, gather_weight(links, w_qkv), gather_weight(links, w_attn_out), gather_weight(links, w_fc1),
                   gather_weight(links, w_fc2), gather_weight(links, w_reassemble),
                   [gather_weight(links, conv_kernels[j]) for j in range(4)], gather_weight(links, w_head), scales, shifts)
    else:
        def whole(part, axis):
            return lax.all_gather(part, "wide", axis=axis, tiled=True)
        weights = (whole(norm_gains, 1), whole(w_qkv, 0), whole(w_attn_out, 0), whole(w_fc1, 0), whole(w_fc2, 0),
                   whole(w_reassemble, 0), whole(conv_kernels, 1), whole(w_head, 0), whole(scale_table, 1),
                   whole(shift_table, 1))
    tokens_out, joined, d_tokens, grads = layer(weights, tokens, live, onehot, flags, d_tokens_out, d_joined)
    g_gains, g_qkv, g_out, g_fc1, g_fc2, g_re, g_conv, g_head, g_scale, g_shift = grads
    if neighbours:
        def by_shard(part):
            return part.reshape(part.shape[0], 8, -1).transpose(1, 0, 2).reshape(8, -1)
        small = jnp.concatenate([by_shard(g_gains), by_shard(g_scale), by_shard(g_shift)], 1)
        small = sum_small(links, small)
        g_gains = small[:2 * g].reshape(2, g)
        g_scale = small[2 * g:2 * g + DATASETS * t].reshape(DATASETS, t)
        g_shift = small[2 * g + DATASETS * t:].reshape(DATASETS, t)
        sums = (g_gains, scatter_grad(links, g_qkv), scatter_grad(links, g_out), scatter_grad(links, g_fc1),
                scatter_grad(links, g_fc2), scatter_grad(links, g_re),
                jnp.stack([scatter_grad(links, part) for part in g_conv]), scatter_grad(links, g_head), g_scale, g_shift)
    else:
        def share(part, axis):
            part = lax.psum_scatter(part.astype(BF16), "wide", scatter_dimension=axis, tiled=True)
            return lax.psum(part, "rep").astype(F32)
        sums = (share(g_gains, 1), share(g_qkv, 0), share(g_out, 0), share(g_fc1, 0), share(g_fc2, 0), share(g_re, 0),
                share(jnp.stack(g_conv), 1), share(g_head, 0), share(g_scale, 1), share(g_shift, 1))
    return (tokens_out, joined, d_tokens) + sums


def solution(mesh):
    images = P(BOTH, None, None)
    slots = P(BOTH)
    rows = P("wide", None)
    cols = P(None, "wide")
    kernels = P(None, "wide", None)
    return jax.shard_map(
        shards,
        mesh=mesh,
        in_specs=(images, slots, slots, slots, cols, rows, rows, rows, rows, rows, kernels, rows, cols, cols, images, images),
        out_specs=(images, images, images, cols, rows, rows, rows, rows, rows, kernels, rows, cols, cols),
        check_vma=False,
    )
```

time: 1830 us -> 1170 us (0.64)
  waiting for transfers between devices: 630 us -> 253 us
  matrix products: 432 us -> 214 us
  starting transfers between devices: 0.69 us -> 176 us
  other arithmetic: 274 us -> 159 us
  blocking collectives: 74.1 us -> 0 us
  local copies, waits for them, and re-layouts: 380 us -> 354 us
    reduce_scatter x7 -> x0, waiting for transfers between devices: 306 us -> none  [the longest x1 55.8 us: shards(): lax.psum_scatter(grad_sums[3].astype(jnp.bfloat16), 'wide', scatter_dimen...]
    scatter-add x56 -> x0, local copies, waits for them, and re-layouts: 286 us -> none  [columns_adjoint(): padded.at[row_off:row_off + GRID, col_off:col_off + GRID, :]]
    dot_general x106 -> x31, matrix products: 432 us -> 179 us  [the longest x10 47.6 us: mm_tn(): lax.dot_general(left, right, (((0,), (0,)), ((), ())), preferred_element_...]
    ppermute x0 -> x188, waiting for transfers between devices: none -> 253 us  [swap(): return lax.ppermute(value, BOTH, pairs)]
    ppermute x0 -> x188, starting transfers between devices: none -> 176 us  [swap(): return lax.ppermute(value, BOTH, pairs)]
    all_gather x5 -> x0, waiting for transfers between devices: 149 us -> none  [the longest x1 52 us: shards(): lax.all_gather(w_fc2, 'wide', axis=0, tiled=True)]
    psum x2 -> x0, waiting for transfers between devices: 118 us -> none  [the longest x1 73.2 us: shards(): lax.psum(shares[1].astype(jnp.bfloat16), 'rep').astype(jnp.float32)]
    add x48 -> x7, other arithmetic: 86.5 us -> 4.72 us  [the longest x3 2.61 us: halve(): return (mine.astype(F32) + got.astype(F32)).astype(value.dtype)]
  transfers between devices with their start and end apart: 17 -> 188, of which waited for: 14 -> 111; matrix products, arithmetic and copies ran while one was open for 3% -> 40% of each run, Pallas kernels for 0% -> 0%
where the time goes in v1:
time: 1170 us; the launch traced here: 1160 us
  local copies, waits for them, and re-layouts  354 us (30%)
  waiting for transfers between devices  253 us (22%)
  matrix products  214 us (18%)
  starting transfers between devices  176 us (15%)
  other arithmetic  159 us (14%)
    ppermute x188, waiting for transfers between devices, swap(): return lax.ppermute(value, BOTH, pairs)  253 us
    ppermute x188, starting transfers between devices, swap(): return lax.ppermute(value, BOTH, pairs)  176 us
    unnamed x592, local copies, waits for them, and re-layouts  67.8 us
    reshape x9, local copies, waits for them, and re-layouts, scatter_grad(): value = grad.astype(BF16).reshape(4, 2, 2, 2, rows // 4, 2, cols // 2)  48.9 us
    another operation x154, other arithmetic, both(): jnp.stack([jnp.where(first, value, other), jnp.where(first, other, value)...  48.7 us
    dot_general x10, matrix products, mm_tn(): lax.dot_general(left, right, (((0,), (0,)), ((), ())), preferred_element_...  47.6 us
    dot_general x6, matrix products, mm_nt(): lax.dot_general(left, right, (((1,), (1,)), ((), ())), preferred_element_...  37.2 us
    dynamic_slice x10, local copies, waits for them, and re-layouts, halve(): mine = lax.dynamic_index_in_dim(value, self.bit[name], axis, keepdims=False)  34.7 us
  transfers between devices with their start and end apart: 188, of which 111 were waited for; matrix products, arithmetic and copies ran while one was open for 40% of the time, Pallas kernels for 0%

profile of v1, /device:TPU:0, one launch (start us, length us, event | category | flops | bytes accessed | tf_op | source)
XLA Modules:
  0.0 1162.7 jit_solution(15506959877748877016)
XLA Ops:
  21.0 4.5 multiply_convert_fusion
  25.5 11.2 reshape.1202
  36.7 4.0 fusion.51
  178.2 4.5 collective-permute-done.41
  184.5 4.9 collective-permute-done.43
  207.1 11.6 collective-permute-done.19
  219.2 8.1 collective-permute-done.21
  229.6 5.5 collective-permute-done.28
  258.9 3.9 reshape_reshape.17
  266.3 4.3 reshape_reshape.16
  274.1 3.9 reshape_reshape.18
  302.0 3.6 copy.489
  308.1 6.2 convolution_convert_fusion
  314.2 8.5 copy.490
  322.8 13.3 %reshape.1000 = bf16[2,576,3,12,64]{1,0,4,3,2:T(2,128)(2,1)} reshape(bf16[1152,2304]{0,1:T(8,128)(2,1)} %copy.490) | data formatting | bytes 10616832 | tf_op jit(solution)/shard_map/reshape | solution.py:195
  336.1 7.2 fusion.387
  343.3 18.6 %fusion.405 = (f32[2,12,576]{2,1,0:T(8,128)S(1)}, f32[2,12,576,576]{2,3,1,0:T(8,128)}) fusion(bf16[2,576,1,12,64]{1,0,4,3,2:T(2,128)(2,1)} %get-tuple-element.85, bf16[2,576,1,12,64]{1,0,4,3,2:T(2,128)(2,1)} %get-tuple-element.84), kind=kOutput, calls=%fused_computation.1201 | convolution fusion | flops 1043104320 | bytes 35444736 | tf_op jit(solution)/shard_map/sub | solution.py:199
  361.9 13.2 %divide_convert_fusion = bf16[2,12,576,576]{2,3,1,0:T(8,128)(2,1)S(1)} fusion(f32[2,12,576,576]{2,3,1,0:T(8,128)} %get-tuple-element.465, f32[2,12,576]{2,1,0:T(8,128)S(1)} %get-tuple-element.464), kind=kLoop, calls=%fused_computation.5 | loop fusion | flops 15925248 | bytes 47831040 | tf_op jit(solution)/shard_map/convert_element_type | solution.py:200
  375.1 7.5 convert_bitcast_fusion.1
  382.7 4.8 copy.495
  387.5 5.1 reshape.1001
  392.6 3.6 fusion.406
  403.6 9.3 copy.504
  412.9 5.4 copy.691
  422.8 9.8 copy.501
  432.6 3.7 copy.690
  436.4 9.7 multiply_convert_fusion.1
  446.1 6.9 fusion.388
  506.6 8.7 convolution_convert_fusion.1
  515.3 13.6 %fusion.12 = bf16[1152,3072]{1,0:T(8,128)(2,1)} fusion(bf16[3072,768]{1,0:T(8,128)(2,1)S(1)} %bitcast.1754, f32[1152,3072]{1,0:T(8,128)} %get-tuple-element.469, f32[1152,768]{1,0:T(8,128)S(1)} %convolution_add_fusion), kind=kOutput, calls=%fused_computation.20 | convolution fusion | flops 5479170048 | bytes 29491200 | tf_op jit(solution)/shard_map/dot_general | solution.py:25
  529.0 8.8 multiply_reduce_fusion.1
  537.8 11.6 convolution_convert_fusion.2
  565.0 4.5 reshape.1026
  569.5 10.1 convert_bitcast_fusion
  579.5 17.8 %fusion.1 = (f32[2,12,576]{2,1,0:T(8,128)S(1)}, f32[2,12,576,576]{2,3,1,0:T(8,128)}) fusion(bf16[2,12,576,576]{2,3,1,0:T(8,128)(2,1)} %copy-done, bf16[2,576,1,12,64]{1,0,4,3,2:T(2,128)(2,1)} %get-tuple-element.83, bf16[2,576,12,64]{1,0,3,2:T(2,128)(2,1)S(1)} %reshape.1026), kind=kOutput, calls=%fused_computation.3 | convolution fusion | flops 1043089920 | bytes 51369984 | tf_op jit(solution)/shard_map/iphd,iqhd->ihpq/dot_general | solution.py:253
  597.3 29.1 %fusion.2 = bf16[2,12,576,576]{2,3,1,0:T(8,128)(2,1)} fusion(f32[2,12,576,576]{2,3,1,0:T(8,128)} %get-tuple-element.478, f32[2,12,576]{2,1,0:T(8,128)S(1)} %get-tuple-element.477, f32[2,12,576,576]{2,3,1,0:T(8,128)} %get-tuple-element.465, f32[2,12,576]{2,1,0:T(8,128)S(1)} %copy-done.206), kind=kLoop, calls=%fused_computation.4 | loop fusion | flops 47775744 | bytes 79736832 | tf_op jit(solution)/shard_map/convert_element_type | solution.py:255
  626.5 10.2 fusion.39
  636.7 10.6 fusion.38
  651.1 3.5 fusion.18
  654.7 4.4 copy.651
  664.5 11.6 %reshape.1033 = bf16[4,2,2,2,24,2,1536]{6,5,4,3,2,1,0:T(2,128)(2,1)} reshape(bf16[768,3072]{1,0:T(8,128)(2,1)} %convolution_convert_fusion.2) | data formatting | bytes 9437184 | tf_op jit(solution)/shard_map/reshape | solution.py:102
  676.8 10.6 reshape.1034
  687.4 8.5 constant_dynamic-slice_fusion.39
  696.0 7.5 constant_dynamic-slice_fusion.41
  703.4 3.7 reshape.1032
  738.7 5.8 copy.561
  744.4 12.4 %convert_element_type.1350 = bf16[1152,2304]{0,1:T(8,128)(2,1)} reshape(bf16[2,576,3,12,64]{1,0,4,3,2:T(2,128)(2,1)} %copy.561) | data formatting | bytes 10616832 | tf_op jit(solution)/shard_map/convert_element_type | solution.py:258
  756.9 8.8 convolution_convert_fusion.3
  765.6 8.4 reshape.1031
  774.0 11.2 multiply_reduce_fusion.2
  802.8 5.4 convolution_convert_fusion.6
  842.5 3.5 reshape.1045
  849.9 3.5 reshape.1038
  877.9 3.9 reshape.1043
  942.6 3.6 collective-permute-done.90
  958.9 4.1 collective-permute-done.134
  965.2 3.7 collective-permute-done.156
  1065.1 4.7 collective-permute-done.79
  1070.2 4.4 collective-permute-done.81
  1084.1 8.8 collective-permute-done.83
  1093.2 5.4 collective-permute-done.84
  1105.1 6.5 collective-permute-done.88
  1112.1 4.5 collective-permute-done.86
  1130.3 9.6 collective-permute-done.116
  (1552 shorter events, 659.6 us)
Async XLA Ops:
  3.1 42.9 %collective-permute-start = (bf16[832]{0:T(1024)(128)(2,1)S(1)}, bf16[832]{0:T(1024)(128)(2,1)S(1)}, u32[]{:S(2)}, u32[]{:S(2)}) collective-permute-start(bf16[832]{0:T(1024)(128)(2,1)S(1)} %pad_maximum_fusion.76), channel_id=1, source_target_pairs={{0,2},{1,3},{2,0},{3,1},{4,6},{5,7},{6,4},{7,5},{8,10},{9,11},{10,... | collective-permute-start | bytes 5000 | tf_op jit(solution)/shard_map/ppermute | solution.py:43
  7.0 39.4 %collective-permute-start.66 = (bf16[2,8,128]{2,1,0:T(8,128)(2,1)S(1)}, bf16[2,8,128]{2,1,0:T(8,128)(2,1)S(1)}, u32[]{:S(2)}, u32[]{:S(2)}) collective-permute-start(bf16[2,8,128]{2,1,0:T(8,128)(2,1)S(1)} %dynamic-slice_bitcast_fusion.38), channel_id=1, source_target_pairs={{0,2},{1,3},{2,0},{3,1},{4,6},{5,7},{6,4},{7,5},{8,10},{9,11},{10,... | collective-permute-start | bytes 12296 | tf_op jit(solution)/shard_map/ppermute | solution.py:43
  7.8 53.6 %collective-permute-start.31 = (bf16[2,24,128]{2,1,0:T(8,128)(2,1)S(1)}, bf16[2,24,128]{2,1,0:T(8,128)(2,1)S(1)}, u32[]{:S(2)}, u32[]{:S(2)}) collective-permute-start(bf16[2,24,128]{2,1,0:T(8,128)(2,1)S(1)} %bitcast.1889), channel_id=1, source_target_pairs={{0,2},{1,3},{2,0},{3,1},{4,6},{5,7},{6,4},{7,5},{8,10},{9,11},{10,... | collective-permute-start | bytes 36872 | tf_op jit(solution)/shard_map/ppermute | solution.py:43
  10.7 66.0 %collective-permute-start.10 = (bf16[2,24,384]{2,1,0:T(8,128)(2,1)S(1)}, bf16[2,24,384]{2,1,0:T(8,128)(2,1)S(1)}, u32[]{:S(2)}, u32[]{:S(2)}) collective-permute-start(bf16[2,24,384]{2,1,0:T(8,128)(2,1)S(1)} %bitcast.1868), channel_id=1, source_target_pairs={{0,2},{1,3},{2,0},{3,1},{4,6},{5,7},{6,4},{7,5},{8,10},{9,11},{10,... | collective-permute-start | bytes 110600 | tf_op jit(solution)/shard_map/ppermute | solution.py:43
  12.5 96.9 %collective-permute-start.3 = (bf16[2,24,1152]{2,1,0:T(8,128)(2,1)}, bf16[2,24,1152]{2,1,0:T(8,128)(2,1)}, u32[]{:S(2)}, u32[]{:S(2)}) collective-permute-start(bf16[2,24,1152]{2,1,0:T(8,128)(2,1)} %bitcast.7), channel_id=1, source_target_pairs={{0,2},{1,3},{2,0},{3,1},{4,6},{5,7},{6,4},{7,5},{8,10},{9,11},{10,... | collective-permute-start | bytes 331784 | tf_op jit(solution)/shard_map/ppermute | solution.py:43
  46.1 84.7 %collective-permute-start.24 = (bf16[2,96,384]{2,1,0:T(8,128)(2,1)S(1)}, bf16[2,96,384]{2,1,0:T(8,128)(2,1)}, u32[]{:S(2)}, u32[]{:S(2)}) collective-permute-start(bf16[2,96,384]{2,1,0:T(8,128)(2,1)S(1)} %bitcast.1855), channel_id=1, source_target_pairs={{0,2},{1,3},{2,0},{3,1},{4,6},{5,7},{6,4},{7,5},{8,10},{9,11},{10,... | collective-permute-start | bytes 442376 | tf_op jit(solution)/shard_map/ppermute | solution.py:43
  59.2 68.7 %collective-permute-start.17 = (bf16[2,24,1536]{2,1,0:T(8,128)(2,1)}, bf16[2,24,1536]{2,1,0:T(8,128)(2,1)}, u32[]{:S(2)}, u32[]{:S(2)}) collective-permute-start(bf16[2,24,1536]{2,1,0:T(8,128)(2,1)} %bitcast.53), channel_id=1, source_target_pairs={{0,2},{1,3},{2,0},{3,1},{4,6},{5,7},{6,4},{7,5},{8,10},{9,11},{10,... | collective-permute-start | bytes 442376 | tf_op jit(solution)/shard_map/ppermute | solution.py:43
  76.3 17.7 %collective-permute-start.59 = (bf16[2,72,128]{2,1,0:T(8,128)(2,1)S(1)}, bf16[2,72,128]{2,1,0:T(8,128)(2,1)S(1)}, u32[]{:S(2)}, u32[]{:S(2)}) collective-permute-start(bf16[2,72,128]{2,1,0:T(8,128)(2,1)S(1)} %bitcast.1870), channel_id=1, source_target_pairs={{0,2},{1,3},{2,0},{3,1},{4,6},{5,7},{6,4},{7,5},{8,10},{9,11},{10,... | collective-permute-start | bytes 110600 | tf_op jit(solution)/shard_map/ppermute | solution.py:43
  94.0 9.7 collective-permute-start.72
  101.7 17.3 %collective-permute-start.11 = (bf16[2,2,24,384]{3,2,1,0:T(8,128)(2,1)}, bf16[2,2,24,384]{3,2,1,0:T(8,128)(2,1)}, u32[]{:S(2)}, u32[]{:S(2)}) collective-permute-start(bf16[2,2,24,384]{3,2,1,0:T(8,128)(2,1)} %pad_maximum_fusion.44), channel_id=1, source_target_pairs={{0,4},{1,5},{2,6},{3,7},{4,0},{5,1},{6,2},{7,3},{8,12},{9,13},{10,... | collective-permute-start | bytes 221192 | tf_op jit(solution)/shard_map/ppermute | solution.py:43
  103.7 18.0 %collective-permute-start.60 = (bf16[2,2,72,128]{3,2,0,1:T(8,128)(2,1)}, bf16[2,2,72,128]{3,2,0,1:T(8,128)(2,1)}, u32[]{:S(2)}, u32[]{:S(2)}) collective-permute-start(bf16[2,2,72,128]{3,2,0,1:T(8,128)(2,1)} %pad_maximum_fusion.48), channel_id=1, source_target_pairs={{0,4},{1,5},{2,6},{3,7},{4,0},{5,1},{6,2},{7,3},{8,12},{9,13},{10,... | collective-permute-start | bytes 221192 | tf_op jit(solution)/shard_map/ppermute | solution.py:43
  124.1 9.4 collective-permute-start.12
  125.6 9.4 collective-permute-start.14
  127.8 37.1 %collective-permute-start.37 = (bf16[2,2,2,2,2,24,128]{6,5,3,2,0,1,4:T(8,128)(2,1)S(1)}, bf16[2,2,2,2,2,24,128]{6,5,3,2,0,1,4:T(8,128)(2,1)S(1)}, u32[]{:S(2)}, u32[]{:S(2)}) collective-permute-start(bf16[2,2,2,2,2,24,128]{6,5,3,2,0,1,4:T(8,128)(2,1)S(1)} %pad_maximum_fusion.21), channel_id=1, source_target_pairs={{0,1},{1,0},{2,3},{3,2},{4,5},{5,4},{6,7},{7,6},{8,9},{9,8},{10,11... | collective-permute-start | bytes 589832 | tf_op jit(solution)/shard_map/ppermute | solution.py:43
  127.9 39.7 %collective-permute-start.4 = (bf16[2,2,24,1152]{3,2,1,0:T(8,128)(2,1)}, bf16[2,2,24,1152]{3,2,1,0:T(8,128)(2,1)}, u32[]{:S(2)}, u32[]{:S(2)}) collective-permute-start(bf16[2,2,24,1152]{3,2,1,0:T(8,128)(2,1)} %pad_maximum_fusion.20), channel_id=1, source_target_pairs={{0,4},{1,5},{2,6},{3,7},{4,0},{5,1},{6,2},{7,3},{8,12},{9,13},{10,... | collective-permute-start | bytes 663560 | tf_op jit(solution)/shard_map/ppermute | solution.py:43
  133.4 29.1 %collective-permute-start.63 = (bf16[2,2,72,128]{3,2,1,0:T(8,128)(2,1)S(1)}, bf16[2,2,72,128]{3,2,1,0:T(8,128)(2,1)S(1)}, u32[]{:S(2)}, u32[]{:S(2)}) collective-permute-start(bf16[2,2,72,128]{3,2,1,0:T(8,128)(2,1)S(1)} %get-tuple-element.309), channel_id=1, source_target_pairs={{0,16},{1,17},{2,18},{3,19},{4,20},{5,21},{6,22},{7,23},{8,24},{9,... | collective-permute-start | bytes 221192 | tf_op jit(solution)/shard_map/ppermute | solution.py:43
  135.0 26.2 %collective-permute-start.54 = (bf16[2,2,72,128]{3,2,1,0:T(8,128)(2,1)S(1)}, bf16[2,2,72,128]{3,2,1,0:T(8,128)(2,1)S(1)}, u32[]{:S(2)}, u32[]{:S(2)}) collective-permute-start(bf16[2,2,72,128]{3,2,1,0:T(8,128)(2,1)S(1)} %get-tuple-element.300), channel_id=1, source_target_pairs={{0,8},{1,9},{2,10},{3,11},{4,12},{5,13},{6,14},{7,15},{8,0},{9,1},... | collective-permute-start | bytes 221192 | tf_op jit(solution)/shard_map/ppermute | solution.py:43
  158.1 41.9 %collective-permute-start.25 = (bf16[2,2,96,384]{3,2,1,0:T(8,128)(2,1)}, bf16[2,2,96,384]{3,2,1,0:T(8,128)(2,1)}, u32[]{:S(2)}, u32[]{:S(2)}) collective-permute-start(bf16[2,2,96,384]{3,2,1,0:T(8,128)(2,1)} %pad_maximum_fusion.18), channel_id=1, source_target_pairs={{0,4},{1,5},{2,6},{3,7},{4,0},{5,1},{6,2},{7,3},{8,12},{9,13},{10,... | collective-permute-start | bytes 884744 | tf_op jit(solution)/shard_map/ppermute | solution.py:43
  161.2 40.5 %collective-permute-start.18 = (bf16[2,2,24,1536]{3,2,1,0:T(8,128)(2,1)}, bf16[2,2,24,1536]{3,2,1,0:T(8,128)(2,1)}, u32[]{:S(2)}, u32[]{:S(2)}) collective-permute-start(bf16[2,2,24,1536]{3,2,1,0:T(8,128)(2,1)} %pad_maximum_fusion.17), channel_id=1, source_target_pairs={{0,4},{1,5},{2,6},{3,7},{4,0},{5,1},{6,2},{7,3},{8,12},{9,13},{10,... | collective-permute-start | bytes 884744 | tf_op jit(solution)/shard_map/ppermute | solution.py:43
  167.6 23.2 %collective-permute-start.62 = (bf16[2,2,2,72,128]{4,3,2,1,0:T(8,128)(2,1)}, bf16[2,2,2,72,128]{4,3,2,1,0:T(8,128)(2,1)S(1)}, u32[]{:S(2)}, u32[]{:S(2)}) collective-permute-start(bf16[2,2,2,72,128]{4,3,2,1,0:T(8,128)(2,1)} %pad_maximum_fusion.30), channel_id=1, source_target_pairs={{0,16},{1,17},{2,18},{3,19},{4,20},{5,21},{6,22},{7,23},{8,24},{9,... | collective-permute-start | bytes 442376 | tf_op jit(solution)/shard_map/ppermute | solution.py:43
  170.2 26.3 %collective-permute-start.64 = (bf16[2,2,2,72,128]{4,3,2,1,0:T(8,128)(2,1)}, bf16[2,2,2,72,128]{4,3,2,1,0:T(8,128)(2,1)S(1)}, u32[]{:S(2)}, u32[]{:S(2)}) collective-permute-start(bf16[2,2,2,72,128]{4,3,2,1,0:T(8,128)(2,1)} %pad_maximum_fusion.31), channel_id=1, source_target_pairs={{0,8},{1,9},{2,10},{3,11},{4,12},{5,13},{6,14},{7,15},{8,0},{9,1},... | collective-permute-start | bytes 442376 | tf_op jit(solution)/shard_map/ppermute | solution.py:43
  199.7 37.4 %collective-permute-start.65 = (bf16[2,2,2,2,2,72,128]{6,5,3,2,0,1,4:T(8,128)(2,1)S(1)}, bf16[2,2,2,2,2,72,128]{6,5,3,2,0,1,4:T(8,128)(2,1)S(1)}, u32[]{:S(2)}, u32[]{:S(2)}) collective-permute-start(bf16[2,2,2,2,2,72,128]{6,5,3,2,0,1,4:T(8,128)(2,1)S(1)} %pad_maximum_fusion.12), channel_id=1, source_target_pairs={{0,1},{1,0},{2,3},{3,2},{4,5},{5,4},{6,7},{7,6},{8,9},{9,8},{10,11... | collective-permute-start | bytes 1769480 | tf_op jit(solution)/shard_map/ppermute | solution.py:43
  200.0 37.8 %collective-permute-start.51 = (bf16[2,2,2,2,2,72,128]{6,5,3,2,1,0,4:T(8,128)(2,1)S(1)}, bf16[2,2,2,2,2,72,128]{6,5,3,2,1,0,4:T(8,128)(2,1)S(1)}, u32[]{:S(2)}, u32[]{:S(2)}) collective-permute-start(bf16[2,2,2,2,2,72,128]{6,5,3,2,1,0,4:T(8,128)(2,1)S(1)} %pad_maximum_fusion.10), channel_id=1, source_target_pairs={{0,1},{1,0},{2,3},{3,2},{4,5},{5,4},{6,7},{7,6},{8,9},{9,8},{10,11... | collective-permute-start | bytes 1769480 | tf_op jit(solution)/shard_map/ppermute | solution.py:43
  201.7 38.2 %collective-permute-start.44 = (bf16[2,2,2,2,2,72,128]{6,5,3,2,0,1,4:T(8,128)(2,1)S(1)}, bf16[2,2,2,2,2,72,128]{6,5,3,2,0,1,4:T(8,128)(2,1)S(1)}, u32[]{:S(2)}, u32[]{:S(2)}) collective-permute-start(bf16[2,2,2,2,2,72,128]{6,5,3,2,0,1,4:T(8,128)(2,1)S(1)} %pad_maximum_fusion.9), channel_id=1, source_target_pairs={{0,1},{1,0},{2,3},{3,2},{4,5},{5,4},{6,7},{7,6},{8,9},{9,8},{10,11... | collective-permute-start | bytes 1769480 | tf_op jit(solution)/shard_map/ppermute | solution.py:43
  202.9 16.2 %collective-permute-start.26 = (bf16[2,2,96,384]{3,2,1,0:T(8,128)(2,1)S(1)}, bf16[2,2,96,384]{3,2,1,0:T(8,128)(2,1)S(1)}, u32[]{:S(2)}, u32[]{:S(2)}) collective-permute-start(bf16[2,2,96,384]{3,2,1,0:T(8,128)(2,1)S(1)} %get-tuple-element.196), channel_id=1, source_target_pairs={{0,8},{1,9},{2,10},{3,11},{4,12},{5,13},{6,14},{7,15},{8,0},{9,1},... | collective-permute-start | bytes 884744 | tf_op jit(solution)/shard_map/ppermute | solution.py:43
  204.7 13.9 %collective-permute-start.19 = (bf16[2,2,24,1536]{3,2,1,0:T(8,128)(2,1)S(1)}, bf16[2,2,24,1536]{3,2,1,0:T(8,128)(2,1)S(1)}, u32[]{:S(2)}, u32[]{:S(2)}) collective-permute-start(bf16[2,2,24,1536]{3,2,1,0:T(8,128)(2,1)S(1)} %get-tuple-element.204), channel_id=1, source_target_pairs={{0,8},{1,9},{2,10},{3,11},{4,12},{5,13},{6,14},{7,15},{8,0},{9,1},... | collective-permute-start | bytes 884744 | tf_op jit(solution)/shard_map/ppermute | solution.py:43
  218.7 8.7 collective-permute-start.21
  219.1 23.3 %collective-permute-start.58 = (bf16[2,2,2,2,2,72,128]{6,5,3,2,0,1,4:T(8,128)(2,1)S(1)}, bf16[2,2,2,2,2,72,128]{6,5,3,2,0,1,4:T(8,128)(2,1)S(1)}, u32[]{:S(2)}, u32[]{:S(2)}) collective-permute-start(bf16[2,2,2,2,2,72,128]{6,5,3,2,0,1,4:T(8,128)(2,1)S(1)} %pad_maximum_fusion.11), channel_id=1, source_target_pairs={{0,1},{1,0},{2,3},{3,2},{4,5},{5,4},{6,7},{7,6},{8,9},{9,8},{10,11... | collective-permute-start | bytes 1769480 | tf_op jit(solution)/shard_map/ppermute | solution.py:43
  235.1 17.3 %collective-permute-start.16 = (bf16[2,2,2,2,2,24,384]{6,5,3,2,0,1,4:T(8,128)(2,1)}, bf16[2,2,2,2,2,24,384]{6,5,3,2,0,1,4:T(8,128)(2,1)}, u32[]{:S(2)}, u32[]{:S(2)}) collective-permute-start(bf16[2,2,2,2,2,24,384]{6,5,3,2,0,1,4:T(8,128)(2,1)} %pad_maximum_fusion.4), channel_id=1, source_target_pairs={{0,1},{1,0},{2,3},{3,2},{4,5},{5,4},{6,7},{7,6},{8,9},{9,8},{10,11... | collective-permute-start | bytes 1769480 | tf_op jit(solution)/shard_map/ppermute | solution.py:43
  237.1 47.2 %collective-permute-start.6 = (bf16[2,2,2,24,1152]{4,3,2,1,0:T(8,128)(2,1)}, bf16[2,2,2,24,1152]{4,3,2,1,0:T(8,128)(2,1)}, u32[]{:S(2)}, u32[]{:S(2)}) collective-permute-start(bf16[2,2,2,24,1152]{4,3,2,1,0:T(8,128)(2,1)} %pad_maximum_fusion.13), channel_id=1, source_target_pairs={{0,16},{1,17},{2,18},{3,19},{4,20},{5,21},{6,22},{7,23},{8,24},{9,... | collective-permute-start | bytes 1327112 | tf_op jit(solution)/shard_map/ppermute | solution.py:43
  237.8 49.3 %collective-permute-start.8 = (bf16[2,2,2,24,1152]{4,3,2,1,0:T(8,128)(2,1)}, bf16[2,2,2,24,1152]{4,3,2,1,0:T(8,128)(2,1)}, u32[]{:S(2)}, u32[]{:S(2)}) collective-permute-start(bf16[2,2,2,24,1152]{4,3,2,1,0:T(8,128)(2,1)} %pad_maximum_fusion.14), channel_id=1, source_target_pairs={{0,8},{1,9},{2,10},{3,11},{4,12},{5,13},{6,14},{7,15},{8,0},{9,1},... | collective-permute-start | bytes 1327112 | tf_op jit(solution)/shard_map/ppermute | solution.py:43
  239.9 48.9 %collective-permute-start.27 = (bf16[2,2,2,96,384]{4,3,2,1,0:T(8,128)(2,1)}, bf16[2,2,2,96,384]{4,3,2,1,0:T(8,128)(2,1)}, u32[]{:S(2)}, u32[]{:S(2)}) collective-permute-start(bf16[2,2,2,96,384]{4,3,2,1,0:T(8,128)(2,1)} %pad_maximum_fusion.7), channel_id=1, source_target_pairs={{0,16},{1,17},{2,18},{3,19},{4,20},{5,21},{6,22},{7,23},{8,24},{9,... | collective-permute-start | bytes 1769480 | tf_op jit(solution)/shard_map/ppermute | solution.py:43
  242.3 48.4 %collective-permute-start.29 = (bf16[2,2,2,96,384]{4,3,2,1,0:T(8,128)(2,1)}, bf16[2,2,2,96,384]{4,3,2,1,0:T(8,128)(2,1)}, u32[]{:S(2)}, u32[]{:S(2)}) collective-permute-start(bf16[2,2,2,96,384]{4,3,2,1,0:T(8,128)(2,1)} %pad_maximum_fusion.8), channel_id=1, source_target_pairs={{0,8},{1,9},{2,10},{3,11},{4,12},{5,13},{6,14},{7,15},{8,0},{9,1},... | collective-permute-start | bytes 1769480 | tf_op jit(solution)/shard_map/ppermute | solution.py:43
  252.4 41.6 %collective-permute-start.20 = (bf16[2,2,2,24,1536]{4,3,2,1,0:T(8,128)(2,1)}, bf16[2,2,2,24,1536]{4,3,2,1,0:T(8,128)(2,1)}, u32[]{:S(2)}, u32[]{:S(2)}) collective-permute-start(bf16[2,2,2,24,1536]{4,3,2,1,0:T(8,128)(2,1)} %pad_maximum_fusion.5), channel_id=1, source_target_pairs={{0,16},{1,17},{2,18},{3,19},{4,20},{5,21},{6,22},{7,23},{8,24},{9,... | collective-permute-start | bytes 1769480 | tf_op jit(solution)/shard_map/ppermute | solution.py:43
  284.3 14.5 %collective-permute-start.22 = (bf16[2,2,2,24,1536]{4,3,2,1,0:T(8,128)(2,1)S(1)}, bf16[2,2,2,24,1536]{4,3,2,1,0:T(8,128)(2,1)S(1)}, u32[]{:S(2)}, u32[]{:S(2)}) collective-permute-start(bf16[2,2,2,24,1536]{4,3,2,1,0:T(8,128)(2,1)S(1)} %copy-done.180), channel_id=1, source_target_pairs={{0,8},{1,9},{2,10},{3,11},{4,12},{5,13},{6,14},{7,15},{8,0},{9,1},... | collective-permute-start | bytes 1769480 | tf_op jit(solution)/shard_map/ppermute | solution.py:43
  288.7 12.6 %collective-permute-start.9 = (bf16[2,2,2,2,2,24,1152]{6,5,3,2,0,1,4:T(8,128)(2,1)S(1)}, bf16[2,2,2,2,2,24,1152]{6,5,3,2,0,1,4:T(8,128)(2,1)S(1)}, u32[]{:S(2)}, u32[]{:S(2)}) collective-permute-start(bf16[2,2,2,2,2,24,1152]{6,5,3,2,0,1,4:T(8,128)(2,1)S(1)} %pad_maximum_fusion.3), channel_id=1, source_target_pairs={{0,1},{1,0},{2,3},{3,2},{4,5},{5,4},{6,7},{7,6},{8,9},{9,8},{10,11... | collective-permute-start | bytes 5308424 | tf_op jit(solution)/shard_map/ppermute | solution.py:43
  294.1 104.5 %collective-permute-start.30 = (bf16[2,2,2,2,2,96,384]{6,5,3,2,0,1,4:T(8,128)(2,1)}, bf16[2,2,2,2,2,96,384]{6,5,3,2,0,1,4:T(8,128)(2,1)}, u32[]{:S(2)}, u32[]{:S(2)}) collective-permute-start(bf16[2,2,2,2,2,96,384]{6,5,3,2,0,1,4:T(8,128)(2,1)} %pad_maximum_fusion.2), channel_id=1, source_target_pairs={{0,1},{1,0},{2,3},{3,2},{4,5},{5,4},{6,7},{7,6},{8,9},{9,8},{10,11... | collective-permute-start | bytes 7077896 | tf_op jit(solution)/shard_map/ppermute | solution.py:43
  301.2 117.0 %collective-permute-start.23 = (bf16[2,2,2,2,2,24,1536]{6,5,3,2,0,1,4:T(8,128)(2,1)}, bf16[2,2,2,2,2,24,1536]{6,5,3,2,0,1,4:T(8,128)(2,1)}, u32[]{:S(2)}, u32[]{:S(2)}) collective-permute-start(bf16[2,2,2,2,2,24,1536]{6,5,3,2,0,1,4:T(8,128)(2,1)} %pad_maximum_fusion.1), channel_id=1, source_target_pairs={{0,1},{1,0},{2,3},{3,2},{4,5},{5,4},{6,7},{7,6},{8,9},{9,8},{10,11... | collective-permute-start | bytes 7077896 | tf_op jit(solution)/shard_map/ppermute | solution.py:43
  660.8 194.8 %collective-permute-start.177 = (bf16[4,2,2,2,8,128]{5,4,2,3,1,0:T(8,128)(2,1)}, bf16[4,2,2,2,8,128]{5,4,2,3,1,0:T(8,128)(2,1)}, u32[]{:S(2)}, u32[]{:S(2)}) collective-permute-start(bf16[4,2,2,2,8,128]{5,4,2,3,1,0:T(8,128)(2,1)} %dynamic-slice_bitcast_fusion.35), channel_id=1, source_target_pairs={{0,1},{1,0},{2,3},{3,2},{4,5},{5,4},{6,7},{7,6},{8,9},{9,8},{10,11... | collective-permute-start | bytes 196616 | tf_op jit(solution)/shard_map/ppermute | solution.py:43
  664.5 239.1 %collective-permute-start.122 = (bf16[4,2,2,2,24,128]{5,4,1,0,3,2:T(8,128)(2,1)}, bf16[4,2,2,2,24,128]{5,4,1,0,3,2:T(8,128)(2,1)}, u32[]{:S(2)}, u32[]{:S(2)}) collective-permute-start(bf16[4,2,2,2,24,128]{5,4,1,0,3,2:T(8,128)(2,1)} %bitcast.1724), channel_id=1, source_target_pairs={{0,1},{1,0},{2,3},{3,2},{4,5},{5,4},{6,7},{7,6},{8,9},{9,8},{10,11... | collective-permute-start | bytes 589832 | tf_op jit(solution)/shard_map/ppermute | solution.py:43
  711.1 225.3 %collective-permute-start.89 = (bf16[4,2,2,2,24,384]{5,4,1,0,3,2:T(8,128)(2,1)}, bf16[4,2,2,2,24,384]{5,4,1,0,3,2:T(8,128)(2,1)}, u32[]{:S(2)}, u32[]{:S(2)}) collective-permute-start(bf16[4,2,2,2,24,384]{5,4,1,0,3,2:T(8,128)(2,1)} %bitcast.1723), channel_id=1, source_target_pairs={{0,1},{1,0},{2,3},{3,2},{4,5},{5,4},{6,7},{7,6},{8,9},{9,8},{10,11... | collective-permute-start | bytes 1769480 | tf_op jit(solution)/shard_map/ppermute | solution.py:43
  715.2 361.0 %collective-permute-start.111 = (bf16[4,2,2,2,96,384]{5,4,1,0,3,2:T(8,128)(2,1)}, bf16[4,2,2,2,96,384]{5,4,1,0,3,2:T(8,128)(2,1)}, u32[]{:S(2)}, u32[]{:S(2)}) collective-permute-start(bf16[4,2,2,2,96,384]{5,4,1,0,3,2:T(8,128)(2,1)} %bitcast.1716), channel_id=1, source_target_pairs={{0,1},{1,0},{2,3},{3,2},{4,5},{5,4},{6,7},{7,6},{8,9},{9,8},{10,11... | collective-permute-start | bytes 7077896 | tf_op jit(solution)/shard_map/ppermute | solution.py:43
  791.7 41.8 %collective-permute-start.73 = (f32[4,832]{1,0:T(4,128)}, f32[4,832]{1,0:T(4,128)}, u32[]{:S(2)}, u32[]{:S(2)}) collective-permute-start(f32[4,832]{1,0:T(4,128)} %bitcast.1727), channel_id=1, source_target_pairs={{0,1},{1,0},{2,3},{3,2},{4,5},{5,4},{6,7},{7,6},{8,9},{9,8},{10,11... | collective-permute-start | bytes 39944 | tf_op jit(solution)/shard_map/ppermute | solution.py:43
  836.1 9.9 collective-permute-start.74
  854.1 27.8 %collective-permute-start.76 = (f32[832]{0:T(1024)}, f32[832]{0:T(1024)}, u32[]{:S(2)}, u32[]{:S(2)}) collective-permute-start(f32[832]{0:T(1024)} %add.710), channel_id=1, source_target_pairs={{0,8},{1,9},{2,10},{3,11},{4,12},{5,13},{6,14},{7,15},{8,0},{9,1},... | collective-permute-start | bytes 9992 | tf_op jit(solution)/shard_map/ppermute | solution.py:43
  872.0 11.3 collective-permute-start.182
  882.7 9.5 collective-permute-start.77
  884.0 8.1 collective-permute-start.183
  896.1 185.0 %collective-permute-start.100 = (bf16[4,2,2,2,24,1536]{5,4,1,0,3,2:T(8,128)(2,1)}, bf16[4,2,2,2,24,1536]{5,4,1,0,3,2:T(8,128)(2,1)}, u32[]{:S(2)}, u32[]{:S(2)}) collective-permute-start(bf16[4,2,2,2,24,1536]{5,4,1,0,3,2:T(8,128)(2,1)} %bitcast.1780), channel_id=1, source_target_pairs={{0,1},{1,0},{2,3},{3,2},{4,5},{5,4},{6,7},{7,6},{8,9},{9,8},{10,11... | collective-permute-start | bytes 7077896 | tf_op jit(solution)/shard_map/ppermute | solution.py:43
  926.7 11.5 collective-permute-start.144
  939.7 119.8 %collective-permute-start.78 = (bf16[4,2,2,2,24,1152]{5,4,1,0,3,2:T(8,128)(2,1)S(1)}, bf16[4,2,2,2,24,1152]{5,4,1,0,3,2:T(8,128)(2,1)S(1)}, u32[]{:S(2)}, u32[]{:S(2)}) collective-permute-start(bf16[4,2,2,2,24,1152]{5,4,1,0,3,2:T(8,128)(2,1)S(1)} %bitcast.1823), channel_id=1, source_target_pairs={{0,1},{1,0},{2,3},{3,2},{4,5},{5,4},{6,7},{7,6},{8,9},{9,8},{10,11... | collective-permute-start | bytes 5308424 | tf_op jit(solution)/shard_map/ppermute | solution.py:43
  1060.0 9.7 collective-permute-start.79
  1063.4 11.1 collective-permute-start.81
  1069.9 13.6 %collective-permute-start.80 = (bf16[4,24,1152]{2,1,0:T(8,128)(2,1)S(1)}, bf16[4,24,1152]{2,1,0:T(8,128)(2,1)S(1)}, u32[]{:S(2)}, u32[]{:S(2)}) collective-permute-start(bf16[4,24,1152]{2,1,0:T(8,128)(2,1)S(1)} %dynamic-slice_bitcast_fusion.11), channel_id=1, source_target_pairs={{0,16},{1,17},{2,18},{3,19},{4,20},{5,21},{6,22},{7,23},{8,24},{9,... | collective-permute-start | bytes 663560 | tf_op jit(solution)/shard_map/ppermute | solution.py:43
  1074.7 8.8 collective-permute-start.82
  1078.9 39.2 %collective-permute-start.112 = (bf16[4,2,96,384]{3,2,1,0:T(8,128)(2,1)S(1)}, bf16[4,2,96,384]{3,2,1,0:T(8,128)(2,1)S(1)}, u32[]{:S(2)}, u32[]{:S(2)}) collective-permute-start(bf16[4,2,96,384]{3,2,1,0:T(8,128)(2,1)S(1)} %dynamic-slice_bitcast_fusion.1), channel_id=1, source_target_pairs={{0,8},{1,9},{2,10},{3,11},{4,12},{5,13},{6,14},{7,15},{8,0},{9,1},... | collective-permute-start | bytes 1769480 | tf_op jit(solution)/shard_map/ppermute | solution.py:43
  1079.7 39.3 %collective-permute-start.114 = (bf16[4,2,96,384]{3,2,0,1:T(8,128)(2,1)S(1)}, bf16[4,2,96,384]{3,2,0,1:T(8,128)(2,1)S(1)}, u32[]{:S(2)}, u32[]{:S(2)}) collective-permute-start(bf16[4,2,96,384]{3,2,0,1:T(8,128)(2,1)S(1)} %dynamic-slice_bitcast_fusion), channel_id=1, source_target_pairs={{0,16},{1,17},{2,18},{3,19},{4,20},{5,21},{6,22},{7,23},{8,24},{9,... | collective-permute-start | bytes 1769480 | tf_op jit(solution)/shard_map/ppermute | solution.py:43
  1083.7 9.3 collective-permute-start.83
  1100.4 20.4 %collective-permute-start.101 = (bf16[4,2,24,1536]{3,2,1,0:T(8,128)(2,1)S(1)}, bf16[4,2,24,1536]{3,2,1,0:T(8,128)(2,1)S(1)}, u32[]{:S(2)}, u32[]{:S(2)}) collective-permute-start(bf16[4,2,24,1536]{3,2,1,0:T(8,128)(2,1)S(1)} %dynamic-slice_bitcast_fusion.3), channel_id=1, source_target_pairs={{0,8},{1,9},{2,10},{3,11},{4,12},{5,13},{6,14},{7,15},{8,0},{9,1},... | collective-permute-start | bytes 1769480 | tf_op jit(solution)/shard_map/ppermute | solution.py:43
  1102.9 19.0 %collective-permute-start.103 = (bf16[4,2,24,1536]{3,2,0,1:T(8,128)(2,1)S(1)}, bf16[4,2,24,1536]{3,2,0,1:T(8,128)(2,1)S(1)}, u32[]{:S(2)}, u32[]{:S(2)}) collective-permute-start(bf16[4,2,24,1536]{3,2,0,1:T(8,128)(2,1)S(1)} %dynamic-slice_bitcast_fusion.2), channel_id=1, source_target_pairs={{0,16},{1,17},{2,18},{3,19},{4,20},{5,21},{6,22},{7,23},{8,24},{9,... | collective-permute-start | bytes 1769480 | tf_op jit(solution)/shard_map/ppermute | solution.py:43
  1103.3 8.3 collective-permute-start.88
  1121.1 7.9 collective-permute-start.102
  1126.1 13.8 %collective-permute-start.116 = (bf16[2,2,96,384]{3,2,1,0:T(8,128)(2,1)S(1)}, bf16[2,2,96,384]{3,2,1,0:T(8,128)(2,1)S(1)}, u32[]{:S(2)}, u32[]{:S(2)}) collective-permute-start(bf16[2,2,96,384]{3,2,1,0:T(8,128)(2,1)S(1)} %fusion.198), channel_id=1, source_target_pairs={{0,4},{1,5},{2,6},{3,7},{4,0},{5,1},{6,2},{7,3},{8,12},{9,13},{10,... | collective-permute-start | bytes 884744 | tf_op jit(solution)/shard_map/ppermute | solution.py:43
  1129.2 13.8 %collective-permute-start.105 = (bf16[2,2,24,1536]{3,2,1,0:T(8,128)(2,1)S(1)}, bf16[2,2,24,1536]{3,2,1,0:T(8,128)(2,1)S(1)}, u32[]{:S(2)}, u32[]{:S(2)}) collective-permute-start(bf16[2,2,24,1536]{3,2,1,0:T(8,128)(2,1)S(1)} %fusion.202), channel_id=1, source_target_pairs={{0,4},{1,5},{2,6},{3,7},{4,0},{5,1},{6,2},{7,3},{8,12},{9,13},{10,... | collective-permute-start | bytes 884744 | tf_op jit(solution)/shard_map/ppermute | solution.py:43
  (394 other events, 2548.9 us)

commit v2 on v1

v2 whole, which is shorter than its diff:
```python
import math

import jax
import jax.numpy as jnp
from jax import lax
from jax.experimental import pallas as pl
from jax.experimental.pallas import tpu as pltpu
from jax.sharding import PartitionSpec as P

D = 768
HEADS = 12
HD = 64
GRID = 24
COUNT = GRID * GRID
DATASETS = 10
NH = 4
F32 = jnp.float32
BF16 = jnp.bfloat16
BOTH = ("rep", "wide")
VMEM = 60 << 20


def mm(left, right):
    return jnp.dot(left, right, preferred_element_type=F32)


def mm_tn(left, right):
    return lax.dot_general(left, right, (((0,), (0,)), ((), ())), preferred_element_type=F32)


def mm_nt(left, right):
    return lax.dot_general(left, right, (((1,), (1,)), ((), ())), preferred_element_type=F32)


def spec(shape, dtype=BF16):
    return jax.ShapeDtypeStruct(shape, dtype)


def whole(shape):
    return pl.BlockSpec(shape, lambda *_: (0,) * len(shape), pipeline_mode=pl.Buffered(1))


def params():
    return pltpu.CompilerParams(vmem_limit_bytes=VMEM)


def cost(macs, size):
    return pl.CostEstimate(flops=2 * int(macs), bytes_accessed=int(size), transcendentals=0)


FLIP = {"y": 16, "x": 8, "z1": 4, "z0": 2, "c": 1}


def swap(value, *names):
    flip = sum(FLIP[name] for name in names)
    return lax.ppermute(value, BOTH, [(i, i ^ flip) for i in range(32)])


def bits():
    rep, wide = lax.axis_index("rep"), lax.axis_index("wide")
    return {"y": rep // 2, "x": rep % 2, "z1": wide // 4, "z0": (wide // 2) % 2, "c": wide % 2}


def bit_vector():
    b = bits()
    return jnp.stack([b[k] for k in ("y", "x", "z1", "z0", "c")]).astype(jnp.int32)


def both(value, name):
    other = swap(value, name)
    first = bits()[name] == 0
    return jnp.stack([jnp.where(first, value, other), jnp.where(first, other, value)])


def gather(piece, order):
    value = jnp.stack([piece, swap(piece, "z0"), swap(piece, "z1"), swap(piece, "z1", "z0")])
    value = jnp.concatenate([value, swap(value, order[0])])
    other = swap(value, order[1])
    return value, other, swap(value, "c"), swap(other, "c")


def scatter(keep, send, order):
    def add(*terms):
        return sum(term.astype(F32) for term in terms).astype(BF16)

    got = swap(send, "c")
    for name, half in ((order[0], 8), (order[1], 4)):
        mine, theirs = add(keep[:half], got[:half]), add(keep[half:], got[half:])
        keep, got = mine, swap(theirs, name)
    terms = [add(keep[i], got[i]) for i in range(4)]
    total = add(terms[0], swap(terms[1], "z0"), swap(terms[2], "z1"), swap(terms[3], "z1", "z0"))
    return total, swap(total, order[1]), swap(total, order[0]), swap(total, *order)


def locate(me, order, plane, z, core):
    place = {order[0]: plane[0], order[1]: plane[1]}
    shard = ((me[2] ^ z[0]) * 2 + (me[3] ^ z[1])) * 2 + (me[4] ^ core)
    return shard, me[0] ^ place["y"], me[1] ^ place["x"]


def target(ref, lead, shard, y, x):
    rows, cols = ref.shape[-2] // 16, ref.shape[-1] // 2
    at = pl.ds(pl.multiple_of((shard * 2 + y) * rows, 16), rows), pl.ds(pl.multiple_of(x * cols, 128), cols)
    return ref.at[(lead,) + at] if lead is not None else ref.at[at]


def parts_of(shapes):
    entries = []
    for k, shape in enumerate(shapes):
        for lead in (range(shape[0]) if len(shape) == 3 else (None,)):
            entries.append((k, lead, shape[-2] // 16, shape[-1] // 2))
    beside = len({e[2] for e in entries}) == 1 and len({e[3] for e in entries}) > 1
    out, at = [], 0
    for k, lead, r, n in entries:
        out.append((k, lead, (0, r), (at, n)) if beside else (k, lead, (at, r), (0, n)))
        at += n if beside else r
    return out


def piece_shape(shapes):
    parts = parts_of(shapes)
    return max(p[2][0] + p[2][1] for p in parts), max(p[3][0] + p[3][1] for p in parts)


def cut(shards, shapes):
    b = bits()
    out = jnp.zeros(piece_shape(shapes), BF16)
    for k, lead, (r0, r), (c0, n) in parts_of(shapes):
        shard = shards[k] if lead is None else shards[k][lead]
        part = lax.dynamic_slice(shard, (b["y"] * r, b["x"] * n), (r, n))
        out = lax.dynamic_update_slice(out, part, (r0, c0))
    return out


def assemble(pieces, shapes, order, me):
    parts = parts_of(shapes)
    copies = 32 * len(parts)

    def body(me_ref, *refs):
        ins, outs, sem = refs[:4], refs[4:-1], refs[-1]
        started = []
        for a in range(4):
            second, core = a % 2, a // 2
            for s in range(8):
                shard, y, x = locate(me_ref, order, (s // 4, second), (s // 2 % 2, s % 2), core)
                for k, lead, (r0, r), (c0, n) in parts:
                    copy = pltpu.make_async_copy(
                        ins[a].at[s, pl.ds(r0, r), pl.ds(c0, n)], target(outs[k], lead, shard, y, x), sem.at[len(started)])
                    copy.start()
                    started.append(copy)
        for copy in started:
            copy.wait()

    return pl.pallas_call(
        body,
        grid=(1,),
        in_specs=[pl.BlockSpec(memory_space=pltpu.SMEM)] + [pl.BlockSpec(memory_space=pl.ANY)] * 4,
        out_specs=[whole(s) for s in shapes],
        out_shape=[spec(s) for s in shapes],
        scratch_shapes=[pltpu.SemaphoreType.DMA((copies,))],
        compiler_params=params(),
        cost_estimate=cost(0, 4 * sum(math.prod(s) for s in shapes)),
        name="assemble",
    )(me, *pieces)


def pack(grads, order, me):
    shapes = [g.shape for g in grads]
    parts = parts_of(shapes)
    copies = 32 * len(parts)

    def body(me_ref, *refs):
        ins, outs, sem = refs[:-3], refs[-3:-1], refs[-1]
        started = []
        for core in range(2):
            for s in range(16):
                shard, y, x = locate(me_ref, order, (s // 8, s // 4 % 2), (s // 2 % 2, s % 2), core)
                for k, lead, (r0, r), (c0, n) in parts:
                    copy = pltpu.make_async_copy(
                        target(ins[k], lead, shard, y, x), outs[core].at[s, pl.ds(r0, r), pl.ds(c0, n)], sem.at[len(started)])
                    copy.start()
                    started.append(copy)
        for copy in started:
            copy.wait()

    return pl.pallas_call(
        body,
        grid=(1,),
        in_specs=[pl.BlockSpec(memory_space=pltpu.SMEM)] + [whole(s) for s in shapes],
        out_specs=[pl.BlockSpec(memory_space=pl.ANY)] * 2,
        out_shape=[spec((16,) + piece_shape(shapes))] * 2,
        scratch_shapes=[pltpu.SemaphoreType.DMA((copies,))],
        compiler_params=params(),
        cost_estimate=cost(0, 4 * sum(math.prod(s) for s in shapes)),
        name="pack",
    )(me, *grads)


def shares(quarters, shapes, order):
    b = bits()
    first, second = b[order[0]] == 0, b[order[1]] == 0
    q = quarters
    ordered = {}
    for i in range(2):
        one = jnp.where(first, q[i], q[2 + i])
        two = jnp.where(first, q[2 + i], q[i])
        ordered[0, i], ordered[1, i] = one, two
    place = {}
    for i in range(2):
        place[i, 0] = jnp.where(second, ordered[i, 0], ordered[i, 1])
        place[i, 1] = jnp.where(second, ordered[i, 1], ordered[i, 0])

    def at(y, x):
        return place[(y, x) if order[0] == "y" else (x, y)]

    found = {}
    for k, lead, (r0, r), (c0, n) in parts_of(shapes):
        rows = [jnp.concatenate([at(y, x)[r0:r0 + r, c0:c0 + n] for x in range(2)], 1) for y in range(2)]
        found.setdefault(k, []).append(jnp.concatenate(rows, 0).astype(F32))
    return [found[k][0] if len(shapes[k]) == 2 else jnp.stack(found[k]) for k in range(len(shapes))]


def gather_small(value):
    value = both(value, "z0")
    value = both(value, "z1")
    value = jnp.moveaxis(both(value, "c"), 0, 2)
    return value.reshape((8,) + value.shape[3:])


def sum_small(value):
    b = bits()

    def halve(part, name, axis):
        mine = lax.dynamic_index_in_dim(part, b[name], axis, keepdims=False)
        theirs = lax.dynamic_index_in_dim(part, 1 - b[name], axis, keepdims=False)
        return mine + swap(theirs, name)

    value = value.reshape((2, 2, 2) + value.shape[1:])
    value = halve(value, "c", 2)
    value = halve(value, "z1", 0)
    value = halve(value, "z0", 0)
    value = value + swap(value, "x")
    return value + swap(value, "y")


def gelu_pair(values):
    cdf = 0.5 + 0.5 * lax.erf(values * 0.7071067811865476)
    pdf = 0.3989422804014327 * jnp.exp(-0.5 * values * values)
    return values * cdf, cdf + values * pdf


def normalize(values):
    centred = values - jnp.mean(values, -1, keepdims=True)
    recip = lax.rsqrt(jnp.mean(centred * centred, -1, keepdims=True) + 1e-06)
    return centred * recip, recip


def norm_transpose(grad_normed, normed, recip):
    return recip * (
        grad_normed
        - jnp.mean(grad_normed, -1, keepdims=True)
        - normed * jnp.mean(grad_normed * normed, -1, keepdims=True)
    )


def attention_body(q_ref, k_ref, v_ref, o_ref, e_ref, r_ref):
    for h in range(NH):
        c = slice(HD * h, HD * h + HD)
        s = mm_nt(k_ref[:, c], q_ref[:, c] * jnp.asarray(0.125, BF16))
        e = jnp.exp(s - jnp.max(s, 0, keepdims=True))
        r = 1.0 / jnp.sum(e, 0, keepdims=True)
        low = e.astype(BF16)
        e_ref[h] = low
        o_ref[:, c] = (mm_tn(v_ref[:, c], low) * r).T.astype(BF16)
        r_ref[0, h:h + 1, :] = r


def attention_specs():
    steps = HEADS // NH

    def cols(offset):
        return pl.BlockSpec((COUNT, NH * HD), lambda i, h: (i, offset + h))

    probs = pl.BlockSpec((NH, COUNT, COUNT), lambda i, h: (i * steps + h, 0, 0))
    sums = pl.BlockSpec((1, NH, COUNT), lambda i, h: (i * steps + h, 0, 0))
    return steps, cols, probs, sums


def attention(qkv):
    rows = qkv.shape[0]
    images = rows // COUNT
    steps, cols, probs, sums = attention_specs()
    return pl.pallas_call(
        attention_body,
        grid=(images, steps),
        in_specs=[cols(0), cols(steps), cols(2 * steps)],
        out_specs=[cols(0), probs, sums],
        out_shape=[spec((rows, D)), spec((images * HEADS, COUNT, COUNT)), spec((images * steps, NH, COUNT), F32)],
        compiler_params=params(),
        cost_estimate=cost(8 * images * HEADS * COUNT * COUNT * HD, images * HEADS * COUNT * COUNT * 2),
        name="attention",
    )(qkv, qkv, qkv)


def attention_back_body(q_ref, k_ref, v_ref, o_ref, e_ref, r_ref, do_ref, dq_ref, dk_ref, dv_ref):
    ones = jnp.ones((8, HD), BF16)
    for h in range(NH):
        c = slice(HD * h, HD * h + HD)
        do = do_ref[:, c]
        delta = mm_nt(ones, (do.astype(F32) * o_ref[:, c].astype(F32)).astype(BF16))[0:1]
        prob = e_ref[h].astype(F32) * r_ref[0, h:h + 1, :]
        dp = mm_nt(v_ref[:, c], do)
        ds = (prob * (dp - delta)).astype(BF16)
        dv_ref[:, c] = mm(prob.astype(BF16), do).astype(BF16)
        dk_ref[:, c] = (mm(ds, q_ref[:, c]) * 0.125).astype(BF16)
        dq_ref[:, c] = (mm_tn(ds, k_ref[:, c]) * 0.125).astype(BF16)


def attention_back(qkv, o, e, r, do):
    rows = qkv.shape[0]
    images = rows // COUNT
    steps, cols, probs, sums = attention_specs()
    return pl.pallas_call(
        attention_back_body,
        grid=(images, steps),
        in_specs=[cols(0), cols(steps), cols(2 * steps), cols(0), probs, sums, cols(0)],
        out_specs=[cols(0)] * 3,
        out_shape=[spec((rows, D))] * 3,
        compiler_params=params(),
        cost_estimate=cost(16 * images * HEADS * COUNT * COUNT * HD, images * HEADS * COUNT * COUNT * 2),
        name="attention_back",
    )(qkv, qkv, qkv, o, e, r, do)


def spread(value, out_ref, rows, sign):
    count, ch = value.shape
    at = lax.broadcasted_iota(jnp.int32, (count, 1), 0)
    col = at % GRID
    gap = jnp.zeros((GRID, ch), F32)
    for dx in (-1, 0, 1):
        step = sign * dx
        moved = value
        if step:
            moved = pltpu.roll(value, (-step) % count, 0)
            moved = jnp.where((col + step >= 0) & (col + step < GRID), moved, 0.0)
        for dy in (-1, 0, 1):
            block = 3 * (dy + 1) + dx + 1
            if sign * dy == 1:
                part = jnp.concatenate([moved[GRID:], gap], 0)
            elif sign * dy == -1:
                part = jnp.concatenate([gap, moved[:-GRID]], 0)
            else:
                part = moved
            out_ref[rows, block * ch:(block + 1) * ch] = part.astype(BF16)


def units_body(x_ref, wre_ref, w_ref, t1_ref, s1_ref, t2_ref, s2_ref, z_ref, cols):
    count = x_ref.shape[0]
    z = mm(x_ref[...], wre_ref[...])
    for unit in range(2):
        act, slope = gelu_pair(z)
        t1_ref[unit], s1_ref[unit] = act.astype(BF16), slope.astype(BF16)
        spread(act, cols, slice(0, count), 1)
        act, slope = gelu_pair(mm(cols[...], w_ref[2 * unit]))
        t2_ref[unit], s2_ref[unit] = act.astype(BF16), slope.astype(BF16)
        spread(act, cols, slice(0, count), 1)
        z = z + mm(cols[...], w_ref[2 * unit + 1])
    z_ref[...] = z.astype(BF16)


def units(x3b, w_re, w_conv):
    rows, ch = x3b.shape[0], w_re.shape[1]
    acts = pl.BlockSpec((2, COUNT, ch), lambda i: (0, i, 0))
    return pl.pallas_call(
        units_body,
        grid=(rows // COUNT,),
        in_specs=[pl.BlockSpec((COUNT, D), lambda i: (i, 0)), whole(w_re.shape), whole(w_conv.shape)],
        out_specs=[acts] * 4 + [pl.BlockSpec((COUNT, ch), lambda i: (i, 0))],
        out_shape=[spec((2, rows, ch))] * 4 + [spec((rows, ch))],
        scratch_shapes=[pltpu.VMEM((COUNT, 9 * ch), BF16)],
        compiler_params=params(),
        cost_estimate=cost(8 * rows * 9 * ch * ch, 12 << 20),
        name="units",
    )(x3b, w_re, w_conv)


def units_back_body(dq_ref, z_ref, x3b_ref, gt_ref, live_ref, whead_ref, w_ref, wre_ref, t1_ref, s1_ref, t2_ref, s2_ref,
                    gw_ref, ghead_ref, gre_ref, dx3_ref, moved, turned, dz_ref):
    rows, ch = dq_ref.shape
    images = rows // COUNT
    ghead_ref[...] = mm_tn(z_ref[...], dq_ref[...]).astype(BF16)
    dz_ref[...] = mm_nt(dq_ref[...], whead_ref[...])

    def back(index, grad, act_ref, unit):
        for i in range(images):
            at = slice(COUNT * i, COUNT * (i + 1))
            spread(grad[at], moved, at, -1)
        g = mm_tn(act_ref[unit], moved[...])
        for b in range(9):
            at = slice(ch * b, ch * (b + 1))
            gw_ref[index, at, :] = g[:, at].astype(BF16)
            turned[:, at] = w_ref[index, at, :]
        return mm_nt(moved[...], turned[...])

    for unit in (1, 0):
        grad = back(2 * unit + 1, dz_ref[...], t2_ref, unit) * s2_ref[unit].astype(F32)
        grad = back(2 * unit, grad, t1_ref, unit) * s1_ref[unit].astype(F32)
        dz_ref[...] += grad
    dr = dz_ref[...].astype(BF16)
    gre_ref[...] = mm_tn(x3b_ref[...], dr).astype(BF16)
    dx3_ref[...] = gt_ref[...].astype(F32) * live_ref[...] + mm_nt(dr, wre_ref[...])


def units_back(dq, z, x3b, gt, live, w_head, w_conv, w_re, t1, s1, t2, s2):
    rows, ch = dq.shape
    ins = (dq, z, x3b, gt, live, w_head, w_conv, w_re, t1, s1, t2, s2)
    outs = [spec(w_conv.shape), spec(w_head.shape), spec(w_re.shape), spec((rows, D), F32)]
    return pl.pallas_call(
        units_back_body,
        grid=(1,),
        in_specs=[whole(a.shape) for a in ins],
        out_specs=[whole(a.shape) for a in outs],
        out_shape=outs,
        scratch_shapes=[pltpu.VMEM((rows, 9 * ch), BF16), pltpu.VMEM((ch, 9 * ch), BF16), pltpu.VMEM((rows, ch), F32)],
        compiler_params=params(),
        cost_estimate=cost(14 * rows * 9 * ch * ch, 24 << 20),
        name="units_back",
    )(*ins)


def mlp_back_body(dx3_ref, a2_ref, gg_ref, slope_ref, w1_ref, w2_ref, x2_ref, gain_ref, g1_ref, g2_ref, dx2_ref, ggain_ref,
                  dm, total):
    step = pl.program_id(0)

    @pl.when(step == 0)
    def _():
        dm[...] = dx3_ref[...].astype(BF16)
        total[...] = jnp.zeros_like(total)

    g2_ref[...] = mm_tn(gg_ref[...], dm[...]).astype(BF16)
    du = (mm_nt(dm[...], w2_ref[...]) * slope_ref[...].astype(F32)).astype(BF16)
    g1_ref[...] = mm_tn(a2_ref[...], du).astype(BF16)
    total[...] += mm_nt(du, w1_ref[...])

    @pl.when(step == pl.num_programs(0) - 1)
    def _():
        rows = total.shape[0]
        chunk = rows // 6
        sums = jnp.zeros((1, D), F32)
        for p in range(0, rows, chunk):
            at = slice(p, p + chunk)
            da2 = total[at]
            n2, rs2 = normalize(x2_ref[at])
            sums = sums + jnp.sum(da2 * n2, 0, keepdims=True)
            dx2_ref[at] = dx3_ref[at] + norm_transpose(da2 * gain_ref[...], n2, rs2)
        ggain_ref[...] = sums


def mlp_back(dx3, a2, gg, slope, w1, w2, x2, gain, block=512):
    rows, ff = gg.shape
    cols = pl.BlockSpec((rows, block), lambda i: (0, i))
    one, two = pl.BlockSpec((D, block), lambda i: (0, i)), pl.BlockSpec((block, D), lambda i: (i, 0))
    full = whole((rows, D))
    return pl.pallas_call(
        mlp_back_body,
        grid=(ff // block,),
        in_specs=[full, full, cols, cols, one, two, full, whole((1, D))],
        out_specs=[one, two, full, whole((1, D))],
        out_shape=[spec(w1.shape), spec(w2.shape), spec((rows, D), F32), spec((1, D), F32)],
        scratch_shapes=[pltpu.VMEM((rows, D), BF16), pltpu.VMEM((rows, D), F32)],
        compiler_params=params(),
        cost_estimate=cost(4 * rows * D * ff, 40 << 20),
        name="mlp_back",
    )(dx3, a2, gg, slope, w1, w2, x2, gain)


def upsample_pair():
    size = 2 * GRID

    def weights(target, source):
        numer = target * (GRID - 1)
        lower = numer // (size - 1)
        frac = (numer - lower * (size - 1)).astype(F32) / (size - 1)
        return jnp.where(source == lower, 1.0 - frac, 0.0) + jnp.where(source == lower + 1, frac, 0.0)

    target = lax.broadcasted_iota(jnp.int32, (size * size, COUNT), 0)
    source = lax.broadcasted_iota(jnp.int32, (size * size, COUNT), 1)
    return (weights(target // size, source // GRID) * weights(target % size, source % GRID)).astype(BF16)


CHUNKS = (("x", "y"), ("y", "x"), ("x", "y"), ("y", "x"))


def shards(tokens, live_count, dataset_id, shift_flag, norm_gains, w_qkv, w_attn_out, w_fc1, w_fc2, w_reassemble,
           conv_kernels, w_head, scale_table, shift_table, d_tokens_out, d_joined):
    slots, count = tokens.shape[:2]
    rows = slots * count
    live = (jnp.arange(slots, dtype=jnp.int32) < live_count[0]).astype(F32)
    live_rows = jnp.repeat(live, count)[:, None]
    onehot = (dataset_id[:, None] == jnp.arange(DATASETS, dtype=jnp.int32)[None, :]).astype(F32)
    flags = shift_flag.astype(F32)
    neighbours = (lax.axis_size("rep"), lax.axis_size("wide")) == (4, 8)
    ch = w_head.shape[1]
    shard_sets = ((w_qkv,), (w_attn_out, w_fc1, w_reassemble), (w_fc2,), (conv_kernels, w_head))
    wide = lax.axis_size("wide")
    shape_sets = [[s.shape[:-2] + (s.shape[-2] * wide, s.shape[-1]) for s in group] for group in shard_sets]
    g, t = norm_gains.shape[1], scale_table.shape[1]
    if neighbours:
        me = bit_vector()
        small = jnp.concatenate([norm_gains.reshape(-1), scale_table.reshape(-1), shift_table.reshape(-1)])
        small = gather_small(small)

        def wide_cols(part, lead):
            return part.reshape(8, lead, -1).transpose(1, 0, 2).reshape(lead, -1)

        gains = wide_cols(small[:, :2 * g], 2)
        scales = wide_cols(small[:, 2 * g:2 * g + DATASETS * t], DATASETS)
        shifts = wide_cols(small[:, 2 * g + DATASETS * t:], DATASETS)
        full = []
        for group, shapes, order in zip(shard_sets, shape_sets, CHUNKS):
            full.append(assemble(gather(cut(group, shapes), order), shapes, order, me))
    else:
        def gathered(part, axis):
            return lax.all_gather(part, "wide", axis=axis, tiled=True)

        gains, scales, shifts = gathered(norm_gains, 1), gathered(scale_table, 1), gathered(shift_table, 1)
        full = [[gathered(s, s.ndim - 2) for s in group] for group in shard_sets]
    (f_qkv,), (f_out, f_fc1, f_re), (f_fc2,), (f_conv, f_head) = full

    gains = gains.astype(F32)
    scale = jnp.sum(onehot[:, :, None] * scales.astype(F32)[None], 1)
    shift = flags[:, None] * jnp.sum(onehot[:, :, None] * shifts.astype(F32)[None], 1)
    pair = upsample_pair()
    down = jnp.einsum("ts,itc->isc", pair, d_joined, preferred_element_type=F32) * live[:, None, None]
    g_shift_rows = flags[:, None] * jnp.sum(d_joined.astype(F32), 1) * live[:, None]
    x = tokens.reshape(rows, D).astype(F32)
    n1, rs1 = normalize(x)
    a1 = (n1 * gains[0]).astype(BF16)
    qkv = mm(a1, f_qkv).astype(BF16)
    o, e, r = attention(qkv)
    x2 = x + mm(o, f_out)
    n2, rs2 = normalize(x2)
    a2 = (n2 * gains[1]).astype(BF16)
    gg, slope = gelu_pair(mm(a2, f_fc1))
    gg, slope = gg.astype(BF16), slope.astype(BF16)
    x3 = x2 + mm(gg, f_fc2)
    tokens_out = (x3 * live_rows).astype(BF16).reshape(tokens.shape)
    x3b = x3.astype(BF16)
    t1, s1, t2, s2, zb = units(x3b, f_re, f_conv)
    head = mm(zb, f_head).reshape(slots, count, ch)
    hd = jnp.einsum("ts,isc->itc", pair, head.astype(BF16), preferred_element_type=F32)
    joined = ((hd * scale[:, None] + shift[:, None]) * live[:, None, None]).astype(BF16)

    g_scale_rows = jnp.sum(head * down, 1)
    g_scale = jnp.sum(onehot[:, :, None] * g_scale_rows[:, None, :], 0)
    g_shift = jnp.sum(onehot[:, :, None] * g_shift_rows[:, None, :], 0)
    dq_map = (down * scale[:, None]).astype(BF16).reshape(rows, ch)
    g_conv, g_head, g_re, dx3 = units_back(
        dq_map, zb, x3b, d_tokens_out.reshape(rows, D), live_rows, f_head, f_conv, f_re, t1, s1, t2, s2)
    g_fc1, g_fc2, dx2, g_gain2 = mlp_back(dx3, a2, gg, slope, f_fc1, f_fc2, x2, gains[1:2])
    da = dx2.astype(BF16)
    g_out = mm_tn(o, da).astype(BF16)
    do = mm_nt(da, f_out).astype(BF16)
    dqkv = attention_back(qkv, o, e, r, do)
    g_qkv = jnp.concatenate([mm_tn(a1, part).astype(BF16) for part in dqkv], 1)
    da1 = sum(mm_nt(part, f_qkv[:, D * i:D * (i + 1)]) for i, part in enumerate(dqkv))
    g_gain1 = jnp.sum(da1 * n1, 0)[None]
    d_tokens = (dx2 + norm_transpose(da1 * gains[0], n1, rs1)).astype(BF16).reshape(tokens.shape)

    grad_sets = ((g_qkv,), (g_out, g_fc1, g_re), (g_fc2,), (g_conv, g_head))
    g_gains = jnp.concatenate([g_gain1, g_gain2])
    if neighbours:
        sums = [None] * 4
        for i in (3, 2, 1, 0):
            keep, send = pack(grad_sets[i], CHUNKS[i], me)
            sums[i] = shares(scatter(keep, send, CHUNKS[i]), shape_sets[i], CHUNKS[i])

        def by_shard(part):
            return part.reshape(part.shape[0], 8, -1).transpose(1, 0, 2).reshape(8, -1)

        small = sum_small(jnp.concatenate([by_shard(g_gains), by_shard(g_scale), by_shard(g_shift)], 1))
        g_gains = small[:2 * g].reshape(2, g)
        g_scale = small[2 * g:2 * g + DATASETS * t].reshape(DATASETS, t)
        g_shift = small[2 * g + DATASETS * t:].reshape(DATASETS, t)
    else:
        def share(part, axis):
            part = lax.psum_scatter(part.astype(BF16), "wide", scatter_dimension=axis, tiled=True)
            return lax.psum(part, "rep").astype(F32)

        sums = [[share(part, part.ndim - 2) for part in group] for group in grad_sets]
        g_gains, g_scale, g_shift = share(g_gains, 1), share(g_scale, 1), share(g_shift, 1)
    (s_qkv,), (s_out, s_fc1, s_re), (s_fc2,), (s_conv, s_head) = sums
    return (tokens_out, joined, d_tokens, g_gains, s_qkv, s_out, s_fc1, s_fc2, s_re, s_conv, s_head, g_scale, g_shift)


def solution(mesh):
    images = P(BOTH, None, None)
    slots = P(BOTH)
    rows = P("wide", None)
    cols = P(None, "wide")
    kernels = P(None, "wide", None)
    return jax.shard_map(
        shards,
        mesh=mesh,
        in_specs=(images, slots, slots, slots, cols, rows, rows, rows, rows, rows, kernels, rows, cols, cols, images, images),
        out_specs=(images, images, images, cols, rows, rows, rows, rows, rows, kernels, rows, cols, cols),
        check_vma=False,
    )
```

time: 1170 us -> 667 us (0.57)
  local copies, waits for them, and re-layouts: 354 us -> 59.6 us
  Pallas kernels: 0 us -> 184 us
  matrix products: 214 us -> 73.8 us
  other arithmetic: 159 us -> 50.5 us
  starting transfers between devices: 176 us -> 84.3 us
  waiting for transfers between devices: 253 us -> 201 us
    pallas_call x0 -> x13, Pallas kernels: none -> 184 us  [the longest x1 35.4 us: mlp_back(): pl.pallas_call(mlp_back_body, grid=(ff // block,), in_specs=[full, full,...]
    ppermute x188 -> x72, starting transfers between devices: 176 us -> 84.3 us  [swap(): return lax.ppermute(value, BOTH, [(i, i ^ flip) for i in range(32)])]
    reshape x19 -> x0, local copies, waits for them, and re-layouts: 76.7 us -> none  [the longest x9 48.9 us: scatter_grad(): value = grad.astype(BF16).reshape(4, 2, 2, 2, rows // 4, 2, cols // 2)]
    dot_general x9 -> x2, matrix products: 64.3 us -> 9.47 us  [the longest x1 6.64 us: shards(): jnp.einsum('ts,isc->itc', pair, head.astype(BF16), preferred_element_type...]
    ppermute x188 -> x72, waiting for transfers between devices: 253 us -> 201 us  [swap(): return lax.ppermute(value, BOTH, [(i, i ^ flip) for i in range(32)])]
    another operation x196 -> x9, other arithmetic: 57 us -> 6.25 us  [the longest x4 2.67 us: both(): jnp.stack([jnp.where(first, value, other), jnp.where(first, other, value)])]
    convert_element_type x95 -> x28, other arithmetic: 74.6 us -> 24.9 us  [the longest x16 14.1 us: add(): return sum((term.astype(F32) for term in terms)).astype(BF16)]
    convert_element_type x36 -> x7, local copies, waits for them, and re-layouts: 45.5 us -> 0.43 us  [the longest x3 0.17 us: shards(): scale = jnp.sum(onehot[:, :, None] * scales.astype(F32)[None], 1)]
  transfers between devices with their start and end apart: 188 -> 72, of which waited for: 111 -> 32; matrix products, arithmetic and copies ran while one was open for 40% -> 19% of each run, Pallas kernels for 0% -> 8%
where the time goes in v2:
time: 667 us; the launch traced here: 656 us
  waiting for transfers between devices  201 us (30%)
  Pallas kernels  184 us (28%)
  starting transfers between devices  84.3 us (13%)
  matrix products  73.8 us (11%)
  local copies, waits for them, and re-layouts  59.6 us (9%)
  other arithmetic  50.5 us (8%)
    ppermute x72, waiting for transfers between devices, swap(): return lax.ppermute(value, BOTH, [(i, i ^ flip) for i in range(32)])  201 us
    ppermute x72, starting transfers between devices, swap(): return lax.ppermute(value, BOTH, [(i, i ^ flip) for i in range(32)])  84.3 us
    pallas_call x1, Pallas kernels, mlp_back(): pl.pallas_call(mlp_back_body, grid=(ff // block,), in_specs=[full, full,...  35.4 us
    dot_general x5, matrix products, mm(): return jnp.dot(left, right, preferred_element_type=F32)  32.9 us
    pallas_call x1, Pallas kernels, units_back(): pl.pallas_call(units_back_body, grid=(1,), in_specs=[whole(a.shape) for a...  29.9 us
    pallas_call x1, Pallas kernels, units(): pl.pallas_call(units_body, grid=(rows // COUNT,), in_specs=[pl.BlockSpec(...  26.9 us
    pallas_call x1, Pallas kernels, attention_back(): pl.pallas_call(attention_back_body, grid=(images, steps), in_specs=[cols(...  25.1 us
    unnamed x144, local copies, waits for them, and re-layouts  24.6 us
  transfers between devices with their start and end apart: 72, of which 32 were waited for; matrix products, arithmetic and copies ran while one was open for 19% of the time, Pallas kernels for 8%

profile of v2, /device:TPU:0, one launch (start us, length us, event | category | flops | bytes accessed | tf_op | source)
XLA Modules:
  0.0 656.2 jit_solution(7989644615599928918)
XLA Ops:
  5.8 3.0 collective-permute-start.24
  8.9 2.6 collective-permute-start.25
  33.4 2.4 collective-permute-start.1
  44.2 2.4 collective-permute-start.4
  53.3 2.8 collective-permute-start.17
  57.7 3.4 collective-permute-start.18
  62.8 3.4 collective-permute-start.19
  66.9 5.3 collective-permute-done.18
  72.9 3.2 collective-permute-start.11
  86.3 3.9 collective-permute-done.11
  93.8 24.4 %collective-permute-done.13 = bf16[4,48,2048]{2,1,0:T(8,128)(2,1)S(1)} collective-permute-done((bf16[4,48,2048]{2,1,0:T(8,128)(2,1)S(1)}, bf16[4,48,2048]{2,1,0:T(8,128)(2,1)S(1)}, u32[]{:S(2)}, u32[]{:S(2)}) %collective-permute-start.13) | collective-permute-done | bytes 786464 | tf_op jit(solution)/shard_map/ppermute | solution.py:56
  124.7 12.5 %collective-permute-done.7.refs_1_ = bf16[8,48,1152]{2,1,0:T(8,128)(2,1)} collective-permute-done((bf16[8,48,1152]{2,1,0:T(8,128)(2,1)}, bf16[8,48,1152]{2,1,0:T(8,128)(2,1)}, u32[]{:S(2)}, u32[]{:S(2)}) %collective-permute-start.7) | collective-permute-done | bytes 884768 | tf_op jit(solution)/shard_map/ppermute | solution.py:56
  142.5 4.7 assemble.4
  147.2 12.5 %collective-permute-done.21.refs_1_ = bf16[8,192,384]{2,1,0:T(8,128)(2,1)} collective-permute-done((bf16[8,192,384]{2,1,0:T(8,128)(2,1)}, bf16[8,192,384]{2,1,0:T(8,128)(2,1)}, u32[]{:S(2)}, u32[]{:S(2)}) %collective-permute-start.21) | collective-permute-done | bytes 1179680 | tf_op jit(solution)/shard_map/ppermute | solution.py:56
  160.2 14.9 %collective-permute-done.28.refs_1_ = bf16[8,592,128]{2,1,0:T(8,128)(2,1)} collective-permute-done((bf16[8,592,128]{2,1,0:T(8,128)(2,1)}, bf16[8,592,128]{2,1,0:T(8,128)(2,1)}, u32[]{:S(2)}, u32[]{:S(2)}) %collective-permute-start.28) | collective-permute-done | bytes 1212448 | tf_op jit(solution)/shard_map/ppermute | solution.py:56
  175.6 9.2 %convolution_convert_fusion.q_ref.k_ref.v_ref = bf16[1152,2304]{1,0:T(8,128)(2,1)} fusion(bf16[1152,768]{1,0:T(8,128)(2,1)} %multiply_convert_fusion.4, bf16[768,2304]{1,0:T(8,128)(2,1)} %assemble.4), kind=kOutput, calls=%fused_computation.8 | convolution fusion | flops 4079517696 | bytes 10616832 | tf_op jit(solution)/shard_map/dot_general | solution.py:24
  184.8 21.1 %attention.1 = (bf16[1152,768]{1,0:T(8,128)(2,1)}, bf16[24,576,576]{2,1,0:T(8,128)(2,1)}, f32[6,4,576]{2,1,0:T(4,128)}) custom-call(bf16[1152,2304]{1,0:T(8,128)(2,1)} %convolution_convert_fusion.q_ref.k_ref.v_ref, bf16[1152,2304]{1,0:T(8,128)(2,1)} %convolution_convert_fusion.q_ref.k_ref.v_ref, bf16[1152,2304]{1,0:T(8,128)(2,1)} %convolution_convert_fusion.q_ref.k_ref.v_ref), custom_call_target="tpu_custom_call" | custom-call | flops 8153726976 | bytes 15925248 | tf_op jit(solution)/shard_map/attention/pallas_call | solution.py:293
  206.0 5.5 assemble.6.w2_ref
  211.5 6.8 %assemble.7 = (bf16[4,2304,256]{2,1,0:T(8,128)(2,1)}, bf16[256,256]{1,0:T(8,128)(2,1)}) custom-call(s32[5]{0:T(128)} %stack.129.me_ref, bf16[8,592,128]{2,1,0:T(8,128)(2,1)} %constant_dynamic-update-slice_fusion.15.refs_0_, bf16[8,592,128]{2,1,0:T(8,128)(2,1)} %collective-permute-done.28.refs_1_, bf16[8,592,128]{2,1,0:T(8,128)(2,1)} %collective-permute-done.29.refs_2_, ...), custom_call_target="tpu_custom_call" | custom-call | bytes 9699328 | tf_op jit(solution)/shard_map/assemble/pallas_call | solution.py:154
  218.3 7.2 %assemble.5 = (bf16[768,768]{1,0:T(8,128)(2,1)}, bf16[768,3072]{1,0:T(8,128)(2,1)}, bf16[768,256]{1,0:T(8,128)(2,1)}) custom-call(s32[5]{0:T(128)} %stack.129.me_ref, bf16[8,48,2048]{2,1,0:T(8,128)(2,1)} %copy-done.11, bf16[8,48,2048]{2,1,0:T(8,128)(2,1)} %collective-permute-done.14.refs_1_, bf16[8,48,2048]{2,1,0:T(8,128)(2,1)} %collective-permute-done.15.refs_2_, ...), custom_call_target="tpu_custom_call" | custom-call | bytes 12582912 | tf_op jit(solution)/shard_map/assemble/pallas_call | solution.py:154
  225.6 3.5 fusion.79
  230.1 3.1 copy-done.55
  233.3 11.8 %fusion.4 = (bf16[1152,3072]{1,0:T(8,128)(2,1)}, bf16[1152,3072]{1,0:T(8,128)(2,1)S(1)}) fusion(bf16[1152,768]{1,0:T(8,128)(2,1)S(1)} %multiply_convert_fusion.3.a2_ref, bf16[768,3072]{1,0:T(8,128)(2,1)S(1)} %copy-done.55), kind=kOutput, calls=%fused_computation.5 | convolution fusion | flops 5474746368 | bytes 20643840 | tf_op jit(solution)/shard_map/dot_general | solution.py:24
  245.1 7.1 %fusion.72 = (bf16[1152,768]{1,0:T(8,128)(2,1)}, bf16[1152,768]{1,0:T(8,128)(2,1)}) fusion(f32[1152]{0:T(1024)S(1)} %copy-done.41, f32[1152,768]{1,0:T(8,128)S(1)} %get-tuple-element.226.x2_ref, bf16[1152,3072]{1,0:T(8,128)(2,1)S(1)} %get-tuple-element.145.gg_ref, bf16[3072,768]{1,0:T(8,128)(2,1)S(1)} %bitcast.187), kind=kOutput, calls=%fused_computation.273 | convolution fusion | flops 5439356928 | bytes 18878976 | tf_op jit(solution)/shard_map/dot_general | solution.py:24
  252.4 26.9 %units.1 = (bf16[2,1152,256]{2,1,0:T(8,128)(2,1)}, bf16[2,1152,256]{2,1,0:T(8,128)(2,1)}, bf16[2,1152,256]{2,1,0:T(8,128)(2,1)}, bf16[2,1152,256]{2,1,0:T(8,128)(2,1)}, bf16[1152,256]{1,0:T(8,128)(2,1)}) custom-call(bf16[1152,768]{1,0:T(8,128)(2,1)} %get-tuple-element.154.x_ref.x3b_ref, bf16[768,256]{1,0:T(8,128)(2,1)} %get-tuple-element.48.wre_ref, ...), custom_call_target="tpu_custom_call" | custom-call | flops 10871635968 | bytes 12582912 | tf_op jit(solution)/shard_map/units/pallas_call | solution.py:374
  280.8 2.8 multiply_reduce_fusion.5
  285.4 29.9 %units_back.1 = (bf16[4,2304,256]{2,1,0:T(8,128)(2,1)}, bf16[256,256]{1,0:T(8,128)(2,1)}, bf16[768,256]{1,0:T(8,128)(2,1)}, f32[1152,768]{1,0:T(8,128)}) custom-call(bf16[1152,256]{1,0:T(8,128)(2,1)} %bitcast.199, bf16[1152,256]{1,0:T(8,128)(2,1)} %get-tuple-element.50.z_ref, bf16[1152,768]{1,0:T(8,128)(2,1)} %get-tuple-element.154.x_ref.x3b_ref, ...), custom_call_target="tpu_custom_call" | custom-call | flops 19025362944 | bytes 25165824 | tf_op jit(solution)/shard_map/units_back/pallas_call | solution.py:418
  315.3 35.4 %mlp_back.1 = (bf16[768,3072]{1,0:T(8,128)(2,1)}, bf16[3072,768]{1,0:T(8,128)(2,1)}, f32[1152,768]{1,0:T(8,128)}, f32[1,768]{1,0:T(1,128)}) custom-call(f32[1152,768]{1,0:T(8,128)} %get-tuple-element.56.dx3_ref, bf16[1152,768]{1,0:T(8,128)(2,1)} %copy-done.12, bf16[1152,3072]{1,0:T(8,128)(2,1)} %copy-done.60, ...), custom_call_target="tpu_custom_call" | custom-call | flops 21743271936 | bytes 41943040 | tf_op jit(solution)/shard_map/mlp_back/pallas_call | solution.py:464
  350.7 4.9 convolution_convert_fusion.2.refs_0_
  355.7 2.8 convolution_convert_fusion.1.do_ref
  358.5 25.1 %attention_back.1 = (bf16[1152,768]{1,0:T(8,128)(2,1)}, bf16[1152,768]{1,0:T(8,128)(2,1)}, bf16[1152,768]{1,0:T(8,128)(2,1)}) custom-call(bf16[1152,2304]{1,0:T(8,128)(2,1)} %convolution_convert_fusion.q_ref.k_ref.v_ref, bf16[1152,2304]{1,0:T(8,128)(2,1)} %convolution_convert_fusion.q_ref.k_ref.v_ref, ...), custom_call_target="tpu_custom_call" | custom-call | flops 16307453952 | bytes 15925248 | tf_op jit(solution)/shard_map/attention_back/pallas_call | solution.py:323
  383.7 3.4 convolution_convert_fusion.4
  387.1 3.3 fusion.17
  392.2 3.4 fusion.15
  395.6 5.9 pack.7
  401.6 6.3 pack.5
  408.5 4.8 pack.6
  413.4 3.2 convolution_convert_fusion.5
  416.7 2.1 pad_maximum_fusion.refs_0_
  418.8 4.2 pack.4
  423.6 8.6 %multiply_reduce_fusion = (f32[768]{0:T(1024)}, f32[1152]{0:T(1024)}, f32[1152]{0:T(1024)}, f32[1152,768]{1,0:T(8,128)}) fusion(bf16[2,576,768]{2,1,0:T(8,128)(2,1)S(1)} %copy-done.1, f32[1152]{0:T(1024)S(1)} %copy-done.22, f32[1152]{0:T(1024)S(1)} %copy-done.20, f32[768]{0:T(1024)S(1)} %copy-done.25, f32[1152,768]{1,0:T(8,128)} %fusion.15, ...), kind=kOutput, calls=%fused_computation.37 | convolution fusion | flops 1368683520 | bytes 15360000 | tf_op jit(solution)/shard_map/dot_general | solution.py:32
  449.9 6.6 %fusion.10 = bf16[2,2304,256]{1,2,0:T(8,128)(2,1)} fusion(f32[2]{0:T(128)} %compare_convert_fusion, f32[2,256]{1,0:T(2,128)S(1)} %broadcast_multiply_fusion.4, f32[2,256]{1,0:T(2,128)} %copy-done.42, f32[2,576,256]{2,1,0:T(8,128)} %bitcast.191, s32[2304]{0:T(1024)} %get-tuple-element.233, s32[2304]{0:T(1024)} %get-tuple-element.234, ...), kind=kOutput, calls=%fused_computation.29 | convolution fusion | flops 1425014784 | bytes 3594888 | tf_op jit(solution)/shard_map/ts,isc->itc/dot_general | solution.py:551
  456.6 2.8 collective-permute-start.33
  462.5 2.1 collective-permute-done.34
  467.9 3.0 add_convert_fusion.8
  472.4 2.3 add_convert_fusion
  474.7 4.5 copy.64
  479.9 10.3 %collective-permute-done.37 = bf16[8,48,1152]{2,1,0:T(8,128)(2,1)S(1)} collective-permute-done((bf16[8,48,1152]{2,1,0:T(8,128)(2,1)}, bf16[8,48,1152]{2,1,0:T(8,128)(2,1)S(1)}, u32[]{:S(2)}, u32[]{:S(2)}) %collective-permute-start.37) | collective-permute-done | bytes 884768 | tf_op jit(solution)/shard_map/ppermute | solution.py:56
  493.1 3.2 add_convert_fusion.6
  501.6 2.2 collective-permute-start.41
  503.8 2.4 add_convert_fusion.4
  506.8 2.1 collective-permute-done.40
  512.5 3.2 add_convert_fusion.2
  515.8 8.4 %collective-permute-done.42 = bf16[48,1152]{1,0:T(8,128)(2,1)S(1)} collective-permute-done((bf16[48,1152]{1,0:T(8,128)(2,1)S(1)}, bf16[48,1152]{1,0:T(8,128)(2,1)S(1)}, u32[]{:S(2)}, u32[]{:S(2)}) %collective-permute-start.42) | collective-permute-done | bytes 110624 | tf_op jit(solution)/shard_map/ppermute | solution.py:56
  525.7 14.9 %collective-permute-done.43 = bf16[48,1152]{1,0:T(8,128)(2,1)S(1)} collective-permute-done((bf16[48,1152]{1,0:T(8,128)(2,1)S(1)}, bf16[48,1152]{1,0:T(8,128)(2,1)S(1)}, u32[]{:S(2)}, u32[]{:S(2)}) %collective-permute-start.43) | collective-permute-done | bytes 110624 | tf_op jit(solution)/shard_map/ppermute | solution.py:56
  544.5 36.4 %collective-permute-done.56 = bf16[4,192,384]{2,1,0:T(8,128)(2,1)S(1)} collective-permute-done((bf16[4,192,384]{2,1,0:T(8,128)(2,1)S(1)}, bf16[4,192,384]{2,1,0:T(8,128)(2,1)S(1)}, u32[]{:S(2)}, u32[]{:S(2)}) %collective-permute-start.56) | collective-permute-done | bytes 589856 | tf_op jit(solution)/shard_map/ppermute | solution.py:56
  583.2 2.2 collective-permute-start.59
  588.3 8.2 %collective-permute-done.58 = bf16[192,384]{1,0:T(8,128)(2,1)S(1)} collective-permute-done((bf16[192,384]{1,0:T(8,128)(2,1)S(1)}, bf16[192,384]{1,0:T(8,128)(2,1)S(1)}, u32[]{:S(2)}, u32[]{:S(2)}) %collective-permute-start.58) | collective-permute-done | bytes 147488 | tf_op jit(solution)/shard_map/ppermute | solution.py:56
  610.1 5.7 collective-permute-done.71
  616.7 12.1 %collective-permute-done.47 = bf16[4,48,2048]{2,1,0:T(8,128)(2,1)S(1)} collective-permute-done((bf16[4,48,2048]{2,1,0:T(8,128)(2,1)S(1)}, bf16[4,48,2048]{2,1,0:T(8,128)(2,1)S(1)}, u32[]{:S(2)}, u32[]{:S(2)}) %collective-permute-start.47) | collective-permute-done | bytes 786464 | tf_op jit(solution)/shard_map/ppermute | solution.py:56
  631.1 2.3 collective-permute-start.50
  633.4 4.2 collective-permute-done.48
  637.6 5.9 collective-permute-done.49
  643.6 2.0 collective-permute-start.51
  (412 shorter events, 156.1 us)
Async XLA Ops:
  5.8 71.0 %collective-permute-start.24 = (bf16[592,128]{1,0:T(8,128)(2,1)}, bf16[592,128]{1,0:T(8,128)(2,1)}, u32[]{:S(2)}, u32[]{:S(2)}) collective-permute-start(bf16[592,128]{1,0:T(8,128)(2,1)} %dynamic-slice_dynamic-update-slice_fusion.2), channel_id=1, source_target_pairs={{0,2},{1,3},{2,0},{3,1},{4,6},{5,7},{6,4},{7,5},{8,10},{9,11},{10,... | collective-permute-start | bytes 454664 | tf_op jit(solution)/shard_map/ppermute | solution.py:56
  8.9 69.5 %collective-permute-start.25 = (bf16[592,128]{1,0:T(8,128)(2,1)}, bf16[592,128]{1,0:T(8,128)(2,1)}, u32[]{:S(2)}, u32[]{:S(2)}) collective-permute-start(bf16[592,128]{1,0:T(8,128)(2,1)} %dynamic-slice_dynamic-update-slice_fusion.2), channel_id=1, source_target_pairs={{0,4},{1,5},{2,6},{3,7},{4,0},{5,1},{6,2},{7,3},{8,12},{9,13},{10,... | collective-permute-start | bytes 454664 | tf_op jit(solution)/shard_map/ppermute | solution.py:56
  11.4 68.4 %collective-permute-start.26 = (bf16[592,128]{1,0:T(8,128)(2,1)}, bf16[592,128]{1,0:T(8,128)(2,1)}, u32[]{:S(2)}, u32[]{:S(2)}) collective-permute-start(bf16[592,128]{1,0:T(8,128)(2,1)} %dynamic-slice_dynamic-update-slice_fusion.2), channel_id=1, source_target_pairs={{0,6},{1,7},{2,4},{3,5},{4,2},{5,3},{6,0},{7,1},{8,14},{9,15},{10,... | collective-permute-start | bytes 454664 | tf_op jit(solution)/shard_map/ppermute | solution.py:56
  13.0 36.3 %collective-permute-start.3 = (bf16[48,1152]{1,0:T(8,128)(2,1)}, bf16[48,1152]{1,0:T(8,128)(2,1)}, u32[]{:S(2)}, u32[]{:S(2)}) collective-permute-start(bf16[48,1152]{1,0:T(8,128)(2,1)} %get-tuple-element.143), channel_id=1, source_target_pairs={{0,2},{1,3},{2,0},{3,1},{4,6},{5,7},{6,4},{7,5},{8,10},{9,11},{10,... | collective-permute-start | bytes 331784 | tf_op jit(solution)/shard_map/ppermute | solution.py:56
  16.9 15.1 %collective-permute-start = (bf16[832]{0:T(1024)(128)(2,1)}, bf16[832]{0:T(1024)(128)(2,1)}, u32[]{:S(2)}, u32[]{:S(2)}) collective-permute-start(bf16[832]{0:T(1024)(128)(2,1)} %pad_maximum_fusion.8), channel_id=1, source_target_pairs={{0,2},{1,3},{2,0},{3,1},{4,6},{5,7},{6,4},{7,5},{8,10},{9,11},{10,... | collective-permute-start | bytes 5000 | tf_op jit(solution)/shard_map/ppermute | solution.py:56
  44.2 9.1 %collective-permute-start.4 = (bf16[48,1152]{1,0:T(8,128)(2,1)}, bf16[48,1152]{1,0:T(8,128)(2,1)}, u32[]{:S(2)}, u32[]{:S(2)}) collective-permute-start(bf16[48,1152]{1,0:T(8,128)(2,1)} %get-tuple-element.143), channel_id=1, source_target_pairs={{0,4},{1,5},{2,6},{3,7},{4,0},{5,1},{6,2},{7,3},{8,12},{9,13},{10,... | collective-permute-start | bytes 331784 | tf_op jit(solution)/shard_map/ppermute | solution.py:56
  49.3 8.4 %collective-permute-start.5 = (bf16[48,1152]{1,0:T(8,128)(2,1)}, bf16[48,1152]{1,0:T(8,128)(2,1)S(1)}, u32[]{:S(2)}, u32[]{:S(2)}) collective-permute-start(bf16[48,1152]{1,0:T(8,128)(2,1)} %get-tuple-element.143), channel_id=1, source_target_pairs={{0,6},{1,7},{2,4},{3,5},{4,2},{5,3},{6,0},{7,1},{8,14},{9,15},{10,... | collective-permute-start | bytes 331784 | tf_op jit(solution)/shard_map/ppermute | solution.py:56
  53.3 9.5 %collective-permute-start.17 = (bf16[192,384]{1,0:T(8,128)(2,1)}, bf16[192,384]{1,0:T(8,128)(2,1)S(1)}, u32[]{:S(2)}, u32[]{:S(2)}) collective-permute-start(bf16[192,384]{1,0:T(8,128)(2,1)} %get-tuple-element.141), channel_id=1, source_target_pairs={{0,2},{1,3},{2,0},{3,1},{4,6},{5,7},{6,4},{7,5},{8,10},{9,11},{10,... | collective-permute-start | bytes 442376 | tf_op jit(solution)/shard_map/ppermute | solution.py:56
  57.7 14.5 %collective-permute-start.18 = (bf16[192,384]{1,0:T(8,128)(2,1)}, bf16[192,384]{1,0:T(8,128)(2,1)S(1)}, u32[]{:S(2)}, u32[]{:S(2)}) collective-permute-start(bf16[192,384]{1,0:T(8,128)(2,1)} %get-tuple-element.141), channel_id=1, source_target_pairs={{0,4},{1,5},{2,6},{3,7},{4,0},{5,1},{6,2},{7,3},{8,12},{9,13},{10,... | collective-permute-start | bytes 442376 | tf_op jit(solution)/shard_map/ppermute | solution.py:56
  62.8 10.1 %collective-permute-start.19 = (bf16[192,384]{1,0:T(8,128)(2,1)}, bf16[192,384]{1,0:T(8,128)(2,1)S(1)}, u32[]{:S(2)}, u32[]{:S(2)}) collective-permute-start(bf16[192,384]{1,0:T(8,128)(2,1)} %get-tuple-element.141), channel_id=1, source_target_pairs={{0,6},{1,7},{2,4},{3,5},{4,2},{5,3},{6,0},{7,1},{8,14},{9,15},{10,... | collective-permute-start | bytes 442376 | tf_op jit(solution)/shard_map/ppermute | solution.py:56
  72.2 12.6 %collective-permute-start.10 = (bf16[48,2048]{1,0:T(8,128)(2,1)S(1)}, bf16[48,2048]{1,0:T(8,128)(2,1)S(1)}, u32[]{:S(2)}, u32[]{:S(2)}) collective-permute-start(bf16[48,2048]{1,0:T(8,128)(2,1)S(1)} %dynamic-slice_dynamic-update-slice_fusion.1), channel_id=1, source_target_pairs={{0,2},{1,3},{2,0},{3,1},{4,6},{5,7},{6,4},{7,5},{8,10},{9,11},{10,... | collective-permute-start | bytes 589832 | tf_op jit(solution)/shard_map/ppermute | solution.py:56
  72.9 17.3 %collective-permute-start.11 = (bf16[48,2048]{1,0:T(8,128)(2,1)S(1)}, bf16[48,2048]{1,0:T(8,128)(2,1)S(1)}, u32[]{:S(2)}, u32[]{:S(2)}) collective-permute-start(bf16[48,2048]{1,0:T(8,128)(2,1)S(1)} %dynamic-slice_dynamic-update-slice_fusion.1), channel_id=1, source_target_pairs={{0,4},{1,5},{2,6},{3,7},{4,0},{5,1},{6,2},{7,3},{8,12},{9,13},{10,... | collective-permute-start | bytes 589832 | tf_op jit(solution)/shard_map/ppermute | solution.py:56
  76.8 13.3 %collective-permute-start.12 = (bf16[48,2048]{1,0:T(8,128)(2,1)S(1)}, bf16[48,2048]{1,0:T(8,128)(2,1)S(1)}, u32[]{:S(2)}, u32[]{:S(2)}) collective-permute-start(bf16[48,2048]{1,0:T(8,128)(2,1)S(1)} %dynamic-slice_dynamic-update-slice_fusion.1), channel_id=1, source_target_pairs={{0,6},{1,7},{2,4},{3,5},{4,2},{5,3},{6,0},{7,1},{8,14},{9,15},{10,... | collective-permute-start | bytes 589832 | tf_op jit(solution)/shard_map/ppermute | solution.py:56
  78.3 13.6 %collective-permute-start.6 = (bf16[4,48,1152]{2,1,0:T(8,128)(2,1)S(1)}, bf16[4,48,1152]{2,1,0:T(8,128)(2,1)S(1)}, u32[]{:S(2)}, u32[]{:S(2)}) collective-permute-start(bf16[4,48,1152]{2,1,0:T(8,128)(2,1)S(1)} %pad_maximum_fusion.4), channel_id=1, source_target_pairs={{0,8},{1,9},{2,10},{3,11},{4,12},{5,13},{6,14},{7,15},{8,0},{9,1},... | collective-permute-start | bytes 1327112 | tf_op jit(solution)/shard_map/ppermute | solution.py:56
  79.8 41.6 %collective-permute-start.20 = (bf16[4,192,384]{2,1,0:T(8,128)(2,1)S(1)}, bf16[4,192,384]{2,1,0:T(8,128)(2,1)S(1)}, u32[]{:S(2)}, u32[]{:S(2)}) collective-permute-start(bf16[4,192,384]{2,1,0:T(8,128)(2,1)S(1)} %pad_maximum_fusion.3), channel_id=1, source_target_pairs={{0,8},{1,9},{2,10},{3,11},{4,12},{5,13},{6,14},{7,15},{8,0},{9,1},... | collective-permute-start | bytes 1769480 | tf_op jit(solution)/shard_map/ppermute | solution.py:56
  84.7 39.1 %collective-permute-start.27 = (bf16[4,592,128]{2,1,0:T(8,128)(2,1)S(1)}, bf16[4,592,128]{2,1,0:T(8,128)(2,1)S(1)}, u32[]{:S(2)}, u32[]{:S(2)}) collective-permute-start(bf16[4,592,128]{2,1,0:T(8,128)(2,1)S(1)} %pad_maximum_fusion.2), channel_id=1, source_target_pairs={{0,16},{1,17},{2,18},{3,19},{4,20},{5,21},{6,22},{7,23},{8,24},{9,... | collective-permute-start | bytes 1818632 | tf_op jit(solution)/shard_map/ppermute | solution.py:56
  90.3 27.9 %collective-permute-start.13 = (bf16[4,48,2048]{2,1,0:T(8,128)(2,1)S(1)}, bf16[4,48,2048]{2,1,0:T(8,128)(2,1)S(1)}, u32[]{:S(2)}, u32[]{:S(2)}) collective-permute-start(bf16[4,48,2048]{2,1,0:T(8,128)(2,1)S(1)} %pad_maximum_fusion.1), channel_id=1, source_target_pairs={{0,16},{1,17},{2,18},{3,19},{4,20},{5,21},{6,22},{7,23},{8,24},{9,... | collective-permute-start | bytes 2359304 | tf_op jit(solution)/shard_map/ppermute | solution.py:56
  92.7 44.6 %collective-permute-start.7 = (bf16[8,48,1152]{2,1,0:T(8,128)(2,1)}, bf16[8,48,1152]{2,1,0:T(8,128)(2,1)}, u32[]{:S(2)}, u32[]{:S(2)}) collective-permute-start(bf16[8,48,1152]{2,1,0:T(8,128)(2,1)} %constant_dynamic-update-slice_fusion.refs_0_), channel_id=1, source_target_pairs={{0,16},{1,17},{2,18},{3,19},{4,20},{5,21},{6,22},{7,23},{8,24},{9,... | collective-permute-start | bytes 2654216 | tf_op jit(solution)/shard_map/ppermute | solution.py:56
  93.8 45.1 %collective-permute-start.8 = (bf16[8,48,1152]{2,1,0:T(8,128)(2,1)}, bf16[8,48,1152]{2,1,0:T(8,128)(2,1)}, u32[]{:S(2)}, u32[]{:S(2)}) collective-permute-start(bf16[8,48,1152]{2,1,0:T(8,128)(2,1)} %constant_dynamic-update-slice_fusion.refs_0_), channel_id=1, source_target_pairs={{0,1},{1,0},{2,3},{3,2},{4,5},{5,4},{6,7},{7,6},{8,9},{9,8},{10,11... | collective-permute-start | bytes 2654216 | tf_op jit(solution)/shard_map/ppermute | solution.py:56
  118.3 56.9 %collective-permute-start.14 = (bf16[8,48,2048]{2,1,0:T(8,128)(2,1)S(1)}, bf16[8,48,2048]{2,1,0:T(8,128)(2,1)}, u32[]{:S(2)}, u32[]{:S(2)}) collective-permute-start(bf16[8,48,2048]{2,1,0:T(8,128)(2,1)S(1)} %constant_dynamic-update-slice_fusion.5.refs_0_), channel_id=1, source_target_pairs={{0,8},{1,9},{2,10},{3,11},{4,12},{5,13},{6,14},{7,15},{8,0},{9,1},... | collective-permute-start | bytes 4718600 | tf_op jit(solution)/shard_map/ppermute | solution.py:56
  122.3 37.4 %collective-permute-start.21 = (bf16[8,192,384]{2,1,0:T(8,128)(2,1)}, bf16[8,192,384]{2,1,0:T(8,128)(2,1)}, u32[]{:S(2)}, u32[]{:S(2)}) collective-permute-start(bf16[8,192,384]{2,1,0:T(8,128)(2,1)} %constant_dynamic-update-slice_fusion.10.refs_0_), channel_id=1, source_target_pairs={{0,16},{1,17},{2,18},{3,19},{4,20},{5,21},{6,22},{7,23},{8,24},{9,... | collective-permute-start | bytes 3538952 | tf_op jit(solution)/shard_map/ppermute | solution.py:56
  123.8 35.9 %collective-permute-start.22 = (bf16[8,192,384]{2,1,0:T(8,128)(2,1)}, bf16[8,192,384]{2,1,0:T(8,128)(2,1)}, u32[]{:S(2)}, u32[]{:S(2)}) collective-permute-start(bf16[8,192,384]{2,1,0:T(8,128)(2,1)} %constant_dynamic-update-slice_fusion.10.refs_0_), channel_id=1, source_target_pairs={{0,1},{1,0},{2,3},{3,2},{4,5},{5,4},{6,7},{7,6},{8,9},{9,8},{10,11... | collective-permute-start | bytes 3538952 | tf_op jit(solution)/shard_map/ppermute | solution.py:56
  137.3 37.9 %collective-permute-start.28 = (bf16[8,592,128]{2,1,0:T(8,128)(2,1)}, bf16[8,592,128]{2,1,0:T(8,128)(2,1)}, u32[]{:S(2)}, u32[]{:S(2)}) collective-permute-start(bf16[8,592,128]{2,1,0:T(8,128)(2,1)} %constant_dynamic-update-slice_fusion.15.refs_0_), channel_id=1, source_target_pairs={{0,8},{1,9},{2,10},{3,11},{4,12},{5,13},{6,14},{7,15},{8,0},{9,1},... | collective-permute-start | bytes 3637256 | tf_op jit(solution)/shard_map/ppermute | solution.py:56
  142.0 69.5 %collective-permute-start.29 = (bf16[8,592,128]{2,1,0:T(8,128)(2,1)}, bf16[8,592,128]{2,1,0:T(8,128)(2,1)}, u32[]{:S(2)}, u32[]{:S(2)}) collective-permute-start(bf16[8,592,128]{2,1,0:T(8,128)(2,1)} %constant_dynamic-update-slice_fusion.15.refs_0_), channel_id=1, source_target_pairs={{0,1},{1,0},{2,3},{3,2},{4,5},{5,4},{6,7},{7,6},{8,9},{9,8},{10,11... | collective-permute-start | bytes 3637256 | tf_op jit(solution)/shard_map/ppermute | solution.py:56
  159.7 58.6 %collective-permute-start.15 = (bf16[8,48,2048]{2,1,0:T(8,128)(2,1)S(1)}, bf16[8,48,2048]{2,1,0:T(8,128)(2,1)}, u32[]{:S(2)}, u32[]{:S(2)}) collective-permute-start(bf16[8,48,2048]{2,1,0:T(8,128)(2,1)S(1)} %constant_dynamic-update-slice_fusion.5.refs_0_), channel_id=1, source_target_pairs={{0,1},{1,0},{2,3},{3,2},{4,5},{5,4},{6,7},{7,6},{8,9},{9,8},{10,11... | collective-permute-start | bytes 4718600 | tf_op jit(solution)/shard_map/ppermute | solution.py:56
  159.7 46.3 %collective-permute-start.23 = (bf16[8,192,384]{2,1,0:T(8,128)(2,1)}, bf16[8,192,384]{2,1,0:T(8,128)(2,1)}, u32[]{:S(2)}, u32[]{:S(2)}) collective-permute-start(bf16[8,192,384]{2,1,0:T(8,128)(2,1)} %collective-permute-done.21.refs_1_), channel_id=1, source_target_pairs={{0,1},{1,0},{2,3},{3,2},{4,5},{5,4},{6,7},{7,6},{8,9},{9,8},{10,11... | collective-permute-start | bytes 3538952 | tf_op jit(solution)/shard_map/ppermute | solution.py:56
  175.1 36.4 %collective-permute-start.30 = (bf16[8,592,128]{2,1,0:T(8,128)(2,1)}, bf16[8,592,128]{2,1,0:T(8,128)(2,1)}, u32[]{:S(2)}, u32[]{:S(2)}) collective-permute-start(bf16[8,592,128]{2,1,0:T(8,128)(2,1)} %collective-permute-done.28.refs_1_), channel_id=1, source_target_pairs={{0,1},{1,0},{2,3},{3,2},{4,5},{5,4},{6,7},{7,6},{8,9},{9,8},{10,11... | collective-permute-start | bytes 3637256 | tf_op jit(solution)/shard_map/ppermute | solution.py:56
  175.1 43.2 %collective-permute-start.16 = (bf16[8,48,2048]{2,1,0:T(8,128)(2,1)}, bf16[8,48,2048]{2,1,0:T(8,128)(2,1)}, u32[]{:S(2)}, u32[]{:S(2)}) collective-permute-start(bf16[8,48,2048]{2,1,0:T(8,128)(2,1)} %collective-permute-done.14.refs_1_), channel_id=1, source_target_pairs={{0,1},{1,0},{2,3},{3,2},{4,5},{5,4},{6,7},{7,6},{8,9},{9,8},{10,11... | collective-permute-start | bytes 4718600 | tf_op jit(solution)/shard_map/ppermute | solution.py:56
  401.5 100.0 %collective-permute-start.63 = (bf16[16,592,128]{2,1,0:T(8,128)(2,1)}, bf16[16,592,128]{2,1,0:T(8,128)(2,1)}, u32[]{:S(2)}, u32[]{:S(2)}) collective-permute-start(bf16[16,592,128]{2,1,0:T(8,128)(2,1)} %get-tuple-element.76), channel_id=1, source_target_pairs={{0,1},{1,0},{2,3},{3,2},{4,5},{5,4},{6,7},{7,6},{8,9},{9,8},{10,11... | collective-permute-start | bytes 7274504 | tf_op jit(solution)/shard_map/ppermute | solution.py:56
  407.9 103.1 %collective-permute-start.45 = (bf16[16,48,2048]{2,1,0:T(8,128)(2,1)}, bf16[16,48,2048]{2,1,0:T(8,128)(2,1)}, u32[]{:S(2)}, u32[]{:S(2)}) collective-permute-start(bf16[16,48,2048]{2,1,0:T(8,128)(2,1)} %get-tuple-element.69), channel_id=1, source_target_pairs={{0,1},{1,0},{2,3},{3,2},{4,5},{5,4},{6,7},{7,6},{8,9},{9,8},{10,11... | collective-permute-start | bytes 9437192 | tf_op jit(solution)/shard_map/ppermute | solution.py:56
  413.3 79.7 %collective-permute-start.54 = (bf16[16,192,384]{2,1,0:T(8,128)(2,1)}, bf16[16,192,384]{2,1,0:T(8,128)(2,1)}, u32[]{:S(2)}, u32[]{:S(2)}) collective-permute-start(bf16[16,192,384]{2,1,0:T(8,128)(2,1)} %get-tuple-element.72), channel_id=1, source_target_pairs={{0,1},{1,0},{2,3},{3,2},{4,5},{5,4},{6,7},{7,6},{8,9},{9,8},{10,11... | collective-permute-start | bytes 7077896 | tf_op jit(solution)/shard_map/ppermute | solution.py:56
  423.1 43.6 %collective-permute-start.36 = (bf16[16,48,1152]{2,1,0:T(8,128)(2,1)}, bf16[16,48,1152]{2,1,0:T(8,128)(2,1)S(1)}, u32[]{:S(2)}, u32[]{:S(2)}) collective-permute-start(bf16[16,48,1152]{2,1,0:T(8,128)(2,1)} %get-tuple-element.65), channel_id=1, source_target_pairs={{0,1},{1,0},{2,3},{3,2},{4,5},{5,4},{6,7},{7,6},{8,9},{9,8},{10,11... | collective-permute-start | bytes 5308424 | tf_op jit(solution)/shard_map/ppermute | solution.py:56
  449.8 6.7 %collective-permute-start.32 = (f32[2,832]{1,0:T(2,128)S(1)}, f32[2,832]{1,0:T(2,128)S(1)}, u32[]{:S(2)}, u32[]{:S(2)}) collective-permute-start(f32[2,832]{1,0:T(2,128)S(1)} %dynamic-slice_bitcast_fusion.1), channel_id=1, source_target_pairs={{0,4},{1,5},{2,6},{3,7},{4,0},{5,1},{6,2},{7,3},{8,12},{9,13},{10,... | collective-permute-start | bytes 19976 | tf_op jit(solution)/shard_map/ppermute | solution.py:56
  465.2 14.0 %collective-permute-start.35 = (f32[832]{0:T(1024)}, f32[832]{0:T(1024)}, u32[]{:S(2)}, u32[]{:S(2)}) collective-permute-start(f32[832]{0:T(1024)} %add.378), channel_id=1, source_target_pairs={{0,16},{1,17},{2,18},{3,19},{4,20},{5,21},{6,22},{7,23},{8,24},{9,... | collective-permute-start | bytes 9992 | tf_op jit(solution)/shard_map/ppermute | solution.py:56
  470.9 19.4 %collective-permute-start.37 = (bf16[8,48,1152]{2,1,0:T(8,128)(2,1)}, bf16[8,48,1152]{2,1,0:T(8,128)(2,1)S(1)}, u32[]{:S(2)}, u32[]{:S(2)}) collective-permute-start(bf16[8,48,1152]{2,1,0:T(8,128)(2,1)} %get-tuple-element.153), channel_id=1, source_target_pairs={{0,8},{1,9},{2,10},{3,11},{4,12},{5,13},{6,14},{7,15},{8,0},{9,1},... | collective-permute-start | bytes 2654216 | tf_op jit(solution)/shard_map/ppermute | solution.py:56
  490.4 8.8 %collective-permute-start.38 = (bf16[4,48,1152]{2,1,0:T(8,128)(2,1)S(1)}, bf16[4,48,1152]{2,1,0:T(8,128)(2,1)S(1)}, u32[]{:S(2)}, u32[]{:S(2)}) collective-permute-start(bf16[4,48,1152]{2,1,0:T(8,128)(2,1)S(1)} %get-tuple-element.163), channel_id=1, source_target_pairs={{0,16},{1,17},{2,18},{3,19},{4,20},{5,21},{6,22},{7,23},{8,24},{9,... | collective-permute-start | bytes 1327112 | tf_op jit(solution)/shard_map/ppermute | solution.py:56
  496.3 44.4 %collective-permute-start.55 = (bf16[8,192,384]{2,1,0:T(8,128)(2,1)S(1)}, bf16[8,192,384]{2,1,0:T(8,128)(2,1)S(1)}, u32[]{:S(2)}, u32[]{:S(2)}) collective-permute-start(bf16[8,192,384]{2,1,0:T(8,128)(2,1)S(1)} %get-tuple-element.151), channel_id=1, source_target_pairs={{0,8},{1,9},{2,10},{3,11},{4,12},{5,13},{6,14},{7,15},{8,0},{9,1},... | collective-permute-start | bytes 3538952 | tf_op jit(solution)/shard_map/ppermute | solution.py:56
  499.3 6.9 %collective-permute-start.39 = (bf16[48,1152]{1,0:T(8,128)(2,1)S(1)}, bf16[48,1152]{1,0:T(8,128)(2,1)S(1)}, u32[]{:S(2)}, u32[]{:S(2)}) collective-permute-start(bf16[48,1152]{1,0:T(8,128)(2,1)S(1)} %get-tuple-element.173), channel_id=1, source_target_pairs={{0,2},{1,3},{2,0},{3,1},{4,6},{5,7},{6,4},{7,5},{8,10},{9,11},{10,... | collective-permute-start | bytes 331784 | tf_op jit(solution)/shard_map/ppermute | solution.py:56
  500.8 8.0 %collective-permute-start.40 = (bf16[48,1152]{1,0:T(8,128)(2,1)S(1)}, bf16[48,1152]{1,0:T(8,128)(2,1)S(1)}, u32[]{:S(2)}, u32[]{:S(2)}) collective-permute-start(bf16[48,1152]{1,0:T(8,128)(2,1)S(1)} %get-tuple-element.175), channel_id=1, source_target_pairs={{0,4},{1,5},{2,6},{3,7},{4,0},{5,1},{6,2},{7,3},{8,12},{9,13},{10,... | collective-permute-start | bytes 331784 | tf_op jit(solution)/shard_map/ppermute | solution.py:56
  501.6 7.3 %collective-permute-start.41 = (bf16[48,1152]{1,0:T(8,128)(2,1)S(1)}, bf16[48,1152]{1,0:T(8,128)(2,1)S(1)}, u32[]{:S(2)}, u32[]{:S(2)}) collective-permute-start(bf16[48,1152]{1,0:T(8,128)(2,1)S(1)} %get-tuple-element.174), channel_id=1, source_target_pairs={{0,6},{1,7},{2,4},{3,5},{4,2},{5,3},{6,0},{7,1},{8,14},{9,15},{10,... | collective-permute-start | bytes 331784 | tf_op jit(solution)/shard_map/ppermute | solution.py:56
  506.2 35.4 %collective-permute-start.64 = (bf16[8,592,128]{2,1,0:T(8,128)(2,1)S(1)}, bf16[8,592,128]{2,1,0:T(8,128)(2,1)S(1)}, u32[]{:S(2)}, u32[]{:S(2)}) collective-permute-start(bf16[8,592,128]{2,1,0:T(8,128)(2,1)S(1)} %get-tuple-element.149), channel_id=1, source_target_pairs={{0,16},{1,17},{2,18},{3,19},{4,20},{5,21},{6,22},{7,23},{8,24},{9,... | collective-permute-start | bytes 3637256 | tf_op jit(solution)/shard_map/ppermute | solution.py:56
  508.9 15.2 %collective-permute-start.42 = (bf16[48,1152]{1,0:T(8,128)(2,1)S(1)}, bf16[48,1152]{1,0:T(8,128)(2,1)S(1)}, u32[]{:S(2)}, u32[]{:S(2)}) collective-permute-start(bf16[48,1152]{1,0:T(8,128)(2,1)S(1)} %fusion.34), channel_id=1, source_target_pairs={{0,8},{1,9},{2,10},{3,11},{4,12},{5,13},{6,14},{7,15},{8,0},{9,1},... | collective-permute-start | bytes 331784 | tf_op jit(solution)/shard_map/ppermute | solution.py:56
  510.5 30.1 %collective-permute-start.43 = (bf16[48,1152]{1,0:T(8,128)(2,1)S(1)}, bf16[48,1152]{1,0:T(8,128)(2,1)S(1)}, u32[]{:S(2)}, u32[]{:S(2)}) collective-permute-start(bf16[48,1152]{1,0:T(8,128)(2,1)S(1)} %fusion.34), channel_id=1, source_target_pairs={{0,16},{1,17},{2,18},{3,19},{4,20},{5,21},{6,22},{7,23},{8,24},{9,... | collective-permute-start | bytes 331784 | tf_op jit(solution)/shard_map/ppermute | solution.py:56
  511.0 29.6 %collective-permute-start.44 = (bf16[48,1152]{1,0:T(8,128)(2,1)S(1)}, bf16[48,1152]{1,0:T(8,128)(2,1)S(1)}, u32[]{:S(2)}, u32[]{:S(2)}) collective-permute-start(bf16[48,1152]{1,0:T(8,128)(2,1)S(1)} %fusion.34), channel_id=1, source_target_pairs={{0,24},{1,25},{2,26},{3,27},{4,28},{5,29},{6,30},{7,31},{8,16},{9,... | collective-permute-start | bytes 331784 | tf_op jit(solution)/shard_map/ppermute | solution.py:56
  524.2 91.7 %collective-permute-start.46 = (bf16[8,48,2048]{2,1,0:T(8,128)(2,1)S(1)}, bf16[8,48,2048]{2,1,0:T(8,128)(2,1)S(1)}, u32[]{:S(2)}, u32[]{:S(2)}) collective-permute-start(bf16[8,48,2048]{2,1,0:T(8,128)(2,1)S(1)} %get-tuple-element.147), channel_id=1, source_target_pairs={{0,16},{1,17},{2,18},{3,19},{4,20},{5,21},{6,22},{7,23},{8,24},{9,... | collective-permute-start | bytes 4718600 | tf_op jit(solution)/shard_map/ppermute | solution.py:56
  541.1 39.8 %collective-permute-start.56 = (bf16[4,192,384]{2,1,0:T(8,128)(2,1)S(1)}, bf16[4,192,384]{2,1,0:T(8,128)(2,1)S(1)}, u32[]{:S(2)}, u32[]{:S(2)}) collective-permute-start(bf16[4,192,384]{2,1,0:T(8,128)(2,1)S(1)} %get-tuple-element.161), channel_id=1, source_target_pairs={{0,16},{1,17},{2,18},{3,19},{4,20},{5,21},{6,22},{7,23},{8,24},{9,... | collective-permute-start | bytes 1769480 | tf_op jit(solution)/shard_map/ppermute | solution.py:56
  541.9 43.5 %collective-permute-start.65 = (bf16[4,592,128]{2,1,0:T(8,128)(2,1)S(1)}, bf16[4,592,128]{2,1,0:T(8,128)(2,1)S(1)}, u32[]{:S(2)}, u32[]{:S(2)}) collective-permute-start(bf16[4,592,128]{2,1,0:T(8,128)(2,1)S(1)} %get-tuple-element.159), channel_id=1, source_target_pairs={{0,8},{1,9},{2,10},{3,11},{4,12},{5,13},{6,14},{7,15},{8,0},{9,1},... | collective-permute-start | bytes 1818632 | tf_op jit(solution)/shard_map/ppermute | solution.py:56
  581.0 6.6 %collective-permute-start.57 = (bf16[192,384]{1,0:T(8,128)(2,1)S(1)}, bf16[192,384]{1,0:T(8,128)(2,1)S(1)}, u32[]{:S(2)}, u32[]{:S(2)}) collective-permute-start(bf16[192,384]{1,0:T(8,128)(2,1)S(1)} %get-tuple-element.170), channel_id=1, source_target_pairs={{0,2},{1,3},{2,0},{3,1},{4,6},{5,7},{6,4},{7,5},{8,10},{9,11},{10,... | collective-permute-start | bytes 442376 | tf_op jit(solution)/shard_map/ppermute | solution.py:56
  581.3 15.1 %collective-permute-start.58 = (bf16[192,384]{1,0:T(8,128)(2,1)S(1)}, bf16[192,384]{1,0:T(8,128)(2,1)S(1)}, u32[]{:S(2)}, u32[]{:S(2)}) collective-permute-start(bf16[192,384]{1,0:T(8,128)(2,1)S(1)} %get-tuple-element.172), channel_id=1, source_target_pairs={{0,4},{1,5},{2,6},{3,7},{4,0},{5,1},{6,2},{7,3},{8,12},{9,13},{10,... | collective-permute-start | bytes 442376 | tf_op jit(solution)/shard_map/ppermute | solution.py:56
  583.2 14.8 %collective-permute-start.59 = (bf16[192,384]{1,0:T(8,128)(2,1)S(1)}, bf16[192,384]{1,0:T(8,128)(2,1)S(1)}, u32[]{:S(2)}, u32[]{:S(2)}) collective-permute-start(bf16[192,384]{1,0:T(8,128)(2,1)S(1)} %get-tuple-element.171), channel_id=1, source_target_pairs={{0,6},{1,7},{2,4},{3,5},{4,2},{5,3},{6,0},{7,1},{8,14},{9,15},{10,... | collective-permute-start | bytes 442376 | tf_op jit(solution)/shard_map/ppermute | solution.py:56
  585.5 14.2 %collective-permute-start.66 = (bf16[592,128]{1,0:T(8,128)(2,1)S(1)}, bf16[592,128]{1,0:T(8,128)(2,1)S(1)}, u32[]{:S(2)}, u32[]{:S(2)}) collective-permute-start(bf16[592,128]{1,0:T(8,128)(2,1)S(1)} %get-tuple-element.167), channel_id=1, source_target_pairs={{0,2},{1,3},{2,0},{3,1},{4,6},{5,7},{6,4},{7,5},{8,10},{9,11},{10,... | collective-permute-start | bytes 454664 | tf_op jit(solution)/shard_map/ppermute | solution.py:56
  587.6 13.5 %collective-permute-start.67 = (bf16[592,128]{1,0:T(8,128)(2,1)S(1)}, bf16[592,128]{1,0:T(8,128)(2,1)S(1)}, u32[]{:S(2)}, u32[]{:S(2)}) collective-permute-start(bf16[592,128]{1,0:T(8,128)(2,1)S(1)} %get-tuple-element.169), channel_id=1, source_target_pairs={{0,4},{1,5},{2,6},{3,7},{4,0},{5,1},{6,2},{7,3},{8,12},{9,13},{10,... | collective-permute-start | bytes 454664 | tf_op jit(solution)/shard_map/ppermute | solution.py:56
  596.4 7.1 %collective-permute-start.68 = (bf16[592,128]{1,0:T(8,128)(2,1)S(1)}, bf16[592,128]{1,0:T(8,128)(2,1)S(1)}, u32[]{:S(2)}, u32[]{:S(2)}) collective-permute-start(bf16[592,128]{1,0:T(8,128)(2,1)S(1)} %get-tuple-element.168), channel_id=1, source_target_pairs={{0,6},{1,7},{2,4},{3,5},{4,2},{5,3},{6,0},{7,1},{8,14},{9,15},{10,... | collective-permute-start | bytes 454664 | tf_op jit(solution)/shard_map/ppermute | solution.py:56
  598.2 6.7 %collective-permute-start.60 = (bf16[192,384]{1,0:T(8,128)(2,1)S(1)}, bf16[192,384]{1,0:T(8,128)(2,1)S(1)}, u32[]{:S(2)}, u32[]{:S(2)}) collective-permute-start(bf16[192,384]{1,0:T(8,128)(2,1)S(1)} %fusion.31), channel_id=1, source_target_pairs={{0,8},{1,9},{2,10},{3,11},{4,12},{5,13},{6,14},{7,15},{8,0},{9,1},... | collective-permute-start | bytes 442376 | tf_op jit(solution)/shard_map/ppermute | solution.py:56
  599.7 8.3 %collective-permute-start.61 = (bf16[192,384]{1,0:T(8,128)(2,1)S(1)}, bf16[192,384]{1,0:T(8,128)(2,1)S(1)}, u32[]{:S(2)}, u32[]{:S(2)}) collective-permute-start(bf16[192,384]{1,0:T(8,128)(2,1)S(1)} %fusion.31), channel_id=1, source_target_pairs={{0,16},{1,17},{2,18},{3,19},{4,20},{5,21},{6,22},{7,23},{8,24},{9,... | collective-permute-start | bytes 442376 | tf_op jit(solution)/shard_map/ppermute | solution.py:56
  601.1 7.0 %collective-permute-start.62 = (bf16[192,384]{1,0:T(8,128)(2,1)S(1)}, bf16[192,384]{1,0:T(8,128)(2,1)S(1)}, u32[]{:S(2)}, u32[]{:S(2)}) collective-permute-start(bf16[192,384]{1,0:T(8,128)(2,1)S(1)} %fusion.31), channel_id=1, source_target_pairs={{0,24},{1,25},{2,26},{3,27},{4,28},{5,29},{6,30},{7,31},{8,16},{9,... | collective-permute-start | bytes 442376 | tf_op jit(solution)/shard_map/ppermute | solution.py:56
  603.6 6.1 collective-permute-start.69
  608.1 7.6 %collective-permute-start.71 = (bf16[592,128]{1,0:T(8,128)(2,1)S(1)}, bf16[592,128]{1,0:T(8,128)(2,1)S(1)}, u32[]{:S(2)}, u32[]{:S(2)}) collective-permute-start(bf16[592,128]{1,0:T(8,128)(2,1)S(1)} %fusion.28), channel_id=1, source_target_pairs={{0,24},{1,25},{2,26},{3,27},{4,28},{5,29},{6,30},{7,31},{8,16},{9,... | collective-permute-start | bytes 454664 | tf_op jit(solution)/shard_map/ppermute | solution.py:56
  616.5 12.3 %collective-permute-start.47 = (bf16[4,48,2048]{2,1,0:T(8,128)(2,1)S(1)}, bf16[4,48,2048]{2,1,0:T(8,128)(2,1)S(1)}, u32[]{:S(2)}, u32[]{:S(2)}) collective-permute-start(bf16[4,48,2048]{2,1,0:T(8,128)(2,1)S(1)} %get-tuple-element.157), channel_id=1, source_target_pairs={{0,8},{1,9},{2,10},{3,11},{4,12},{5,13},{6,14},{7,15},{8,0},{9,1},... | collective-permute-start | bytes 2359304 | tf_op jit(solution)/shard_map/ppermute | solution.py:56
  628.9 8.6 %collective-permute-start.48 = (bf16[48,2048]{1,0:T(8,128)(2,1)S(1)}, bf16[48,2048]{1,0:T(8,128)(2,1)S(1)}, u32[]{:S(2)}, u32[]{:S(2)}) collective-permute-start(bf16[48,2048]{1,0:T(8,128)(2,1)S(1)} %get-tuple-element.164), channel_id=1, source_target_pairs={{0,2},{1,3},{2,0},{3,1},{4,6},{5,7},{6,4},{7,5},{8,10},{9,11},{10,... | collective-permute-start | bytes 589832 | tf_op jit(solution)/shard_map/ppermute | solution.py:56
  630.7 12.7 %collective-permute-start.49 = (bf16[48,2048]{1,0:T(8,128)(2,1)S(1)}, bf16[48,2048]{1,0:T(8,128)(2,1)S(1)}, u32[]{:S(2)}, u32[]{:S(2)}) collective-permute-start(bf16[48,2048]{1,0:T(8,128)(2,1)S(1)} %get-tuple-element.166), channel_id=1, source_target_pairs={{0,4},{1,5},{2,6},{3,7},{4,0},{5,1},{6,2},{7,3},{8,12},{9,13},{10,... | collective-permute-start | bytes 589832 | tf_op jit(solution)/shard_map/ppermute | solution.py:56
  631.1 12.4 %collective-permute-start.50 = (bf16[48,2048]{1,0:T(8,128)(2,1)S(1)}, bf16[48,2048]{1,0:T(8,128)(2,1)S(1)}, u32[]{:S(2)}, u32[]{:S(2)}) collective-permute-start(bf16[48,2048]{1,0:T(8,128)(2,1)S(1)} %get-tuple-element.165), channel_id=1, source_target_pairs={{0,6},{1,7},{2,4},{3,5},{4,2},{5,3},{6,0},{7,1},{8,14},{9,15},{10,... | collective-permute-start | bytes 589832 | tf_op jit(solution)/shard_map/ppermute | solution.py:56
  643.6 5.7 collective-permute-start.51
  645.9 7.1 %collective-permute-start.53 = (bf16[48,2048]{1,0:T(8,128)(2,1)S(1)}, bf16[48,2048]{1,0:T(8,128)(2,1)S(1)}, u32[]{:S(2)}, u32[]{:S(2)}) collective-permute-start(bf16[48,2048]{1,0:T(8,128)(2,1)S(1)} %fusion.25), channel_id=1, source_target_pairs={{0,24},{1,25},{2,26},{3,27},{4,28},{5,29},{6,30},{7,31},{8,16},{9,... | collective-permute-start | bytes 589832 | tf_op jit(solution)/shard_map/ppermute | solution.py:56
  (71 other events, 1155.2 us)

commit v3 on v2

v3 whole, which is shorter than its diff:
```python
import math

import jax
import jax.numpy as jnp
from jax import lax
from jax.experimental import pallas as pl
from jax.experimental.pallas import tpu as pltpu
from jax.sharding import PartitionSpec as P

D = 768
HEADS = 12
HD = 64
GRID = 24
COUNT = GRID * GRID
DATASETS = 10
NH = 4
GROUPS = HEADS // NH
WIDTH = NH * HD
LANES = 128
F32 = jnp.float32
BF16 = jnp.bfloat16
BOTH = ("rep", "wide")
VMEM = 60 << 20


def mm(left, right):
    return jnp.dot(left, right, preferred_element_type=F32)


def mm_tn(left, right):
    return lax.dot_general(left, right, (((0,), (0,)), ((), ())), preferred_element_type=F32)


def mm_nt(left, right):
    return lax.dot_general(left, right, (((1,), (1,)), ((), ())), preferred_element_type=F32)


def spec(shape, dtype=BF16):
    return jax.ShapeDtypeStruct(shape, dtype)


def whole(shape):
    return pl.BlockSpec(shape, lambda *_: (0,) * len(shape), pipeline_mode=pl.Buffered(1))


def params():
    return pltpu.CompilerParams(vmem_limit_bytes=VMEM)


def cost(macs, size):
    return pl.CostEstimate(flops=2 * int(macs), bytes_accessed=int(size), transcendentals=0)


def lasts(microseconds):
    return pl.CostEstimate(flops=int(microseconds * 1.15e9), bytes_accessed=0, transcendentals=0)


FLIP = {"y": 16, "x": 8, "z1": 4, "z0": 2, "c": 1}
XY, YX = ("x", "y"), ("y", "x")


def swap(value, *names):
    flip = sum(FLIP[name] for name in names)
    return lax.ppermute(value, BOTH, [(i, i ^ flip) for i in range(32)])


def bits():
    rep, wide = lax.axis_index("rep"), lax.axis_index("wide")
    return {"y": rep // 2, "x": rep % 2, "z1": wide // 4, "z0": (wide // 2) % 2, "c": wide % 2}


def bit_vector():
    b = bits()
    return jnp.stack([b[k] for k in ("y", "x", "z1", "z0", "c")]).astype(jnp.int32)


class Line:
    def __init__(self):
        self.tokens = []

    def after(self, value):
        return lax.optimization_barrier((value, *self.tokens))[0] if self.tokens else value

    def run(self, call, first, *rest):
        out = call(self.after(first), *rest)
        self.tokens = jax.tree.leaves(out)[-1:]
        return out

    def run_all(self, call, *values):
        out = call(*(lax.optimization_barrier((*values, *self.tokens))[:len(values)]))
        self.tokens = jax.tree.leaves(out)
        return out


def locate(me, order, plane, z, core):
    place = {order[0]: plane[0], order[1]: plane[1]}
    shard = ((me[2] ^ z[0]) * 2 + (me[3] ^ z[1])) * 2 + (me[4] ^ core)
    return shard, me[0] ^ place["y"], me[1] ^ place["x"]


class Gather:
    def __init__(self, line, piece, at, axis):
        self.line, self.at, self.axis = line, at, axis
        self.got = [piece, swap(piece, "z0"), swap(piece, "z1"), swap(piece, "z1", "z0")]

    def over_first(self):
        def call(*parts):
            value = jnp.stack(parts)
            return [lax.slice_in_dim(value, 0, self.at, axis=self.axis + 1),
                    lax.slice_in_dim(value, self.at, value.shape[self.axis + 1], axis=self.axis + 1)]

        one, two = self.line.run_all(call, *self.got)
        self.got = [one, swap(one, "x"), two, swap(two, "y")]

    def over_second(self):
        def call(one, one_x, two, two_y):
            return [jnp.concatenate([one, one_x]), jnp.concatenate([two, two_y])]

        one, two = self.line.run_all(call, *self.got)
        self.pieces = []
        for value, name in ((one, "y"), (two, "x")):
            other = swap(value, name)
            self.pieces += [value, other, swap(value, "c"), swap(other, "c")]


PLANE = [[(s // 4, a % 2, s // 2 % 2, s % 2, a // 2) for s in range(8)] for a in range(4)]


def assemble(me, gathered, shapes, parts):
    at, axis = gathered.at, gathered.axis

    def halves(rows, cols):
        first, size = (rows, cols)[axis]
        out = []
        for low, high, shift in ((first, min(first + size, at), 0), (max(first, at), first + size, at)):
            span = (low - shift, high - low)
            out.append(None if high <= low else (span, cols, low - first, 0) if axis == 0 else (rows, span, 0, low - first))
        return out

    def body(me_ref, *refs):
        ins, outs, sem = refs[:8], refs[8:-1], refs[-1]
        started = []
        for half, order in enumerate((XY, YX)):
            for a, places in enumerate(PLANE):
                for s, (first, second, z1, z0, core) in enumerate(places):
                    shard, y, x = locate(me_ref, order, (first, second), (z1, z0), core)
                    for k, rows, cols, row, col in parts:
                        share = halves(rows, cols)[half]
                        if share is None or (row is None and (first or second)):
                            continue
                        (r0, r), (c0, n), down, across = share
                        source = ins[4 * half + a].at[s, pl.ds(r0, r), pl.ds(c0, n)]
                        if row is None:
                            place = outs[k].at[shard, pl.ds(down, r), pl.ds(across, n)]
                        else:
                            place = outs[k].at[pl.ds(pl.multiple_of(row(shard, y) + down, 16), r),
                                               pl.ds(pl.multiple_of(col(x) + across, LANES), n)]
                        copy = pltpu.make_async_copy(source, place, sem.at[len(started)])
                        copy.start()
                        started.append(copy)
        for copy in started:
            copy.wait()

    return pl.pallas_call(
        body,
        grid=(1,),
        in_specs=[pl.BlockSpec(memory_space=pltpu.SMEM)] + [pl.BlockSpec(memory_space=pl.ANY)] * 8,
        out_specs=[whole(s) for s in shapes],
        out_shape=[spec(s) for s in shapes],
        scratch_shapes=[pltpu.SemaphoreType.DMA((64 * len(parts),))],
        compiler_params=params(),
        cost_estimate=lasts(5),
        name="assemble",
    )(me, *gathered.pieces)


def total_of(terms):
    if len(terms) == 2:
        return terms[0] + terms[1]
    return sum(term.astype(F32) for term in terms).astype(BF16)


def in_four(total):
    size = total.shape[0] // 4
    return [total[size * i:size * (i + 1)] for i in range(4)]


def together(line, *jobs):
    counts = [len(job.terms) for job in jobs]

    def call(*terms):
        out = []
        for job, count in zip(jobs, counts):
            out.append(job.add(*terms[:count]))
            terms = terms[count:]
        return out

    for job, out in zip(jobs, line.run_all(call, *[term for job in jobs for term in job.terms])):
        job.send(out)


class Chunk:
    def __init__(self, line, keep, send, split):
        self.split, self.stage = split, 0
        self.terms = [keep, swap(line.after(send), "c")]

    def add(self, *terms):
        split = self.split
        if self.stage == 0 and split is None:
            return in_four(total_of(terms))
        if self.stage == 0:
            total = total_of(terms)
            return [total[:8, :split], total[8:, :split], total[:8, split:], total[8:, split:]]
        if split is None:
            return [total_of(terms)]
        one, two = terms[0] + terms[1], terms[2] + terms[3]
        if self.stage == 1:
            return [one[:4], one[4:], two[:4], two[4:]]
        return [jnp.concatenate([one, two], 1)]

    def send(self, out):
        if len(out) == 1:
            self.total = out[0]
        elif self.split is None:
            self.terms = [out[0], swap(out[1], "y"), swap(out[2], "x"), swap(out[3], "x", "y")]
        else:
            one, two = ("x", "y") if self.stage == 0 else ("y", "x")
            self.terms = [out[0], swap(out[1], one), out[2], swap(out[3], two)]
        self.stage += 1


class Along:
    def __init__(self, line, chunks):
        self.stage, self.rows = 0, [chunk.total.shape[1] for chunk in chunks]
        out = line.run_all(lambda *totals: in_four(jnp.concatenate(totals, 1)), *[chunk.total for chunk in chunks])
        self.terms = [out[0], swap(out[1], "z0"), swap(out[2], "z1"), swap(out[3], "z1", "z0")]

    def add(self, *terms):
        return [total_of(terms)[0]]

    def send(self, out):
        total = out[0]
        self.terms = [total, swap(total, "x"), swap(total, "y"), swap(total, "x", "y")]


class Whole:
    def __init__(self, value):
        self.terms, self.stage = [value, swap(value, "y")], 0

    def add(self, *terms):
        return [total_of(terms)]

    def send(self, out):
        self.terms = [out[0], swap(out[0], "x")]


def finish(me, alongs, places, shapes):
    ins = [t for along in alongs for t in along.terms]

    def body(me_ref, *refs):
        outs = refs[len(ins):len(ins) + len(shapes)]
        held = refs[len(ins) + len(shapes):]
        for c, parts in enumerate(places):
            for q in range(4):
                held[c][q] = refs[4 * c + q][...]
            for y in range(2):
                for x in range(2):
                    at = 2 * (me_ref[0] ^ y) + (me_ref[1] ^ x)
                    for k, r, r0, blocks, row, col in parts:
                        for b in range(blocks):
                            at_row = row(y) + (r * x if shapes[k][1] == LANES else 0)
                            outs[k][at_row:at_row + r, col(x, b):col(x, b) + LANES] = (
                                held[c][at, r0 + b * r:r0 + (b + 1) * r, :].astype(F32))

    return pl.pallas_call(
        body,
        grid=(1,),
        in_specs=[pl.BlockSpec(memory_space=pltpu.SMEM)] + [whole(a.shape) for a in ins],
        out_specs=[whole(s) for s in shapes],
        out_shape=[spec(s, F32) for s in shapes],
        scratch_shapes=[pltpu.VMEM((4,) + along.terms[0].shape, BF16) for along in alongs],
        compiler_params=params(),
        cost_estimate=lasts(3),
        name="finish",
    )(me, *ins)


PLAIN = "plain"


TABLE = 64


class Sink:
    def __init__(self, shapes, split, table=False):
        self.shapes, self.split, self.table = shapes, split, table
        rows = sum(k // 16 * (n // 2 // LANES) for k, n in shapes) + (TABLE // 4 if table else 0)
        if split == PLAIN:
            self.outs, self.scratch = [spec(s) for s in shapes], []
        else:
            self.outs = [spec((16, rows, LANES))] * 2
            self.scratch = [pltpu.VMEM((2, k, n // 2), BF16) for k, n in shapes]
            self.scratch += [pltpu.VMEM((TABLE, LANES), BF16)] if table else []

    def out_specs(self):
        return [whole(o.shape) for o in self.outs]

    def put(self, outs, held, k, rows, value):
        value = value.astype(BF16)
        half = self.shapes[k][1] // 2
        if self.split == PLAIN:
            outs[k][rows, :] = value
        else:
            held[k][0, rows, :] = value[:, :half]
            held[k][1, rows, :] = value[:, half:]

    def deliver(self, me_ref, outs, held):
        if self.split == PLAIN:
            return
        for core in range(2):
            for s in range(16):
                z = (s // 2 % 2, s % 2)
                places = [locate(me_ref, order, (s // 8, s // 4 % 2), z, core) for order in (XY, YX)]
                at = 0
                for k, (rows, cols) in enumerate(self.shapes):
                    r = rows // 16
                    for b in range(cols // 2 // LANES):
                        shard, y, x = places[0 if self.split is None or at < self.split else 1]
                        start = pl.multiple_of((shard * 2 + y) * r, 16)
                        outs[core][s, at:at + r, :] = held[k][x, pl.ds(start, r), b * LANES:(b + 1) * LANES]
                        at += r
                if self.table:
                    r = TABLE // 4
                    _, y, x = places[0 if self.split is None or at < self.split else 1]
                    outs[core][s, at:at + r, :] = held[-1][pl.ds(pl.multiple_of((2 * y + x) * r, 16), r), :]


def gelu_pair(values):
    cdf = 0.5 + 0.5 * lax.erf(values * 0.7071067811865476)
    pdf = 0.3989422804014327 * jnp.exp(-0.5 * values * values)
    return values * cdf, cdf + values * pdf


def normalize(values):
    centred = values - jnp.mean(values, -1, keepdims=True)
    recip = lax.rsqrt(jnp.mean(centred * centred, -1, keepdims=True) + 1e-06)
    return centred * recip, recip


def norm_transpose(grad_normed, normed, recip):
    return recip * (
        grad_normed
        - jnp.mean(grad_normed, -1, keepdims=True)
        - normed * jnp.mean(grad_normed * normed, -1, keepdims=True)
    )


SMALL = 16


def prepare(me, w_qkv, w_out, w_fc1, w_fc2, w_re, w_head, gains, scales, shifts):
    ff, ch = w_fc1.shape[1], w_re.shape[1]
    half = w_qkv.shape[0] // 2
    rows_two, rows_head = w_fc2.shape[0] // 2, w_head.shape[0] // 2
    n = w_qkv.shape[1] // 2

    def body(me_ref, qkv_ref, out_ref, fc1_ref, fc2_ref, re_ref, head_ref, gains_ref, scales_ref, shifts_ref,
             zero_ref, one_ref, two_ref):
        zero_ref[half:half + SMALL, :] = jnp.zeros((SMALL, n), BF16)
        zero_ref[half:half + DATASETS, 0:scales.shape[1]] = scales_ref[...]
        zero_ref[half:half + DATASETS, LANES:LANES + shifts.shape[1]] = shifts_ref[...]
        zero_ref[half:half + 2, 2 * LANES:2 * LANES + gains.shape[1]] = gains_ref[...]
        rows = pl.ds(pl.multiple_of(me_ref[0] * half, 16), half)
        rows_of_two = pl.ds(pl.multiple_of(me_ref[0] * rows_two, 16), rows_two)
        rows_of_head = pl.ds(pl.multiple_of(me_ref[0] * rows_head, 16), rows_head)
        for x in range(2):
            @pl.when(me_ref[1] == x)
            def _():
                zero_ref[0:half, :] = qkv_ref[rows, n * x:n * (x + 1)]
                one_ref[:, :D // 2] = out_ref[rows, D // 2 * x:D // 2 * (x + 1)]
                at = D // 2 + ff // 2
                one_ref[:, D // 2:at] = fc1_ref[rows, ff // 2 * x:ff // 2 * (x + 1)]
                one_ref[:, at:at + ch // 2] = re_ref[rows, ch // 2 * x:ch // 2 * (x + 1)]
                one_ref[0:rows_head, at + ch // 2:] = head_ref[rows_of_head, ch // 2 * x:ch // 2 * (x + 1)]
                two_ref[...] = fc2_ref[rows_of_two, D // 2 * x:D // 2 * (x + 1)]
        one_ref[rows_head:, D // 2 + ff // 2 + ch // 2:] = jnp.zeros((half - rows_head, LANES), BF16)

    ins = (w_qkv, w_out, w_fc1, w_fc2, w_re, w_head, gains, scales, shifts)
    outs = [spec((half + SMALL, n)), spec((half, D // 2 + ff // 2 + ch // 2 + LANES)), spec((rows_two, D // 2))]
    return pl.pallas_call(
        body,
        grid=(1,),
        in_specs=[pl.BlockSpec(memory_space=pltpu.SMEM)] + [whole(a.shape) for a in ins],
        out_specs=[whole(o.shape) for o in outs],
        out_shape=outs,
        compiler_params=params(),
        cost_estimate=lasts(2.4),
        name="prepare",
    )(me, *ins)


def norm_body(x_ref, out_ref):
    out_ref[...] = normalize(x_ref[...].astype(F32))[0]


def norm(x):
    rows = x.shape[0]
    block = pl.BlockSpec((rows // 4, D), lambda i: (i, 0))
    return pl.pallas_call(
        norm_body,
        grid=(4,),
        in_specs=[block],
        out_specs=block,
        out_shape=spec((rows, D), F32),
        compiler_params=params(),
        cost_estimate=lasts(4.4),
        name="norm",
    )(x)


def bilinear(targets, sources, first):
    size = 2 * GRID
    step = (GRID - 1) / (size - 1)

    def hat(target, source):
        return jnp.maximum(1.0 - jnp.abs(target.astype(F32) * step - source.astype(F32)), 0.0)

    target = lax.broadcasted_iota(jnp.int32, targets, targets.index(max(targets))) + first
    source = lax.broadcasted_iota(jnp.int32, sources, sources.index(max(sources)))
    return (hat(target // size, source // GRID) * hat(target % size, source % GRID)).astype(BF16)


def down_body(dj_ref, live_ref, flag_ref, down_ref, gshift_ref):
    step, images, size = pl.program_id(0), dj_ref.shape[0], dj_ref.shape[1]
    table = bilinear((1, size), (COUNT, 1), step * size)
    for i in range(images):
        part = mm(table, dj_ref[i])
        sums = jnp.sum(dj_ref[i].astype(F32), 0, keepdims=True)

        @pl.when(step == 0)
        def _():
            down_ref[i] = part
            gshift_ref[i] = sums

        @pl.when(step > 0)
        def _():
            down_ref[i] += part
            gshift_ref[i] += sums

        @pl.when(step == pl.num_programs(0) - 1)
        def _():
            down_ref[i] = down_ref[i] * live_ref[i]
            gshift_ref[i] = gshift_ref[i] * (live_ref[i] * flag_ref[i])


def bring_down(dj, live, flag):
    images, count, ch = dj.shape
    one = whole((images, 1, ch))
    return pl.pallas_call(
        down_body,
        grid=(4,),
        in_specs=[pl.BlockSpec((images, count // 4, ch), lambda i: (0, i, 0)), one, one],
        out_specs=[whole((images, COUNT, ch)), one],
        out_shape=[spec((images, COUNT, ch), F32), spec((images, 1, ch), F32)],
        compiler_params=params(),
        cost_estimate=lasts(8.9),
        name="bring_down",
    )(dj, live, flag)


def attention_body(a1_ref, wq_ref, wk_ref, wv_ref, qkv_ref, o_ref, e_ref, r_ref):
    for i, ref in enumerate((wq_ref, wk_ref, wv_ref)):
        qkv_ref[:, WIDTH * i:WIDTH * (i + 1)] = mm(a1_ref[...], ref[...]).astype(BF16)
    for h in range(NH):
        q, k, v = (slice(WIDTH * i + HD * h, WIDTH * i + HD * (h + 1)) for i in range(3))
        s = mm_nt(qkv_ref[:, k], qkv_ref[:, q] * jnp.asarray(0.125, BF16))
        e = jnp.exp(s - jnp.max(s, 0, keepdims=True))
        r = 1.0 / jnp.sum(e, 0, keepdims=True)
        low = e.astype(BF16)
        e_ref[h] = low
        o_ref[:, HD * h:HD * (h + 1)] = (mm_tn(qkv_ref[:, v], low) * r).T.astype(BF16)
        r_ref[0, h:h + 1, :] = r


def group_specs():
    def cols(n):
        return pl.BlockSpec((COUNT, n), lambda i: (i, 0))

    return cols, pl.BlockSpec((NH, COUNT, COUNT), lambda i: (i, 0, 0)), pl.BlockSpec((1, NH, COUNT), lambda i: (i, 0, 0))


def group_columns(group):
    return [pl.BlockSpec((D, WIDTH), lambda i, p=p: (0, GROUPS * p + group), pipeline_mode=pl.Buffered(1)) for p in range(3)]


def attention(a1, w, group):
    rows = a1.shape[0]
    images = rows // COUNT
    cols, probs, sums = group_specs()
    return pl.pallas_call(
        attention_body,
        grid=(images,),
        in_specs=[cols(D)] + group_columns(group),
        out_specs=[cols(3 * WIDTH), cols(WIDTH), probs, sums],
        out_shape=[spec((rows, 3 * WIDTH)), spec((rows, WIDTH)), spec((images * NH, COUNT, COUNT)),
                   spec((images, NH, COUNT), F32)],
        compiler_params=params(),
        cost_estimate=lasts(11),
        name="attention",
    )(a1, w, w, w)


def attention_back(da, me, group, qkv, o, e, r, a1, w_out, extra, split):
    rows = da.shape[0]
    images = rows // COUNT
    cols, probs, sums = group_specs()
    shape = (D, 3 * WIDTH)
    sink = Sink([shape], PLAIN) if extra is None else Sink([shape, (D, D)], split)
    n_out = len(sink.outs)
    extra = list(extra) if isinstance(extra, (list, tuple)) else [] if extra is None else [extra]

    def body(da_ref, me_ref, qkv_ref, o_ref, e_ref, r_ref, a1_ref, wout_ref, *refs):
        more, refs = refs[:len(extra)], refs[len(extra):]
        grads, dqkv, total, held = refs[:n_out], refs[n_out], refs[n_out + 1], refs[n_out + 2:]
        if len(extra) > 1:
            total_out, held = held[0], held[1:]
        step = pl.program_id(0)
        ones = jnp.ones((8, HD), BF16)
        do_all = mm_nt(da_ref[...], wout_ref[...]).astype(BF16)
        for h in range(NH):
            q, k, v = (slice(WIDTH * i + HD * h, WIDTH * i + HD * (h + 1)) for i in range(3))
            do = do_all[:, HD * h:HD * (h + 1)]
            delta = mm_nt(ones, (do.astype(F32) * o_ref[:, HD * h:HD * (h + 1)].astype(F32)).astype(BF16))[0:1]
            prob = e_ref[h].astype(F32) * r_ref[0, h:h + 1, :]
            dp = mm_nt(qkv_ref[:, v], do)
            ds = (prob * (dp - delta)).astype(BF16)
            dqkv[:, v] = mm(prob.astype(BF16), do).astype(BF16)
            dqkv[:, k] = (mm(ds, qkv_ref[:, q]) * 0.125).astype(BF16)
            dqkv[:, q] = (mm_tn(ds, qkv_ref[:, k]) * 0.125).astype(BF16)
        g = mm_tn(a1_ref[...], dqkv[...])
        g_out = [mm_tn(ref[...], da_ref[...]) for ref in more] if len(extra) > 1 else []

        @pl.when(step == 0)
        def _():
            total[...] = g
            for i, part in enumerate(g_out):
                total_out[WIDTH * i:WIDTH * (i + 1)] = part

        @pl.when(step > 0)
        def _():
            total[...] += g
            for i, part in enumerate(g_out):
                total_out[WIDTH * i:WIDTH * (i + 1)] += part

        @pl.when(step == images - 1)
        def _():
            sink.put(grads, held, 0, slice(0, D), total[...])
            if len(extra) > 1:
                sink.put(grads, held, 1, slice(0, D), total_out[...])
            elif extra:
                sink.put(grads, held, 1, slice(0, D), more[0][...])
            sink.deliver(me_ref, grads, held)

    more_specs = [cols(WIDTH)] * len(extra) if len(extra) > 1 else [whole(a.shape) for a in extra]
    out = pl.pallas_call(
        body,
        grid=(images,),
        in_specs=[cols(D), pl.BlockSpec(memory_space=pltpu.SMEM), cols(3 * WIDTH), cols(WIDTH), probs, sums, cols(D),
                  pl.BlockSpec((WIDTH, D), lambda i: (group, 0))] + more_specs,
        out_specs=sink.out_specs() + [cols(3 * WIDTH)],
        out_shape=sink.outs + [spec((rows, 3 * WIDTH))],
        scratch_shapes=[pltpu.VMEM(shape, F32)] + ([pltpu.VMEM((D, D), F32)] if len(extra) > 1 else []) + sink.scratch,
        compiler_params=params(),
        cost_estimate=lasts(18),
        name="attention_back",
    )(da, me, qkv, o, e, r, a1, w_out, *extra)
    return out[:n_out], out[n_out]


def input_back(dqkv, w, dx2, x, gains):
    rows = x.shape[0]
    block = rows // 4

    def body(*refs):
        (w_ref, dx2_ref, x_ref, gains_ref), out_ref = refs[GROUPS:-1], refs[-1]
        da1 = jnp.zeros((block, D), F32)
        for i, ref in enumerate(refs[:GROUPS]):
            for p in range(3):
                at = D * p + WIDTH * i
                da1 = da1 + mm_nt(ref[:, WIDTH * p:WIDTH * (p + 1)], w_ref[:, at:at + WIDTH])
        n1, rs1 = normalize(x_ref[...].astype(F32))
        out_ref[...] = (dx2_ref[...] + norm_transpose(da1 * gains_ref[0:1], n1, rs1)).astype(BF16)

    def cols(n):
        return pl.BlockSpec((block, n), lambda i: (i, 0))

    return pl.pallas_call(
        body,
        grid=(4,),
        in_specs=[cols(3 * WIDTH)] * GROUPS + [whole(w.shape), cols(D), cols(D), whole(gains.shape)],
        out_specs=cols(D),
        out_shape=spec((rows, D)),
        compiler_params=params(),
        cost_estimate=lasts(9),
        name="input_back",
    )(*dqkv, w, dx2, x, gains)


def mlp_up_body(x_ref, o0_ref, o1_ref, o2_ref, wout_ref, w1_ref, gains_ref, x2_ref, a2_ref, gg_ref, slope_ref):
    rows = x2_ref.shape[0]
    chunk = rows // 4

    @pl.when(pl.program_id(0) == 0)
    def _():
        for p in range(0, rows, chunk):
            at = slice(p, p + chunk)
            x2 = x_ref[at].astype(F32)
            for i, ref in enumerate((o0_ref, o1_ref, o2_ref)):
                x2 = x2 + mm(ref[at], wout_ref[WIDTH * i:WIDTH * (i + 1)])
            x2_ref[at] = x2
            a2_ref[at] = (normalize(x2)[0] * gains_ref[1:2]).astype(BF16)

    act, slope = gelu_pair(mm(a2_ref[...], w1_ref[...]))
    gg_ref[...], slope_ref[...] = act.astype(BF16), slope.astype(BF16)


def mlp_up(x, heads_out, w_out, w1, gains, block=512):
    rows, ff = x.shape[0], w1.shape[1]
    full, cols = whole((rows, D)), pl.BlockSpec((rows, block), lambda i: (0, i))
    return pl.pallas_call(
        mlp_up_body,
        grid=(ff // block,),
        in_specs=[full] + [whole((rows, WIDTH))] * 3 + [whole((D, D)), pl.BlockSpec((D, block), lambda i: (0, i)), whole((2, D))],
        out_specs=[full, full, cols, cols],
        out_shape=[spec((rows, D), F32), spec((rows, D)), spec((rows, ff)), spec((rows, ff))],
        compiler_params=params(),
        cost_estimate=lasts(18),
        name="mlp_up",
    )(x, *heads_out, w_out, w1, gains)


def mlp_down_body(gg_ref, w2_ref, x2_ref, count_ref, x3b_ref, out_ref):
    x3 = x2_ref[...] + mm(gg_ref[...], w2_ref[...])
    x3b_ref[...] = x3.astype(BF16)
    image = pl.program_id(0) * x3b_ref.shape[0] // COUNT
    out_ref[...] = (x3 * (image < count_ref[0]).astype(F32)).astype(BF16)


def mlp_down(gg, w2, x2, live_count):
    rows, ff = gg.shape
    block = rows // 4
    at = pl.BlockSpec((block, D), lambda i: (i, 0))
    return pl.pallas_call(
        mlp_down_body,
        grid=(4,),
        in_specs=[pl.BlockSpec((block, ff), lambda i: (i, 0)), whole(w2.shape), at, pl.BlockSpec(memory_space=pltpu.SMEM)],
        out_specs=[at, at],
        out_shape=[spec((rows, D))] * 2,
        compiler_params=params(),
        cost_estimate=lasts(11),
        name="mlp_down",
    )(gg, w2, x2, live_count)


def spread(value, out_ref, rows, sign):
    count, ch = value.shape
    at = lax.broadcasted_iota(jnp.int32, (count, 1), 0)
    col = at % GRID
    gap = jnp.zeros((GRID, ch), F32)
    for dx in (-1, 0, 1):
        step = sign * dx
        moved = value
        if step:
            moved = pltpu.roll(value, (-step) % count, 0)
            moved = jnp.where((col + step >= 0) & (col + step < GRID), moved, 0.0)
        for dy in (-1, 0, 1):
            block = 3 * (dy + 1) + dx + 1
            if sign * dy == 1:
                part = jnp.concatenate([moved[GRID:], gap], 0)
            elif sign * dy == -1:
                part = jnp.concatenate([gap, moved[:-GRID]], 0)
            else:
                part = moved
            out_ref[rows, block * ch:(block + 1) * ch] = part.astype(BF16)


def units_body(x_ref, wre_ref, w_ref, t1_ref, s1_ref, t2_ref, s2_ref, z_ref, cols):
    count = x_ref.shape[0]
    z = mm(x_ref[...], wre_ref[...])
    for unit in range(2):
        act, slope = gelu_pair(z)
        t1_ref[unit], s1_ref[unit] = act.astype(BF16), slope.astype(BF16)
        spread(act, cols, slice(0, count), 1)
        act, slope = gelu_pair(mm(cols[...], w_ref[2 * unit]))
        t2_ref[unit], s2_ref[unit] = act.astype(BF16), slope.astype(BF16)
        spread(act, cols, slice(0, count), 1)
        z = z + mm(cols[...], w_ref[2 * unit + 1])
    z_ref[...] = z.astype(BF16)


def units(x3b, w_re, w_conv):
    rows, ch = x3b.shape[0], w_re.shape[1]
    acts = pl.BlockSpec((2, COUNT, ch), lambda i: (0, i, 0))
    return pl.pallas_call(
        units_body,
        grid=(rows // COUNT,),
        in_specs=[pl.BlockSpec((COUNT, D), lambda i: (i, 0)), whole(w_re.shape), whole(w_conv.shape)],
        out_specs=[acts] * 4 + [pl.BlockSpec((COUNT, ch), lambda i: (i, 0))],
        out_shape=[spec((2, rows, ch))] * 4 + [spec((rows, ch))],
        scratch_shapes=[pltpu.VMEM((COUNT, 9 * ch), BF16)],
        compiler_params=params(),
        cost_estimate=lasts(18),
        name="units",
    )(x3b, w_re, w_conv)


def units_back_body(down_ref, scale_ref, gshift_ref, hot_ref, z_ref, x3b_ref, gt_ref, count_ref, whead_ref, w_ref, wre_ref, t1_ref, s1_ref, t2_ref, s2_ref,
                    gw_ref, ghead_ref, gre_ref, dx3_ref, dm_ref, table_ref, moved, turned, dz_ref):
    images, _, ch = down_ref.shape
    dq = jnp.concatenate([(down_ref[i] * scale_ref[i]).astype(BF16) for i in range(images)], 0)
    ghead_ref[...] = mm_tn(z_ref[...], dq).astype(BF16)
    dz_ref[...] = mm_nt(dq, whead_ref[...])
    table_ref[...] = jnp.zeros_like(table_ref)
    for i in range(images):
        head = mm(z_ref[COUNT * i:COUNT * (i + 1)], whead_ref[...])
        sums = (jnp.sum(head * down_ref[i], 0, keepdims=True), gshift_ref[i])
        for b in range(2 * ch // LANES):
            at, row = SMALL * b, sums[b // (ch // LANES)]
            cols = slice(LANES * (b % (ch // LANES)), LANES * (b % (ch // LANES) + 1))
            table_ref[at:at + SMALL] += hot_ref[i] * row[:, cols]

    def back(index, grad, act_ref, unit):
        for i in range(images):
            at = slice(COUNT * i, COUNT * (i + 1))
            spread(grad[at], moved, at, -1)
        g = mm_tn(act_ref[unit], moved[...])
        for b in range(9):
            at = slice(ch * b, ch * (b + 1))
            gw_ref[index, at, :] = g[:, at].astype(BF16)
            turned[:, at] = w_ref[index, at, :]
        return mm_nt(moved[...], turned[...])

    for unit in (1, 0):
        grad = back(2 * unit + 1, dz_ref[...], t2_ref, unit) * s2_ref[unit].astype(F32)
        grad = back(2 * unit, grad, t1_ref, unit) * s1_ref[unit].astype(F32)
        dz_ref[...] += grad
    dr = dz_ref[...].astype(BF16)
    gre_ref[...] = mm_tn(x3b_ref[...], dr).astype(BF16)
    dx3 = mm_nt(dr, wre_ref[...])
    for i in range(images):
        at = slice(COUNT * i, COUNT * (i + 1))
        part = gt_ref[at].astype(F32) * (i < count_ref[0]).astype(F32) + dx3[at]
        dx3_ref[at] = part
        dm_ref[at] = part.astype(BF16)


def units_back(down, scale, gshift, hot, z, x3b, gt, live_count, w_head, w_conv, w_re, t1, s1, t2, s2):
    rows, ch = z.shape
    ins = (down, scale, gshift, hot, z, x3b, gt, live_count, w_head, w_conv, w_re, t1, s1, t2, s2)
    outs = [spec(w_conv.shape), spec(w_head.shape), spec(w_re.shape), spec((rows, D), F32), spec((rows, D)),
            spec((2 * ch // LANES * SMALL, LANES), F32)]
    return pl.pallas_call(
        units_back_body,
        grid=(1,),
        in_specs=[pl.BlockSpec(memory_space=pltpu.SMEM) if a is live_count else whole(a.shape) for a in ins],
        out_specs=[whole(a.shape) for a in outs],
        out_shape=outs,
        scratch_shapes=[pltpu.VMEM((rows, 9 * ch), BF16), pltpu.VMEM((ch, 9 * ch), BF16), pltpu.VMEM((rows, ch), F32)],
        compiler_params=params(),
        cost_estimate=lasts(30),
        name="units_back",
    )(*ins)


def hidden_back(dm, me, gg, slope, w2, split, block=512):
    rows, ff = gg.shape
    sink = Sink([(ff, D)], split)
    n_out = len(sink.outs)

    def body(dm_ref, me_ref, gg_ref, slope_ref, w2_ref, *refs):
        grads, du_ref, held = refs[:n_out], refs[n_out], refs[n_out + 1:]
        step = pl.program_id(0)
        at = pl.ds(pl.multiple_of(step * block, block), block)
        sink.put(grads, held, 0, at, mm_tn(gg_ref[...], dm_ref[...]))
        du_ref[...] = (mm_nt(dm_ref[...], w2_ref[...]) * slope_ref[...].astype(F32)).astype(BF16)

        @pl.when(step == pl.num_programs(0) - 1)
        def _():
            sink.deliver(me_ref, grads, held)

    cols = pl.BlockSpec((rows, block), lambda i: (0, i))
    out = pl.pallas_call(
        body,
        grid=(ff // block,),
        in_specs=[whole((rows, D)), pl.BlockSpec(memory_space=pltpu.SMEM), cols, cols, pl.BlockSpec((block, D), lambda i: (i, 0))],
        out_specs=sink.out_specs() + [cols],
        out_shape=sink.outs + [spec((rows, ff))],
        scratch_shapes=sink.scratch,
        compiler_params=params(),
        cost_estimate=lasts(20),
        name="hidden_back",
    )(dm, me, gg, slope, w2)
    return out[:n_out], out[n_out]


def mlp_back(du, me, a2, w1, dx3, x2, gains, g_re, g_head, table, split, block=512):
    rows, ff = du.shape
    sink = Sink([(D, ff), g_re.shape, g_head.shape], split, True)
    n_out = len(sink.outs)
    half = ff // 2 // block

    def body(du_ref, me_ref, a2_ref, w1_ref, dx3_ref, x2_ref, gains_ref, gre_ref, ghead_ref, table_ref, *refs):
        step = pl.program_id(0)
        grads, (dx2_ref, da_ref, total), held = refs[:n_out], refs[n_out:n_out + 3], refs[n_out + 3:]
        g = mm_tn(a2_ref[...], du_ref[...]).astype(BF16)
        cols = pl.ds(pl.multiple_of(step % half * block, block), block)
        if split == PLAIN:
            grads[0][:, pl.ds(pl.multiple_of(step * block, block), block)] = g
        else:
            held[0][step // half, :, cols] = g
        da2 = mm_nt(du_ref[...], w1_ref[...])

        @pl.when(step == 0)
        def _():
            total[...] = da2

        @pl.when(step > 0)
        def _():
            total[...] += da2

        @pl.when(step == pl.num_programs(0) - 1)
        def _():
            sink.put(grads, held, 1, slice(0, g_re.shape[0]), gre_ref[...])
            sink.put(grads, held, 2, slice(0, g_head.shape[0]), ghead_ref[...])
            if split != PLAIN:
                held[-1][...] = table_ref[...].astype(BF16)
            sink.deliver(me_ref, grads, held)
            chunk = rows // 6
            for p in range(0, rows, chunk):
                at = slice(p, p + chunk)
                n2, rs2 = normalize(x2_ref[at])
                dx2 = dx3_ref[at] + norm_transpose(total[at] * gains_ref[1:2], n2, rs2)
                dx2_ref[at] = dx2
                da_ref[at] = dx2.astype(BF16)

    full = whole((rows, D))
    others = [spec((rows, D), F32), spec((rows, D))]
    out = pl.pallas_call(
        body,
        grid=(ff // block,),
        in_specs=[pl.BlockSpec((rows, block), lambda i: (0, i)), pl.BlockSpec(memory_space=pltpu.SMEM), full,
                  pl.BlockSpec((D, block), lambda i: (0, i)), full, full, whole((2, D)), whole(g_re.shape), whole(g_head.shape),
                  whole(table.shape)],
        out_specs=sink.out_specs() + [whole(o.shape) for o in others],
        out_shape=sink.outs + others,
        scratch_shapes=[pltpu.VMEM((rows, D), F32)] + sink.scratch,
        compiler_params=params(),
        cost_estimate=lasts(27),
        name="mlp_back",
    )(du, me, a2, w1, dx3, x2, gains, g_re, g_head, table)
    return out[:n_out], out[n_out:]


def join_body(z_ref, w_ref, scale_ref, shift_ref, live_ref, out_ref, head_ref):
    step, images, size = pl.program_id(0), out_ref.shape[0], out_ref.shape[1]

    @pl.when(step == 0)
    def _():
        for i in range(images):
            head = mm(z_ref[COUNT * i:COUNT * (i + 1)], w_ref[...])
            head_ref[i] = head.astype(BF16)

    table = bilinear((size, 1), (1, COUNT), step * size)
    for i in range(images):
        out_ref[i] = ((mm(table, head_ref[i]) * scale_ref[i] + shift_ref[i]) * live_ref[i]).astype(BF16)


def join(z, w_head, scale, shift, live):
    images, ch = scale.shape[0], w_head.shape[1]
    one = whole((images, 1, ch))
    return pl.pallas_call(
        join_body,
        grid=(4,),
        in_specs=[whole(z.shape), whole(w_head.shape), one, one, one],
        out_specs=pl.BlockSpec((images, COUNT, ch), lambda i: (0, i, 0)),
        out_shape=spec((images, 4 * COUNT, ch)),
        scratch_shapes=[pltpu.VMEM((images, COUNT, ch), BF16)],
        compiler_params=params(),
        cost_estimate=lasts(7),
        name="join",
    )(z, w_head, scale, shift, live)


def shards(tokens, live_count, dataset_id, shift_flag, norm_gains, w_qkv, w_attn_out, w_fc1, w_fc2, w_reassemble,
           conv_kernels, w_head, scale_table, shift_table, d_tokens_out, d_joined):
    slots, count = tokens.shape[:2]
    rows = slots * count
    neighbours = (lax.axis_size("rep"), lax.axis_size("wide")) == (4, 8)
    ch, ff = w_head.shape[1], w_fc1.shape[1]
    wide = lax.axis_size("wide")
    at_wide = lax.axis_index("wide")
    g, t = norm_gains.shape[1], scale_table.shape[1]
    me = bit_vector()
    line = Line()
    r = D // 16

    def gathered(part, axis):
        return lax.all_gather(part, "wide", axis=axis, tiled=True)

    def rows_of(size):
        return lambda shard, y: (shard * 2 + y) * size

    def cols_of(size):
        return lambda x: x * size

    def lanes(v):
        return jnp.broadcast_to(v[:, None, None], (slots, 1, ch))

    live = (jnp.arange(slots, dtype=jnp.int32) < live_count[0]).astype(F32)
    flags = shift_flag.astype(F32)
    x = tokens.reshape(rows, D)

    if neighbours:
        pieces = line.run(lambda v: prepare(me, v, w_attn_out, w_fc1, w_fc2, w_reassemble, w_head, norm_gains, scale_table,
                                            shift_table), w_qkv)
        zero = Gather(line, pieces[0], 5 * LANES, 1)
    n1 = line.run(norm, x)
    if neighbours:
        zero.over_first()
    down, g_shift_rows = line.run(bring_down, d_joined, lanes(live), lanes(flags))
    if neighbours:
        zero.over_second()
        f_qkv, small = line.run(lambda v: assemble(me, zero, [(D, 3 * D), (wide, SMALL, 3 * LANES)], [
            (0, (0, r), (0, 3 * D // 2), rows_of(r), cols_of(3 * D // 2)), (1, (r, SMALL), (0, 3 * LANES), None, None)]), zero.pieces[0])

        def table(lead, start, n):
            return small[:, :lead, start:start + n].transpose(1, 0, 2).reshape(lead, wide * n)

        gains, scales, shifts = table(2, 2 * LANES, g), table(DATASETS, 0, t), table(DATASETS, LANES, t)
    else:
        gains, scales, shifts = gathered(norm_gains, 1), gathered(scale_table, 1), gathered(shift_table, 1)
        f_qkv = gathered(w_qkv, 0)

    gains = gains.astype(F32)
    a1 = line.run(lambda n: (n * gains[0:1]).astype(BF16), n1)
    groups = []
    if neighbours:
        one = Gather(line, line.after(pieces[1]), 9 * LANES, 1)
    for i in range(GROUPS):
        groups.append(line.run(attention, a1, f_qkv, i))
        if i == 0:
            if neighbours:
                one.over_first()
                two = Gather(line, line.after(pieces[2]), ff // 32, 0)
            f_conv = gathered(line.after(conv_kernels), 1)
        if neighbours and i == 1:
            one.over_second()
            two.over_first()

    def weights_one():
        if not neighbours:
            return gathered(w_attn_out, 0), gathered(w_fc1, 0), gathered(w_reassemble, 0), gathered(w_head, 0)
        rh, at = ch // 16, D // 2 + ff // 2
        return line.run(lambda v: assemble(me, one, [(D, D), (D, ff), (D, ch), (ch, ch)], [
            (0, (0, r), (0, D // 2), rows_of(r), cols_of(D // 2)),
            (1, (0, r), (D // 2, ff // 2), rows_of(r), cols_of(ff // 2)),
            (2, (0, r), (at, ch // 2), rows_of(r), cols_of(ch // 2)),
            (3, (0, rh), (at + ch // 2, ch // 2), rows_of(rh), cols_of(ch // 2))]), one.pieces[0])

    def weights_two():
        if not neighbours:
            return gathered(w_fc2, 0)
        n = ff // 16
        return line.run(lambda v: assemble(me, two, [(ff, D)], [(0, (0, n), (0, D // 2), rows_of(n), cols_of(D // 2))])[0],
                        two.pieces[0])

    heads_out = [group[1] for group in groups]
    onehot = (dataset_id[:, None] == jnp.arange(DATASETS, dtype=jnp.int32)[None, :]).astype(F32)
    scale = jnp.sum(onehot[:, :, None] * scales.astype(F32)[None], 1)[:, None]
    shift = (flags[:, None] * jnp.sum(onehot[:, :, None] * shifts.astype(F32)[None], 1))[:, None]
    f_out, f_fc1, f_re, f_head = weights_one()
    if neighbours:
        two.over_second()
    x2, a2, gg, slope = line.run(lambda v: mlp_up(v, heads_out, f_out, f_fc1, gains), x)
    f_fc2 = weights_two()
    x3b, tokens_out = line.run(mlp_down, gg, f_fc2, x2, live_count)
    t1, s1, t2, s2, zb = line.run(units, x3b, f_re, f_conv)

    def packed(split):
        return split if neighbours else PLAIN

    def chunk(grads, split):
        return Chunk(line, grads[0], grads[1], split) if neighbours else grads

    def go(*jobs):
        if neighbours:
            together(line, *jobs)

    hot = jnp.pad(onehot, ((0, 0), (0, SMALL - DATASETS)))[:, :, None]
    g_conv, g_head, g_re, dx3, dm, small = line.run(
        lambda v: units_back(v, scale, g_shift_rows, hot, zb, x3b, d_tokens_out.reshape(rows, D), live_count, f_head, f_conv, f_re,
                             t1, s1, t2, s2), down)
    s_conv = lax.psum_scatter(g_conv, "wide", scatter_dimension=1, tiled=True)
    split_two = ff // 16
    grads, du = line.run(lambda v: hidden_back(v, me, gg, slope, f_fc2, packed(split_two)), dm)
    c_two = chunk(grads, split_two)
    split_one = 7 * r
    grads, (dx2, da) = line.run(
        lambda v: mlp_back(v, me, a2, f_fc1, dx3, x2, gains, g_re, g_head, small, packed(split_one)), du)
    go(c_two)
    c_one = chunk(grads, split_one)

    def attention_step(i, extra):
        qkv, o, e, rs = groups[i]
        return line.run(lambda v: attention_back(v, me, i, qkv, o, e, rs, a1, f_out, extra, packed(None)), da)

    grads, dqkv_0 = attention_step(0, heads_out)
    go(c_two, c_one)
    c_first = chunk(grads, None)
    (g_second,), dqkv_1 = attention_step(1, None)
    go(c_two, c_one, c_first)
    if neighbours:
        c_conv = Whole(s_conv)
    grads, dqkv_2 = attention_step(2, g_second)
    if neighbours:
        together(line, c_one, c_first, c_conv)
        early = Along(line, [c_two, c_one, c_first])
    c_last = chunk(grads, None)
    d_tokens = line.run(lambda v: input_back((dqkv_0, dqkv_1, v), f_qkv, dx2, x, gains), dqkv_2)
    go(c_last)
    joined = line.run(join, zb, f_head, scale, shift, lanes(live))

    if neighbours:
        together(line, c_last, early)
        late = Along(line, [c_last])
        s_conv = line.run_all(lambda p, q: p.astype(F32) + q.astype(F32), *c_conv.terms)
        rh, rows_two, half = ch // 16, ff // 16, D // 2
        blocks, n, quarter = half // LANES, ff // 2 // LANES, TABLE // 4

        def up_to(size):
            return lambda y: size * y

        def across(size):
            return lambda x, b: x * size + b * LANES

        def group_col(i):
            def col(x, b):
                at = blocks * x + b
                return at // 2 * D + WIDTH * i + at % 2 * LANES
            return col

        together(line, late)
        starts = [0, early.rows[0], early.rows[0] + early.rows[1]]
        s_fc2, s_fc1, s_re, s_head, small, s_out = line.run(lambda m: finish(m, [early], [[
            (0, rows_two, 0, blocks, up_to(rows_two), across(half)),
            (1, r, starts[1], n, up_to(r), across(ff // 2)),
            (2, r, starts[1] + r * n, 1, up_to(r), across(ch // 2)),
            (3, rh, starts[1] + r * (n + 1), 1, up_to(rh), across(ch // 2)),
            (4, quarter, starts[1] + r * (n + 1) + rh, 1, up_to(2 * quarter), lambda x, b: 0),
            (5, r, starts[2] + r * blocks, blocks, up_to(r), across(half))]],
            [w_fc2.shape, w_fc1.shape, w_reassemble.shape, w_head.shape, (TABLE, LANES), w_attn_out.shape]), me)
        (s_qkv,) = finish(me, [early, late], [
            [(0, r, starts[2], blocks, up_to(r), group_col(0))],
            [(0, r, 0, blocks, up_to(r), group_col(2)), (0, r, r * blocks, blocks, up_to(r), group_col(1))]], [w_qkv.shape])
        small = small.reshape(2, ch // LANES, SMALL, LANES).transpose(0, 2, 1, 3).reshape(2, SMALL, ch)
        small = lax.dynamic_slice(small, (0, 0, at_wide * t), (2, DATASETS, t))
        g_scale, g_shift = small[0], small[1]
    else:
        def share(part, axis):
            part = lax.psum_scatter(part.astype(BF16), "wide", scatter_dimension=axis, tiled=True)
            return lax.psum(part, "rep").astype(F32)

        s_conv = lax.psum(s_conv, "rep").astype(F32)
        small = small.reshape(2, ch // LANES, SMALL, LANES).transpose(0, 2, 1, 3).reshape(2, SMALL, ch)[:, :DATASETS]
        g_scale, g_shift = share(small[0], 1), share(small[1], 1)
        s_fc2, s_fc1, s_re, s_head = share(c_two[0], 0), share(c_one[0], 0), share(c_one[1], 0), share(c_one[2], 0)
        s_out = share(c_first[1], 0)
        by_group = (c_first[0], c_last[1], c_last[0])
        s_qkv = share(jnp.concatenate([c[:, WIDTH * p:WIDTH * (p + 1)] for p in range(3) for c in by_group], 1), 0)
    g_gains = jnp.stack([jnp.sum(w_qkv.astype(F32) * s_qkv, 1), jnp.sum(w_fc1.astype(F32) * s_fc1, 1)]) / norm_gains.astype(F32)
    return (tokens_out.reshape(tokens.shape), joined, d_tokens.reshape(tokens.shape), g_gains, s_qkv, s_out, s_fc1, s_fc2,
            s_re, s_conv, s_head, g_scale, g_shift)


def solution(mesh):
    images = P(BOTH, None, None)
    slots = P(BOTH)
    rows = P("wide", None)
    cols = P(None, "wide")
    kernels = P(None, "wide", None)
    return jax.shard_map(
        shards,
        mesh=mesh,
        in_specs=(images, slots, slots, slots, cols, rows, rows, rows, rows, rows, kernels, rows, cols, cols, images, images),
        out_specs=(images, images, images, cols, rows, rows, rows, rows, rows, kernels, rows, cols, cols),
        check_vma=False,
    )
```

time: 667 us -> 512 us (0.77)
  Pallas kernels: 184 us -> 275 us
  waiting for transfers between devices: 201 us -> 115 us
  matrix products: 73.8 us -> 0 us
  local copies, waits for them, and re-layouts: 59.6 us -> 16.7 us
  other arithmetic: 50.5 us -> 21.9 us
  starting transfers between devices: 84.3 us -> 59.1 us
  between operations: 3.24 us -> 16.3 us
    pallas_call x8 -> x18, Pallas kernels: 133 us -> 236 us  [the longest x3 56.7 us: attention_back(): pl.pallas_call(body, grid=(images,), in_specs=[cols(D), pl.BlockSpec(memo...]
    ppermute x72 -> x65, waiting for transfers between devices: 201 us -> 115 us  [swap(): return lax.ppermute(value, BOTH, [(i, i ^ flip) for i in range(32)])]
    dot_general x15 -> x0, matrix products: 73.8 us -> none  [the longest x5 32.9 us: mm(): return jnp.dot(left, right, preferred_element_type=F32)]
    ppermute x72 -> x65, starting transfers between devices: 84.3 us -> 58.5 us  [swap(): return lax.ppermute(value, BOTH, [(i, i ^ flip) for i in range(32)])]
    convert_element_type x27 -> x4, other arithmetic: 24.9 us -> 3.72 us  [the longest x1 1.48 us: shards(): a1 = line.run(lambda n: (n * gains[0:1]).astype(BF16), n1)]
    unnamed x144 -> x102, local copies, waits for them, and re-layouts: 24.6 us -> 5 us
    concatenate x9 -> x7, local copies, waits for them, and re-layouts: 9.77 us -> 0.27 us  [the longest x6 0.23 us: call(): return [jnp.concatenate([one, one_x]), jnp.concatenate([two, two_y])]]
    pallas_call x1, Pallas kernels: 26.9 us -> 18.5 us  [units(): pl.pallas_call(units_body, grid=(rows // COUNT,), in_specs=[pl.BlockSpec(...]
  transfers between devices with their start and end apart: 72 -> 67, of which waited for: 32 -> 16; matrix products, arithmetic and copies ran while one was open for 19% -> 5% of each run, Pallas kernels for 8% -> 38%
where the time goes in v3:
time: 512 us; the launch traced here: 505 us
  Pallas kernels  275 us (54%)
  waiting for transfers between devices  115 us (22%)
  starting transfers between devices  59.1 us (12%)
  other arithmetic  21.9 us (4%)
  local copies, waits for them, and re-layouts  16.7 us (3%)
  between operations  16.3 us (3%)
    ppermute x65, waiting for transfers between devices, swap(): return lax.ppermute(value, BOTH, [(i, i ^ flip) for i in range(32)])  115 us
    ppermute x65, starting transfers between devices, swap(): return lax.ppermute(value, BOTH, [(i, i ^ flip) for i in range(32)])  58.5 us
    pallas_call x3, Pallas kernels, attention_back(): pl.pallas_call(body, grid=(images,), in_specs=[cols(D), pl.BlockSpec(memo...  56.7 us
    pallas_call x3, Pallas kernels, attention(): pl.pallas_call(attention_body, grid=(images,), in_specs=[cols(D)] + group...  33.5 us
    pallas_call x1, Pallas kernels, units_back(): pl.pallas_call(units_back_body, grid=(1,), in_specs=[pl.BlockSpec(memory_...  31.2 us
    pallas_call x1, Pallas kernels, mlp_back(): pl.pallas_call(body, grid=(ff // block,), in_specs=[pl.BlockSpec((rows, b...  26.8 us
    pallas_call x3, Pallas kernels, assemble(): pl.pallas_call(body, grid=(1,), in_specs=[pl.BlockSpec(memory_space=pltpu...  20.6 us
    pallas_call x1, Pallas kernels, hidden_back(): pl.pallas_call(body, grid=(ff // block,), in_specs=[whole((rows, D)), pl....  20.2 us
  transfers between devices with their start and end apart: 67, of which 16 were waited for; matrix products, arithmetic and copies ran while one was open for 5% of the time, Pallas kernels for 38%

profile of v3, /device:TPU:0, one launch (start us, length us, event | category | flops | bytes accessed | tf_op | source)
XLA Modules:
  0.0 504.6 jit_solution(17861704411941168319)
XLA Ops:
  7.9 2.3 prepare.1
  10.2 5.0 %collective-permute-start.2 = (bf16[64,1152]{1,0:T(8,128)(2,1)}, bf16[64,1152]{1,0:T(8,128)(2,1)S(1)}, u32[]{:S(2)}, u32[]{:S(2)}) collective-permute-start(bf16[64,1152]{1,0:T(8,128)(2,1)} %get-tuple-element.175), channel_id=1, source_target_pairs={{0,6},{1,7},{2,4},{3,5},{4,2},{5,3},{6,0},{7,1},{8,14},{9,15},{10,... | collective-permute-start | bytes 442376 | tf_op jit(solution)/shard_map/ppermute | solution.py:64
  15.9 4.6 norm.1
  21.2 6.8 %collective-permute-done.1 = bf16[64,1152]{1,0:T(8,128)(2,1)S(1)} collective-permute-done((bf16[64,1152]{1,0:T(8,128)(2,1)}, bf16[64,1152]{1,0:T(8,128)(2,1)S(1)}, u32[]{:S(2)}, u32[]{:S(2)}) %collective-permute-start.1) | collective-permute-done | bytes 147488 | tf_op jit(solution)/shard_map/ppermute | solution.py:64
  28.1 1.6 collective-permute-start.4
  29.7 1.5 collective-permute-start.3
  32.5 8.6 %bring_down.1 = (f32[2,576,256]{2,1,0:T(8,128)}, f32[2,1,256]{2,1,0:T(1,128)}) custom-call(bf16[2,2304,256]{2,1,0:T(8,128)(2,1)} %dj_ref, f32[2,1,256]{2,1,0:T(1,128)} %broadcast_in_dim.8.live_ref, f32[2,1,256]{2,1,0:T(1,128)} %broadcast_in_dim.9.flag_ref), custom_call_target="tpu_custom_call" | custom-call | flops 10234999808 | tf_op jit(solution)/shard_map/bring_down/pallas_call | solution.py:459
  42.4 14.1 %collective-permute-done.5.refs_1_ = bf16[8,64,640]{2,1,0:T(8,128)(2,1)S(1)} collective-permute-done((bf16[8,64,640]{2,1,0:T(8,128)(2,1)S(1)}, bf16[8,64,640]{2,1,0:T(8,128)(2,1)S(1)}, u32[]{:S(2)}, u32[]{:S(2)}) %collective-permute-start.5) | collective-permute-done | bytes 655392 | tf_op jit(solution)/shard_map/ppermute | solution.py:64
  57.1 2.1 collective-permute-done.9.refs_6_
  61.0 6.0 %assemble.3 = (bf16[768,2304]{1,0:T(8,128)(2,1)}, bf16[8,16,384]{2,1,0:T(8,128)(2,1)}) custom-call(s32[5]{0:T(128)} %stack.77.me_ref, bf16[8,64,640]{2,1,0:T(8,128)(2,1)} %copy-done.17, bf16[8,64,640]{2,1,0:T(8,128)(2,1)} %copy-done.29, bf16[8,64,640]{2,1,0:T(8,128)(2,1)} %copy-done.30, bf16[8,64,640]{2,1,0:T(8,128)(2,1)} %collective-permute-done.7.refs_3_, ...), custom_call_target="tpu_custom_call" | custom-call | flops 5750000128 | tf_op jit(solution)/shard_map/assemble/pallas_call | solution.py:164
  67.8 1.5 multiply_convert_fusion.a1_ref
  69.3 2.3 collective-permute-start.13
  71.6 2.1 collective-permute-start.11
  73.7 11.1 %attention.3 = (bf16[1152,768]{1,0:T(8,128)(2,1)}, bf16[1152,256]{1,0:T(8,128)(2,1)}, bf16[8,576,576]{2,1,0:T(8,128)(2,1)}, f32[2,4,576]{2,1,0:T(4,128)}) custom-call(bf16[1152,768]{1,0:T(8,128)(2,1)} %multiply_convert_fusion.a1_ref, bf16[768,2304]{1,0:T(8,128)(2,1)} %get-tuple-element.189.wq_ref.wk_ref.wv_ref.refs_3_, ...), custom_call_target="tpu_custom_call" | custom-call | flops 12650000384 | tf_op jit(solution)/shard_map/attention/pallas_call | solution.py:500
  84.8 4.2 collective-permute-done.12
  90.9 11.2 %attention.4 = (bf16[1152,768]{1,0:T(8,128)(2,1)}, bf16[1152,256]{1,0:T(8,128)(2,1)}, bf16[8,576,576]{2,1,0:T(8,128)(2,1)}, f32[2,4,576]{2,1,0:T(4,128)}) custom-call(bf16[1152,768]{1,0:T(8,128)(2,1)} %multiply_convert_fusion.a1_ref, bf16[768,2304]{1,0:T(8,128)(2,1)} %get-tuple-element.189.wq_ref.wk_ref.wv_ref.refs_3_, ...), custom_call_target="tpu_custom_call" | custom-call | flops 12650000384 | tf_op jit(solution)/shard_map/attention/pallas_call | solution.py:500
  102.2 1.6 collective-permute-start.21
  103.9 1.6 collective-permute-start.24
  105.5 1.6 collective-permute-start.16
  107.0 15.7 %collective-permute-done.21.refs_1_ = bf16[8,48,1152]{2,1,0:T(8,128)(2,1)} collective-permute-done((bf16[8,48,1152]{2,1,0:T(8,128)(2,1)S(1)}, bf16[8,48,1152]{2,1,0:T(8,128)(2,1)}, u32[]{:S(2)}, u32[]{:S(2)}) %collective-permute-start.21) | collective-permute-done | bytes 884768 | tf_op jit(solution)/shard_map/ppermute | solution.py:64
  124.2 13.0 %collective-permute-done.15 = bf16[192,384]{1,0:T(8,128)(2,1)S(1)} collective-permute-done((bf16[192,384]{1,0:T(8,128)(2,1)S(1)}, bf16[192,384]{1,0:T(8,128)(2,1)S(1)}, u32[]{:S(2)}, u32[]{:S(2)}) %collective-permute-start.15) | collective-permute-done | bytes 147488 | tf_op jit(solution)/shard_map/ppermute | solution.py:64
  140.1 8.0 %collective-permute-done.14 = bf16[192,384]{1,0:T(8,128)(2,1)S(1)} collective-permute-done((bf16[192,384]{1,0:T(8,128)(2,1)S(1)}, bf16[192,384]{1,0:T(8,128)(2,1)S(1)}, u32[]{:S(2)}, u32[]{:S(2)}) %collective-permute-start.14) | collective-permute-done | bytes 147488 | tf_op jit(solution)/shard_map/ppermute | solution.py:64
  148.4 2.7 collective-permute-start.19
  152.0 8.7 %assemble.4 = (bf16[768,768]{1,0:T(8,128)(2,1)}, bf16[768,3072]{1,0:T(8,128)(2,1)}, bf16[768,256]{1,0:T(8,128)(2,1)}, bf16[256,256]{1,0:T(8,128)(2,1)}) custom-call(s32[5]{0:T(128)} %stack.77.me_ref, bf16[8,48,1152]{2,1,0:T(8,128)(2,1)} %copy-done.13, bf16[8,48,1152]{2,1,0:T(8,128)(2,1)} %collective-permute-done.21.refs_1_, bf16[8,48,1152]{2,1,0:T(8,128)(2,1)} %copy-done.28, ...), custom_call_target="tpu_custom_call" | custom-call | flops 5750000128 | tf_op jit(solution)/shard_map/assemble/pallas_call | solution.py:164
  161.1 1.4 collective-permute-start.27
  162.5 11.2 %attention.5 = (bf16[1152,768]{1,0:T(8,128)(2,1)}, bf16[1152,256]{1,0:T(8,128)(2,1)}, bf16[8,576,576]{2,1,0:T(8,128)(2,1)}, f32[2,4,576]{2,1,0:T(4,128)}) custom-call(bf16[1152,768]{1,0:T(8,128)(2,1)} %multiply_convert_fusion.a1_ref, bf16[768,2304]{1,0:T(8,128)(2,1)} %get-tuple-element.189.wq_ref.wk_ref.wv_ref.refs_3_, ...), custom_call_target="tpu_custom_call" | custom-call | flops 12650000384 | tf_op jit(solution)/shard_map/attention/pallas_call | solution.py:500
  174.8 18.0 %mlp_up.1 = (f32[1152,768]{1,0:T(8,128)}, bf16[1152,768]{1,0:T(8,128)(2,1)}, bf16[1152,3072]{1,0:T(8,128)(2,1)}, bf16[1152,3072]{1,0:T(8,128)(2,1)}) custom-call(bf16[1152,768]{1,0:T(8,128)(2,1)} %bitcast.74, bf16[1152,256]{1,0:T(8,128)(2,1)} %get-tuple-element.212.o0_ref.o_ref.refs_0_, bf16[1152,256]{1,0:T(8,128)(2,1)} %get-tuple-element.213.o1_ref.refs_1_.o_ref, ...), custom_call_target="tpu_custom_call" | custom-call | flops 20700000256 | tf_op jit(solution)/shard_map/mlp_up/pallas_call | solution.py:630
  194.1 5.9 %assemble.5.w2_ref = bf16[3072,768]{1,0:T(8,128)(2,1)} custom-call(s32[5]{0:T(128)} %stack.77.me_ref, bf16[8,96,384]{2,1,0:T(8,128)(2,1)} %copy-done.20, bf16[8,96,384]{2,1,0:T(8,128)(2,1)} %copy-done.32, bf16[8,96,384]{2,1,0:T(8,128)(2,1)} %copy-done.34, bf16[8,96,384]{2,1,0:T(8,128)(2,1)} %collective-permute-done.29.refs_3_, ...), custom_call_target="tpu_custom_call" | custom-call | flops 5750000128 | tf_op jit(solution)/shard_map/assemble/pallas_call | solution.py:164
  200.0 11.4 %mlp_down.1 = (bf16[1152,768]{1,0:T(8,128)(2,1)}, bf16[1152,768]{1,0:T(8,128)(2,1)}) custom-call(bf16[1152,3072]{1,0:T(8,128)(2,1)} %get-tuple-element.219.gg_ref, bf16[3072,768]{1,0:T(8,128)(2,1)} %assemble.5.w2_ref, f32[1152,768]{1,0:T(8,128)} %get-tuple-element.220.x2_ref, s32[1]{0:T(128)} %copy.54.count_ref), custom_call_target="tpu_custom_call" | custom-call | flops 12650000384 | tf_op jit(solution)/shard_map/mlp_down/pallas_call | solution.py:653
  211.4 18.5 %units.1 = (bf16[2,1152,256]{2,1,0:T(8,128)(2,1)}, bf16[2,1152,256]{2,1,0:T(8,128)(2,1)}, bf16[2,1152,256]{2,1,0:T(8,128)(2,1)}, bf16[2,1152,256]{2,1,0:T(8,128)(2,1)}, bf16[1152,256]{1,0:T(8,128)(2,1)}) custom-call(bf16[1152,768]{1,0:T(8,128)(2,1)} %get-tuple-element.222.x_ref.x3b_ref, bf16[768,256]{1,0:T(8,128)(2,1)} %get-tuple-element.223.wre_ref, ...), custom_call_target="tpu_custom_call" | custom-call | flops 20700000256 | tf_op jit(solution)/shard_map/units/pallas_call | solution.py:704
  229.9 31.2 %units_back.1 = (bf16[4,2304,256]{2,1,0:T(8,128)(2,1)}, bf16[256,256]{1,0:T(8,128)(2,1)}, bf16[768,256]{1,0:T(8,128)(2,1)}, f32[1152,768]{1,0:T(8,128)}, bf16[1152,768]{1,0:T(8,128)(2,1)}, /*index=5*/f32[64,128]{1,0:T(8,128)}) custom-call(f32[2,576,256]{2,1,0:T(8,128)} %get-tuple-element.227.down_ref, f32[2,1,256]{2,1,0:T(1,128)} %broadcast_in_dim.10.scale_ref, ...), custom_call_target="tpu_custom_call" | custom-call | flops 34500001792 | tf_op jit(solution)/shard_map/units_back/pallas_call | solution.py:762
  261.1 20.2 %hidden_back.1 = (bf16[16,576,128]{2,1,0:T(8,128)(2,1)}, bf16[16,576,128]{2,1,0:T(8,128)(2,1)}, bf16[1152,3072]{1,0:T(8,128)(2,1)}) custom-call(bf16[1152,768]{1,0:T(8,128)(2,1)} %get-tuple-element.234.dm_ref, s32[5]{0:T(128)} %stack.77.me_ref, bf16[1152,3072]{1,0:T(8,128)(2,1)} %get-tuple-element.219.gg_ref, ...), custom_call_target="tpu_custom_call" | custom-call | flops 23000000512 | tf_op jit(solution)/shard_map/hidden_back/pallas_call | solution.py:792
  281.4 26.8 %mlp_back.1 = (bf16[16,656,128]{2,1,0:T(8,128)(2,1)}, bf16[16,656,128]{2,1,0:T(8,128)(2,1)}, f32[1152,768]{1,0:T(8,128)}, bf16[1152,768]{1,0:T(8,128)(2,1)}) custom-call(bf16[1152,3072]{1,0:T(8,128)(2,1)} %get-tuple-element.237.du_ref, s32[5]{0:T(128)} %stack.77.me_ref, bf16[1152,768]{1,0:T(8,128)(2,1)} %get-tuple-element.238.a2_ref, ...), custom_call_target="tpu_custom_call" | custom-call | flops 31050000384 | tf_op jit(solution)/shard_map/mlp_back/pallas_call | solution.py:848
  308.2 2.3 add.101
  312.8 1.3 collective-permute-start.34
  314.1 1.4 collective-permute-start.35
  315.4 21.0 %attention_back.3 = (bf16[16,288,128]{2,1,0:T(8,128)(2,1)}, bf16[16,288,128]{2,1,0:T(8,128)(2,1)}, bf16[1152,768]{1,0:T(8,128)(2,1)}) custom-call(bf16[1152,768]{1,0:T(8,128)(2,1)} %get-tuple-element.278.da_ref, s32[5]{0:T(128)} %stack.77.me_ref, bf16[1152,768]{1,0:T(8,128)(2,1)} %get-tuple-element.252.qkv_ref, ...), custom_call_target="tpu_custom_call" | custom-call | flops 20700000256 | tf_op jit(solution)/shard_map/attention_back/pallas_call | solution.py:565
  338.9 1.5 add.103
  344.6 1.9 collective-permute-start.39
  346.5 17.0 %attention_back.4 = (bf16[768,768]{1,0:T(8,128)(2,1)}, bf16[1152,768]{1,0:T(8,128)(2,1)}) custom-call(bf16[1152,768]{1,0:T(8,128)(2,1)} %get-tuple-element.278.da_ref, s32[5]{0:T(128)} %stack.77.me_ref, bf16[1152,768]{1,0:T(8,128)(2,1)} %get-tuple-element.265.qkv_ref, bf16[1152,256]{1,0:T(8,128)(2,1)} %get-tuple-element.213.o1_ref.refs_1_.o_ref, ...), custom_call_target="tpu_custom_call" | custom-call | flops 20700000256 | tf_op jit(solution)/shard_map/attention_back/pallas_call | solution.py:565
  363.6 3.1 collective-permute-done.39
  366.7 1.3 add.108
  368.4 1.6 add.109
  370.9 2.2 collective-permute-start.46
  376.0 9.7 %collective-permute-done.46 = bf16[4,288,128]{2,1,0:T(8,128)(2,1)} collective-permute-done((bf16[4,288,128]{2,1,0:T(8,128)(2,1)S(1)}, bf16[4,288,128]{2,1,0:T(8,128)(2,1)}, u32[]{:S(2)}, u32[]{:S(2)}) %collective-permute-start.46) | collective-permute-done | bytes 294944 | tf_op jit(solution)/shard_map/ppermute | solution.py:64
  386.7 18.7 %attention_back.5 = (bf16[16,288,128]{2,1,0:T(8,128)(2,1)}, bf16[16,288,128]{2,1,0:T(8,128)(2,1)}, bf16[1152,768]{1,0:T(8,128)(2,1)}) custom-call(bf16[1152,768]{1,0:T(8,128)(2,1)} %get-tuple-element.278.da_ref, s32[5]{0:T(128)} %stack.77.me_ref, bf16[1152,768]{1,0:T(8,128)(2,1)} %get-tuple-element.279.qkv_ref, ...), custom_call_target="tpu_custom_call" | custom-call | flops 20700000256 | tf_op jit(solution)/shard_map/attention_back/pallas_call | solution.py:565
  407.0 1.3 add_convert_fusion.2
  410.0 4.9 collective-permute-start.54
  415.5 10.6 %input_back.1 = bf16[1152,768]{1,0:T(8,128)(2,1)} custom-call(bf16[1152,768]{1,0:T(8,128)(2,1)} %get-tuple-element.254.refs_0_, bf16[1152,768]{1,0:T(8,128)(2,1)} %get-tuple-element.267.refs_1_, bf16[1152,768]{1,0:T(8,128)(2,1)} %get-tuple-element.301.refs_2_, bf16[768,2304]{1,0:T(8,128)(2,1)} %get-tuple-element.189.wq_ref.wk_ref.wv_ref.refs_3_, ...), custom_call_target="tpu_custom_call" | custom-call | flops 10350000128 | tf_op jit(solution)/shard_map/input_back/pallas_call | solution.py:597
  427.7 1.4 collective-permute-start.50
  430.0 6.6 %join.1 = bf16[2,2304,256]{2,1,0:T(8,128)(2,1)} custom-call(bf16[1152,256]{1,0:T(8,128)(2,1)} %get-tuple-element.305.z_ref, bf16[256,256]{1,0:T(8,128)(2,1)} %get-tuple-element.206.whead_ref.w_ref, f32[2,1,256]{2,1,0:T(1,128)} %broadcast_in_dim.10.scale_ref, f32[2,1,256]{2,1,0:T(1,128)} %reshape_multiply_fusion.shift_ref, f32[2,1,256]{2,1,0:T(1,128)} %broadcast_in_dim.8.live_ref), custom_call_target="tpu_custom_call" | custom-call | flops 8049999872 | tf_op jit(solution)/shard_map/join/pallas_call | solution.py:881
  436.7 10.8 %collective-permute-done.53 = bf16[1,1520,128]{2,1,0:T(8,128)(2,1)} collective-permute-done((bf16[1,1520,128]{2,1,0:T(8,128)(2,1)S(1)}, bf16[1,1520,128]{2,1,0:T(8,128)(2,1)}, u32[]{:S(2)}, u32[]{:S(2)}) %collective-permute-start.53) | collective-permute-done | bytes 389152 | tf_op jit(solution)/shard_map/ppermute | solution.py:64
  447.8 1.4 fusion.refs_0_
  449.5 2.7 collective-permute-start.60
  452.2 2.1 collective-permute-start.57
  455.4 8.3 %collective-permute-done.61 = bf16[4,288,256]{2,1,0:T(8,128)(2,1)S(1)} collective-permute-done((bf16[4,288,256]{2,1,0:T(8,128)(2,1)S(1)}, bf16[4,288,256]{2,1,0:T(8,128)(2,1)S(1)}, u32[]{:S(2)}, u32[]{:S(2)}) %collective-permute-start.61) | collective-permute-done | bytes 589856 | tf_op jit(solution)/shard_map/ppermute | solution.py:64
  465.7 2.3 collective-permute-done.58
  468.1 1.2 collective-permute-start.64
  470.0 11.4 %collective-permute-done.64.refs_7_ = bf16[288,128]{1,0:T(8,128)(2,1)S(1)} collective-permute-done((bf16[288,128]{1,0:T(8,128)(2,1)S(1)}, bf16[288,128]{1,0:T(8,128)(2,1)S(1)}, u32[]{:S(2)}, u32[]{:S(2)}) %collective-permute-start.64) | collective-permute-done | bytes 73760 | tf_op jit(solution)/shard_map/ppermute | solution.py:64
  482.1 3.6 collective-permute-done.62.refs_5_
  487.4 2.5 finish.2
  489.9 1.4 multiply_reduce_fusion.1
  491.3 3.1 finish.3
  494.4 1.5 multiply_reduce_fusion
  (271 shorter events, 45.8 us)
Async XLA Ops:
  7.2 204.2 %all-gather.2.cloned.1.call-start = ((), (), s32[]{:S(2)}) async-start(), calls=%async_computation.1 | async-start | bytes 5308416 | tf_op jit(solution)/shard_map/all_gather | solution.py:908
  10.2 10.9 %collective-permute-start.2 = (bf16[64,1152]{1,0:T(8,128)(2,1)}, bf16[64,1152]{1,0:T(8,128)(2,1)S(1)}, u32[]{:S(2)}, u32[]{:S(2)}) collective-permute-start(bf16[64,1152]{1,0:T(8,128)(2,1)} %get-tuple-element.175), channel_id=1, source_target_pairs={{0,6},{1,7},{2,4},{3,5},{4,2},{5,3},{6,0},{7,1},{8,14},{9,15},{10,... | collective-permute-start | bytes 442376 | tf_op jit(solution)/shard_map/ppermute | solution.py:64
  15.3 12.7 %collective-permute-start.1 = (bf16[64,1152]{1,0:T(8,128)(2,1)}, bf16[64,1152]{1,0:T(8,128)(2,1)S(1)}, u32[]{:S(2)}, u32[]{:S(2)}) collective-permute-start(bf16[64,1152]{1,0:T(8,128)(2,1)} %get-tuple-element.175), channel_id=1, source_target_pairs={{0,4},{1,5},{2,6},{3,7},{4,0},{5,1},{6,2},{7,3},{8,12},{9,13},{10,... | collective-permute-start | bytes 442376 | tf_op jit(solution)/shard_map/ppermute | solution.py:64
  15.3 12.7 %collective-permute-start = (bf16[64,1152]{1,0:T(8,128)(2,1)}, bf16[64,1152]{1,0:T(8,128)(2,1)S(1)}, u32[]{:S(2)}, u32[]{:S(2)}) collective-permute-start(bf16[64,1152]{1,0:T(8,128)(2,1)} %get-tuple-element.175), channel_id=1, source_target_pairs={{0,2},{1,3},{2,0},{3,1},{4,6},{5,7},{6,4},{7,5},{8,10},{9,11},{10,... | collective-permute-start | bytes 442376 | tf_op jit(solution)/shard_map/ppermute | solution.py:64
  28.1 13.0 %collective-permute-start.4 = (bf16[4,64,512]{2,1,0:T(8,128)(2,1)S(1)}, bf16[4,64,512]{2,1,0:T(8,128)(2,1)S(1)}, u32[]{:S(2)}, u32[]{:S(2)}) collective-permute-start(bf16[4,64,512]{2,1,0:T(8,128)(2,1)S(1)} %pad_maximum_fusion.6), channel_id=1, source_target_pairs={{0,16},{1,17},{2,18},{3,19},{4,20},{5,21},{6,22},{7,23},{8,24},{9,... | collective-permute-start | bytes 786440 | tf_op jit(solution)/shard_map/ppermute | solution.py:64
  29.7 11.4 %collective-permute-start.3 = (bf16[4,64,640]{2,1,0:T(8,128)(2,1)S(1)}, bf16[4,64,640]{2,1,0:T(8,128)(2,1)S(1)}, u32[]{:S(2)}, u32[]{:S(2)}) collective-permute-start(bf16[4,64,640]{2,1,0:T(8,128)(2,1)S(1)} %slice.177), channel_id=1, source_target_pairs={{0,8},{1,9},{2,10},{3,11},{4,12},{5,13},{6,14},{7,15},{8,0},{9,1},... | collective-permute-start | bytes 983048 | tf_op jit(solution)/shard_map/ppermute | solution.py:64
  41.2 15.3 %collective-permute-start.5 = (bf16[8,64,640]{2,1,0:T(8,128)(2,1)S(1)}, bf16[8,64,640]{2,1,0:T(8,128)(2,1)S(1)}, u32[]{:S(2)}, u32[]{:S(2)}) collective-permute-start(bf16[8,64,640]{2,1,0:T(8,128)(2,1)S(1)} %constant_dynamic-update-slice_fusion.refs_0_), channel_id=1, source_target_pairs={{0,16},{1,17},{2,18},{3,19},{4,20},{5,21},{6,22},{7,23},{8,24},{9,... | collective-permute-start | bytes 1966088 | tf_op jit(solution)/shard_map/ppermute | solution.py:64
  41.8 15.2 %collective-permute-start.8 = (bf16[8,64,512]{2,1,0:T(8,128)(2,1)S(1)}, bf16[8,64,512]{2,1,0:T(8,128)(2,1)S(1)}, u32[]{:S(2)}, u32[]{:S(2)}) collective-permute-start(bf16[8,64,512]{2,1,0:T(8,128)(2,1)S(1)} %constant_dynamic-update-slice_fusion.2.refs_4_), channel_id=1, source_target_pairs={{0,8},{1,9},{2,10},{3,11},{4,12},{5,13},{6,14},{7,15},{8,0},{9,1},... | collective-permute-start | bytes 1572872 | tf_op jit(solution)/shard_map/ppermute | solution.py:64
  42.4 16.8 %collective-permute-start.6 = (bf16[8,64,640]{2,1,0:T(8,128)(2,1)S(1)}, bf16[8,64,640]{2,1,0:T(8,128)(2,1)S(1)}, u32[]{:S(2)}, u32[]{:S(2)}) collective-permute-start(bf16[8,64,640]{2,1,0:T(8,128)(2,1)S(1)} %constant_dynamic-update-slice_fusion.refs_0_), channel_id=1, source_target_pairs={{0,1},{1,0},{2,3},{3,2},{4,5},{5,4},{6,7},{7,6},{8,9},{9,8},{10,11... | collective-permute-start | bytes 1966088 | tf_op jit(solution)/shard_map/ppermute | solution.py:64
  56.5 4.5 collective-permute-start.7
  69.3 15.5 %collective-permute-start.13 = (bf16[48,2176]{1,0:T(8,128)(2,1)S(1)}, bf16[48,2176]{1,0:T(8,128)(2,1)S(1)}, u32[]{:S(2)}, u32[]{:S(2)}) collective-permute-start(bf16[48,2176]{1,0:T(8,128)(2,1)S(1)} %copy-done.5), channel_id=1, source_target_pairs={{0,6},{1,7},{2,4},{3,5},{4,2},{5,3},{6,0},{7,1},{8,14},{9,15},{10,... | collective-permute-start | bytes 626696 | tf_op jit(solution)/shard_map/ppermute | solution.py:64
  71.6 17.4 %collective-permute-start.12 = (bf16[48,2176]{1,0:T(8,128)(2,1)S(1)}, bf16[48,2176]{1,0:T(8,128)(2,1)S(1)}, u32[]{:S(2)}, u32[]{:S(2)}) collective-permute-start(bf16[48,2176]{1,0:T(8,128)(2,1)S(1)} %copy-done.5), channel_id=1, source_target_pairs={{0,4},{1,5},{2,6},{3,7},{4,0},{5,1},{6,2},{7,3},{8,12},{9,13},{10,... | collective-permute-start | bytes 626696 | tf_op jit(solution)/shard_map/ppermute | solution.py:64
  71.6 17.4 %collective-permute-start.11 = (bf16[48,2176]{1,0:T(8,128)(2,1)S(1)}, bf16[48,2176]{1,0:T(8,128)(2,1)S(1)}, u32[]{:S(2)}, u32[]{:S(2)}) collective-permute-start(bf16[48,2176]{1,0:T(8,128)(2,1)S(1)} %copy-done.5), channel_id=1, source_target_pairs={{0,2},{1,3},{2,0},{3,1},{4,6},{5,7},{6,4},{7,5},{8,10},{9,11},{10,... | collective-permute-start | bytes 626696 | tf_op jit(solution)/shard_map/ppermute | solution.py:64
  89.2 12.9 %collective-permute-start.18 = (bf16[4,48,1024]{2,1,0:T(8,128)(2,1)S(1)}, bf16[4,48,1024]{2,1,0:T(8,128)(2,1)S(1)}, u32[]{:S(2)}, u32[]{:S(2)}) collective-permute-start(bf16[4,48,1024]{2,1,0:T(8,128)(2,1)S(1)} %pad_maximum_fusion.5), channel_id=1, source_target_pairs={{0,16},{1,17},{2,18},{3,19},{4,20},{5,21},{6,22},{7,23},{8,24},{9,... | collective-permute-start | bytes 1179656 | tf_op jit(solution)/shard_map/ppermute | solution.py:64
  89.8 12.3 %collective-permute-start.17 = (bf16[4,48,1152]{2,1,0:T(8,128)(2,1)S(1)}, bf16[4,48,1152]{2,1,0:T(8,128)(2,1)S(1)}, u32[]{:S(2)}, u32[]{:S(2)}) collective-permute-start(bf16[4,48,1152]{2,1,0:T(8,128)(2,1)S(1)} %slice.179), channel_id=1, source_target_pairs={{0,8},{1,9},{2,10},{3,11},{4,12},{5,13},{6,14},{7,15},{8,0},{9,1},... | collective-permute-start | bytes 1327112 | tf_op jit(solution)/shard_map/ppermute | solution.py:64
  90.4 295.4 %reduce-scatter.2.cloned.1.call-start = ((), (), s32[]{:S(2)}) async-start(), calls=%async_computation.2 | async-start | bytes 5308416 | tf_op jit(solution)/shard_map/reduce_scatter | solution.py:1003
  102.2 20.5 %collective-permute-start.21 = (bf16[8,48,1152]{2,1,0:T(8,128)(2,1)S(1)}, bf16[8,48,1152]{2,1,0:T(8,128)(2,1)}, u32[]{:S(2)}, u32[]{:S(2)}) collective-permute-start(bf16[8,48,1152]{2,1,0:T(8,128)(2,1)S(1)} %constant_dynamic-update-slice_fusion.4.refs_0_), channel_id=1, source_target_pairs={{0,16},{1,17},{2,18},{3,19},{4,20},{5,21},{6,22},{7,23},{8,24},{9,... | collective-permute-start | bytes 2654216 | tf_op jit(solution)/shard_map/ppermute | solution.py:64
  103.9 19.5 %collective-permute-start.24 = (bf16[8,48,1024]{2,1,0:T(8,128)(2,1)S(1)}, bf16[8,48,1024]{2,1,0:T(8,128)(2,1)}, u32[]{:S(2)}, u32[]{:S(2)}) collective-permute-start(bf16[8,48,1024]{2,1,0:T(8,128)(2,1)S(1)} %constant_dynamic-update-slice_fusion.6.refs_4_), channel_id=1, source_target_pairs={{0,8},{1,9},{2,10},{3,11},{4,12},{5,13},{6,14},{7,15},{8,0},{9,1},... | collective-permute-start | bytes 2359304 | tf_op jit(solution)/shard_map/ppermute | solution.py:64
  105.5 17.4 %collective-permute-start.16 = (bf16[192,384]{1,0:T(8,128)(2,1)S(1)}, bf16[192,384]{1,0:T(8,128)(2,1)S(1)}, u32[]{:S(2)}, u32[]{:S(2)}) collective-permute-start(bf16[192,384]{1,0:T(8,128)(2,1)S(1)} %copy-done.18), channel_id=1, source_target_pairs={{0,6},{1,7},{2,4},{3,5},{4,2},{5,3},{6,0},{7,1},{8,14},{9,15},{10,... | collective-permute-start | bytes 442376 | tf_op jit(solution)/shard_map/ppermute | solution.py:64
  107.0 30.1 %collective-permute-start.15 = (bf16[192,384]{1,0:T(8,128)(2,1)S(1)}, bf16[192,384]{1,0:T(8,128)(2,1)S(1)}, u32[]{:S(2)}, u32[]{:S(2)}) collective-permute-start(bf16[192,384]{1,0:T(8,128)(2,1)S(1)} %copy-done.18), channel_id=1, source_target_pairs={{0,4},{1,5},{2,6},{3,7},{4,0},{5,1},{6,2},{7,3},{8,12},{9,13},{10,... | collective-permute-start | bytes 442376 | tf_op jit(solution)/shard_map/ppermute | solution.py:64
  107.0 44.0 %collective-permute-start.22 = (bf16[8,48,1152]{2,1,0:T(8,128)(2,1)S(1)}, bf16[8,48,1152]{2,1,0:T(8,128)(2,1)S(1)}, u32[]{:S(2)}, u32[]{:S(2)}) collective-permute-start(bf16[8,48,1152]{2,1,0:T(8,128)(2,1)S(1)} %constant_dynamic-update-slice_fusion.4.refs_0_), channel_id=1, source_target_pairs={{0,1},{1,0},{2,3},{3,2},{4,5},{5,4},{6,7},{7,6},{8,9},{9,8},{10,11... | collective-permute-start | bytes 2654216 | tf_op jit(solution)/shard_map/ppermute | solution.py:64
  122.7 28.4 %collective-permute-start.23 = (bf16[8,48,1152]{2,1,0:T(8,128)(2,1)}, bf16[8,48,1152]{2,1,0:T(8,128)(2,1)}, u32[]{:S(2)}, u32[]{:S(2)}) collective-permute-start(bf16[8,48,1152]{2,1,0:T(8,128)(2,1)} %collective-permute-done.21.refs_1_), channel_id=1, source_target_pairs={{0,1},{1,0},{2,3},{3,2},{4,5},{5,4},{6,7},{7,6},{8,9},{9,8},{10,11... | collective-permute-start | bytes 2654216 | tf_op jit(solution)/shard_map/ppermute | solution.py:64
  122.9 25.5 %collective-permute-start.25 = (bf16[8,48,1024]{2,1,0:T(8,128)(2,1)S(1)}, bf16[8,48,1024]{2,1,0:T(8,128)(2,1)}, u32[]{:S(2)}, u32[]{:S(2)}) collective-permute-start(bf16[8,48,1024]{2,1,0:T(8,128)(2,1)S(1)} %constant_dynamic-update-slice_fusion.6.refs_4_), channel_id=1, source_target_pairs={{0,1},{1,0},{2,3},{3,2},{4,5},{5,4},{6,7},{7,6},{8,9},{9,8},{10,11... | collective-permute-start | bytes 2359304 | tf_op jit(solution)/shard_map/ppermute | solution.py:64
  123.4 27.7 %collective-permute-start.26 = (bf16[8,48,1024]{2,1,0:T(8,128)(2,1)}, bf16[8,48,1024]{2,1,0:T(8,128)(2,1)}, u32[]{:S(2)}, u32[]{:S(2)}) collective-permute-start(bf16[8,48,1024]{2,1,0:T(8,128)(2,1)} %collective-permute-done.24.refs_5_), channel_id=1, source_target_pairs={{0,1},{1,0},{2,3},{3,2},{4,5},{5,4},{6,7},{7,6},{8,9},{9,8},{10,11... | collective-permute-start | bytes 2359304 | tf_op jit(solution)/shard_map/ppermute | solution.py:64
  137.2 11.0 %collective-permute-start.14 = (bf16[192,384]{1,0:T(8,128)(2,1)S(1)}, bf16[192,384]{1,0:T(8,128)(2,1)S(1)}, u32[]{:S(2)}, u32[]{:S(2)}) collective-permute-start(bf16[192,384]{1,0:T(8,128)(2,1)S(1)} %copy-done.18), channel_id=1, source_target_pairs={{0,2},{1,3},{2,0},{3,1},{4,6},{5,7},{6,4},{7,5},{8,10},{9,11},{10,... | collective-permute-start | bytes 442376 | tf_op jit(solution)/shard_map/ppermute | solution.py:64
  148.3 12.4 %collective-permute-start.20 = (bf16[4,96,384]{2,1,0:T(8,128)(2,1)S(1)}, bf16[4,96,384]{2,1,0:T(8,128)(2,1)S(1)}, u32[]{:S(2)}, u32[]{:S(2)}) collective-permute-start(bf16[4,96,384]{2,1,0:T(8,128)(2,1)S(1)} %get-tuple-element.209), channel_id=1, source_target_pairs={{0,16},{1,17},{2,18},{3,19},{4,20},{5,21},{6,22},{7,23},{8,24},{9,... | collective-permute-start | bytes 884744 | tf_op jit(solution)/shard_map/ppermute | solution.py:64
  148.4 12.4 %collective-permute-start.19 = (bf16[4,96,384]{2,1,0:T(8,128)(2,1)S(1)}, bf16[4,96,384]{2,1,0:T(8,128)(2,1)S(1)}, u32[]{:S(2)}, u32[]{:S(2)}) collective-permute-start(bf16[4,96,384]{2,1,0:T(8,128)(2,1)S(1)} %get-tuple-element.207), channel_id=1, source_target_pairs={{0,8},{1,9},{2,10},{3,11},{4,12},{5,13},{6,14},{7,15},{8,0},{9,1},... | collective-permute-start | bytes 884744 | tf_op jit(solution)/shard_map/ppermute | solution.py:64
  160.9 13.4 %collective-permute-start.30 = (bf16[8,96,384]{2,1,0:T(8,128)(2,1)S(1)}, bf16[8,96,384]{2,1,0:T(8,128)(2,1)S(1)}, u32[]{:S(2)}, u32[]{:S(2)}) collective-permute-start(bf16[8,96,384]{2,1,0:T(8,128)(2,1)S(1)} %constant_dynamic-update-slice_fusion.10.refs_4_), channel_id=1, source_target_pairs={{0,8},{1,9},{2,10},{3,11},{4,12},{5,13},{6,14},{7,15},{8,0},{9,1},... | collective-permute-start | bytes 1769480 | tf_op jit(solution)/shard_map/ppermute | solution.py:64
  161.1 13.3 %collective-permute-start.27 = (bf16[8,96,384]{2,1,0:T(8,128)(2,1)S(1)}, bf16[8,96,384]{2,1,0:T(8,128)(2,1)S(1)}, u32[]{:S(2)}, u32[]{:S(2)}) collective-permute-start(bf16[8,96,384]{2,1,0:T(8,128)(2,1)S(1)} %constant_dynamic-update-slice_fusion.8.refs_0_), channel_id=1, source_target_pairs={{0,16},{1,17},{2,18},{3,19},{4,20},{5,21},{6,22},{7,23},{8,24},{9,... | collective-permute-start | bytes 1769480 | tf_op jit(solution)/shard_map/ppermute | solution.py:64
  173.7 19.2 %collective-permute-start.31 = (bf16[8,96,384]{2,1,0:T(8,128)(2,1)S(1)}, bf16[8,96,384]{2,1,0:T(8,128)(2,1)S(1)}, u32[]{:S(2)}, u32[]{:S(2)}) collective-permute-start(bf16[8,96,384]{2,1,0:T(8,128)(2,1)S(1)} %constant_dynamic-update-slice_fusion.10.refs_4_), channel_id=1, source_target_pairs={{0,1},{1,0},{2,3},{3,2},{4,5},{5,4},{6,7},{7,6},{8,9},{9,8},{10,11... | collective-permute-start | bytes 1769480 | tf_op jit(solution)/shard_map/ppermute | solution.py:64
  173.8 19.1 %collective-permute-start.28 = (bf16[8,96,384]{2,1,0:T(8,128)(2,1)S(1)}, bf16[8,96,384]{2,1,0:T(8,128)(2,1)S(1)}, u32[]{:S(2)}, u32[]{:S(2)}) collective-permute-start(bf16[8,96,384]{2,1,0:T(8,128)(2,1)S(1)} %constant_dynamic-update-slice_fusion.8.refs_0_), channel_id=1, source_target_pairs={{0,1},{1,0},{2,3},{3,2},{4,5},{5,4},{6,7},{7,6},{8,9},{9,8},{10,11... | collective-permute-start | bytes 1769480 | tf_op jit(solution)/shard_map/ppermute | solution.py:64
  174.3 18.6 %collective-permute-start.32 = (bf16[8,96,384]{2,1,0:T(8,128)(2,1)S(1)}, bf16[8,96,384]{2,1,0:T(8,128)(2,1)S(1)}, u32[]{:S(2)}, u32[]{:S(2)}) collective-permute-start(bf16[8,96,384]{2,1,0:T(8,128)(2,1)S(1)} %collective-permute-done.30.refs_5_), channel_id=1, source_target_pairs={{0,1},{1,0},{2,3},{3,2},{4,5},{5,4},{6,7},{7,6},{8,9},{9,8},{10,11... | collective-permute-start | bytes 1769480 | tf_op jit(solution)/shard_map/ppermute | solution.py:64
  174.3 18.5 %collective-permute-start.29 = (bf16[8,96,384]{2,1,0:T(8,128)(2,1)S(1)}, bf16[8,96,384]{2,1,0:T(8,128)(2,1)}, u32[]{:S(2)}, u32[]{:S(2)}) collective-permute-start(bf16[8,96,384]{2,1,0:T(8,128)(2,1)S(1)} %collective-permute-done.27.refs_1_), channel_id=1, source_target_pairs={{0,1},{1,0},{2,3},{3,2},{4,5},{5,4},{6,7},{7,6},{8,9},{9,8},{10,11... | collective-permute-start | bytes 1769480 | tf_op jit(solution)/shard_map/ppermute | solution.py:64
  281.2 26.9 %collective-permute-start.33 = (bf16[16,576,128]{2,1,0:T(8,128)(2,1)}, bf16[16,576,128]{2,1,0:T(8,128)(2,1)}, u32[]{:S(2)}, u32[]{:S(2)}) collective-permute-start(bf16[16,576,128]{2,1,0:T(8,128)(2,1)} %get-tuple-element.245), channel_id=1, source_target_pairs={{0,1},{1,0},{2,3},{3,2},{4,5},{5,4},{6,7},{7,6},{8,9},{9,8},{10,11... | collective-permute-start | bytes 7077896 | tf_op jit(solution)/shard_map/ppermute | solution.py:64
  312.3 24.1 %collective-permute-start.36 = (bf16[16,656,128]{2,1,0:T(8,128)(2,1)}, bf16[16,656,128]{2,1,0:T(8,128)(2,1)S(1)}, u32[]{:S(2)}, u32[]{:S(2)}) collective-permute-start(bf16[16,656,128]{2,1,0:T(8,128)(2,1)} %get-tuple-element.250), channel_id=1, source_target_pairs={{0,1},{1,0},{2,3},{3,2},{4,5},{5,4},{6,7},{7,6},{8,9},{9,8},{10,11... | collective-permute-start | bytes 8060936 | tf_op jit(solution)/shard_map/ppermute | solution.py:64
  312.8 23.6 %collective-permute-start.34 = (bf16[8,192,128]{2,1,0:T(8,128)(2,1)}, bf16[8,192,128]{2,1,0:T(8,128)(2,1)}, u32[]{:S(2)}, u32[]{:S(2)}) collective-permute-start(bf16[8,192,128]{2,1,0:T(8,128)(2,1)} %get-tuple-element.336), channel_id=1, source_target_pairs={{0,8},{1,9},{2,10},{3,11},{4,12},{5,13},{6,14},{7,15},{8,0},{9,1},... | collective-permute-start | bytes 1179656 | tf_op jit(solution)/shard_map/ppermute | solution.py:64
  314.1 22.3 %collective-permute-start.35 = (bf16[8,384,128]{2,1,0:T(8,128)(2,1)}, bf16[8,384,128]{2,1,0:T(8,128)(2,1)}, u32[]{:S(2)}, u32[]{:S(2)}) collective-permute-start(bf16[8,384,128]{2,1,0:T(8,128)(2,1)} %get-tuple-element.334), channel_id=1, source_target_pairs={{0,16},{1,17},{2,18},{3,19},{4,20},{5,21},{6,22},{7,23},{8,24},{9,... | collective-permute-start | bytes 2359304 | tf_op jit(solution)/shard_map/ppermute | solution.py:64
  338.2 25.3 %collective-permute-start.37 = (bf16[4,192,128]{2,1,0:T(8,128)(2,1)}, bf16[4,192,128]{2,1,0:T(8,128)(2,1)S(1)}, u32[]{:S(2)}, u32[]{:S(2)}) collective-permute-start(bf16[4,192,128]{2,1,0:T(8,128)(2,1)} %get-tuple-element.358), channel_id=1, source_target_pairs={{0,16},{1,17},{2,18},{3,19},{4,20},{5,21},{6,22},{7,23},{8,24},{9,... | collective-permute-start | bytes 589832 | tf_op jit(solution)/shard_map/ppermute | solution.py:64
  341.2 22.3 %collective-permute-start.38 = (bf16[4,384,128]{2,1,0:T(8,128)(2,1)}, bf16[4,384,128]{2,1,0:T(8,128)(2,1)S(1)}, u32[]{:S(2)}, u32[]{:S(2)}) collective-permute-start(bf16[4,384,128]{2,1,0:T(8,128)(2,1)} %get-tuple-element.350), channel_id=1, source_target_pairs={{0,8},{1,9},{2,10},{3,11},{4,12},{5,13},{6,14},{7,15},{8,0},{9,1},... | collective-permute-start | bytes 1179656 | tf_op jit(solution)/shard_map/ppermute | solution.py:64
  343.7 19.9 %collective-permute-start.40 = (bf16[8,320,128]{2,1,0:T(8,128)(2,1)}, bf16[8,320,128]{2,1,0:T(8,128)(2,1)}, u32[]{:S(2)}, u32[]{:S(2)}) collective-permute-start(bf16[8,320,128]{2,1,0:T(8,128)(2,1)} %get-tuple-element.330), channel_id=1, source_target_pairs={{0,16},{1,17},{2,18},{3,19},{4,20},{5,21},{6,22},{7,23},{8,24},{9,... | collective-permute-start | bytes 1966088 | tf_op jit(solution)/shard_map/ppermute | solution.py:64
  344.6 22.1 %collective-permute-start.39 = (bf16[8,336,128]{2,1,0:T(8,128)(2,1)S(1)}, bf16[8,336,128]{2,1,0:T(8,128)(2,1)S(1)}, u32[]{:S(2)}, u32[]{:S(2)}) collective-permute-start(bf16[8,336,128]{2,1,0:T(8,128)(2,1)S(1)} %get-tuple-element.332), channel_id=1, source_target_pairs={{0,8},{1,9},{2,10},{3,11},{4,12},{5,13},{6,14},{7,15},{8,0},{9,1},... | collective-permute-start | bytes 2064392 | tf_op jit(solution)/shard_map/ppermute | solution.py:64
  346.5 20.2 %collective-permute-start.41 = (bf16[16,288,128]{2,1,0:T(8,128)(2,1)}, bf16[16,288,128]{2,1,0:T(8,128)(2,1)}, u32[]{:S(2)}, u32[]{:S(2)}) collective-permute-start(bf16[16,288,128]{2,1,0:T(8,128)(2,1)} %get-tuple-element.263), channel_id=1, source_target_pairs={{0,1},{1,0},{2,3},{3,2},{4,5},{5,4},{6,7},{7,6},{8,9},{9,8},{10,11... | collective-permute-start | bytes 3538952 | tf_op jit(solution)/shard_map/ppermute | solution.py:64
  368.0 37.4 %collective-permute-start.43 = (bf16[4,320,128]{2,1,0:T(8,128)(2,1)S(1)}, bf16[4,320,128]{2,1,0:T(8,128)(2,1)S(1)}, u32[]{:S(2)}, u32[]{:S(2)}) collective-permute-start(bf16[4,320,128]{2,1,0:T(8,128)(2,1)S(1)} %get-tuple-element.354), channel_id=1, source_target_pairs={{0,8},{1,9},{2,10},{3,11},{4,12},{5,13},{6,14},{7,15},{8,0},{9,1},... | collective-permute-start | bytes 983048 | tf_op jit(solution)/shard_map/ppermute | solution.py:64
  370.9 14.8 %collective-permute-start.46 = (bf16[4,288,128]{2,1,0:T(8,128)(2,1)S(1)}, bf16[4,288,128]{2,1,0:T(8,128)(2,1)}, u32[]{:S(2)}, u32[]{:S(2)}) collective-permute-start(bf16[4,288,128]{2,1,0:T(8,128)(2,1)S(1)} %get-tuple-element.346), channel_id=1, source_target_pairs={{0,24},{1,25},{2,26},{3,27},{4,28},{5,29},{6,30},{7,31},{8,16},{9,... | collective-permute-start | bytes 884744 | tf_op jit(solution)/shard_map/ppermute | solution.py:64
  373.4 32.1 %collective-permute-start.42 = (bf16[4,336,128]{2,1,0:T(8,128)(2,1)S(1)}, bf16[4,336,128]{2,1,0:T(8,128)(2,1)S(1)}, u32[]{:S(2)}, u32[]{:S(2)}) collective-permute-start(bf16[4,336,128]{2,1,0:T(8,128)(2,1)S(1)} %get-tuple-element.352), channel_id=1, source_target_pairs={{0,16},{1,17},{2,18},{3,19},{4,20},{5,21},{6,22},{7,23},{8,24},{9,... | collective-permute-start | bytes 1032200 | tf_op jit(solution)/shard_map/ppermute | solution.py:64
  374.4 31.0 %collective-permute-start.45 = (bf16[4,288,128]{2,1,0:T(8,128)(2,1)}, bf16[4,288,128]{2,1,0:T(8,128)(2,1)}, u32[]{:S(2)}, u32[]{:S(2)}) collective-permute-start(bf16[4,288,128]{2,1,0:T(8,128)(2,1)} %get-tuple-element.347), channel_id=1, source_target_pairs={{0,8},{1,9},{2,10},{3,11},{4,12},{5,13},{6,14},{7,15},{8,0},{9,1},... | collective-permute-start | bytes 884744 | tf_op jit(solution)/shard_map/ppermute | solution.py:64
  374.7 30.7 %collective-permute-start.44 = (bf16[4,288,128]{2,1,0:T(8,128)(2,1)}, bf16[4,288,128]{2,1,0:T(8,128)(2,1)}, u32[]{:S(2)}, u32[]{:S(2)}) collective-permute-start(bf16[4,288,128]{2,1,0:T(8,128)(2,1)} %get-tuple-element.348), channel_id=1, source_target_pairs={{0,16},{1,17},{2,18},{3,19},{4,20},{5,21},{6,22},{7,23},{8,24},{9,... | collective-permute-start | bytes 884744 | tf_op jit(solution)/shard_map/ppermute | solution.py:64
  385.7 20.8 %collective-permute-start.47 = (bf16[4,288,256]{2,1,0:T(8,128)(2,1)}, bf16[4,288,256]{2,1,0:T(8,128)(2,1)S(1)}, u32[]{:S(2)}, u32[]{:S(2)}) collective-permute-start(bf16[4,288,256]{2,1,0:T(8,128)(2,1)} %reduce-scatter.2.cloned.1.call-done), channel_id=1, source_target_pairs={{0,16},{1,17},{2,18},{3,19},{4,20},{5,21},{6,22},{7,23},{8,24},{9,... | collective-permute-start | bytes 1769480 | tf_op jit(solution)/shard_map/ppermute | solution.py:64
  409.3 16.7 %collective-permute-start.48 = (bf16[16,288,128]{2,1,0:T(8,128)(2,1)}, bf16[16,288,128]{2,1,0:T(8,128)(2,1)S(1)}, u32[]{:S(2)}, u32[]{:S(2)}) collective-permute-start(bf16[16,288,128]{2,1,0:T(8,128)(2,1)} %get-tuple-element.300), channel_id=1, source_target_pairs={{0,1},{1,0},{2,3},{3,2},{4,5},{5,4},{6,7},{7,6},{8,9},{9,8},{10,11... | collective-permute-start | bytes 3538952 | tf_op jit(solution)/shard_map/ppermute | solution.py:64
  410.0 19.1 %collective-permute-start.54 = (bf16[1,1520,128]{2,1,0:T(8,128)(2,1)}, bf16[1,1520,128]{2,1,0:T(8,128)(2,1)}, u32[]{:S(2)}, u32[]{:S(2)}) collective-permute-start(bf16[1,1520,128]{2,1,0:T(8,128)(2,1)} %get-tuple-element.338), channel_id=1, source_target_pairs={{0,6},{1,7},{2,4},{3,5},{4,2},{5,3},{6,0},{7,1},{8,14},{9,15},{10,... | collective-permute-start | bytes 1167368 | tf_op jit(solution)/shard_map/ppermute | solution.py:64
  414.9 32.6 %collective-permute-start.53 = (bf16[1,1520,128]{2,1,0:T(8,128)(2,1)S(1)}, bf16[1,1520,128]{2,1,0:T(8,128)(2,1)}, u32[]{:S(2)}, u32[]{:S(2)}) collective-permute-start(bf16[1,1520,128]{2,1,0:T(8,128)(2,1)S(1)} %get-tuple-element.339), channel_id=1, source_target_pairs={{0,4},{1,5},{2,6},{3,7},{4,0},{5,1},{6,2},{7,3},{8,12},{9,13},{10,... | collective-permute-start | bytes 1167368 | tf_op jit(solution)/shard_map/ppermute | solution.py:64
  414.9 32.9 %collective-permute-start.52 = (bf16[1,1520,128]{2,1,0:T(8,128)(2,1)S(1)}, bf16[1,1520,128]{2,1,0:T(8,128)(2,1)}, u32[]{:S(2)}, u32[]{:S(2)}) collective-permute-start(bf16[1,1520,128]{2,1,0:T(8,128)(2,1)S(1)} %get-tuple-element.340), channel_id=1, source_target_pairs={{0,2},{1,3},{2,0},{3,1},{4,6},{5,7},{6,4},{7,5},{8,10},{9,11},{10,... | collective-permute-start | bytes 1167368 | tf_op jit(solution)/shard_map/ppermute | solution.py:64
  426.5 21.3 %collective-permute-start.51 = (bf16[4,288,128]{2,1,0:T(8,128)(2,1)S(1)}, bf16[4,288,128]{2,1,0:T(8,128)(2,1)S(1)}, u32[]{:S(2)}, u32[]{:S(2)}) collective-permute-start(bf16[4,288,128]{2,1,0:T(8,128)(2,1)S(1)} %get-tuple-element.342), channel_id=1, source_target_pairs={{0,24},{1,25},{2,26},{3,27},{4,28},{5,29},{6,30},{7,31},{8,16},{9,... | collective-permute-start | bytes 884744 | tf_op jit(solution)/shard_map/ppermute | solution.py:64
  427.7 20.1 %collective-permute-start.50 = (bf16[4,288,128]{2,1,0:T(8,128)(2,1)S(1)}, bf16[4,288,128]{2,1,0:T(8,128)(2,1)S(1)}, u32[]{:S(2)}, u32[]{:S(2)}) collective-permute-start(bf16[4,288,128]{2,1,0:T(8,128)(2,1)S(1)} %get-tuple-element.343), channel_id=1, source_target_pairs={{0,8},{1,9},{2,10},{3,11},{4,12},{5,13},{6,14},{7,15},{8,0},{9,1},... | collective-permute-start | bytes 884744 | tf_op jit(solution)/shard_map/ppermute | solution.py:64
  429.1 18.7 %collective-permute-start.49 = (bf16[4,288,128]{2,1,0:T(8,128)(2,1)S(1)}, bf16[4,288,128]{2,1,0:T(8,128)(2,1)S(1)}, u32[]{:S(2)}, u32[]{:S(2)}) collective-permute-start(bf16[4,288,128]{2,1,0:T(8,128)(2,1)S(1)} %get-tuple-element.344), channel_id=1, source_target_pairs={{0,16},{1,17},{2,18},{3,19},{4,20},{5,21},{6,22},{7,23},{8,24},{9,... | collective-permute-start | bytes 884744 | tf_op jit(solution)/shard_map/ppermute | solution.py:64
  447.5 16.2 %collective-permute-start.61 = (bf16[4,288,256]{2,1,0:T(8,128)(2,1)S(1)}, bf16[4,288,256]{2,1,0:T(8,128)(2,1)S(1)}, u32[]{:S(2)}, u32[]{:S(2)}) collective-permute-start(bf16[4,288,256]{2,1,0:T(8,128)(2,1)S(1)} %add.115), channel_id=1, source_target_pairs={{0,8},{1,9},{2,10},{3,11},{4,12},{5,13},{6,14},{7,15},{8,0},{9,1},... | collective-permute-start | bytes 1769480 | tf_op jit(solution)/shard_map/ppermute | solution.py:64
  449.5 14.4 %collective-permute-start.60 = (bf16[1,288,128]{2,1,0:T(8,128)(2,1)S(1)}, bf16[1,288,128]{2,1,0:T(8,128)(2,1)S(1)}, u32[]{:S(2)}, u32[]{:S(2)}) collective-permute-start(bf16[1,288,128]{2,1,0:T(8,128)(2,1)S(1)} %get-tuple-element.360), channel_id=1, source_target_pairs={{0,6},{1,7},{2,4},{3,5},{4,2},{5,3},{6,0},{7,1},{8,14},{9,15},{10,... | collective-permute-start | bytes 221192 | tf_op jit(solution)/shard_map/ppermute | solution.py:64
  452.2 33.5 %collective-permute-start.57 = (bf16[1520,128]{1,0:T(8,128)(2,1)S(1)}, bf16[1520,128]{1,0:T(8,128)(2,1)S(1)}, u32[]{:S(2)}, u32[]{:S(2)}) collective-permute-start(bf16[1520,128]{1,0:T(8,128)(2,1)S(1)} %fusion.refs_0_), channel_id=1, source_target_pairs={{0,24},{1,25},{2,26},{3,27},{4,28},{5,29},{6,30},{7,31},{8,16},{9,... | collective-permute-start | bytes 1167368 | tf_op jit(solution)/shard_map/ppermute | solution.py:64
  454.3 31.4 %collective-permute-start.56 = (bf16[1520,128]{1,0:T(8,128)(2,1)S(1)}, bf16[1520,128]{1,0:T(8,128)(2,1)S(1)}, u32[]{:S(2)}, u32[]{:S(2)}) collective-permute-start(bf16[1520,128]{1,0:T(8,128)(2,1)S(1)} %fusion.refs_0_), channel_id=1, source_target_pairs={{0,16},{1,17},{2,18},{3,19},{4,20},{5,21},{6,22},{7,23},{8,24},{9,... | collective-permute-start | bytes 1167368 | tf_op jit(solution)/shard_map/ppermute | solution.py:64
  455.4 10.4 %collective-permute-start.59 = (bf16[1,288,128]{2,1,0:T(8,128)(2,1)S(1)}, bf16[1,288,128]{2,1,0:T(8,128)(2,1)S(1)}, u32[]{:S(2)}, u32[]{:S(2)}) collective-permute-start(bf16[1,288,128]{2,1,0:T(8,128)(2,1)S(1)} %get-tuple-element.361), channel_id=1, source_target_pairs={{0,4},{1,5},{2,6},{3,7},{4,0},{5,1},{6,2},{7,3},{8,12},{9,13},{10,... | collective-permute-start | bytes 221192 | tf_op jit(solution)/shard_map/ppermute | solution.py:64
  463.7 4.4 collective-permute-start.58
  463.8 21.9 %collective-permute-start.55 = (bf16[1520,128]{1,0:T(8,128)(2,1)S(1)}, bf16[1520,128]{1,0:T(8,128)(2,1)S(1)}, u32[]{:S(2)}, u32[]{:S(2)}) collective-permute-start(bf16[1520,128]{1,0:T(8,128)(2,1)S(1)} %fusion.refs_0_), channel_id=1, source_target_pairs={{0,8},{1,9},{2,10},{3,11},{4,12},{5,13},{6,14},{7,15},{8,0},{9,1},... | collective-permute-start | bytes 1167368 | tf_op jit(solution)/shard_map/ppermute | solution.py:64
  468.1 13.2 %collective-permute-start.64 = (bf16[288,128]{1,0:T(8,128)(2,1)S(1)}, bf16[288,128]{1,0:T(8,128)(2,1)S(1)}, u32[]{:S(2)}, u32[]{:S(2)}) collective-permute-start(bf16[288,128]{1,0:T(8,128)(2,1)S(1)} %fusion.1.refs_4_), channel_id=1, source_target_pairs={{0,24},{1,25},{2,26},{3,27},{4,28},{5,29},{6,30},{7,31},{8,16},{9,... | collective-permute-start | bytes 221192 | tf_op jit(solution)/shard_map/ppermute | solution.py:64
  469.3 12.8 %collective-permute-start.63 = (bf16[288,128]{1,0:T(8,128)(2,1)S(1)}, bf16[288,128]{1,0:T(8,128)(2,1)S(1)}, u32[]{:S(2)}, u32[]{:S(2)}) collective-permute-start(bf16[288,128]{1,0:T(8,128)(2,1)S(1)} %fusion.1.refs_4_), channel_id=1, source_target_pairs={{0,16},{1,17},{2,18},{3,19},{4,20},{5,21},{6,22},{7,23},{8,24},{9,... | collective-permute-start | bytes 221192 | tf_op jit(solution)/shard_map/ppermute | solution.py:64
  (50 other events, 402.7 us)
Sparse Core Ops, SparseCore 0:
  90.5 63.2 all-gather.1
  281.4 56.4 reduce-scatter.1

commit v4 on v3

--- a/solution.py
+++ b/solution.py
@@ -74,6 +74,12 @@
     return jnp.stack([b[k] for k in ("y", "x", "z1", "z0", "c")]).astype(jnp.int32)
 
 
+def along_z(parts):
+    size = lax.axis_size("wide") // 2
+    groups = [[2 * z + core for z in range(size)] for core in range(2)]
+    return lax.all_to_all(parts, "wide", 0, 0, tiled=True, axis_index_groups=groups)
+
+
 class Line:
     def __init__(self):
         self.tokens = []
@@ -86,6 +92,11 @@
         self.tokens = jax.tree.leaves(out)[-1:]
         return out
 
+    def touch(self, *values):
+        out = lax.optimization_barrier((*values, *self.tokens))
+        self.tokens = list(out[:len(values)])
+        return self.tokens
+
     def run_all(self, call, *values):
         out = call(*(lax.optimization_barrier((*values, *self.tokens))[:len(values)]))
         self.tokens = jax.tree.leaves(out)
@@ -99,28 +110,36 @@
 
 
 class Gather:
-    def __init__(self, line, piece, at, axis):
-        self.line, self.at, self.axis = line, at, axis
-        self.got = [piece, swap(piece, "z0"), swap(piece, "z1"), swap(piece, "z1", "z0")]
-
-    def over_first(self):
-        def call(*parts):
-            value = jnp.stack(parts)
+    def __init__(self, piece, at, axis, swaps=False):
+        self.at, self.axis, self.stage = at, axis, 0
+        if swaps:
+            self.terms = [piece, swap(piece, "z0"), swap(piece, "z1"), swap(piece, "z1", "z0")]
+        else:
+            self.terms = [along_z(jnp.broadcast_to(piece[None], (4,) + piece.shape))]
+        self.relative = swaps
+
+    def add(self, *terms):
+        if self.stage == 0:
+            value = jnp.stack(terms) if self.relative else terms[0]
             return [lax.slice_in_dim(value, 0, self.at, axis=self.axis + 1),
                     lax.slice_in_dim(value, self.at, value.shape[self.axis + 1], axis=self.axis + 1)]
-
-        one, two = self.line.run_all(call, *self.got)
-        self.got = [one, swap(one, "x"), two, swap(two, "y")]
-
-    def over_second(self):
-        def call(one, one_x, two, two_y):
-            return [jnp.concatenate([one, one_x]), jnp.concatenate([two, two_y])]
-
-        one, two = self.line.run_all(call, *self.got)
-        self.pieces = []
-        for value, name in ((one, "y"), (two, "x")):
-            other = swap(value, name)
-            self.pieces += [value, other, swap(value, "c"), swap(other, "c")]
+        return [jnp.concatenate(terms[:2]), jnp.concatenate(terms[2:])]
+
+    def send(self, out):
+        one, two = out
+        if self.stage == 0:
+            self.terms = [one, swap(one, "x"), two, swap(two, "y")]
+        else:
+            self.terms = [one, swap(one, "y"), two, swap(two, "x")]
+        self.stage += 1
+
+    def starting(self, first):
+        self.pieces[0] = first
+        return self
+
+    def between_cores(self):
+        one, one_y, two, two_x = self.terms
+        self.pieces = [one, one_y, swap(one, "c"), swap(one_y, "c"), two, two_x, swap(two, "c"), swap(two_x, "c")]
 
 
 PLANE = [[(s // 4, a % 2, s // 2 % 2, s % 2, a // 2) for s in range(8)] for a in range(4)]
@@ -143,7 +162,8 @@
         for half, order in enumerate((XY, YX)):
             for a, places in enumerate(PLANE):
                 for s, (first, second, z1, z0, core) in enumerate(places):
-                    shard, y, x = locate(me_ref, order, (first, second), (z1, z0), core)
+                    z = (z1, z0) if gathered.relative else (me_ref[2] ^ z1, me_ref[3] ^ z0)
+                    shard, y, x = locate(me_ref, order, (first, second), z, core)
                     for k, rows, cols, row, col in parts:
                         share = halves(rows, cols)[half]
                         if share is None or (row is None and (first or second)):
@@ -169,20 +189,9 @@
         out_shape=[spec(s) for s in shapes],
         scratch_shapes=[pltpu.SemaphoreType.DMA((64 * len(parts),))],
         compiler_params=params(),
-        cost_estimate=lasts(5),
+        cost_estimate=lasts(0),
         name="assemble",
     )(me, *gathered.pieces)
-
-
-def total_of(terms):
-    if len(terms) == 2:
-        return terms[0] + terms[1]
-    return sum(term.astype(F32) for term in terms).astype(BF16)
-
-
-def in_four(total):
-    size = total.shape[0] // 4
-    return [total[size * i:size * (i + 1)] for i in range(4)]
 
 
 def together(line, *jobs):
@@ -205,57 +214,76 @@
         self.terms = [keep, swap(line.after(send), "c")]
 
     def add(self, *terms):
-        split = self.split
-        if self.stage == 0 and split is None:
-            return in_four(total_of(terms))
         if self.stage == 0:
-            total = total_of(terms)
-            return [total[:8, :split], total[8:, :split], total[:8, split:], total[8:, split:]]
-        if split is None:
-            return [total_of(terms)]
-        one, two = terms[0] + terms[1], terms[2] + terms[3]
-        if self.stage == 1:
-            return [one[:4], one[4:], two[:4], two[4:]]
-        return [jnp.concatenate([one, two], 1)]
+            parts = [(slots, rows) for rows in (slice(0, self.split), slice(self.split, None)) for slots in (slice(0, 8), slice(8, 16))]
+            return [terms[0][part] + terms[1][part] for part in parts]
+        return [terms[i][part] + terms[i + 1][part] for i in (0, 2) for part in (slice(0, 4), slice(4, 8))]
 
     def send(self, out):
-        if len(out) == 1:
+        one, two = ("x", "y") if self.stage == 0 else ("y", "x")
+        self.terms = [out[0], swap(out[1], one), out[2], swap(out[3], two)]
+        self.stage += 1
+
+
+class Single(Chunk):
+    def __init__(self, line, keep, send, order):
+        super().__init__(line, keep, send, None)
+        self.order = order
+
+    def add(self, *terms):
+        if self.stage == 2:
+            return [terms[0] + terms[1]]
+        half = terms[0].shape[0] // 2
+        return [terms[0][part] + terms[1][part] for part in (slice(0, half), slice(half, None))]
+
+    def send(self, out):
+        self.terms = out if self.stage == 2 else [out[0], swap(out[1], self.order[self.stage])]
+        self.stage += 1
+
+
+class Along:
+    def __init__(self, *chunks):
+        self.stage, self.terms = 0, [term for chunk in chunks for term in chunk.terms]
+        self.done = [len(chunk.terms) == 1 for chunk in chunks for _ in range(max(1, len(chunk.terms) // 2))]
+
+    def add(self, *terms):
+        if self.stage:
+            return [sum(terms[0][i].astype(F32) for i in range(4)).astype(BF16)]
+        terms = list(terms)
+        sums = [terms.pop(0) if done else terms.pop(0) + terms.pop(0) for done in self.done]
+        return [jnp.concatenate(sums, 1)]
+
+    def send(self, out):
+        if self.stage:
             self.total = out[0]
-        elif self.split is None:
-            self.terms = [out[0], swap(out[1], "y"), swap(out[2], "x"), swap(out[3], "x", "y")]
         else:
-            one, two = ("x", "y") if self.stage == 0 else ("y", "x")
-            self.terms = [out[0], swap(out[1], one), out[2], swap(out[3], two)]
+            self.terms = [along_z(out[0])]
         self.stage += 1
 
 
-class Along:
-    def __init__(self, line, chunks):
-        self.stage, self.rows = 0, [chunk.total.shape[1] for chunk in chunks]
-        out = line.run_all(lambda *totals: in_four(jnp.concatenate(totals, 1)), *[chunk.total for chunk in chunks])
-        self.terms = [out[0], swap(out[1], "z0"), swap(out[2], "z1"), swap(out[3], "z1", "z0")]
-
-    def add(self, *terms):
-        return [total_of(terms)[0]]
-
-    def send(self, out):
-        total = out[0]
+class Back:
+    def __init__(self, line, *alongs):
+        self.rows = [along.total.shape[0] for along in alongs]
+        if len(alongs) > 1:
+            (total,) = line.run_all(lambda *parts: [jnp.concatenate(parts)], *[along.total for along in alongs])
+        else:
+            total = alongs[0].total
         self.terms = [total, swap(total, "x"), swap(total, "y"), swap(total, "x", "y")]
 
 
 class Whole:
     def __init__(self, value):
-        self.terms, self.stage = [value, swap(value, "y")], 0
+        self.terms = [value, swap(value, "y")]
 
     def add(self, *terms):
-        return [total_of(terms)]
+        return [terms[0] + terms[1]]
 
     def send(self, out):
         self.terms = [out[0], swap(out[0], "x")]
 
 
-def finish(me, alongs, places, shapes):
-    ins = [t for along in alongs for t in along.terms]
+def finish(me, backs, places, shapes):
+    ins = [t for back in backs for t in back.terms]
 
     def body(me_ref, *refs):
         outs = refs[len(ins):len(ins) + len(shapes)]
@@ -278,7 +306,7 @@
         in_specs=[pl.BlockSpec(memory_space=pltpu.SMEM)] + [whole(a.shape) for a in ins],
         out_specs=[whole(s) for s in shapes],
         out_shape=[spec(s, F32) for s in shapes],
-        scratch_shapes=[pltpu.VMEM((4,) + along.terms[0].shape, BF16) for along in alongs],
+        scratch_shapes=[pltpu.VMEM((4,) + back.terms[0].shape, BF16) for back in backs],
         compiler_params=params(),
         cost_estimate=lasts(3),
         name="finish",
@@ -286,6 +314,7 @@
 
 
 PLAIN = "plain"
+ALL_XY, ALL_YX = 1 << 30, 0
 
 
 TABLE = 64
@@ -319,19 +348,19 @@
             return
         for core in range(2):
             for s in range(16):
-                z = (s // 2 % 2, s % 2)
+                z = (me_ref[2] ^ (s // 2 % 2), me_ref[3] ^ (s % 2))
                 places = [locate(me_ref, order, (s // 8, s // 4 % 2), z, core) for order in (XY, YX)]
                 at = 0
                 for k, (rows, cols) in enumerate(self.shapes):
                     r = rows // 16
                     for b in range(cols // 2 // LANES):
-                        shard, y, x = places[0 if self.split is None or at < self.split else 1]
+                        shard, y, x = places[0 if at < self.split else 1]
                         start = pl.multiple_of((shard * 2 + y) * r, 16)
                         outs[core][s, at:at + r, :] = held[k][x, pl.ds(start, r), b * LANES:(b + 1) * LANES]
                         at += r
                 if self.table:
                     r = TABLE // 4
-                    _, y, x = places[0 if self.split is None or at < self.split else 1]
+                    _, y, x = places[0 if at < self.split else 1]
                     outs[core][s, at:at + r, :] = held[-1][pl.ds(pl.multiple_of((2 * y + x) * r, 16), r), :]
 
 
@@ -339,6 +368,10 @@
     cdf = 0.5 + 0.5 * lax.erf(values * 0.7071067811865476)
     pdf = 0.3989422804014327 * jnp.exp(-0.5 * values * values)
     return values * cdf, cdf + values * pdf
+
+
+def gelu(values):
+    return values * (0.5 + 0.5 * lax.erf(values * 0.7071067811865476))
 
 
 def normalize(values):
@@ -589,7 +622,7 @@
                 at = D * p + WIDTH * i
                 da1 = da1 + mm_nt(ref[:, WIDTH * p:WIDTH * (p + 1)], w_ref[:, at:at + WIDTH])
         n1, rs1 = normalize(x_ref[...].astype(F32))
-        out_ref[...] = (dx2_ref[...] + norm_transpose(da1 * gains_ref[0:1], n1, rs1)).astype(BF16)
+        out_ref[...] = (dx2_ref[...].astype(F32) + norm_transpose(da1 * gains_ref[0:1], n1, rs1)).astype(BF16)
 
     def cols(n):
         return pl.BlockSpec((block, n), lambda i: (i, 0))
@@ -606,7 +639,7 @@
     )(*dqkv, w, dx2, x, gains)
 
 
-def mlp_up_body(x_ref, o0_ref, o1_ref, o2_ref, wout_ref, w1_ref, gains_ref, x2_ref, a2_ref, gg_ref, slope_ref):
+def mlp_up_body(x_ref, o0_ref, o1_ref, o2_ref, wout_ref, w1_ref, gains_ref, x2_ref, a2_ref, u_ref):
     rows = x2_ref.shape[0]
     chunk = rows // 4
 
@@ -617,30 +650,34 @@
             x2 = x_ref[at].astype(F32)
             for i, ref in enumerate((o0_ref, o1_ref, o2_ref)):
                 x2 = x2 + mm(ref[at], wout_ref[WIDTH * i:WIDTH * (i + 1)])
-            x2_ref[at] = x2
+            x2_ref[at] = x2.astype(BF16)
             a2_ref[at] = (normalize(x2)[0] * gains_ref[1:2]).astype(BF16)
 
-    act, slope = gelu_pair(mm(a2_ref[...], w1_ref[...]))
-    gg_ref[...], slope_ref[...] = act.astype(BF16), slope.astype(BF16)
-
-
-def mlp_up(x, heads_out, w_out, w1, gains, block=512):
+    u_ref[...] = mm(a2_ref[...], w1_ref[...]).astype(BF16)
+
+
+def mlp_up(x, heads_out, w_out, w1, gains, block=1024):
     rows, ff = x.shape[0], w1.shape[1]
     full, cols = whole((rows, D)), pl.BlockSpec((rows, block), lambda i: (0, i))
     return pl.pallas_call(
         mlp_up_body,
         grid=(ff // block,),
         in_specs=[full] + [whole((rows, WIDTH))] * 3 + [whole((D, D)), pl.BlockSpec((D, block), lambda i: (0, i)), whole((2, D))],
-        out_specs=[full, full, cols, cols],
-        out_shape=[spec((rows, D), F32), spec((rows, D)), spec((rows, ff)), spec((rows, ff))],
+        out_specs=[full, full, cols],
+        out_shape=[spec((rows, D)), spec((rows, D)), spec((rows, ff))],
         compiler_params=params(),
         cost_estimate=lasts(18),
         name="mlp_up",
     )(x, *heads_out, w_out, w1, gains)
 
 
-def mlp_down_body(gg_ref, w2_ref, x2_ref, count_ref, x3b_ref, out_ref):
-    x3 = x2_ref[...] + mm(gg_ref[...], w2_ref[...])
+def mlp_down_body(u_ref, w2_ref, x2_ref, count_ref, x3b_ref, out_ref):
+    x3 = x2_ref[...].astype(F32)
+    size = u_ref.shape[1] // 6
+    for k in range(6):
+        at = slice(size * k, size * (k + 1))
+        act = gelu(u_ref[:, at].astype(F32)).astype(BF16)
+        x3 = x3 + mm(act, w2_ref[at, :])
     x3b_ref[...] = x3.astype(BF16)
     image = pl.program_id(0) * x3b_ref.shape[0] // COUNT
     out_ref[...] = (x3 * (image < count_ref[0]).astype(F32)).astype(BF16)
@@ -684,105 +721,120 @@
             out_ref[rows, block * ch:(block + 1) * ch] = part.astype(BF16)
 
 
-def units_body(x_ref, wre_ref, w_ref, t1_ref, s1_ref, t2_ref, s2_ref, z_ref, cols):
-    count = x_ref.shape[0]
-    z = mm(x_ref[...], wre_ref[...])
-    for unit in range(2):
-        act, slope = gelu_pair(z)
-        t1_ref[unit], s1_ref[unit] = act.astype(BF16), slope.astype(BF16)
-        spread(act, cols, slice(0, count), 1)
-        act, slope = gelu_pair(mm(cols[...], w_ref[2 * unit]))
-        t2_ref[unit], s2_ref[unit] = act.astype(BF16), slope.astype(BF16)
-        spread(act, cols, slice(0, count), 1)
-        z = z + mm(cols[...], w_ref[2 * unit + 1])
-    z_ref[...] = z.astype(BF16)
+def units_body(x_ref, wre_ref, w_ref, t1_ref, s1_ref, t2_ref, s2_ref, zb_ref, cols, z_ref):
+    unit, count = pl.program_id(1), x_ref.shape[0]
+
+    @pl.when(unit == 0)
+    def _():
+        z_ref[...] = mm(x_ref[...], wre_ref[...])
+
+    act, slope = gelu_pair(z_ref[...])
+    t1_ref[0], s1_ref[0] = act.astype(BF16), slope.astype(BF16)
+    spread(act, cols, slice(0, count), 1)
+    act, slope = gelu_pair(mm(cols[...], w_ref[0]))
+    t2_ref[0], s2_ref[0] = act.astype(BF16), slope.astype(BF16)
+    spread(act, cols, slice(0, count), 1)
+    z_ref[...] += mm(cols[...], w_ref[1])
+
+    @pl.when(unit == 1)
+    def _():
+        zb_ref[...] = z_ref[...].astype(BF16)
 
 
 def units(x3b, w_re, w_conv):
     rows, ch = x3b.shape[0], w_re.shape[1]
-    acts = pl.BlockSpec((2, COUNT, ch), lambda i: (0, i, 0))
+    acts = pl.BlockSpec((1, COUNT, ch), lambda i, j: (j, i, 0))
     return pl.pallas_call(
         units_body,
-        grid=(rows // COUNT,),
-        in_specs=[pl.BlockSpec((COUNT, D), lambda i: (i, 0)), whole(w_re.shape), whole(w_conv.shape)],
-        out_specs=[acts] * 4 + [pl.BlockSpec((COUNT, ch), lambda i: (i, 0))],
+        grid=(rows // COUNT, 2),
+        in_specs=[pl.BlockSpec((COUNT, D), lambda i, j: (i, 0)), whole(w_re.shape),
+                  pl.BlockSpec((2,) + w_conv.shape[1:], lambda i, j: (j, 0, 0))],
+        out_specs=[acts] * 4 + [pl.BlockSpec((COUNT, ch), lambda i, j: (i, 0))],
         out_shape=[spec((2, rows, ch))] * 4 + [spec((rows, ch))],
-        scratch_shapes=[pltpu.VMEM((COUNT, 9 * ch), BF16)],
+        scratch_shapes=[pltpu.VMEM((COUNT, 9 * ch), BF16), pltpu.VMEM((COUNT, ch), F32)],
         compiler_params=params(),
         cost_estimate=lasts(18),
         name="units",
     )(x3b, w_re, w_conv)
 
 
-def units_back_body(down_ref, scale_ref, gshift_ref, hot_ref, z_ref, x3b_ref, gt_ref, count_ref, whead_ref, w_ref, wre_ref, t1_ref, s1_ref, t2_ref, s2_ref,
-                    gw_ref, ghead_ref, gre_ref, dx3_ref, dm_ref, table_ref, moved, turned, dz_ref):
+def units_back_body(down_ref, scale_ref, gshift_ref, hot_ref, z_ref, x3b_ref, gt_ref, count_ref, whead_ref, wre_ref,
+                    w_ref, t1_ref, s1_ref, t2_ref, s2_ref,
+                    gw_ref, ghead_ref, gre_ref, dm_ref, table_ref, moved, turned, dz_ref):
     images, _, ch = down_ref.shape
-    dq = jnp.concatenate([(down_ref[i] * scale_ref[i]).astype(BF16) for i in range(images)], 0)
-    ghead_ref[...] = mm_tn(z_ref[...], dq).astype(BF16)
-    dz_ref[...] = mm_nt(dq, whead_ref[...])
-    table_ref[...] = jnp.zeros_like(table_ref)
-    for i in range(images):
-        head = mm(z_ref[COUNT * i:COUNT * (i + 1)], whead_ref[...])
-        sums = (jnp.sum(head * down_ref[i], 0, keepdims=True), gshift_ref[i])
-        for b in range(2 * ch // LANES):
-            at, row = SMALL * b, sums[b // (ch // LANES)]
-            cols = slice(LANES * (b % (ch // LANES)), LANES * (b % (ch // LANES) + 1))
-            table_ref[at:at + SMALL] += hot_ref[i] * row[:, cols]
-
-    def back(index, grad, act_ref, unit):
+
+    @pl.when(pl.program_id(0) == 0)
+    def _():
+        dq = jnp.concatenate([(down_ref[i] * scale_ref[i]).astype(BF16) for i in range(images)], 0)
+        ghead_ref[...] = mm_tn(z_ref[...], dq).astype(BF16)
+        dz_ref[...] = mm_nt(dq, whead_ref[...])
+        table_ref[...] = jnp.zeros_like(table_ref)
+        for i in range(images):
+            head = mm(z_ref[COUNT * i:COUNT * (i + 1)], whead_ref[...])
+            sums = (jnp.sum(head * down_ref[i], 0, keepdims=True), gshift_ref[i])
+            for b in range(2 * ch // LANES):
+                at, row = SMALL * b, sums[b // (ch // LANES)]
+                cols = slice(LANES * (b % (ch // LANES)), LANES * (b % (ch // LANES) + 1))
+                table_ref[at:at + SMALL] += hot_ref[i] * row[:, cols]
+
+    def back(index, grad, act_ref):
         for i in range(images):
             at = slice(COUNT * i, COUNT * (i + 1))
             spread(grad[at], moved, at, -1)
-        g = mm_tn(act_ref[unit], moved[...])
+        g = mm_tn(act_ref[0], moved[...])
         for b in range(9):
             at = slice(ch * b, ch * (b + 1))
             gw_ref[index, at, :] = g[:, at].astype(BF16)
             turned[:, at] = w_ref[index, at, :]
         return mm_nt(moved[...], turned[...])
 
-    for unit in (1, 0):
-        grad = back(2 * unit + 1, dz_ref[...], t2_ref, unit) * s2_ref[unit].astype(F32)
-        grad = back(2 * unit, grad, t1_ref, unit) * s1_ref[unit].astype(F32)
-        dz_ref[...] += grad
-    dr = dz_ref[...].astype(BF16)
-    gre_ref[...] = mm_tn(x3b_ref[...], dr).astype(BF16)
-    dx3 = mm_nt(dr, wre_ref[...])
-    for i in range(images):
-        at = slice(COUNT * i, COUNT * (i + 1))
-        part = gt_ref[at].astype(F32) * (i < count_ref[0]).astype(F32) + dx3[at]
-        dx3_ref[at] = part
-        dm_ref[at] = part.astype(BF16)
+    grad = back(1, dz_ref[...], t2_ref) * s2_ref[0].astype(F32)
+    grad = back(0, grad, t1_ref) * s1_ref[0].astype(F32)
+    dz_ref[...] += grad
+
+    @pl.when(pl.program_id(0) == 1)
+    def _():
+        dr = dz_ref[...].astype(BF16)
+        gre_ref[...] = mm_tn(x3b_ref[...], dr).astype(BF16)
+        dx3 = mm_nt(dr, wre_ref[...])
+        for i in range(images):
+            at = slice(COUNT * i, COUNT * (i + 1))
+            part = gt_ref[at].astype(F32) * (i < count_ref[0]).astype(F32) + dx3[at]
+            dm_ref[at] = part.astype(BF16)
 
 
 def units_back(down, scale, gshift, hot, z, x3b, gt, live_count, w_head, w_conv, w_re, t1, s1, t2, s2):
     rows, ch = z.shape
-    ins = (down, scale, gshift, hot, z, x3b, gt, live_count, w_head, w_conv, w_re, t1, s1, t2, s2)
-    outs = [spec(w_conv.shape), spec(w_head.shape), spec(w_re.shape), spec((rows, D), F32), spec((rows, D)),
+    ins = (down, scale, gshift, hot, z, x3b, gt, live_count, w_head, w_re)
+    outs = [spec(w_conv.shape), spec(w_head.shape), spec(w_re.shape), spec((rows, D)),
             spec((2 * ch // LANES * SMALL, LANES), F32)]
+    kernels = pl.BlockSpec((2,) + w_conv.shape[1:], lambda i: (1 - i, 0, 0))
+    act = pl.BlockSpec((1, rows, ch), lambda i: (1 - i, 0, 0))
     return pl.pallas_call(
         units_back_body,
-        grid=(1,),
-        in_specs=[pl.BlockSpec(memory_space=pltpu.SMEM) if a is live_count else whole(a.shape) for a in ins],
-        out_specs=[whole(a.shape) for a in outs],
+        grid=(2,),
+        in_specs=[pl.BlockSpec(memory_space=pltpu.SMEM) if a is live_count else whole(a.shape) for a in ins] + [kernels] + [act] * 4,
+        out_specs=[kernels] + [whole(a.shape) for a in outs[1:]],
         out_shape=outs,
         scratch_shapes=[pltpu.VMEM((rows, 9 * ch), BF16), pltpu.VMEM((ch, 9 * ch), BF16), pltpu.VMEM((rows, ch), F32)],
         compiler_params=params(),
         cost_estimate=lasts(30),
         name="units_back",
-    )(*ins)
-
-
-def hidden_back(dm, me, gg, slope, w2, split, block=512):
-    rows, ff = gg.shape
+    )(*ins, w_conv, t1, s1, t2, s2)
+
+
+def hidden_back(dm, me, u, w2, split, block=512):
+    rows, ff = u.shape
     sink = Sink([(ff, D)], split)
     n_out = len(sink.outs)
 
-    def body(dm_ref, me_ref, gg_ref, slope_ref, w2_ref, *refs):
+    def body(dm_ref, me_ref, u_ref, w2_ref, *refs):
         grads, du_ref, held = refs[:n_out], refs[n_out], refs[n_out + 1:]
         step = pl.program_id(0)
         at = pl.ds(pl.multiple_of(step * block, block), block)
-        sink.put(grads, held, 0, at, mm_tn(gg_ref[...], dm_ref[...]))
-        du_ref[...] = (mm_nt(dm_ref[...], w2_ref[...]) * slope_ref[...].astype(F32)).astype(BF16)
+        act, slope = gelu_pair(u_ref[...].astype(F32))
+        sink.put(grads, held, 0, at, mm_tn(act.astype(BF16), dm_ref[...]))
+        du_ref[...] = (mm_nt(dm_ref[...], w2_ref[...]) * slope).astype(BF16)
 
         @pl.when(step == pl.num_programs(0) - 1)
         def _():
@@ -792,41 +844,32 @@
     out = pl.pallas_call(
         body,
         grid=(ff // block,),
-        in_specs=[whole((rows, D)), pl.BlockSpec(memory_space=pltpu.SMEM), cols, cols, pl.BlockSpec((block, D), lambda i: (i, 0))],
+        in_specs=[whole((rows, D)), pl.BlockSpec(memory_space=pltpu.SMEM), cols, pl.BlockSpec((block, D), lambda i: (i, 0))],
         out_specs=sink.out_specs() + [cols],
         out_shape=sink.outs + [spec((rows, ff))],
         scratch_shapes=sink.scratch,
         compiler_params=params(),
         cost_estimate=lasts(20),
         name="hidden_back",
-    )(dm, me, gg, slope, w2)
+    )(dm, me, u, w2)
     return out[:n_out], out[n_out]
 
 
-def mlp_back(du, me, a2, w1, dx3, x2, gains, g_re, g_head, table, split, block=512):
+def first_weight_back(du, me, a2, g_re, g_head, table, split, block=512):
     rows, ff = du.shape
     sink = Sink([(D, ff), g_re.shape, g_head.shape], split, True)
     n_out = len(sink.outs)
     half = ff // 2 // block
 
-    def body(du_ref, me_ref, a2_ref, w1_ref, dx3_ref, x2_ref, gains_ref, gre_ref, ghead_ref, table_ref, *refs):
+    def body(du_ref, me_ref, a2_ref, gre_ref, ghead_ref, table_ref, *refs):
         step = pl.program_id(0)
-        grads, (dx2_ref, da_ref, total), held = refs[:n_out], refs[n_out:n_out + 3], refs[n_out + 3:]
+        grads, held = refs[:n_out], refs[n_out:]
         g = mm_tn(a2_ref[...], du_ref[...]).astype(BF16)
         cols = pl.ds(pl.multiple_of(step % half * block, block), block)
         if split == PLAIN:
             grads[0][:, pl.ds(pl.multiple_of(step * block, block), block)] = g
         else:
             held[0][step // half, :, cols] = g
-        da2 = mm_nt(du_ref[...], w1_ref[...])
-
-        @pl.when(step == 0)
-        def _():
-            total[...] = da2
-
-        @pl.when(step > 0)
-        def _():
-            total[...] += da2
 
         @pl.when(step == pl.num_programs(0) - 1)
         def _():
@@ -835,30 +878,44 @@
             if split != PLAIN:
                 held[-1][...] = table_ref[...].astype(BF16)
             sink.deliver(me_ref, grads, held)
-            chunk = rows // 6
-            for p in range(0, rows, chunk):
-                at = slice(p, p + chunk)
-                n2, rs2 = normalize(x2_ref[at])
-                dx2 = dx3_ref[at] + norm_transpose(total[at] * gains_ref[1:2], n2, rs2)
-                dx2_ref[at] = dx2
-                da_ref[at] = dx2.astype(BF16)
-
-    full = whole((rows, D))
-    others = [spec((rows, D), F32), spec((rows, D))]
-    out = pl.pallas_call(
+
+    return pl.pallas_call(
         body,
         grid=(ff // block,),
-        in_specs=[pl.BlockSpec((rows, block), lambda i: (0, i)), pl.BlockSpec(memory_space=pltpu.SMEM), full,
-                  pl.BlockSpec((D, block), lambda i: (0, i)), full, full, whole((2, D)), whole(g_re.shape), whole(g_head.shape),
-                  whole(table.shape)],
-        out_specs=sink.out_specs() + [whole(o.shape) for o in others],
-        out_shape=sink.outs + others,
-        scratch_shapes=[pltpu.VMEM((rows, D), F32)] + sink.scratch,
-        compiler_params=params(),
-        cost_estimate=lasts(27),
+        in_specs=[pl.BlockSpec((rows, block), lambda i: (0, i)), pl.BlockSpec(memory_space=pltpu.SMEM), whole((rows, D)),
+                  whole(g_re.shape), whole(g_head.shape), whole(table.shape)],
+        out_specs=sink.out_specs(),
+        out_shape=sink.outs,
+        scratch_shapes=sink.scratch,
+        compiler_params=params(),
+        cost_estimate=lasts(13),
+        name="first_weight_back",
+    )(du, me, a2, g_re, g_head, table)
+
+
+def mlp_back_body(du_ref, w1_ref, dm_ref, x2_ref, gains_ref, da_ref):
+    n2, rs2 = normalize(x2_ref[...].astype(F32))
+    da2 = mm_nt(du_ref[...], w1_ref[...])
+    da_ref[...] = (dm_ref[...].astype(F32) + norm_transpose(da2 * gains_ref[1:2], n2, rs2)).astype(BF16)
+
+
+def mlp_back(du, w1, dm, x2, gains):
+    rows, ff = du.shape
+    block = rows // 4
+
+    def cols(n):
+        return pl.BlockSpec((block, n), lambda i: (i, 0))
+
+    return pl.pallas_call(
+        mlp_back_body,
+        grid=(4,),
+        in_specs=[cols(ff), whole(w1.shape), cols(D), cols(D), whole((2, D))],
+        out_specs=cols(D),
+        out_shape=spec((rows, D)),
+        compiler_params=params(),
+        cost_estimate=lasts(13),
         name="mlp_back",
-    )(du, me, a2, w1, dx3, x2, gains, g_re, g_head, table)
-    return out[:n_out], out[n_out:]
+    )(du, w1, dm, x2, gains)
 
 
 def join_body(z_ref, w_ref, scale_ref, shift_ref, live_ref, out_ref, head_ref):
@@ -923,15 +980,18 @@
     if neighbours:
         pieces = line.run(lambda v: prepare(me, v, w_attn_out, w_fc1, w_fc2, w_reassemble, w_head, norm_gains, scale_table,
                                             shift_table), w_qkv)
-        zero = Gather(line, pieces[0], 5 * LANES, 1)
+        zero = Gather(pieces[0], 5 * LANES, 1, True)
     n1 = line.run(norm, x)
     if neighbours:
-        zero.over_first()
+        together(line, zero)
+        together(line, zero)
+        zero.between_cores()
+        one = Gather(line.after(pieces[1]), 9 * LANES, 1)
     down, g_shift_rows = line.run(bring_down, d_joined, lanes(live), lanes(flags))
     if neighbours:
-        zero.over_second()
-        f_qkv, small = line.run(lambda v: assemble(me, zero, [(D, 3 * D), (wide, SMALL, 3 * LANES)], [
+        f_qkv, small = line.run(lambda v: assemble(me, zero.starting(v), [(D, 3 * D), (wide, SMALL, 3 * LANES)], [
             (0, (0, r), (0, 3 * D // 2), rows_of(r), cols_of(3 * D // 2)), (1, (r, SMALL), (0, 3 * LANES), None, None)]), zero.pieces[0])
+        together(line, one)
 
         def table(lead, start, n):
             return small[:, :lead, start:start + n].transpose(1, 0, 2).reshape(lead, wide * n)
@@ -944,24 +1004,25 @@
     gains = gains.astype(F32)
     a1 = line.run(lambda n: (n * gains[0:1]).astype(BF16), n1)
     groups = []
-    if neighbours:
-        one = Gather(line, line.after(pieces[1]), 9 * LANES, 1)
     for i in range(GROUPS):
         groups.append(line.run(attention, a1, f_qkv, i))
-        if i == 0:
-            if neighbours:
-                one.over_first()
-                two = Gather(line, line.after(pieces[2]), ff // 32, 0)
+        if neighbours and i == 0:
+            together(line, one)
+            two = Gather(line.after(pieces[2]), ff // 32, 0)
+        if neighbours and i == 1:
+            one.terms = line.touch(*one.terms)
+            one.between_cores()
+            together(line, two)
+        if neighbours and i == 2:
+            together(line, two)
+        if i == 1:
             f_conv = gathered(line.after(conv_kernels), 1)
-        if neighbours and i == 1:
-            one.over_second()
-            two.over_first()
 
     def weights_one():
         if not neighbours:
             return gathered(w_attn_out, 0), gathered(w_fc1, 0), gathered(w_reassemble, 0), gathered(w_head, 0)
         rh, at = ch // 16, D // 2 + ff // 2
-        return line.run(lambda v: assemble(me, one, [(D, D), (D, ff), (D, ch), (ch, ch)], [
+        return line.run(lambda v: assemble(me, one.starting(v), [(D, D), (D, ff), (D, ch), (ch, ch)], [
             (0, (0, r), (0, D // 2), rows_of(r), cols_of(D // 2)),
             (1, (0, r), (D // 2, ff // 2), rows_of(r), cols_of(ff // 2)),
             (2, (0, r), (at, ch // 2), rows_of(r), cols_of(ch // 2)),
@@ -971,7 +1032,7 @@
         if not neighbours:
             return gathered(w_fc2, 0)
         n = ff // 16
-        return line.run(lambda v: assemble(me, two, [(ff, D)], [(0, (0, n), (0, D // 2), rows_of(n), cols_of(D // 2))])[0],
+        return line.run(lambda v: assemble(me, two.starting(v), [(ff, D)], [(0, (0, n), (0, D // 2), rows_of(n), cols_of(D // 2))])[0],
                         two.pieces[0])
 
     heads_out = [group[1] for group in groups]
@@ -979,11 +1040,12 @@
     scale = jnp.sum(onehot[:, :, None] * scales.astype(F32)[None], 1)[:, None]
     shift = (flags[:, None] * jnp.sum(onehot[:, :, None] * shifts.astype(F32)[None], 1))[:, None]
     f_out, f_fc1, f_re, f_head = weights_one()
+    x2, a2, u = line.run(lambda v: mlp_up(v, heads_out, f_out, f_fc1, gains), x)
     if neighbours:
-        two.over_second()
-    x2, a2, gg, slope = line.run(lambda v: mlp_up(v, heads_out, f_out, f_fc1, gains), x)
+        two.terms = line.touch(*two.terms)
+        two.between_cores()
     f_fc2 = weights_two()
-    x3b, tokens_out = line.run(mlp_down, gg, f_fc2, x2, live_count)
+    x3b, tokens_out = line.run(mlp_down, u, f_fc2, x2, live_count)
     t1, s1, t2, s2, zb = line.run(units, x3b, f_re, f_conv)
 
     def packed(split):
@@ -997,42 +1059,51 @@
             together(line, *jobs)
 
     hot = jnp.pad(onehot, ((0, 0), (0, SMALL - DATASETS)))[:, :, None]
-    g_conv, g_head, g_re, dx3, dm, small = line.run(
+    g_conv, g_head, g_re, dm, small = line.run(
         lambda v: units_back(v, scale, g_shift_rows, hot, zb, x3b, d_tokens_out.reshape(rows, D), live_count, f_head, f_conv, f_re,
                              t1, s1, t2, s2), down)
     s_conv = lax.psum_scatter(g_conv, "wide", scatter_dimension=1, tiled=True)
-    split_two = ff // 16
-    grads, du = line.run(lambda v: hidden_back(v, me, gg, slope, f_fc2, packed(split_two)), dm)
+    split_two, split_one = ff // 16, 7 * r
+    grads, du = line.run(lambda v: hidden_back(v, me, u, f_fc2, packed(split_two)), dm)
     c_two = chunk(grads, split_two)
-    split_one = 7 * r
-    grads, (dx2, da) = line.run(
-        lambda v: mlp_back(v, me, a2, f_fc1, dx3, x2, gains, g_re, g_head, small, packed(split_one)), du)
+    grads = line.run(lambda v: first_weight_back(v, me, a2, g_re, g_head, small, packed(split_one)), du)
     go(c_two)
     c_one = chunk(grads, split_one)
-
-    def attention_step(i, extra):
+    da = line.run(lambda v: mlp_back(v, f_fc1, dm, x2, gains), du)
+    go(c_two, c_one)
+
+    def attention_step(i, extra, split):
         qkv, o, e, rs = groups[i]
-        return line.run(lambda v: attention_back(v, me, i, qkv, o, e, rs, a1, f_out, extra, packed(None)), da)
-
-    grads, dqkv_0 = attention_step(0, heads_out)
-    go(c_two, c_one)
-    c_first = chunk(grads, None)
-    (g_second,), dqkv_1 = attention_step(1, None)
-    go(c_two, c_one, c_first)
+        return line.run(lambda v: attention_back(v, me, i, qkv, o, e, rs, a1, f_out, extra, packed(split)), da)
+
+    grads, dqkv_0 = attention_step(0, heads_out, ALL_XY)
     if neighbours:
+        z_two = Along(c_two)
+        together(line, z_two, c_one)
+        c_first = Single(line, grads[0], grads[1], XY)
+    else:
+        c_first = grads
+    (g_second,), dqkv_1 = attention_step(1, None, PLAIN)
+    split_last = 3 * r
+    if neighbours:
+        z_one = Along(c_one)
+        together(line, z_two, z_one, c_first)
         c_conv = Whole(s_conv)
-    grads, dqkv_2 = attention_step(2, g_second)
+        b_two = Back(line, z_two)
+    grads, dqkv_2 = attention_step(2, g_second, split_last)
     if neighbours:
-        together(line, c_one, c_first, c_conv)
-        early = Along(line, [c_two, c_one, c_first])
-    c_last = chunk(grads, None)
-    d_tokens = line.run(lambda v: input_back((dqkv_0, dqkv_1, v), f_qkv, dx2, x, gains), dqkv_2)
-    go(c_last)
+        together(line, z_one, c_first, c_conv)
+        b_one = Back(line, z_one)
+        c_last = Chunk(line, grads[0], grads[1], split_last)
+    else:
+        c_last = grads
     joined = line.run(join, zb, f_head, scale, shift, lanes(live))
-
     if neighbours:
-        together(line, c_last, early)
-        late = Along(line, [c_last])
+        together(line, c_last)
+    d_tokens = line.run(lambda v: input_back((dqkv_0, dqkv_1, v), f_qkv, da, x, gains), dqkv_2)
+
+    if neighbours:
+        together(line, c_last, c_first)
         s_conv = line.run_all(lambda p, q: p.astype(F32) + q.astype(F32), *c_conv.terms)
         rh, rows_two, half = ch // 16, ff // 16, D // 2
         blocks, n, quarter = half // LANES, ff // 2 // LANES, TABLE // 4
@@ -1049,19 +1120,22 @@
                 return at // 2 * D + WIDTH * i + at % 2 * LANES
             return col
 
-        together(line, late)
-        starts = [0, early.rows[0], early.rows[0] + early.rows[1]]
-        s_fc2, s_fc1, s_re, s_head, small, s_out = line.run(lambda m: finish(m, [early], [[
-            (0, rows_two, 0, blocks, up_to(rows_two), across(half)),
-            (1, r, starts[1], n, up_to(r), across(ff // 2)),
-            (2, r, starts[1] + r * n, 1, up_to(r), across(ch // 2)),
-            (3, rh, starts[1] + r * (n + 1), 1, up_to(rh), across(ch // 2)),
-            (4, quarter, starts[1] + r * (n + 1) + rh, 1, up_to(2 * quarter), lambda x, b: 0),
-            (5, r, starts[2] + r * blocks, blocks, up_to(r), across(half))]],
-            [w_fc2.shape, w_fc1.shape, w_reassemble.shape, w_head.shape, (TABLE, LANES), w_attn_out.shape]), me)
-        (s_qkv,) = finish(me, [early, late], [
-            [(0, r, starts[2], blocks, up_to(r), group_col(0))],
-            [(0, r, 0, blocks, up_to(r), group_col(2)), (0, r, r * blocks, blocks, up_to(r), group_col(1))]], [w_qkv.shape])
+        (s_fc2,) = line.run(lambda m: finish(m, [b_two], [[(0, rows_two, 0, blocks, up_to(rows_two), across(half))]],
+                                             [w_fc2.shape]), me)
+        z_last = Along(c_first, c_last)
+        together(line, z_last)
+        s_fc1, s_re, s_head, small = line.run(lambda m: finish(m, [b_one], [[
+            (0, r, 0, n, up_to(r), across(ff // 2)),
+            (1, r, r * n, 1, up_to(r), across(ch // 2)),
+            (2, rh, r * (n + 1), 1, up_to(rh), across(ch // 2)),
+            (3, quarter, r * (n + 1) + rh, 1, up_to(2 * quarter), lambda x, b: 0)]],
+            [w_fc1.shape, w_reassemble.shape, w_head.shape, (TABLE, LANES)]), me)
+        together(line, z_last)
+        late = Back(line, z_last)
+        s_qkv, s_out = finish(me, [late], [
+            [(0, r, 0, blocks, up_to(r), group_col(0)), (1, r, r * blocks, blocks, up_to(r), across(half)),
+             (0, r, 2 * r * blocks, blocks, up_to(r), group_col(2)), (0, r, 3 * r * blocks, blocks, up_to(r), group_col(1))]],
+            [w_qkv.shape, w_attn_out.shape])
         small = small.reshape(2, ch // LANES, SMALL, LANES).transpose(0, 2, 1, 3).reshape(2, SMALL, ch)
         small = lax.dynamic_slice(small, (0, 0, at_wide * t), (2, DATASETS, t))
         g_scale, g_shift = small[0], small[1]

time: 512 us -> 464 us (0.906)
  waiting for transfers between devices: 115 us -> 47.3 us
  starting transfers between devices: 59.1 us -> 73.6 us
  Pallas kernels: 275 us -> 262 us
  other arithmetic: 21.9 us -> 34.8 us
  local copies, waits for them, and re-layouts: 16.7 us -> 22.2 us
    ppermute x65 -> x56, waiting for transfers between devices: 115 us -> 44.8 us  [swap(): return lax.ppermute(value, BOTH, [(i, i ^ flip) for i in range(32)])]
    all_to_all x0 -> x5, starting transfers between devices: none -> 21.9 us  [along_z(): lax.all_to_all(parts, 'wide', 0, 0, tiled=True, axis_index_groups=groups)]
    add x13 -> x24, other arithmetic: 9.56 us -> 22.8 us  [the longest x5 7.58 us: add(): return [terms[0][part] + terms[1][part] for part in parts]]
    pallas_call x3 -> x4, Pallas kernels: 76.4 us -> 69.2 us  [the longest x1 25.7 us: units_back(): pl.pallas_call(units_back_body, grid=(2,), in_specs=[pl.BlockSpec(memory_...]
    ppermute x65 -> x56, starting transfers between devices: 58.5 us -> 51.4 us  [swap(): return lax.ppermute(value, BOTH, [(i, i ^ flip) for i in range(32)])]
  transfers between devices with their start and end apart: 67 -> 63, of which waited for: 16 -> 18; matrix products, arithmetic and copies ran while one was open for 5% -> 8% of each run, Pallas kernels for 38% -> 43%
where the time goes in v4:
time: 464 us; the launch traced here: 456 us
  Pallas kernels  262 us (56%)
  starting transfers between devices  73.6 us (16%)
  waiting for transfers between devices  47.3 us (10%)
  other arithmetic  34.8 us (7%)
  local copies, waits for them, and re-layouts  22.2 us (5%)
  between operations  16 us (3%)
    pallas_call x3, Pallas kernels, attention_back(): pl.pallas_call(body, grid=(images,), in_specs=[cols(D), pl.BlockSpec(memo...  56.3 us
    ppermute x56, starting transfers between devices, swap(): return lax.ppermute(value, BOTH, [(i, i ^ flip) for i in range(32)])  51.4 us
    ppermute x56, waiting for transfers between devices, swap(): return lax.ppermute(value, BOTH, [(i, i ^ flip) for i in range(32)])  44.8 us
    pallas_call x3, Pallas kernels, attention(): pl.pallas_call(attention_body, grid=(images,), in_specs=[cols(D)] + group...  33.7 us
    pallas_call x1, Pallas kernels, units_back(): pl.pallas_call(units_back_body, grid=(2,), in_specs=[pl.BlockSpec(memory_...  25.7 us
    all_to_all x5, starting transfers between devices, along_z(): lax.all_to_all(parts, 'wide', 0, 0, tiled=True, axis_index_groups=groups)  21.9 us
    pallas_call x3, Pallas kernels, assemble(): pl.pallas_call(body, grid=(1,), in_specs=[pl.BlockSpec(memory_space=pltpu...  20.7 us
    pallas_call x1, Pallas kernels, hidden_back(): pl.pallas_call(body, grid=(ff // block,), in_specs=[whole((rows, D)), pl....  19.3 us
  transfers between devices with their start and end apart: 63, of which 18 were waited for; matrix products, arithmetic and copies ran while one was open for 8% of the time, Pallas kernels for 43%

profile of v4, /device:TPU:0, one launch (start us, length us, event | category | flops | bytes accessed | tf_op | source)
XLA Modules:
  0.0 456.3 jit_solution(5846428234259604939)
XLA Ops:
  7.9 2.3 prepare.1
  10.2 5.0 %collective-permute-start.2 = (bf16[64,1152]{1,0:T(8,128)(2,1)}, bf16[64,1152]{1,0:T(8,128)(2,1)S(1)}, u32[]{:S(2)}, u32[]{:S(2)}) collective-permute-start(bf16[64,1152]{1,0:T(8,128)(2,1)} %get-tuple-element.174), channel_id=1, source_target_pairs={{0,6},{1,7},{2,4},{3,5},{4,2},{5,3},{6,0},{7,1},{8,14},{9,15},{10,... | collective-permute-start | bytes 442376 | tf_op jit(solution)/shard_map/ppermute | solution.py:64
  15.8 4.6 %norm.1 = f32[1152,768]{1,0:T(8,128)} custom-call(bf16[1152,768]{1,0:T(8,128)(2,1)} %bitcast.55), custom_call_target="tpu_custom_call" | custom-call | flops 5059999744 | tf_op jit(solution)/shard_map/norm/pallas_call | solution.py:442
  20.4 7.5 %collective-permute-done.1 = bf16[64,1152]{1,0:T(8,128)(2,1)S(1)} collective-permute-done((bf16[64,1152]{1,0:T(8,128)(2,1)}, bf16[64,1152]{1,0:T(8,128)(2,1)S(1)}, u32[]{:S(2)}, u32[]{:S(2)}) %collective-permute-start.1) | collective-permute-done | bytes 147488 | tf_op jit(solution)/shard_map/ppermute | solution.py:64
  28.1 1.6 collective-permute-start.3
  29.7 1.6 collective-permute-start.4
  31.3 5.6 %collective-permute-done.4 = bf16[4,64,512]{2,1,0:T(8,128)(2,1)S(1)} collective-permute-done((bf16[4,64,512]{2,1,0:T(8,128)(2,1)S(1)}, bf16[4,64,512]{2,1,0:T(8,128)(2,1)S(1)}, u32[]{:S(2)}, u32[]{:S(2)}) %collective-permute-start.4) | collective-permute-done | bytes 262176 | tf_op jit(solution)/shard_map/ppermute | solution.py:64
  37.0 1.6 collective-permute-start.5
  38.7 1.6 collective-permute-start.8
  41.9 4.2 all-to-all-start
  46.7 3.8 collective-permute-done.8.refs_5_
  53.3 8.6 %bring_down.1 = (f32[2,576,256]{2,1,0:T(8,128)}, f32[2,1,256]{2,1,0:T(1,128)}) custom-call(bf16[2,2304,256]{2,1,0:T(8,128)(2,1)} %dj_ref, f32[2,1,256]{2,1,0:T(1,128)} %broadcast_in_dim.13.live_ref, f32[2,1,256]{2,1,0:T(1,128)} %broadcast_in_dim.14.flag_ref), custom_call_target="tpu_custom_call" | custom-call | flops 10234999808 | tf_op jit(solution)/shard_map/bring_down/pallas_call | solution.py:492
  63.7 6.0 %assemble.3 = (bf16[768,2304]{1,0:T(8,128)(2,1)}, bf16[8,16,384]{2,1,0:T(8,128)(2,1)}) custom-call(s32[5]{0:T(128)} %stack.47.me_ref, bf16[8,64,640]{2,1,0:T(8,128)(2,1)} %copy-done.8, bf16[8,64,640]{2,1,0:T(8,128)(2,1)} %copy-done.15, bf16[8,64,640]{2,1,0:T(8,128)(2,1)} %copy-done.16, bf16[8,64,640]{2,1,0:T(8,128)(2,1)} %collective-permute-done.7.refs_3_, ...), custom_call_target="tpu_custom_call" | custom-call | tf_op jit(solution)/shard_map/assemble/pallas_call | solution.py:184
  70.4 1.8 slice.244
  72.2 1.8 slice.243
  74.0 1.5 collective-permute-start.12
  75.5 1.5 collective-permute-start.11
  77.1 1.5 multiply_convert_fusion.a1_ref
  78.6 11.1 %attention.3 = (bf16[1152,768]{1,0:T(8,128)(2,1)}, bf16[1152,256]{1,0:T(8,128)(2,1)}, bf16[8,576,576]{2,1,0:T(8,128)(2,1)}, f32[2,4,576]{2,1,0:T(4,128)}) custom-call(bf16[1152,768]{1,0:T(8,128)(2,1)} %multiply_convert_fusion.a1_ref, bf16[768,2304]{1,0:T(8,128)(2,1)} %get-tuple-element.190.wq_ref.wk_ref.wv_ref.refs_3_, ...), custom_call_target="tpu_custom_call" | custom-call | flops 12650000384 | tf_op jit(solution)/shard_map/attention/pallas_call | solution.py:533
  96.2 3.5 all-to-all-start.1
  100.0 11.3 %attention.4 = (bf16[1152,768]{1,0:T(8,128)(2,1)}, bf16[1152,256]{1,0:T(8,128)(2,1)}, bf16[8,576,576]{2,1,0:T(8,128)(2,1)}, f32[2,4,576]{2,1,0:T(4,128)}) custom-call(bf16[1152,768]{1,0:T(8,128)(2,1)} %multiply_convert_fusion.a1_ref, bf16[768,2304]{1,0:T(8,128)(2,1)} %get-tuple-element.190.wq_ref.wk_ref.wv_ref.refs_3_, ...), custom_call_target="tpu_custom_call" | custom-call | flops 12650000384 | tf_op jit(solution)/shard_map/attention/pallas_call | solution.py:533
  111.3 2.5 collective-permute-done.14.refs_5_
  113.7 2.4 collective-permute-done.13.refs_1_
  117.7 1.5 collective-permute-start.15
  119.7 4.2 collective-permute-done.16
  123.9 11.2 %attention.5 = (bf16[1152,768]{1,0:T(8,128)(2,1)}, bf16[1152,256]{1,0:T(8,128)(2,1)}, bf16[8,576,576]{2,1,0:T(8,128)(2,1)}, f32[2,4,576]{2,1,0:T(4,128)}) custom-call(bf16[1152,768]{1,0:T(8,128)(2,1)} %multiply_convert_fusion.a1_ref, bf16[768,2304]{1,0:T(8,128)(2,1)} %get-tuple-element.190.wq_ref.wk_ref.wv_ref.refs_3_, ...), custom_call_target="tpu_custom_call" | custom-call | flops 12650000384 | tf_op jit(solution)/shard_map/attention/pallas_call | solution.py:533
  135.3 1.6 collective-permute-start.22
  138.4 8.8 %assemble.4 = (bf16[768,768]{1,0:T(8,128)(2,1)}, bf16[768,3072]{1,0:T(8,128)(2,1)}, bf16[768,256]{1,0:T(8,128)(2,1)}, bf16[256,256]{1,0:T(8,128)(2,1)}) custom-call(s32[5]{0:T(128)} %stack.47.me_ref, bf16[8,48,1152]{2,1,0:T(8,128)(2,1)} %copy-done.4, bf16[8,48,1152]{2,1,0:T(8,128)(2,1)} %collective-permute-done.13.refs_1_, ...), custom_call_target="tpu_custom_call" | custom-call | tf_op jit(solution)/shard_map/assemble/pallas_call | solution.py:184
  147.3 13.0 %mlp_up.1 = (bf16[1152,768]{1,0:T(8,128)(2,1)}, bf16[1152,768]{1,0:T(8,128)(2,1)}, bf16[1152,3072]{1,0:T(8,128)(2,1)}) custom-call(bf16[1152,768]{1,0:T(8,128)(2,1)} %bitcast.56, bf16[1152,256]{1,0:T(8,128)(2,1)} %get-tuple-element.213.o0_ref.o_ref.refs_0_, bf16[1152,256]{1,0:T(8,128)(2,1)} %get-tuple-element.214.o1_ref.refs_1_.o_ref, ...), custom_call_target="tpu_custom_call" | custom-call | flops 20700000256 | tf_op jit(solution)/shard_map/mlp_up/pallas_call | solution.py:662
  165.7 5.9 %assemble.5.w2_ref = bf16[3072,768]{1,0:T(8,128)(2,1)} custom-call(s32[5]{0:T(128)} %stack.47.me_ref, bf16[8,96,384]{2,1,0:T(8,128)(2,1)} %copy-done.10, bf16[8,96,384]{2,1,0:T(8,128)(2,1)} %copy-done.17, bf16[8,96,384]{2,1,0:T(8,128)(2,1)} %copy-done.18, bf16[8,96,384]{2,1,0:T(8,128)(2,1)} %copy-done.19, bf16[8,96,384]{2,1,0:T(8,128)(2,1)} %copy-done.9, ...), custom_call_target="tpu_custom_call" | custom-call | tf_op jit(solution)/shard_map/assemble/pallas_call | solution.py:184
  171.6 11.5 %mlp_down.1 = (bf16[1152,768]{1,0:T(8,128)(2,1)}, bf16[1152,768]{1,0:T(8,128)(2,1)}) custom-call(bf16[1152,3072]{1,0:T(8,128)(2,1)} %get-tuple-element.224.u_ref, bf16[3072,768]{1,0:T(8,128)(2,1)} %assemble.5.w2_ref, bf16[1152,768]{1,0:T(8,128)(2,1)} %get-tuple-element.225.x2_ref, s32[1]{0:T(128)} %copy.52.count_ref), custom_call_target="tpu_custom_call" | custom-call | flops 12650000384 | tf_op jit(solution)/shard_map/mlp_down/pallas_call | solution.py:690
  183.1 18.3 %units.1 = (bf16[2,1152,256]{2,1,0:T(8,128)(2,1)}, bf16[2,1152,256]{2,1,0:T(8,128)(2,1)}, bf16[2,1152,256]{2,1,0:T(8,128)(2,1)}, bf16[2,1152,256]{2,1,0:T(8,128)(2,1)}, bf16[1152,256]{1,0:T(8,128)(2,1)}) custom-call(bf16[1152,768]{1,0:T(8,128)(2,1)} %get-tuple-element.227.x_ref.x3b_ref, bf16[768,256]{1,0:T(8,128)(2,1)} %get-tuple-element.228.wre_ref, ...), custom_call_target="tpu_custom_call" | custom-call | flops 20700000256 | tf_op jit(solution)/shard_map/units/pallas_call | solution.py:747
  201.4 25.7 %units_back.1 = (bf16[4,2304,256]{2,1,0:T(8,128)(2,1)}, bf16[256,256]{1,0:T(8,128)(2,1)}, bf16[768,256]{1,0:T(8,128)(2,1)}, bf16[1152,768]{1,0:T(8,128)(2,1)}, f32[64,128]{1,0:T(8,128)}) custom-call(f32[2,576,256]{2,1,0:T(8,128)} %get-tuple-element.232.down_ref, f32[2,1,256]{2,1,0:T(1,128)} %broadcast_in_dim.16.scale_ref, ...), custom_call_target="tpu_custom_call" | custom-call | flops 34500001792 | tf_op jit(solution)/shard_map/units_back/pallas_call | solution.py:813
  227.1 19.3 %hidden_back.1 = (bf16[16,576,128]{2,1,0:T(8,128)(2,1)}, bf16[16,576,128]{2,1,0:T(8,128)(2,1)}, bf16[1152,3072]{1,0:T(8,128)(2,1)}) custom-call(bf16[1152,768]{1,0:T(8,128)(2,1)} %get-tuple-element.239.dm_ref, s32[5]{0:T(128)} %stack.47.me_ref, bf16[1152,3072]{1,0:T(8,128)(2,1)} %get-tuple-element.224.u_ref, bf16[3072,768]{1,0:T(8,128)(2,1)} %assemble.5.w2_ref), custom_call_target="tpu_custom_call" | custom-call | flops 23000000512 | tf_op jit(solution)/shard_map/hidden_back/pallas_call | solution.py:844
  246.6 13.4 %first_weight_back.1 = (bf16[16,656,128]{2,1,0:T(8,128)(2,1)}, bf16[16,656,128]{2,1,0:T(8,128)(2,1)}) custom-call(bf16[1152,3072]{1,0:T(8,128)(2,1)} %get-tuple-element.253.du_ref, s32[5]{0:T(128)} %stack.47.me_ref, bf16[1152,768]{1,0:T(8,128)(2,1)} %get-tuple-element.245.a2_ref, bf16[768,256]{1,0:T(8,128)(2,1)} %get-tuple-element.246.gre_ref, ...), custom_call_target="tpu_custom_call" | custom-call | flops 14949999616 | tf_op jit(solution)/shard_map/first_weight_back/pallas_call | solution.py:882
  260.0 2.1 slice_add_fusion.10
  262.1 2.4 slice_add_fusion
  266.2 11.8 %mlp_back.1.da_ref.refs_4_ = bf16[1152,768]{1,0:T(8,128)(2,1)} custom-call(bf16[1152,3072]{1,0:T(8,128)(2,1)} %get-tuple-element.253.du_ref, bf16[768,3072]{1,0:T(8,128)(2,1)} %get-tuple-element.217.w1_ref, bf16[1152,768]{1,0:T(8,128)(2,1)} %get-tuple-element.239.dm_ref, bf16[1152,768]{1,0:T(8,128)(2,1)} %get-tuple-element.225.x2_ref, ...), custom_call_target="tpu_custom_call" | custom-call | flops 14949999616 | tf_op jit(solution)/shard_map/mlp_back/pallas_call | solution.py:909
  277.9 7.1 %collective-permute-done.29 = bf16[8,384,128]{2,1,0:T(8,128)(2,1)} collective-permute-done((bf16[8,384,128]{2,1,0:T(8,128)(2,1)}, bf16[8,384,128]{2,1,0:T(8,128)(2,1)}, u32[]{:S(2)}, u32[]{:S(2)}) %collective-permute-start.29) | collective-permute-done | bytes 786464 | tf_op jit(solution)/shard_map/ppermute | solution.py:64
  285.1 2.0 slice_add_fusion.22
  287.8 2.1 slice_add_fusion.8
  295.4 21.2 %attention_back.3 = (bf16[16,288,128]{2,1,0:T(8,128)(2,1)}, bf16[16,288,128]{2,1,0:T(8,128)(2,1)}, bf16[1152,768]{1,0:T(8,128)(2,1)}) custom-call(bf16[1152,768]{1,0:T(8,128)(2,1)} %mlp_back.1.da_ref.refs_4_, s32[5]{0:T(128)} %stack.47.me_ref, bf16[1152,768]{1,0:T(8,128)(2,1)} %get-tuple-element.261.qkv_ref, ...), custom_call_target="tpu_custom_call" | custom-call | flops 20700000256 | tf_op jit(solution)/shard_map/attention_back/pallas_call | solution.py:598
  319.7 3.7 all-to-all-start.2
  323.4 1.9 slice_add_fusion.14
  325.3 1.5 collective-permute-start.36
  327.6 16.9 %attention_back.4 = (bf16[768,768]{1,0:T(8,128)(2,1)}, bf16[1152,768]{1,0:T(8,128)(2,1)}) custom-call(bf16[1152,768]{1,0:T(8,128)(2,1)} %mlp_back.1.da_ref.refs_4_, s32[5]{0:T(128)} %stack.47.me_ref, bf16[1152,768]{1,0:T(8,128)(2,1)} %get-tuple-element.276.qkv_ref, bf16[1152,256]{1,0:T(8,128)(2,1)} %get-tuple-element.214.o1_ref.refs_1_.o_ref, ...), custom_call_target="tpu_custom_call" | custom-call | flops 20700000256 | tf_op jit(solution)/shard_map/attention_back/pallas_call | solution.py:598
  347.4 5.4 %all-to-all-start.3 = ((bf16[4,656,128]{2,1,0:T(8,128)(2,1)}), bf16[4,656,128]{2,1,0:T(8,128)(2,1)S(1)}, u32[]{:S(2)}, u32[]{:S(2)}) async-start(bf16[4,656,128]{2,1,0:T(8,128)(2,1)} %pad_maximum_fusion), calls=%async_computation.3 | async-start | bytes 1343488 | tf_op jit(solution)/shard_map/all_to_all | solution.py:80
  352.8 2.2 slice_add_fusion.6
  357.5 18.2 %attention_back.5 = (bf16[16,288,128]{2,1,0:T(8,128)(2,1)}, bf16[16,288,128]{2,1,0:T(8,128)(2,1)}, bf16[1152,768]{1,0:T(8,128)(2,1)}) custom-call(bf16[1152,768]{1,0:T(8,128)(2,1)} %mlp_back.1.da_ref.refs_4_, s32[5]{0:T(128)} %stack.47.me_ref, bf16[1152,768]{1,0:T(8,128)(2,1)} %get-tuple-element.288.qkv_ref, ...), custom_call_target="tpu_custom_call" | custom-call | flops 20700000256 | tf_op jit(solution)/shard_map/attention_back/pallas_call | solution.py:598
  378.2 1.7 collective-permute-start.49
  381.6 6.4 %join.1 = bf16[2,2304,256]{2,1,0:T(8,128)(2,1)} custom-call(bf16[1152,256]{1,0:T(8,128)(2,1)} %get-tuple-element.297.z_ref, bf16[256,256]{1,0:T(8,128)(2,1)} %get-tuple-element.211.whead_ref.w_ref, f32[2,1,256]{2,1,0:T(1,128)} %broadcast_in_dim.16.scale_ref, f32[2,1,256]{2,1,0:T(1,128)} %reshape_multiply_fusion.shift_ref, f32[2,1,256]{2,1,0:T(1,128)} %broadcast_in_dim.13.live_ref), custom_call_target="tpu_custom_call" | custom-call | flops 8049999872 | tf_op jit(solution)/shard_map/join/pallas_call | solution.py:938
  391.1 10.1 %input_back.1 = bf16[1152,768]{1,0:T(8,128)(2,1)} custom-call(bf16[1152,768]{1,0:T(8,128)(2,1)} %get-tuple-element.263.refs_0_, bf16[1152,768]{1,0:T(8,128)(2,1)} %get-tuple-element.278.refs_1_, bf16[1152,768]{1,0:T(8,128)(2,1)} %get-tuple-element.303.refs_2_, bf16[768,2304]{1,0:T(8,128)(2,1)} %get-tuple-element.190.wq_ref.wk_ref.wv_ref.refs_3_, ...), custom_call_target="tpu_custom_call" | custom-call | flops 10350000128 | tf_op jit(solution)/shard_map/input_back/pallas_call | solution.py:630
  406.4 1.9 collective-permute-start.45
  408.2 2.2 convert_add_fusion
  411.7 2.3 finish.3
  415.0 5.1 %all-to-all-start.4 = ((bf16[4,576,128]{2,1,0:T(8,128)(2,1)}), bf16[4,576,128]{2,1,0:T(8,128)(2,1)S(1)}, u32[]{:S(2)}, u32[]{:S(2)}) async-start(bf16[4,576,128]{2,1,0:T(8,128)(2,1)} %pad_maximum_fusion.3), calls=%async_computation.5 | async-start | bytes 1179648 | tf_op jit(solution)/shard_map/all_to_all | solution.py:80
  421.8 1.8 collective-permute-start.50
  423.6 4.0 collective-permute-done.52.refs_3_
  430.1 2.3 finish.4
  432.5 2.4 all-to-all-done.4
  437.1 1.5 collective-permute-start.53
  438.5 1.5 multiply_reduce_fusion
  440.7 1.7 collective-permute-done.55.refs_3_
  444.8 2.2 finish.5
  (260 shorter events, 67.6 us)
Async XLA Ops:
  10.2 10.2 %collective-permute-start.2 = (bf16[64,1152]{1,0:T(8,128)(2,1)}, bf16[64,1152]{1,0:T(8,128)(2,1)S(1)}, u32[]{:S(2)}, u32[]{:S(2)}) collective-permute-start(bf16[64,1152]{1,0:T(8,128)(2,1)} %get-tuple-element.174), channel_id=1, source_target_pairs={{0,6},{1,7},{2,4},{3,5},{4,2},{5,3},{6,0},{7,1},{8,14},{9,15},{10,... | collective-permute-start | bytes 442376 | tf_op jit(solution)/shard_map/ppermute | solution.py:64
  15.2 12.7 %collective-permute-start.1 = (bf16[64,1152]{1,0:T(8,128)(2,1)}, bf16[64,1152]{1,0:T(8,128)(2,1)S(1)}, u32[]{:S(2)}, u32[]{:S(2)}) collective-permute-start(bf16[64,1152]{1,0:T(8,128)(2,1)} %get-tuple-element.174), channel_id=1, source_target_pairs={{0,4},{1,5},{2,6},{3,7},{4,0},{5,1},{6,2},{7,3},{8,12},{9,13},{10,... | collective-permute-start | bytes 442376 | tf_op jit(solution)/shard_map/ppermute | solution.py:64
  15.2 12.7 %collective-permute-start = (bf16[64,1152]{1,0:T(8,128)(2,1)}, bf16[64,1152]{1,0:T(8,128)(2,1)S(1)}, u32[]{:S(2)}, u32[]{:S(2)}) collective-permute-start(bf16[64,1152]{1,0:T(8,128)(2,1)} %get-tuple-element.174), channel_id=1, source_target_pairs={{0,2},{1,3},{2,0},{3,1},{4,6},{5,7},{6,4},{7,5},{8,10},{9,11},{10,... | collective-permute-start | bytes 442376 | tf_op jit(solution)/shard_map/ppermute | solution.py:64
  28.1 8.8 %collective-permute-start.3 = (bf16[4,64,640]{2,1,0:T(8,128)(2,1)S(1)}, bf16[4,64,640]{2,1,0:T(8,128)(2,1)S(1)}, u32[]{:S(2)}, u32[]{:S(2)}) collective-permute-start(bf16[4,64,640]{2,1,0:T(8,128)(2,1)S(1)} %slice.321), channel_id=1, source_target_pairs={{0,8},{1,9},{2,10},{3,11},{4,12},{5,13},{6,14},{7,15},{8,0},{9,1},... | collective-permute-start | bytes 983048 | tf_op jit(solution)/shard_map/ppermute | solution.py:64
  29.7 7.1 %collective-permute-start.4 = (bf16[4,64,512]{2,1,0:T(8,128)(2,1)S(1)}, bf16[4,64,512]{2,1,0:T(8,128)(2,1)S(1)}, u32[]{:S(2)}, u32[]{:S(2)}) collective-permute-start(bf16[4,64,512]{2,1,0:T(8,128)(2,1)S(1)} %pad_maximum_fusion.4), channel_id=1, source_target_pairs={{0,16},{1,17},{2,18},{3,19},{4,20},{5,21},{6,22},{7,23},{8,24},{9,... | collective-permute-start | bytes 786440 | tf_op jit(solution)/shard_map/ppermute | solution.py:64
  37.0 14.9 %collective-permute-start.5 = (bf16[8,64,640]{2,1,0:T(8,128)(2,1)S(1)}, bf16[8,64,640]{2,1,0:T(8,128)(2,1)S(1)}, u32[]{:S(2)}, u32[]{:S(2)}) collective-permute-start(bf16[8,64,640]{2,1,0:T(8,128)(2,1)S(1)} %constant_dynamic-update-slice_fusion.refs_0_), channel_id=1, source_target_pairs={{0,16},{1,17},{2,18},{3,19},{4,20},{5,21},{6,22},{7,23},{8,24},{9,... | collective-permute-start | bytes 1966088 | tf_op jit(solution)/shard_map/ppermute | solution.py:64
  38.7 11.8 %collective-permute-start.8 = (bf16[8,64,512]{2,1,0:T(8,128)(2,1)S(1)}, bf16[8,64,512]{2,1,0:T(8,128)(2,1)S(1)}, u32[]{:S(2)}, u32[]{:S(2)}) collective-permute-start(bf16[8,64,512]{2,1,0:T(8,128)(2,1)S(1)} %constant_dynamic-update-slice_fusion.2.refs_4_), channel_id=1, source_target_pairs={{0,8},{1,9},{2,10},{3,11},{4,12},{5,13},{6,14},{7,15},{8,0},{9,1},... | collective-permute-start | bytes 1572872 | tf_op jit(solution)/shard_map/ppermute | solution.py:64
  41.9 28.6 %all-to-all-start = ((bf16[4,48,2176]{2,1,0:T(8,128)(2,1)}), bf16[4,48,2176]{2,1,0:T(8,128)(2,1)}, u32[]{:S(2)}, u32[]{:S(2)}) async-start(bf16[4,48,2176]{2,1,0:T(8,128)(2,1)} %broadcast_in_dim.12), calls=%async_computation | async-start | bytes 1671168 | tf_op jit(solution)/shard_map/all_to_all | solution.py:80
  46.1 15.9 %collective-permute-start.9 = (bf16[8,64,512]{2,1,0:T(8,128)(2,1)S(1)}, bf16[8,64,512]{2,1,0:T(8,128)(2,1)S(1)}, u32[]{:S(2)}, u32[]{:S(2)}) collective-permute-start(bf16[8,64,512]{2,1,0:T(8,128)(2,1)S(1)} %constant_dynamic-update-slice_fusion.2.refs_4_), channel_id=1, source_target_pairs={{0,1},{1,0},{2,3},{3,2},{4,5},{5,4},{6,7},{7,6},{8,9},{9,8},{10,11... | collective-permute-start | bytes 1572872 | tf_op jit(solution)/shard_map/ppermute | solution.py:64
  46.2 15.8 %collective-permute-start.6 = (bf16[8,64,640]{2,1,0:T(8,128)(2,1)S(1)}, bf16[8,64,640]{2,1,0:T(8,128)(2,1)S(1)}, u32[]{:S(2)}, u32[]{:S(2)}) collective-permute-start(bf16[8,64,640]{2,1,0:T(8,128)(2,1)S(1)} %constant_dynamic-update-slice_fusion.refs_0_), channel_id=1, source_target_pairs={{0,1},{1,0},{2,3},{3,2},{4,5},{5,4},{6,7},{7,6},{8,9},{9,8},{10,11... | collective-permute-start | bytes 1966088 | tf_op jit(solution)/shard_map/ppermute | solution.py:64
  50.5 11.5 %collective-permute-start.10 = (bf16[8,64,512]{2,1,0:T(8,128)(2,1)S(1)}, bf16[8,64,512]{2,1,0:T(8,128)(2,1)S(1)}, u32[]{:S(2)}, u32[]{:S(2)}) collective-permute-start(bf16[8,64,512]{2,1,0:T(8,128)(2,1)S(1)} %collective-permute-done.8.refs_5_), channel_id=1, source_target_pairs={{0,1},{1,0},{2,3},{3,2},{4,5},{5,4},{6,7},{7,6},{8,9},{9,8},{10,11... | collective-permute-start | bytes 1572872 | tf_op jit(solution)/shard_map/ppermute | solution.py:64
  51.9 11.7 %collective-permute-start.7 = (bf16[8,64,640]{2,1,0:T(8,128)(2,1)S(1)}, bf16[8,64,640]{2,1,0:T(8,128)(2,1)}, u32[]{:S(2)}, u32[]{:S(2)}) collective-permute-start(bf16[8,64,640]{2,1,0:T(8,128)(2,1)S(1)} %collective-permute-done.5.refs_1_), channel_id=1, source_target_pairs={{0,1},{1,0},{2,3},{3,2},{4,5},{5,4},{6,7},{7,6},{8,9},{9,8},{10,11... | collective-permute-start | bytes 1966088 | tf_op jit(solution)/shard_map/ppermute | solution.py:64
  74.0 15.7 %collective-permute-start.12 = (bf16[4,48,1024]{2,1,0:T(8,128)(2,1)}, bf16[4,48,1024]{2,1,0:T(8,128)(2,1)}, u32[]{:S(2)}, u32[]{:S(2)}) collective-permute-start(bf16[4,48,1024]{2,1,0:T(8,128)(2,1)} %slice.244), channel_id=1, source_target_pairs={{0,16},{1,17},{2,18},{3,19},{4,20},{5,21},{6,22},{7,23},{8,24},{9,... | collective-permute-start | bytes 1179656 | tf_op jit(solution)/shard_map/ppermute | solution.py:64
  75.5 14.2 %collective-permute-start.11 = (bf16[4,48,1152]{2,1,0:T(8,128)(2,1)}, bf16[4,48,1152]{2,1,0:T(8,128)(2,1)}, u32[]{:S(2)}, u32[]{:S(2)}) collective-permute-start(bf16[4,48,1152]{2,1,0:T(8,128)(2,1)} %slice.243), channel_id=1, source_target_pairs={{0,8},{1,9},{2,10},{3,11},{4,12},{5,13},{6,14},{7,15},{8,0},{9,1},... | collective-permute-start | bytes 1327112 | tf_op jit(solution)/shard_map/ppermute | solution.py:64
  92.9 26.8 %copy-start.4 = (bf16[8,48,1152]{2,1,0:T(8,128)(2,1)}, bf16[8,48,1152]{2,1,0:T(8,128)(2,1)S(1)}, u32[]{:S(2)}) copy-start(bf16[8,48,1152]{2,1,0:T(8,128)(2,1)S(1)} %constant_dynamic-update-slice_fusion.4.refs_0_) | copy-start | bytes 2654212
  94.3 19.5 %collective-permute-start.14 = (bf16[8,48,1024]{2,1,0:T(8,128)(2,1)S(1)}, bf16[8,48,1024]{2,1,0:T(8,128)(2,1)}, u32[]{:S(2)}, u32[]{:S(2)}) collective-permute-start(bf16[8,48,1024]{2,1,0:T(8,128)(2,1)S(1)} %constant_dynamic-update-slice_fusion.6.refs_4_), channel_id=1, source_target_pairs={{0,8},{1,9},{2,10},{3,11},{4,12},{5,13},{6,14},{7,15},{8,0},{9,1},... | collective-permute-start | bytes 2359304 | tf_op jit(solution)/shard_map/ppermute | solution.py:64
  94.8 21.3 %collective-permute-start.13 = (bf16[8,48,1152]{2,1,0:T(8,128)(2,1)S(1)}, bf16[8,48,1152]{2,1,0:T(8,128)(2,1)}, u32[]{:S(2)}, u32[]{:S(2)}) collective-permute-start(bf16[8,48,1152]{2,1,0:T(8,128)(2,1)S(1)} %constant_dynamic-update-slice_fusion.4.refs_0_), channel_id=1, source_target_pairs={{0,16},{1,17},{2,18},{3,19},{4,20},{5,21},{6,22},{7,23},{8,24},{9,... | collective-permute-start | bytes 2654216 | tf_op jit(solution)/shard_map/ppermute | solution.py:64
  96.2 19.9 %all-to-all-start.1 = ((bf16[4,192,384]{2,1,0:T(8,128)(2,1)}), bf16[4,192,384]{2,1,0:T(8,128)(2,1)S(1)}, u32[]{:S(2)}, u32[]{:S(2)}) async-start(bf16[4,192,384]{2,1,0:T(8,128)(2,1)} %broadcast_in_dim.15), calls=%async_computation.1 | async-start | bytes 1179648 | tf_op jit(solution)/shard_map/all_to_all | solution.py:80
  99.7 83.4 %all-gather.2.cloned.1.call-start = ((), (), s32[]{:S(2)}) async-start(), calls=%async_computation.6 | async-start | bytes 5308416 | tf_op jit(solution)/shard_map/all_gather | solution.py:965
  116.2 240.1 %reduce-scatter.2.cloned.1.call-start = ((), (), s32[]{:S(2)}) async-start(), calls=%async_computation.7 | async-start | bytes 5308416 | tf_op jit(solution)/shard_map/reduce_scatter | solution.py:1065
  116.2 7.7 %collective-permute-start.16 = (bf16[4,96,384]{2,1,0:T(8,128)(2,1)S(1)}, bf16[4,96,384]{2,1,0:T(8,128)(2,1)S(1)}, u32[]{:S(2)}, u32[]{:S(2)}) collective-permute-start(bf16[4,96,384]{2,1,0:T(8,128)(2,1)S(1)} %get-tuple-element.208), channel_id=1, source_target_pairs={{0,16},{1,17},{2,18},{3,19},{4,20},{5,21},{6,22},{7,23},{8,24},{9,... | collective-permute-start | bytes 884744 | tf_op jit(solution)/shard_map/ppermute | solution.py:64
  117.7 17.4 %collective-permute-start.15 = (bf16[4,96,384]{2,1,0:T(8,128)(2,1)S(1)}, bf16[4,96,384]{2,1,0:T(8,128)(2,1)S(1)}, u32[]{:S(2)}, u32[]{:S(2)}) collective-permute-start(bf16[4,96,384]{2,1,0:T(8,128)(2,1)S(1)} %get-tuple-element.206), channel_id=1, source_target_pairs={{0,8},{1,9},{2,10},{3,11},{4,12},{5,13},{6,14},{7,15},{8,0},{9,1},... | collective-permute-start | bytes 884744 | tf_op jit(solution)/shard_map/ppermute | solution.py:64
  119.2 17.8 %collective-permute-start.19 = (bf16[8,48,1024]{2,1,0:T(8,128)(2,1)S(1)}, bf16[8,48,1024]{2,1,0:T(8,128)(2,1)}, u32[]{:S(2)}, u32[]{:S(2)}) collective-permute-start(bf16[8,48,1024]{2,1,0:T(8,128)(2,1)S(1)} %constant_dynamic-update-slice_fusion.6.refs_4_), channel_id=1, source_target_pairs={{0,1},{1,0},{2,3},{3,2},{4,5},{5,4},{6,7},{7,6},{8,9},{9,8},{10,11... | collective-permute-start | bytes 2359304 | tf_op jit(solution)/shard_map/ppermute | solution.py:64
  119.2 19.2 %collective-permute-start.20 = (bf16[8,48,1024]{2,1,0:T(8,128)(2,1)}, bf16[8,48,1024]{2,1,0:T(8,128)(2,1)}, u32[]{:S(2)}, u32[]{:S(2)}) collective-permute-start(bf16[8,48,1024]{2,1,0:T(8,128)(2,1)} %collective-permute-done.14.refs_5_), channel_id=1, source_target_pairs={{0,1},{1,0},{2,3},{3,2},{4,5},{5,4},{6,7},{7,6},{8,9},{9,8},{10,11... | collective-permute-start | bytes 2359304 | tf_op jit(solution)/shard_map/ppermute | solution.py:64
  119.7 18.7 %collective-permute-start.17 = (bf16[8,48,1152]{2,1,0:T(8,128)(2,1)S(1)}, bf16[8,48,1152]{2,1,0:T(8,128)(2,1)}, u32[]{:S(2)}, u32[]{:S(2)}) collective-permute-start(bf16[8,48,1152]{2,1,0:T(8,128)(2,1)S(1)} %constant_dynamic-update-slice_fusion.4.refs_0_), channel_id=1, source_target_pairs={{0,1},{1,0},{2,3},{3,2},{4,5},{5,4},{6,7},{7,6},{8,9},{9,8},{10,11... | collective-permute-start | bytes 2654216 | tf_op jit(solution)/shard_map/ppermute | solution.py:64
  123.9 14.5 %collective-permute-start.18 = (bf16[8,48,1152]{2,1,0:T(8,128)(2,1)}, bf16[8,48,1152]{2,1,0:T(8,128)(2,1)}, u32[]{:S(2)}, u32[]{:S(2)}) collective-permute-start(bf16[8,48,1152]{2,1,0:T(8,128)(2,1)} %collective-permute-done.13.refs_1_), channel_id=1, source_target_pairs={{0,1},{1,0},{2,3},{3,2},{4,5},{5,4},{6,7},{7,6},{8,9},{9,8},{10,11... | collective-permute-start | bytes 2654216 | tf_op jit(solution)/shard_map/ppermute | solution.py:64
  135.3 25.0 %collective-permute-start.22 = (bf16[8,96,384]{2,1,0:T(8,128)(2,1)S(1)}, bf16[8,96,384]{2,1,0:T(8,128)(2,1)}, u32[]{:S(2)}, u32[]{:S(2)}) collective-permute-start(bf16[8,96,384]{2,1,0:T(8,128)(2,1)S(1)} %constant_dynamic-update-slice_fusion.10.refs_4_), channel_id=1, source_target_pairs={{0,8},{1,9},{2,10},{3,11},{4,12},{5,13},{6,14},{7,15},{8,0},{9,1},... | collective-permute-start | bytes 1769480 | tf_op jit(solution)/shard_map/ppermute | solution.py:64
  137.0 23.2 %collective-permute-start.21 = (bf16[8,96,384]{2,1,0:T(8,128)(2,1)S(1)}, bf16[8,96,384]{2,1,0:T(8,128)(2,1)S(1)}, u32[]{:S(2)}, u32[]{:S(2)}) collective-permute-start(bf16[8,96,384]{2,1,0:T(8,128)(2,1)S(1)} %constant_dynamic-update-slice_fusion.8.refs_0_), channel_id=1, source_target_pairs={{0,16},{1,17},{2,18},{3,19},{4,20},{5,21},{6,22},{7,23},{8,24},{9,... | collective-permute-start | bytes 1769480 | tf_op jit(solution)/shard_map/ppermute | solution.py:64
  160.3 3.4 collective-permute-start.23
  160.3 4.5 collective-permute-start.24
  160.8 4.2 collective-permute-start.25
  160.9 4.3 collective-permute-start.26
  246.4 13.6 %collective-permute-start.27 = (bf16[16,576,128]{2,1,0:T(8,128)(2,1)}, bf16[16,576,128]{2,1,0:T(8,128)(2,1)}, u32[]{:S(2)}, u32[]{:S(2)}) collective-permute-start(bf16[16,576,128]{2,1,0:T(8,128)(2,1)} %get-tuple-element.243), channel_id=1, source_target_pairs={{0,1},{1,0},{2,3},{3,2},{4,5},{5,4},{6,7},{7,6},{8,9},{9,8},{10,11... | collective-permute-start | bytes 7077896 | tf_op jit(solution)/shard_map/ppermute | solution.py:64
  264.5 20.5 %collective-permute-start.30 = (bf16[16,656,128]{2,1,0:T(8,128)(2,1)}, bf16[16,656,128]{2,1,0:T(8,128)(2,1)S(1)}, u32[]{:S(2)}, u32[]{:S(2)}) collective-permute-start(bf16[16,656,128]{2,1,0:T(8,128)(2,1)} %get-tuple-element.252), channel_id=1, source_target_pairs={{0,1},{1,0},{2,3},{3,2},{4,5},{5,4},{6,7},{7,6},{8,9},{9,8},{10,11... | collective-permute-start | bytes 8060936 | tf_op jit(solution)/shard_map/ppermute | solution.py:64
  264.9 13.0 %collective-permute-start.28 = (bf16[8,192,128]{2,1,0:T(8,128)(2,1)}, bf16[8,192,128]{2,1,0:T(8,128)(2,1)}, u32[]{:S(2)}, u32[]{:S(2)}) collective-permute-start(bf16[8,192,128]{2,1,0:T(8,128)(2,1)} %get-tuple-element.334), channel_id=1, source_target_pairs={{0,8},{1,9},{2,10},{3,11},{4,12},{5,13},{6,14},{7,15},{8,0},{9,1},... | collective-permute-start | bytes 1179656 | tf_op jit(solution)/shard_map/ppermute | solution.py:64
  265.4 19.6 %collective-permute-start.29 = (bf16[8,384,128]{2,1,0:T(8,128)(2,1)}, bf16[8,384,128]{2,1,0:T(8,128)(2,1)}, u32[]{:S(2)}, u32[]{:S(2)}) collective-permute-start(bf16[8,384,128]{2,1,0:T(8,128)(2,1)} %get-tuple-element.332), channel_id=1, source_target_pairs={{0,16},{1,17},{2,18},{3,19},{4,20},{5,21},{6,22},{7,23},{8,24},{9,... | collective-permute-start | bytes 2359304 | tf_op jit(solution)/shard_map/ppermute | solution.py:64
  287.0 29.6 %collective-permute-start.31 = (bf16[4,192,128]{2,1,0:T(8,128)(2,1)}, bf16[4,192,128]{2,1,0:T(8,128)(2,1)}, u32[]{:S(2)}, u32[]{:S(2)}) collective-permute-start(bf16[4,192,128]{2,1,0:T(8,128)(2,1)} %get-tuple-element.350), channel_id=1, source_target_pairs={{0,16},{1,17},{2,18},{3,19},{4,20},{5,21},{6,22},{7,23},{8,24},{9,... | collective-permute-start | bytes 589832 | tf_op jit(solution)/shard_map/ppermute | solution.py:64
  289.9 26.7 %collective-permute-start.32 = (bf16[4,384,128]{2,1,0:T(8,128)(2,1)}, bf16[4,384,128]{2,1,0:T(8,128)(2,1)}, u32[]{:S(2)}, u32[]{:S(2)}) collective-permute-start(bf16[4,384,128]{2,1,0:T(8,128)(2,1)} %get-tuple-element.342), channel_id=1, source_target_pairs={{0,8},{1,9},{2,10},{3,11},{4,12},{5,13},{6,14},{7,15},{8,0},{9,1},... | collective-permute-start | bytes 1179656 | tf_op jit(solution)/shard_map/ppermute | solution.py:64
  292.5 24.1 %collective-permute-start.34 = (bf16[8,320,128]{2,1,0:T(8,128)(2,1)}, bf16[8,320,128]{2,1,0:T(8,128)(2,1)}, u32[]{:S(2)}, u32[]{:S(2)}) collective-permute-start(bf16[8,320,128]{2,1,0:T(8,128)(2,1)} %get-tuple-element.328), channel_id=1, source_target_pairs={{0,16},{1,17},{2,18},{3,19},{4,20},{5,21},{6,22},{7,23},{8,24},{9,... | collective-permute-start | bytes 1966088 | tf_op jit(solution)/shard_map/ppermute | solution.py:64
  294.9 21.8 %collective-permute-start.33 = (bf16[8,336,128]{2,1,0:T(8,128)(2,1)}, bf16[8,336,128]{2,1,0:T(8,128)(2,1)S(1)}, u32[]{:S(2)}, u32[]{:S(2)}) collective-permute-start(bf16[8,336,128]{2,1,0:T(8,128)(2,1)} %get-tuple-element.330), channel_id=1, source_target_pairs={{0,8},{1,9},{2,10},{3,11},{4,12},{5,13},{6,14},{7,15},{8,0},{9,1},... | collective-permute-start | bytes 2064392 | tf_op jit(solution)/shard_map/ppermute | solution.py:64
  319.7 24.9 %all-to-all-start.2 = ((bf16[4,576,128]{2,1,0:T(8,128)(2,1)}), bf16[4,576,128]{2,1,0:T(8,128)(2,1)S(1)}, u32[]{:S(2)}, u32[]{:S(2)}) async-start(bf16[4,576,128]{2,1,0:T(8,128)(2,1)} %pad_maximum_fusion.2), calls=%async_computation.2 | async-start | bytes 1179648 | tf_op jit(solution)/shard_map/all_to_all | solution.py:80
  325.3 19.2 %collective-permute-start.36 = (bf16[4,320,128]{2,1,0:T(8,128)(2,1)}, bf16[4,320,128]{2,1,0:T(8,128)(2,1)S(1)}, u32[]{:S(2)}, u32[]{:S(2)}) collective-permute-start(bf16[4,320,128]{2,1,0:T(8,128)(2,1)} %get-tuple-element.346), channel_id=1, source_target_pairs={{0,8},{1,9},{2,10},{3,11},{4,12},{5,13},{6,14},{7,15},{8,0},{9,1},... | collective-permute-start | bytes 983048 | tf_op jit(solution)/shard_map/ppermute | solution.py:64
  326.8 17.7 %collective-permute-start.35 = (bf16[4,336,128]{2,1,0:T(8,128)(2,1)S(1)}, bf16[4,336,128]{2,1,0:T(8,128)(2,1)S(1)}, u32[]{:S(2)}, u32[]{:S(2)}) collective-permute-start(bf16[4,336,128]{2,1,0:T(8,128)(2,1)S(1)} %get-tuple-element.344), channel_id=1, source_target_pairs={{0,16},{1,17},{2,18},{3,19},{4,20},{5,21},{6,22},{7,23},{8,24},{9,... | collective-permute-start | bytes 1032200 | tf_op jit(solution)/shard_map/ppermute | solution.py:64
  327.6 16.9 %collective-permute-start.37 = (bf16[16,288,128]{2,1,0:T(8,128)(2,1)}, bf16[16,288,128]{2,1,0:T(8,128)(2,1)}, u32[]{:S(2)}, u32[]{:S(2)}) collective-permute-start(bf16[16,288,128]{2,1,0:T(8,128)(2,1)} %get-tuple-element.274), channel_id=1, source_target_pairs={{0,1},{1,0},{2,3},{3,2},{4,5},{5,4},{6,7},{7,6},{8,9},{9,8},{10,11... | collective-permute-start | bytes 3538952 | tf_op jit(solution)/shard_map/ppermute | solution.py:64
  347.4 28.4 %all-to-all-start.3 = ((bf16[4,656,128]{2,1,0:T(8,128)(2,1)}), bf16[4,656,128]{2,1,0:T(8,128)(2,1)S(1)}, u32[]{:S(2)}, u32[]{:S(2)}) async-start(bf16[4,656,128]{2,1,0:T(8,128)(2,1)} %pad_maximum_fusion), calls=%async_computation.3 | async-start | bytes 1343488 | tf_op jit(solution)/shard_map/all_to_all | solution.py:80
  355.0 20.8 %collective-permute-start.38 = (bf16[8,288,128]{2,1,0:T(8,128)(2,1)}, bf16[8,288,128]{2,1,0:T(8,128)(2,1)S(1)}, u32[]{:S(2)}, u32[]{:S(2)}) collective-permute-start(bf16[8,288,128]{2,1,0:T(8,128)(2,1)} %get-tuple-element.340), channel_id=1, source_target_pairs={{0,8},{1,9},{2,10},{3,11},{4,12},{5,13},{6,14},{7,15},{8,0},{9,1},... | collective-permute-start | bytes 1769480 | tf_op jit(solution)/shard_map/ppermute | solution.py:64
  356.3 19.5 %collective-permute-start.39 = (bf16[4,288,256]{2,1,0:T(8,128)(2,1)}, bf16[4,288,256]{2,1,0:T(8,128)(2,1)S(1)}, u32[]{:S(2)}, u32[]{:S(2)}) collective-permute-start(bf16[4,288,256]{2,1,0:T(8,128)(2,1)} %reduce-scatter.2.cloned.1.call-done), channel_id=1, source_target_pairs={{0,16},{1,17},{2,18},{3,19},{4,20},{5,21},{6,22},{7,23},{8,24},{9,... | collective-permute-start | bytes 1769480 | tf_op jit(solution)/shard_map/ppermute | solution.py:64
  377.5 10.5 %collective-permute-start.40 = (bf16[16,288,128]{2,1,0:T(8,128)(2,1)}, bf16[16,288,128]{2,1,0:T(8,128)(2,1)S(1)}, u32[]{:S(2)}, u32[]{:S(2)}) collective-permute-start(bf16[16,288,128]{2,1,0:T(8,128)(2,1)} %get-tuple-element.300), channel_id=1, source_target_pairs={{0,1},{1,0},{2,3},{3,2},{4,5},{5,4},{6,7},{7,6},{8,9},{9,8},{10,11... | collective-permute-start | bytes 3538952 | tf_op jit(solution)/shard_map/ppermute | solution.py:64
  378.2 32.3 %collective-permute-start.49 = (bf16[576,128]{1,0:T(8,128)(2,1)}, bf16[576,128]{1,0:T(8,128)(2,1)}, u32[]{:S(2)}, u32[]{:S(2)}) collective-permute-start(bf16[576,128]{1,0:T(8,128)(2,1)} %fusion.1.refs_0_), channel_id=1, source_target_pairs={{0,24},{1,25},{2,26},{3,27},{4,28},{5,29},{6,30},{7,31},{8,16},{9,... | collective-permute-start | bytes 442376 | tf_op jit(solution)/shard_map/ppermute | solution.py:64
  379.8 21.4 %collective-permute-start.43 = (bf16[4,288,128]{2,1,0:T(8,128)(2,1)}, bf16[4,288,128]{2,1,0:T(8,128)(2,1)}, u32[]{:S(2)}, u32[]{:S(2)}) collective-permute-start(bf16[4,288,128]{2,1,0:T(8,128)(2,1)} %get-tuple-element.348), channel_id=1, source_target_pairs={{0,16},{1,17},{2,18},{3,19},{4,20},{5,21},{6,22},{7,23},{8,24},{9,... | collective-permute-start | bytes 884744 | tf_op jit(solution)/shard_map/ppermute | solution.py:64
  381.1 25.2 %collective-permute-start.46 = (bf16[4,288,256]{2,1,0:T(8,128)(2,1)S(1)}, bf16[4,288,256]{2,1,0:T(8,128)(2,1)}, u32[]{:S(2)}, u32[]{:S(2)}) collective-permute-start(bf16[4,288,256]{2,1,0:T(8,128)(2,1)S(1)} %add.208), channel_id=1, source_target_pairs={{0,8},{1,9},{2,10},{3,11},{4,12},{5,13},{6,14},{7,15},{8,0},{9,1},... | collective-permute-start | bytes 1769480 | tf_op jit(solution)/shard_map/ppermute | solution.py:64
  388.8 13.7 %collective-permute-start.42 = (bf16[8,144,128]{2,1,0:T(8,128)(2,1)}, bf16[8,144,128]{2,1,0:T(8,128)(2,1)S(1)}, u32[]{:S(2)}, u32[]{:S(2)}) collective-permute-start(bf16[8,144,128]{2,1,0:T(8,128)(2,1)} %get-tuple-element.336), channel_id=1, source_target_pairs={{0,16},{1,17},{2,18},{3,19},{4,20},{5,21},{6,22},{7,23},{8,24},{9,... | collective-permute-start | bytes 884744 | tf_op jit(solution)/shard_map/ppermute | solution.py:64
  389.6 14.2 %collective-permute-start.41 = (bf16[8,144,128]{2,1,0:T(8,128)(2,1)S(1)}, bf16[8,144,128]{2,1,0:T(8,128)(2,1)S(1)}, u32[]{:S(2)}, u32[]{:S(2)}) collective-permute-start(bf16[8,144,128]{2,1,0:T(8,128)(2,1)S(1)} %get-tuple-element.338), channel_id=1, source_target_pairs={{0,8},{1,9},{2,10},{3,11},{4,12},{5,13},{6,14},{7,15},{8,0},{9,1},... | collective-permute-start | bytes 884744 | tf_op jit(solution)/shard_map/ppermute | solution.py:64
  401.2 9.2 %collective-permute-start.48 = (bf16[576,128]{1,0:T(8,128)(2,1)}, bf16[576,128]{1,0:T(8,128)(2,1)S(1)}, u32[]{:S(2)}, u32[]{:S(2)}) collective-permute-start(bf16[576,128]{1,0:T(8,128)(2,1)} %fusion.1.refs_0_), channel_id=1, source_target_pairs={{0,16},{1,17},{2,18},{3,19},{4,20},{5,21},{6,22},{7,23},{8,24},{9,... | collective-permute-start | bytes 442376 | tf_op jit(solution)/shard_map/ppermute | solution.py:64
  402.6 7.9 %collective-permute-start.47 = (bf16[576,128]{1,0:T(8,128)(2,1)}, bf16[576,128]{1,0:T(8,128)(2,1)S(1)}, u32[]{:S(2)}, u32[]{:S(2)}) collective-permute-start(bf16[576,128]{1,0:T(8,128)(2,1)} %fusion.1.refs_0_), channel_id=1, source_target_pairs={{0,8},{1,9},{2,10},{3,11},{4,12},{5,13},{6,14},{7,15},{8,0},{9,1},... | collective-permute-start | bytes 442376 | tf_op jit(solution)/shard_map/ppermute | solution.py:64
  403.8 10.2 %collective-permute-start.44 = (bf16[4,144,128]{2,1,0:T(8,128)(2,1)S(1)}, bf16[4,144,128]{2,1,0:T(8,128)(2,1)S(1)}, u32[]{:S(2)}, u32[]{:S(2)}) collective-permute-start(bf16[4,144,128]{2,1,0:T(8,128)(2,1)S(1)} %get-tuple-element.354), channel_id=1, source_target_pairs={{0,16},{1,17},{2,18},{3,19},{4,20},{5,21},{6,22},{7,23},{8,24},{9,... | collective-permute-start | bytes 442376 | tf_op jit(solution)/shard_map/ppermute | solution.py:64
  406.4 7.7 %collective-permute-start.45 = (bf16[4,144,128]{2,1,0:T(8,128)(2,1)S(1)}, bf16[4,144,128]{2,1,0:T(8,128)(2,1)S(1)}, u32[]{:S(2)}, u32[]{:S(2)}) collective-permute-start(bf16[4,144,128]{2,1,0:T(8,128)(2,1)S(1)} %get-tuple-element.352), channel_id=1, source_target_pairs={{0,8},{1,9},{2,10},{3,11},{4,12},{5,13},{6,14},{7,15},{8,0},{9,1},... | collective-permute-start | bytes 442376 | tf_op jit(solution)/shard_map/ppermute | solution.py:64
  415.0 19.9 %all-to-all-start.4 = ((bf16[4,576,128]{2,1,0:T(8,128)(2,1)}), bf16[4,576,128]{2,1,0:T(8,128)(2,1)S(1)}, u32[]{:S(2)}, u32[]{:S(2)}) async-start(bf16[4,576,128]{2,1,0:T(8,128)(2,1)} %pad_maximum_fusion.3), calls=%async_computation.5 | async-start | bytes 1179648 | tf_op jit(solution)/shard_map/all_to_all | solution.py:80
  420.1 7.5 %collective-permute-start.52 = (bf16[656,128]{1,0:T(8,128)(2,1)S(1)}, bf16[656,128]{1,0:T(8,128)(2,1)S(1)}, u32[]{:S(2)}, u32[]{:S(2)}) collective-permute-start(bf16[656,128]{1,0:T(8,128)(2,1)S(1)} %copy-done.29), channel_id=1, source_target_pairs={{0,24},{1,25},{2,26},{3,27},{4,28},{5,29},{6,30},{7,31},{8,16},{9,... | collective-permute-start | bytes 503816 | tf_op jit(solution)/shard_map/ppermute | solution.py:64
  420.4 8.4 %collective-permute-start.51 = (bf16[656,128]{1,0:T(8,128)(2,1)S(1)}, bf16[656,128]{1,0:T(8,128)(2,1)S(1)}, u32[]{:S(2)}, u32[]{:S(2)}) collective-permute-start(bf16[656,128]{1,0:T(8,128)(2,1)S(1)} %copy-done.29), channel_id=1, source_target_pairs={{0,16},{1,17},{2,18},{3,19},{4,20},{5,21},{6,22},{7,23},{8,24},{9,... | collective-permute-start | bytes 503816 | tf_op jit(solution)/shard_map/ppermute | solution.py:64
  421.8 7.1 %collective-permute-start.50 = (bf16[656,128]{1,0:T(8,128)(2,1)S(1)}, bf16[656,128]{1,0:T(8,128)(2,1)S(1)}, u32[]{:S(2)}, u32[]{:S(2)}) collective-permute-start(bf16[656,128]{1,0:T(8,128)(2,1)S(1)} %copy-done.29), channel_id=1, source_target_pairs={{0,8},{1,9},{2,10},{3,11},{4,12},{5,13},{6,14},{7,15},{8,0},{9,1},... | collective-permute-start | bytes 503816 | tf_op jit(solution)/shard_map/ppermute | solution.py:64
  435.0 7.4 %collective-permute-start.55 = (bf16[576,128]{1,0:T(8,128)(2,1)S(1)}, bf16[576,128]{1,0:T(8,128)(2,1)S(1)}, u32[]{:S(2)}, u32[]{:S(2)}) collective-permute-start(bf16[576,128]{1,0:T(8,128)(2,1)S(1)} %fusion.2.refs_0_), channel_id=1, source_target_pairs={{0,24},{1,25},{2,26},{3,27},{4,28},{5,29},{6,30},{7,31},{8,16},{9,... | collective-permute-start | bytes 442376 | tf_op jit(solution)/shard_map/ppermute | solution.py:64
  435.8 7.7 %collective-permute-start.54 = (bf16[576,128]{1,0:T(8,128)(2,1)S(1)}, bf16[576,128]{1,0:T(8,128)(2,1)S(1)}, u32[]{:S(2)}, u32[]{:S(2)}) collective-permute-start(bf16[576,128]{1,0:T(8,128)(2,1)S(1)} %fusion.2.refs_0_), channel_id=1, source_target_pairs={{0,16},{1,17},{2,18},{3,19},{4,20},{5,21},{6,22},{7,23},{8,24},{9,... | collective-permute-start | bytes 442376 | tf_op jit(solution)/shard_map/ppermute | solution.py:64
  437.1 6.4 %collective-permute-start.53 = (bf16[576,128]{1,0:T(8,128)(2,1)S(1)}, bf16[576,128]{1,0:T(8,128)(2,1)S(1)}, u32[]{:S(2)}, u32[]{:S(2)}) collective-permute-start(bf16[576,128]{1,0:T(8,128)(2,1)S(1)} %fusion.2.refs_0_), channel_id=1, source_target_pairs={{0,8},{1,9},{2,10},{3,11},{4,12},{5,13},{6,14},{7,15},{8,0},{9,1},... | collective-permute-start | bytes 442376 | tf_op jit(solution)/shard_map/ppermute | solution.py:64
  (47 other events, 430.9 us)
Sparse Core Ops, SparseCore 0:
  116.3 50.4 all-gather.1
  246.7 53.2 reduce-scatter.1
